TPU v7x, 32 devices: a whole 2x2x4 slice. The times are simulated.
32 devices in a mesh: seq: 4 (over y, core), head: 2 (over x), dp: 4 (over z).
Axes of the slice: x: 2, y: 2, z: 4, core: 2. Of those that a mesh axis runs over, the one named last changes fastest.
Arguments:
- queries: bfloat16 [4, 2048, 1024], P('dp', 'seq', 'head'), may hold values from -2 to 2
- keys: bfloat16 [4, 2048, 1024], P('dp', 'seq', 'head'), may hold values from -2 to 2
- values: bfloat16 [4, 2048, 1024], P('dp', 'seq', 'head'), may hold values from -6 to 6
- out_proj: bfloat16 [1024, 1024], P('head', 'dp'), may hold values from -0.1875 to 0.1875
- depth_proj: bfloat16 [1024, 1024], P(None, ('head', 'dp')), may hold values from -0.1875 to 0.1875
- code_table: bfloat16 [2, 1024, 1024], P(None, ('head', 'dp')), may hold values from -6 to 6
- code_ids: int32 [4, 2048, 2], P('dp', ('seq', 'head')), may hold values from 0 to 1023
- depth_cotangent: bfloat16 [4, 2048, 2, 1024], P('dp', ('seq', 'head')), may hold values from -6 to 6
Outputs:
- grad_queries: bfloat16 [4, 2048, 1024], P('dp', 'seq', 'head')
- grad_keys: bfloat16 [4, 2048, 1024], P('dp', 'seq', 'head')
- grad_values: bfloat16 [4, 2048, 1024], P('dp', 'seq', 'head')
- grad_out_proj: float32 [1024, 1024], P('head', 'dp')
All inputs are finite; a program needn't handle non-finite values.
Results may differ from a plain program's by a relative error of at most 0.024.
Values may be sent and summed in bfloat16 or wider, within the bound.
No kernel may reach another device: no remote copies, remote signals or barrier semaphores. Data moves between devices by JAX's collectives and lax.ppermute only.
A program may use at most 64 MiB of HBM per device.

v0:
```python
import jax
import jax.numpy as jnp
from jax import lax
from jax.sharding import PartitionSpec as P

DH = 128


def from_behind(block, axis, distance):
    devices = range(lax.axis_size(axis))
    route = [(i - distance, i) for i in devices if i - distance in devices]
    return lax.ppermute(block, axis, route)


def causal_mask(size):
    places = jnp.arange(size, dtype=jnp.int32)
    return (places[:, None] >= places[None, :]).astype(jnp.float32)


def depth_forward(carried, code_tab, proj_mat, code_rows):
    vocab_idx = jnp.arange(code_tab.shape[1], dtype=jnp.int32)
    level_outs = []
    for level_idx in range(code_tab.shape[0]):
        onehot = (code_rows[:, level_idx][:, None] == vocab_idx[None, :]).astype(jnp.bfloat16)
        embedded = jnp.dot(onehot, code_tab[level_idx], preferred_element_type=jnp.float32)
        summed = carried + embedded
        normed = (
            summed * lax.rsqrt(jnp.mean(summed * summed, axis=-1, keepdims=True) + 1e-05)
        ).astype(jnp.bfloat16)
        projected = jnp.dot(normed, proj_mat, preferred_element_type=jnp.float32)
        level_outs.append(projected)
        carried = summed + jax.nn.silu(projected)
    return jnp.stack(level_outs, axis=1)


def on_device(queries, keys, values, out_proj, depth_proj, code_table, code_ids, depth_cotangent):
    group_len = queries.shape[1]
    width_dev = queries.shape[2]
    heads_here = width_dev // DH
    att_scale = float(group_len * lax.axis_size("seq")) ** (-0.5)
    query_rows = queries[0].reshape(group_len, heads_here, DH)
    key_rows = keys[0].reshape(group_len, heads_here, DH)
    value_rows = values[0].reshape(group_len, heads_here, DH)
    causal = causal_mask(group_len)
    state_zero = jnp.zeros((heads_here, DH, DH), jnp.float32)
    state_local = jnp.einsum(
        "thd,the->hde", key_rows, value_rows, preferred_element_type=jnp.float32
    )
    state_acc = state_zero
    moving = state_local
    for hop_idx in range(lax.axis_size("seq") - 1):
        moving = from_behind(moving.astype(jnp.bfloat16), "seq", 1).astype(moving.dtype)
        state_acc = state_acc + moving
    state_in = state_acc.astype(jnp.bfloat16)
    scores = (
        jnp.einsum("thd,shd->hts", query_rows, key_rows, preferred_element_type=jnp.float32)
        * causal
    ).astype(jnp.bfloat16)
    attended = (
        att_scale
        * (
            jnp.einsum("hts,she->the", scores, value_rows, preferred_element_type=jnp.float32)
            + jnp.einsum("thd,hde->the", query_rows, state_in, preferred_element_type=jnp.float32)
        )
    ).astype(jnp.bfloat16)
    attended_flat = attended.reshape(group_len, width_dev)
    proj_full = lax.all_gather(out_proj, "dp", axis=1, tiled=True)
    mixed = lax.psum_scatter(
        jnp.dot(attended_flat, proj_full, preferred_element_type=jnp.float32).astype(jnp.bfloat16),
        "head",
        scatter_dimension=0,
        tiled=True,
    ).astype(jnp.float32)
    proj_mat, code_tab = (
        lax.all_gather(depth_proj, ("head", "dp"), axis=1, tiled=True),
        lax.all_gather(code_table, ("head", "dp"), axis=1, tiled=True),
    )
    code_rows = code_ids[0]
    cotangent = depth_cotangent[0].astype(jnp.float32)
    _, pullback = jax.vjp(
        lambda inputs: depth_forward(inputs, code_tab, proj_mat, code_rows), mixed
    )
    grad_mixed = pullback(cotangent)[0].astype(jnp.bfloat16)
    grad_block = lax.all_gather(grad_mixed, "head", axis=0, tiled=True)
    grad_att = lax.dot_general(
        grad_block, proj_full, (((1,), (1,)), ((), ())), preferred_element_type=jnp.float32
    )
    grad_rows = grad_att.astype(jnp.bfloat16).reshape(group_len, heads_here, DH)
    weight_term = lax.dot_general(
        attended_flat, grad_block, (((0,), (0,)), ((), ())), preferred_element_type=jnp.float32
    )
    weight_part = lax.psum_scatter(
        weight_term.astype(jnp.bfloat16), "dp", scatter_dimension=1, tiled=True
    )
    grad_out_proj = lax.psum(weight_part, "seq").astype(jnp.float32)
    back_local = jnp.einsum(
        "thd,the->hde", query_rows, grad_rows, preferred_element_type=jnp.float32
    )
    back_acc = state_zero
    moving_back = back_local
    for hop_idx in range(lax.axis_size("seq") - 1):
        moving_back = from_behind(moving_back.astype(jnp.bfloat16), "seq", -1).astype(
            moving_back.dtype
        )
        back_acc = back_acc + moving_back
    back_state = back_acc.astype(jnp.bfloat16)
    grad_scores = (
        jnp.einsum("the,she->hts", grad_rows, value_rows, preferred_element_type=jnp.float32)
        * causal
    ).astype(jnp.bfloat16)
    grad_query = att_scale * (
        jnp.einsum("hts,shd->thd", grad_scores, key_rows, preferred_element_type=jnp.float32)
        + jnp.einsum("the,hde->thd", grad_rows, state_in, preferred_element_type=jnp.float32)
    )
    grad_key = att_scale * (
        jnp.einsum("hts,thd->shd", grad_scores, query_rows, preferred_element_type=jnp.float32)
        + jnp.einsum("she,hde->shd", value_rows, back_state, preferred_element_type=jnp.float32)
    )
    grad_value = att_scale * (
        jnp.einsum("hts,the->she", scores, grad_rows, preferred_element_type=jnp.float32)
        + jnp.einsum("shd,hde->she", key_rows, back_state, preferred_element_type=jnp.float32)
    )
    out_shape = (1, group_len, width_dev)
    return (
        grad_query.reshape(out_shape).astype(jnp.bfloat16),
        grad_key.reshape(out_shape).astype(jnp.bfloat16),
        grad_value.reshape(out_shape).astype(jnp.bfloat16),
        grad_out_proj,
    )


def solution(mesh):
    in_specs = (
        P("dp", "seq", "head"),
        P("dp", "seq", "head"),
        P("dp", "seq", "head"),
        P("head", "dp"),
        P(None, ("head", "dp")),
        P(None, ("head", "dp"), None),
        P("dp", ("seq", "head"), None),
        P("dp", ("seq", "head"), None, None),
    )
    out_specs = (
        P("dp", "seq", "head"),
        P("dp", "seq", "head"),
        P("dp", "seq", "head"),
        P("head", "dp"),
    )
    return jax.shard_map(
        on_device, mesh=mesh, in_specs=in_specs, out_specs=out_specs, check_vma=False
    )
```

profile of v0, /device:TPU:0, one launch (start us, length us, event | category | flops | bytes accessed | tf_op | source)
XLA Modules:
  0.0 289.8 jit_solution(5207005634121219280)
XLA Ops:
  7.2 0.0 all-gather.7.cloned.1.call-start
  7.2 0.7 all-gather.7.cloned.1.call-update
  7.9 0.0 all-gather.5.cloned.1.call-start
  7.9 0.7 all-gather.5.cloned.1.call-update
  8.7 0.0 reduce-scatter.3.cloned.1.call-start
  8.7 1.2 reshape_squeeze.11
  9.9 1.4 reshape_squeeze.10
  11.3 0.3 copy.16
  11.6 0.3 convolution_convert_fusion.6
  11.9 2.4 collective-permute-start
  14.3 0.9 reshape_squeeze.9
  15.3 0.1 fusion.27
  15.4 5.4 %collective-permute-start.1 = (bf16[4,128,128]{2,1,0:T(8,128)(2,1)S(1)}, bf16[4,128,128]{2,1,0:T(8,128)(2,1)S(1)}, u32[]{:S(2)}, u32[]{:S(2)}) collective-permute-start(bf16[4,128,128]{2,1,0:T(8,128)(2,1)S(1)} %collective-permute-done), channel_id=1, source_target_pairs={{0,8},{8,16},{16,24},{1,9},{9,17},{17,25},{2,10},{10,18},{18,26},{... | collective-permute-start | bytes 393224 | tf_op jit(solution)/shard_map/ppermute | solution.py:12
  20.8 1.9 multiply_convert_fusion.1
  22.7 4.5 %collective-permute-start.2 = (bf16[4,128,128]{2,1,0:T(8,128)(2,1)S(1)}, bf16[4,128,128]{2,1,0:T(8,128)(2,1)S(1)}, u32[]{:S(2)}, u32[]{:S(2)}) collective-permute-start(bf16[4,128,128]{2,1,0:T(8,128)(2,1)S(1)} %collective-permute-done.1), channel_id=1, source_target_pairs={{0,8},{8,16},{16,24},{1,9},{9,17},{17,25},{2,10},{10,18},{18,26},{... | collective-permute-start | bytes 393224 | tf_op jit(solution)/shard_map/ppermute | solution.py:12
  27.2 0.8 convolution_bitcast_fusion.2
  28.0 0.1 collective-permute-done.2
  28.2 1.2 fusion.11
  29.3 13.2 %all-gather.7.cloned.1.call-done = bf16[512,1024]{1,0:T(8,128)(2,1)} async-done(((bf16[512,256]{1,0:T(8,128)(2,1)}), bf16[512,1024]{1,0:T(8,128)(2,1)}) %all-gather.7.cloned.1.call-update) | async-done | bytes 1048592 | tf_op jit(solution)/shard_map/all_gather | solution.py:67
  42.5 3.2 %convolution_convert_fusion.1 = bf16[512,1024]{1,0:T(8,128)(2,1)} fusion(bf16[512,512]{0,1:T(8,128)(2,1)} %bitcast.98, bf16[512,1024]{1,0:T(8,128)(2,1)} %all-gather.7.cloned.1.call-done), kind=kOutput, calls=%fused_computation.10 | convolution fusion | flops 537395200 | bytes 2621440 | tf_op jit(solution)/shard_map/dot_general | solution.py:69
  45.6 0.0 reduce-scatter.3.cloned.1.call-update
  45.7 0.0 all-gather.9.cloned.1.call-start
  45.7 0.5 all-gather.9.cloned.1.call-update
  46.2 0.0 all-gather.11.cloned.1.call-start
  46.3 2.6 copy.57
  48.9 45.0 %all-gather.5.cloned.1.call-done = bf16[1024,1024]{1,0:T(8,128)(2,1)} async-done(((bf16[1024,128]{1,0:T(8,128)(2,1)}), bf16[1024,1024]{1,0:T(8,128)(2,1)}) %all-gather.5.cloned.1.call-update) | async-done | bytes 2097168 | tf_op jit(solution)/shard_map/all_gather | solution.py:75
  93.9 3.3 %convolution_convert_fusion.3 = bf16[256,1024]{1,0:T(8,128)(2,1)} fusion(bf16[1024,1024]{1,0:T(8,128)(2,1)} %all-gather.5.cloned.1.call-done, bf16[256,2,1024]{2,0,1:T(8,128)(2,1)} %bitcast.96), kind=kOutput, calls=%fused_computation.36 | convolution fusion | flops 537133056 | bytes 3145728 | tf_op jit(solution)/shard_map/transpose(jvp())/dot_general | solution.py:30
  97.2 17.5 %reduce-scatter.3.cloned.1.call-done = bf16[256,1024]{1,0:T(8,128)(2,1)} async-done(((bf16[512,1024]{1,0:T(8,128)(2,1)}), bf16[256,1024]{1,0:T(8,128)(2,1)}) %reduce-scatter.3.cloned.1.call-update) | async-done | bytes 524304 | tf_op jit(solution)/shard_map/reduce_scatter | solution.py:68
  114.7 75.6 %all-gather.9.cloned.1.call-done = bf16[2,1024,1024]{2,1,0:T(8,128)(2,1)} async-done(((bf16[2,128,1024]{2,1,0:T(8,128)(2,1)}), bf16[2,1024,1024]{2,1,0:T(8,128)(2,1)}) %all-gather.9.cloned.1.call-update) | async-done | bytes 4194320 | tf_op jit(solution)/shard_map/all_gather | solution.py:76
  190.3 2.7 multiply_reduce_fusion.1
  193.0 0.8 fusion.28
  193.8 0.1 copy-done.19
  193.9 0.4 copy-done.17
  194.3 1.2 multiply_reduce_fusion
  195.5 0.0 copy-done.13
  195.5 1.2 fusion.18
  196.8 1.3 fusion.23
  198.1 0.0 all-gather.11.cloned.1.call-update
  198.1 0.0 reduce-scatter.5.cloned.1.call-start
  198.1 19.7 %all-gather.11.cloned.1.call-done = bf16[512,1024]{1,0:T(8,128)(2,1)} async-done(((bf16[256,1024]{1,0:T(8,128)(2,1)}), bf16[512,1024]{1,0:T(8,128)(2,1)}) %all-gather.11.cloned.1.call-update) | async-done | bytes 1048592 | tf_op jit(solution)/shard_map/all_gather | solution.py:84
  217.8 3.1 %convolution_convert_fusion = bf16[512,1024]{1,0:T(8,128)(2,1)} fusion(bf16[512,512]{0,1:T(8,128)(2,1)} %bitcast.99, bf16[512,1024]{1,0:T(8,128)(2,1)} %all-gather.11.cloned.1.call-done), kind=kOutput, calls=%fused_computation.9 | convolution fusion | flops 537395200 | bytes 2621440 | tf_op jit(solution)/shard_map/dot_general | solution.py:89
  220.9 0.0 reduce-scatter.5.cloned.1.call-update
  220.9 0.0 all-reduce.2.cloned.1.call-start
  221.0 2.3 convolution_convert_fusion.4
  223.3 0.3 fusion.15
  223.6 1.4 collective-permute-start.3
  225.1 1.4 fusion.49
  226.5 0.8 multiply_convert_fusion
  227.3 0.5 convolution_bitcast_fusion
  227.8 1.3 collective-permute-start.4
  229.1 0.8 convolution_bitcast_fusion.1
  230.0 3.2 %collective-permute-done.4 = bf16[4,128,128]{1,2,0:T(8,128)(2,1)} collective-permute-done((bf16[4,128,128]{1,2,0:T(8,128)(2,1)S(1)}, bf16[4,128,128]{1,2,0:T(8,128)(2,1)}, u32[]{:S(2)}, u32[]{:S(2)}) %collective-permute-start.4) | collective-permute-done | bytes 131104 | tf_op jit(solution)/shard_map/ppermute | solution.py:12
  233.2 1.3 collective-permute-start.5
  234.5 1.1 fusion.12
  235.6 2.1 copy.29
  237.7 2.4 collective-permute-done.5
  240.1 2.1 fusion.14
  242.2 6.0 %reduce-scatter.5.cloned.1.call-done = bf16[512,256]{1,0:T(8,128)(2,1)} async-done(((bf16[512,1024]{1,0:T(8,128)(2,1)}), bf16[512,256]{1,0:T(8,128)(2,1)}) %reduce-scatter.5.cloned.1.call-update) | async-done | bytes 262160 | tf_op jit(solution)/shard_map/reduce_scatter | solution.py:92
  248.2 0.0 all-reduce.2.cloned.1.call-update
  248.3 1.3 fusion.13
  249.6 1.0 copy.31
  250.6 1.0 copy.30
  251.6 29.6 %all-reduce.2.cloned.1.call-done = bf16[512,256]{1,0:T(8,128)(2,1)} async-done(((bf16[512,256]{1,0:T(8,128)(2,1)}), bf16[512,256]{1,0:T(8,128)(2,1)}) %all-reduce.2.cloned.1.call-update) | async-done | bytes 262160 | tf_op jit(solution)/shard_map/psum | solution.py:95
  281.2 1.8 convert_element_type.168
  (44 shorter events, 0.1 us)
Async XLA Ops:
  7.2 35.3 %all-gather.7.cloned.1.call-start = ((), (), s32[]{:S(2)}) async-start(), calls=%async_computation.3 | async-start | bytes 1310720 | tf_op jit(solution)/shard_map/all_gather | solution.py:67
  7.9 86.0 %all-gather.5.cloned.1.call-start = ((), (), s32[]{:S(2)}) async-start(), calls=%async_computation.2 | async-start | bytes 2359296 | tf_op jit(solution)/shard_map/all_gather | solution.py:75
  8.6 5.7 %copy-start.16 = (bf16[1,512,512]{2,1,0:T(8,128)(2,1)S(1)}, bf16[1,512,512]{2,1,0:T(8,128)(2,1)}, u32[]{:S(2)}) copy-start(bf16[1,512,512]{2,1,0:T(8,128)(2,1)} %param.8) | copy-start | bytes 1572868
  8.7 106.0 %reduce-scatter.3.cloned.1.call-start = ((), (), s32[]{:S(2)}) async-start(), calls=%async_computation.4 | async-start | bytes 1572864 | tf_op jit(solution)/shard_map/reduce_scatter | solution.py:68
  9.9 5.3 %copy-start = (bf16[512,4,128]{2,1,0:T(4,128)(2,1)}, bf16[512,4,128]{2,1,0:T(4,128)(2,1)S(1)}, u32[]{:S(2)}) copy-start(bf16[512,4,128]{2,1,0:T(4,128)(2,1)S(1)} %reshape_squeeze.11) | copy-start | bytes 1572868
  11.3 3.0 %copy-start.6 = (bf16[512,4,128]{2,1,0:T(4,128)(2,1)}, bf16[512,4,128]{2,1,0:T(4,128)(2,1)S(1)}, u32[]{:S(2)}) copy-start(bf16[512,4,128]{2,1,0:T(4,128)(2,1)S(1)} %reshape_squeeze.10) | copy-start | bytes 1572868
  11.6 2.7 copy-start.10
  11.9 3.5 %collective-permute-start = (bf16[4,128,128]{2,1,0:T(8,128)(2,1)S(1)}, bf16[4,128,128]{2,1,0:T(8,128)(2,1)S(1)}, u32[]{:S(2)}, u32[]{:S(2)}) collective-permute-start(bf16[4,128,128]{2,1,0:T(8,128)(2,1)S(1)} %convolution_convert_fusion.6), channel_id=1, source_target_pairs={{0,8},{8,16},{16,24},{1,9},{9,17},{17,25},{2,10},{10,18},{18,26},{... | collective-permute-start | bytes 393224 | tf_op jit(solution)/shard_map/ppermute | solution.py:12
  15.4 11.8 %copy-start.1 = (bf16[512,4,128]{2,1,0:T(4,128)(2,1)S(1)}, bf16[512,4,128]{2,1,0:T(4,128)(2,1)}, u32[]{:S(2)}) copy-start(bf16[512,4,128]{2,1,0:T(4,128)(2,1)} %copy-done) | copy-start | bytes 1572868
  15.4 7.3 %collective-permute-start.1 = (bf16[4,128,128]{2,1,0:T(8,128)(2,1)S(1)}, bf16[4,128,128]{2,1,0:T(8,128)(2,1)S(1)}, u32[]{:S(2)}, u32[]{:S(2)}) collective-permute-start(bf16[4,128,128]{2,1,0:T(8,128)(2,1)S(1)} %collective-permute-done), channel_id=1, source_target_pairs={{0,8},{8,16},{16,24},{1,9},{9,17},{17,25},{2,10},{10,18},{18,26},{... | collective-permute-start | bytes 393224 | tf_op jit(solution)/shard_map/ppermute | solution.py:12
  22.7 5.5 %copy-start.4 = (bf16[512,4,128]{2,1,0:T(4,128)(2,1)S(1)}, bf16[512,4,128]{2,1,0:T(4,128)(2,1)}, u32[]{:S(2)}) copy-start(bf16[512,4,128]{2,1,0:T(4,128)(2,1)} %reshape_squeeze.9) | copy-start | bytes 1572868
  22.7 5.4 %collective-permute-start.2 = (bf16[4,128,128]{2,1,0:T(8,128)(2,1)S(1)}, bf16[4,128,128]{2,1,0:T(8,128)(2,1)S(1)}, u32[]{:S(2)}, u32[]{:S(2)}) collective-permute-start(bf16[4,128,128]{2,1,0:T(8,128)(2,1)S(1)} %collective-permute-done.1), channel_id=1, source_target_pairs={{0,8},{8,16},{16,24},{1,9},{9,17},{17,25},{2,10},{10,18},{18,26},{... | collective-permute-start | bytes 393224 | tf_op jit(solution)/shard_map/ppermute | solution.py:12
  45.6 3.2 %copy-start.18 = (s32[1,256,2]{1,2,0:T(2,128)S(1)}, s32[1,256,2]{1,2,0:T(2,128)}, u32[]{:S(2)}) copy-start(s32[1,256,2]{1,2,0:T(2,128)} %param.14) | copy-start | bytes 6148
  45.7 144.7 %all-gather.9.cloned.1.call-start = ((), (), s32[]{:S(2)}) async-start(), calls=%async_computation.5 | async-start | bytes 4718592 | tf_op jit(solution)/shard_map/all_gather | solution.py:76
  46.2 171.6 %all-gather.11.cloned.1.call-start = ((), (), s32[]{:S(2)}) async-start(), calls=%async_computation.6 | async-start | bytes 1572864 | tf_op jit(solution)/shard_map/all_gather | solution.py:84
  190.3 2.7 copy-start.9
  190.3 3.6 %copy-start.19 = (bf16[2,1024,1024]{2,1,0:T(8,128)(2,1)S(1)}, bf16[2,1024,1024]{2,1,0:T(8,128)(2,1)}, u32[]{:S(2)}) copy-start(bf16[2,1024,1024]{2,1,0:T(8,128)(2,1)} %all-gather.9.cloned.1.call-done) | copy-start | bytes 12582916
  193.0 1.3 copy-start.17
  194.3 1.2 copy-start.13
  198.1 50.1 %reduce-scatter.5.cloned.1.call-start = ((), (), s32[]{:S(2)}) async-start(), calls=%async_computation.7 | async-start | bytes 1310720 | tf_op jit(solution)/shard_map/reduce_scatter | solution.py:92
  220.9 60.3 %all-reduce.2.cloned.1.call-start = ((), (), s32[]{:S(2)}) async-start(), calls=%async_computation.8 | async-start | bytes 524288 | tf_op jit(solution)/shard_map/psum | solution.py:95
  221.0 2.4 copy-start.5
  223.6 2.9 copy-start.2
  223.6 4.1 %collective-permute-start.3 = (bf16[4,128,128]{1,2,0:T(8,128)(2,1)S(1)}, bf16[4,128,128]{1,2,0:T(8,128)(2,1)S(1)}, u32[]{:S(2)}, u32[]{:S(2)}) collective-permute-start(bf16[4,128,128]{1,2,0:T(8,128)(2,1)S(1)} %fusion.15), channel_id=1, source_target_pairs={{8,0},{16,8},{24,16},{9,1},{17,9},{25,17},{10,2},{18,10},{26,18},{... | collective-permute-start | bytes 393224 | tf_op jit(solution)/shard_map/ppermute | solution.py:12
  227.3 1.8 copy-start.11
  227.8 7.8 %copy-start.14 = (bf16[4,128,128]{1,2,0:T(8,128)(2,1)}, bf16[4,128,128]{1,2,0:T(8,128)(2,1)S(1)}, u32[]{:S(2)}) copy-start(bf16[4,128,128]{1,2,0:T(8,128)(2,1)S(1)} %collective-permute-done.3) | copy-start | bytes 393220
  227.8 5.4 %collective-permute-start.4 = (bf16[4,128,128]{1,2,0:T(8,128)(2,1)S(1)}, bf16[4,128,128]{1,2,0:T(8,128)(2,1)}, u32[]{:S(2)}, u32[]{:S(2)}) collective-permute-start(bf16[4,128,128]{1,2,0:T(8,128)(2,1)S(1)} %collective-permute-done.3), channel_id=1, source_target_pairs={{8,0},{16,8},{24,16},{9,1},{17,9},{25,17},{10,2},{18,10},{26,18},{... | collective-permute-start | bytes 393224 | tf_op jit(solution)/shard_map/ppermute | solution.py:12
  229.9 10.1 %copy-start.7 = (bf16[512,4,128]{2,1,0:T(4,128)(2,1)S(1)}, bf16[512,4,128]{2,1,0:T(4,128)(2,1)}, u32[]{:S(2)}) copy-start(bf16[512,4,128]{2,1,0:T(4,128)(2,1)} %copy-done.6) | copy-start | bytes 1572868
  229.9 10.1 %copy-start.8 = (f32[4,128,512]{2,1,0:T(8,128)S(1)}, f32[4,128,512]{2,1,0:T(8,128)}, u32[]{:S(2)}) copy-start(f32[4,128,512]{2,1,0:T(8,128)} %fusion.49) | copy-start | bytes 3145732
  233.2 6.9 %collective-permute-start.5 = (bf16[4,128,128]{1,2,0:T(8,128)(2,1)}, bf16[4,128,128]{1,2,0:T(8,128)(2,1)}, u32[]{:S(2)}, u32[]{:S(2)}) collective-permute-start(bf16[4,128,128]{1,2,0:T(8,128)(2,1)} %collective-permute-done.4), channel_id=1, source_target_pairs={{8,0},{16,8},{24,16},{9,1},{17,9},{25,17},{10,2},{18,10},{26,18},{... | collective-permute-start | bytes 393224 | tf_op jit(solution)/shard_map/ppermute | solution.py:12
  235.6 12.7 %copy-start.3 = (bf16[512,4,128]{2,1,0:T(4,128)(2,1)S(1)}, bf16[512,4,128]{2,1,0:T(4,128)(2,1)}, u32[]{:S(2)}) copy-start(bf16[512,4,128]{2,1,0:T(4,128)(2,1)} %copy-done) | copy-start | bytes 1572868
  235.6 12.7 %copy-start.15 = (bf16[4,128,128]{1,2,0:T(8,128)(2,1)S(1)}, bf16[4,128,128]{1,2,0:T(8,128)(2,1)}, u32[]{:S(2)}) copy-start(bf16[4,128,128]{1,2,0:T(8,128)(2,1)} %copy-done.14) | copy-start | bytes 393220
  242.2 7.4 %copy-start.12 = (bf16[4,128,512]{2,1,0:T(8,128)(2,1)S(1)}, bf16[4,128,512]{2,1,0:T(8,128)(2,1)}, u32[]{:S(2)}) copy-start(bf16[4,128,512]{2,1,0:T(8,128)(2,1)} %fusion.14) | copy-start | bytes 1572868
Sparse Core Ops, SparseCore 0:
  9.6 32.8 all-gather.6
  44.5 49.3 all-gather.4
  96.2 18.4 reduce-scatter.2
  116.9 73.3 all-gather.8
  198.2 19.5 all-gather.10
  221.0 27.1 reduce-scatter.4
  250.5 30.6 all-reduce.1
where the time goes:
time: 290 us
  waiting for transfers between devices  214 us (74%)
  matrix products  30.2 us (10%)
  starting transfers between devices  16.5 us (6%)
  between operations  14.5 us (5%)
  local copies, waits for them, and re-layouts  11.1 us (4%)
  other arithmetic  3.22 us (1%)
    all_gather x1, waiting for transfers between devices, on_device(): lax.all_gather(code_table, ('head', 'dp'), axis=1, tiled=True)  75.6 us
    all_gather x1, waiting for transfers between devices, on_device(): lax.all_gather(depth_proj, ('head', 'dp'), axis=1, tiled=True)  45 us
    psum x1, waiting for transfers between devices, on_device(): grad_out_proj = lax.psum(weight_part, 'seq').astype(jnp.float32)  29.6 us
    all_gather x1, waiting for transfers between devices, on_device(): grad_block = lax.all_gather(grad_mixed, 'head', axis=0, tiled=True)  19.7 us
    reduce_scatter x1, waiting for transfers between devices, on_device(): lax.psum_scatter(jnp.dot(attended_flat, proj_full, preferred_element_type...  17.5 us
    ppermute x6, starting transfers between devices, from_behind(): return lax.ppermute(block, axis, route)  16.2 us
    all_gather x1, waiting for transfers between devices, on_device(): proj_full = lax.all_gather(out_proj, 'dp', axis=1, tiled=True)  13.2 us
    unnamed x44, local copies, waits for them, and re-layouts  7.31 us
  transfers between devices with their start and end apart: 13, of which 10 were waited for; matrix products, arithmetic and copies ran while one was open for 11% of the time, Pallas kernels for 0%

commit v1 on v0

v1 whole, which is shorter than its diff:
```python
import jax
import jax.numpy as jnp
from jax import lax
from jax.sharding import PartitionSpec as P

DH = 128
F32 = jnp.float32
BF16 = jnp.bfloat16


def swap(block, axis, mask):
    return lax.ppermute(block, axis, [(i, i ^ mask) for i in range(lax.axis_size(axis))])


def has_bit(index, bit):
    return lax.bitwise_and(index, jnp.int32(bit)) != 0


def in_order(pieces, index):
    pieces = list(pieces)
    bit = 1
    while bit < len(pieces):
        odd = has_bit(index, bit)
        pieces = [jnp.where(odd, pieces[j ^ bit], pieces[j]) for j in range(len(pieces))]
        bit *= 2
    return pieces


def pick(array, index, dim):
    return lax.dynamic_index_in_dim(array, index, dim, keepdims=False)


def exchange(block, axis):
    return [block] + [swap(block, axis, k) for k in range(1, lax.axis_size(axis))]


def dot(a, b, dims):
    return lax.dot_general(a, b, ((dims[0], dims[1]), ((), ())), preferred_element_type=F32)


def earlier_sum(state, backward):
    n_seq = lax.axis_size("seq")
    me = lax.axis_index("seq")
    before = jnp.zeros_like(state)
    total = state
    bit = 1
    while bit < n_seq:
        got = swap(total.astype(BF16), "seq", bit).astype(F32)
        mine = has_bit(me, bit)
        takes = jnp.logical_not(mine) if backward else mine
        before = before + jnp.where(takes, got, 0.0)
        total = total + got
        bit *= 2
    return before.astype(BF16)


def on_device(queries, keys, values, out_proj, depth_proj, code_table, code_ids, depth_cotangent):
    n_seq, n_head, n_dp = (lax.axis_size(a) for a in ("seq", "head", "dp"))
    me_seq, me_head, me_dp = (lax.axis_index(a) for a in ("seq", "head", "dp"))
    group_len, width_dev = queries.shape[1:]
    heads_here = width_dev // DH
    tokens = group_len // n_head
    n_far = n_seq // 2
    me_core = lax.bitwise_and(me_seq, jnp.int32(1))
    me_far = lax.shift_right_logical(me_seq, jnp.int32(1))
    lane = me_core * n_far + me_far
    att_scale = float(group_len * n_seq) ** (-0.5)
    width = code_table.shape[2]
    wide = width // n_seq
    far = [2 * m for m in range(n_far)]

    def far_exchange(block):
        return [block] + [swap(block, "seq", m) for m in far[1:]]

    def seq_lanes(block):
        near = jnp.stack(in_order(far_exchange(block), me_far))
        both = in_order([near, swap(near, "seq", 1)], me_core)
        return jnp.concatenate(both, axis=0)

    ids = code_ids[0].T
    ids_far = jnp.stack(far_exchange(ids))
    ids_rel = jnp.stack([ids_far, swap(ids_far, "seq", 1)])

    table = lax.dynamic_slice_in_dim(code_table, lane * wide, wide, axis=2)
    rows_dev = table.shape[1]
    embedded = []
    row_no = []
    for k_head in range(n_head):
        for k_dp in range(n_dp):
            owner = (me_head ^ k_head) * n_dp + (me_dp ^ k_dp)
            row_no.append(owner * rows_dev + jnp.arange(rows_dev, dtype=jnp.int32))
    row_no = jnp.concatenate(row_no)
    for level in range(table.shape[0]):
        part = jnp.concatenate(exchange(table[level], "dp"), axis=0)
        part = jnp.concatenate(exchange(part, "head"), axis=0)
        level_ids = ids_rel[:, :, level].reshape(-1)
        onehot = (level_ids[:, None] == row_no[None, :]).astype(BF16)
        rel = dot(onehot, part, ((1,), (0,))).astype(BF16).reshape(2, n_far, tokens, wide)
        mine = [rel[:, 0]] + [swap(rel[:, m // 2], "seq", m) for m in far[1:]]
        near = jnp.stack([block[0] for block in mine])
        other = swap(jnp.stack([block[1] for block in mine]), "seq", 1)
        near = jnp.stack(in_order(list(near), me_far))
        other = jnp.stack(in_order(list(other), me_far))
        lanes = jnp.concatenate(in_order([near, other], me_core), axis=0)
        embedded.append(lanes.transpose(1, 0, 2).reshape(tokens, width))

    out_rows = out_proj.shape[0] // n_seq
    out_lane = lax.dynamic_slice_in_dim(out_proj, lane * out_rows, out_rows, axis=0)
    out_part = jnp.concatenate(in_order(exchange(out_lane, "dp"), me_dp), axis=1)
    out_part = jnp.stack(in_order(exchange(out_part, "head"), me_head))
    out_full = seq_lanes(out_part).transpose(1, 0, 2, 3).reshape(n_head * width_dev, width)

    depth_rows = depth_proj.shape[0] // n_seq
    depth_lane = lax.dynamic_slice_in_dim(depth_proj, lane * depth_rows, depth_rows, axis=0)
    depth_part = jnp.concatenate(in_order(exchange(depth_lane, "dp"), me_dp), axis=1)
    depth_part = jnp.concatenate(in_order(exchange(depth_part, "head"), me_head), axis=1)
    proj_mat = seq_lanes(depth_part).reshape(width, width)

    query_rows = queries[0].reshape(group_len, heads_here, DH)
    key_rows = keys[0].reshape(group_len, heads_here, DH)
    value_rows = values[0].reshape(group_len, heads_here, DH)
    places = jnp.arange(group_len, dtype=jnp.int32)
    causal = (places[:, None] >= places[None, :]).astype(F32)
    state_local = jnp.einsum("thd,the->hde", key_rows, value_rows, preferred_element_type=F32)
    state_in = earlier_sum(state_local, False)
    scores = (
        jnp.einsum("thd,shd->hts", query_rows, key_rows, preferred_element_type=F32) * causal
    ).astype(BF16)
    attended = (
        att_scale
        * (
            jnp.einsum("hts,she->the", scores, value_rows, preferred_element_type=F32)
            + jnp.einsum("thd,hde->the", query_rows, state_in, preferred_element_type=F32)
        )
    ).astype(BF16)
    attended = attended.reshape(n_head, tokens, width_dev)
    att_all = [pick(attended, me_head, 0)]
    att_all += [swap(pick(attended, me_head ^ k, 0), "head", k) for k in range(1, n_head)]
    att_all = jnp.concatenate(in_order(att_all, me_head), axis=1)
    mixed = dot(att_all, out_full, ((1,), (0,)))

    cot = depth_cotangent[0]
    n_level = cot.shape[1]
    carried = mixed
    kept = []
    for level in range(n_level):
        summed = carried + embedded[level].astype(F32)
        inv = lax.rsqrt(jnp.mean(summed * summed, axis=-1, keepdims=True) + 1e-05)
        if level < n_level - 1:
            projected = dot((summed * inv).astype(BF16), proj_mat, ((1,), (0,)))
            carried = summed + projected * jax.nn.sigmoid(projected)
        else:
            projected = None
        kept.append((summed, inv, projected))
    grad = None
    for level in reversed(range(n_level)):
        summed, inv, projected = kept[level]
        grad_proj = cot[:, level, :]
        if grad is not None:
            gate = jax.nn.sigmoid(projected)
            slope = gate * (1.0 + projected * (1.0 - gate))
            grad_proj = (grad_proj.astype(F32) + grad * slope).astype(BF16)
        grad_normed = dot(grad_proj, proj_mat, ((1,), (1,)))
        along = jnp.mean(grad_normed * summed, axis=-1, keepdims=True)
        grad_sum = grad_normed * inv - summed * (along * inv * inv * inv)
        grad = grad_sum if grad is None else grad + grad_sum
    grad_mixed = grad.astype(BF16)

    out_heads = out_full.reshape(n_head, width_dev, width)
    grad_rows = []
    for k in range(1, n_head):
        part = dot(grad_mixed, pick(out_heads, me_head ^ k, 0), ((1,), (1,))).astype(BF16)
        grad_rows.append(swap(part, "head", k))
    own_part = dot(grad_mixed, pick(out_heads, me_head, 0), ((1,), (1,))).astype(BF16)
    grad_rows = jnp.concatenate(in_order([own_part] + grad_rows, me_head), axis=0)
    grad_rows = grad_rows.reshape(group_len, heads_here, DH)

    rows = width_dev // n_seq
    att_lanes = att_all.reshape(tokens, n_head, 2, n_far, rows)

    def term(core):
        part = pick(att_lanes, core, 2).reshape(tokens, n_head * n_far * rows)
        return dot(part, grad_mixed, ((0,), (0,)))

    got = swap(term(1 - me_core).astype(BF16), "seq", 1)
    chip = term(me_core) + got.astype(F32)
    chip = chip.reshape(n_head, n_far, rows, width)
    total = pick(pick(chip, me_head, 0), me_far, 0)
    for m in far:
        for k in range(n_head):
            if m or k:
                piece = pick(pick(chip, me_head ^ k, 0), me_far ^ (m // 2), 0).astype(BF16)
                mask = m * n_head + k
                total = total + swap(piece, ("seq", "head"), mask).astype(F32)
    columns = total.reshape(rows, n_dp, width // n_dp)
    block = pick(columns, me_dp, 1)
    for k in range(1, n_dp):
        block = block + swap(pick(columns, me_dp ^ k, 1).astype(BF16), "dp", k).astype(F32)
    grad_out_proj = seq_lanes(block.astype(BF16)).reshape(width_dev, width // n_dp).astype(F32)

    back_local = jnp.einsum("thd,the->hde", query_rows, grad_rows, preferred_element_type=F32)
    back_state = earlier_sum(back_local, True)
    grad_scores = (
        jnp.einsum("the,she->hts", grad_rows, value_rows, preferred_element_type=F32) * causal
    ).astype(BF16)
    grad_query = att_scale * (
        jnp.einsum("hts,shd->thd", grad_scores, key_rows, preferred_element_type=F32)
        + jnp.einsum("the,hde->thd", grad_rows, state_in, preferred_element_type=F32)
    )
    grad_key = att_scale * (
        jnp.einsum("hts,thd->shd", grad_scores, query_rows, preferred_element_type=F32)
        + jnp.einsum("she,hde->shd", value_rows, back_state, preferred_element_type=F32)
    )
    grad_value = att_scale * (
        jnp.einsum("hts,the->she", scores, grad_rows, preferred_element_type=F32)
        + jnp.einsum("shd,hde->she", key_rows, back_state, preferred_element_type=F32)
    )
    out_shape = (1, group_len, width_dev)
    return (
        grad_query.reshape(out_shape).astype(BF16),
        grad_key.reshape(out_shape).astype(BF16),
        grad_value.reshape(out_shape).astype(BF16),
        grad_out_proj,
    )


def solution(mesh):
    in_specs = (
        P("dp", "seq", "head"),
        P("dp", "seq", "head"),
        P("dp", "seq", "head"),
        P("head", "dp"),
        P(None, ("head", "dp")),
        P(None, ("head", "dp"), None),
        P("dp", ("seq", "head"), None),
        P("dp", ("seq", "head"), None, None),
    )
    out_specs = (
        P("dp", "seq", "head"),
        P("dp", "seq", "head"),
        P("dp", "seq", "head"),
        P("head", "dp"),
    )
    return jax.shard_map(
        on_device, mesh=mesh, in_specs=in_specs, out_specs=out_specs, check_vma=False
    )
```

time: 290 us -> 184 us (0.63)
  waiting for transfers between devices: 214 us -> 29.6 us
  local copies, waits for them, and re-layouts: 11.1 us -> 57.4 us
  starting transfers between devices: 16.5 us -> 42.2 us
  other arithmetic: 3.22 us -> 25.9 us
  between operations: 14.5 us -> 1.56 us
  matrix products: 30.2 us -> 26.1 us
    all_gather x4 -> x0, waiting for transfers between devices: 154 us -> none  [the longest x1 75.6 us: on_device(): lax.all_gather(code_table, ('head', 'dp'), axis=1, tiled=True)]
    psum x1 -> x0, waiting for transfers between devices: 29.6 us -> none  [on_device(): grad_out_proj = lax.psum(weight_part, 'seq').astype(jnp.float32)]
    ppermute x6 -> x41, starting transfers between devices: 16.2 us -> 42.2 us  [swap(): lax.ppermute(block, axis, [(i, i ^ mask) for i in range(lax.axis_size(axi...]
    ppermute x6 -> x41, waiting for transfers between devices: 5.76 us -> 29.6 us  [swap(): lax.ppermute(block, axis, [(i, i ^ mask) for i in range(lax.axis_size(axi...]
    reduce_scatter x2 -> x0, waiting for transfers between devices: 23.5 us -> none  [the longest x1 17.5 us: on_device(): lax.psum_scatter(jnp.dot(attended_flat, proj_full, preferred_element_type...]
    unnamed x44 -> x118, local copies, waits for them, and re-layouts: 7.31 us -> 28.4 us
    reshape x0 -> x6, local copies, waits for them, and re-layouts: none -> 11.1 us  [the longest x2 3.52 us: term(): part = pick(att_lanes, core, 2).reshape(tokens, n_head * n_far * rows)]
    concatenate x0 -> x11, other arithmetic: none -> 8.03 us  [the longest x2 2.32 us: on_device(): part = jnp.concatenate(exchange(table[level], 'dp'), axis=0)]
  transfers between devices with their start and end apart: 13 -> 41, of which waited for: 10 -> 12; matrix products, arithmetic and copies ran while one was open for 11% -> 52% of each run, Pallas kernels for 0% -> 0%
where the time goes in v1:
time: 184 us; the launch traced here: 183 us
  local copies, waits for them, and re-layouts  57.4 us (31%)
  starting transfers between devices  42.2 us (23%)
  waiting for transfers between devices  29.6 us (16%)
  matrix products  26.1 us (14%)
  other arithmetic  25.9 us (14%)
    ppermute x41, starting transfers between devices, swap(): lax.ppermute(block, axis, [(i, i ^ mask) for i in range(lax.axis_size(axi...  42.2 us
    ppermute x41, waiting for transfers between devices, swap(): lax.ppermute(block, axis, [(i, i ^ mask) for i in range(lax.axis_size(axi...  29.6 us
    unnamed x118, local copies, waits for them, and re-layouts  28.4 us
    dot_general x10, matrix products, dot(): lax.dot_general(a, b, ((dims[0], dims[1]), ((), ())), preferred_element_t...  11 us
    select_n x13, other arithmetic, in_order(): jnp.where(odd, pieces[j ^ bit], pieces[j])  6.78 us
  transfers between devices with their start and end apart: 41, of which 12 were waited for; matrix products, arithmetic and copies ran while one was open for 52% of the time, Pallas kernels for 0%

profile of v1, /device:TPU:0, one launch (start us, length us, event | category | flops | bytes accessed | tf_op | source)
XLA Modules:
  0.0 182.7 jit_solution(10665034887471637732)
XLA Ops:
  0.7 1.6 constant_dynamic-update-slice_fusion.10
  2.3 3.0 %collective-permute-start.23 = (bf16[128,256]{1,0:T(8,128)(2,1)}, bf16[128,256]{1,0:T(8,128)(2,1)S(1)}, u32[]{:S(2)}, u32[]{:S(2)}) collective-permute-start(bf16[128,256]{1,0:T(8,128)(2,1)} %get-tuple-element.16), channel_id=1, source_target_pairs={{0,1},{1,0},{2,3},{3,2},{4,5},{5,4},{6,7},{7,6},{8,9},{9,8},{10,11... | collective-permute-start | bytes 196616 | tf_op jit(solution)/shard_map/ppermute | solution.py:12
  5.3 2.6 %collective-permute-start.24 = (bf16[128,256]{1,0:T(8,128)(2,1)}, bf16[128,256]{1,0:T(8,128)(2,1)S(1)}, u32[]{:S(2)}, u32[]{:S(2)}) collective-permute-start(bf16[128,256]{1,0:T(8,128)(2,1)} %get-tuple-element.16), channel_id=1, source_target_pairs={{0,2},{1,3},{2,0},{3,1},{4,6},{5,7},{6,4},{7,5},{8,10},{9,11},{10,... | collective-permute-start | bytes 196616 | tf_op jit(solution)/shard_map/ppermute | solution.py:12
  7.9 1.5 constant_dynamic-slice_fusion.7
  9.4 1.9 %collective-permute-start.1 = (bf16[256,128]{1,0:T(8,128)(2,1)}, bf16[256,128]{1,0:T(8,128)(2,1)}, u32[]{:S(2)}, u32[]{:S(2)}) collective-permute-start(bf16[256,128]{1,0:T(8,128)(2,1)} %constant_dynamic-slice_fusion.7), channel_id=1, source_target_pairs={{0,2},{1,3},{2,0},{3,1},{4,6},{5,7},{6,4},{7,5},{8,10},{9,11},{10,... | collective-permute-start | bytes 196616 | tf_op jit(solution)/shard_map/ppermute | solution.py:12
  11.3 1.5 collective-permute-start.15
  13.9 1.2 reshape_squeeze.10
  18.0 2.1 %multiply_convert_fusion.1 = bf16[4,512,512]{2,1,0:T(8,128)(2,1)S(1)} fusion(f32[512,512]{1,0:T(8,128)} %fusion.30, bf16[512,4,128]{2,1,0:T(4,128)(2,1)} %copy-done.4, bf16[512,4,128]{2,1,0:T(4,128)(2,1)S(1)} %reshape_squeeze.9), kind=kOutput, calls=%fused_computation.1 | convolution fusion | flops 270532608 | bytes 4194304 | tf_op jit(solution)/shard_map/thd,shd->hts/dot_general | solution.py:127
  20.1 1.7 convolution_bitcast_fusion.2
  21.8 1.5 constant_dynamic-slice_fusion.6
  23.9 1.3 constant_dynamic-update-slice_fusion.15
  25.2 3.6 %copy.53 = bf16[1,256,2,1024]{1,3,2,0:T(8,128)(2,1)} copy(bf16[1,256,2,1024]{3,2,1,0:T(2,128)(2,1)} %param.15) | data formatting | bytes 2097152 | tf_op args[7]
  28.8 2.5 %collective-permute-start.2 = (bf16[256,128]{1,0:T(8,128)(2,1)}, bf16[256,128]{1,0:T(8,128)(2,1)S(1)}, u32[]{:S(2)}, u32[]{:S(2)}) collective-permute-start(bf16[256,128]{1,0:T(8,128)(2,1)} %constant_dynamic-slice_fusion.7), channel_id=1, source_target_pairs={{0,1},{1,0},{2,3},{3,2},{4,5},{5,4},{6,7},{7,6},{8,9},{9,8},{10,11... | collective-permute-start | bytes 196616 | tf_op jit(solution)/shard_map/ppermute | solution.py:12
  31.6 1.3 collective-permute-start.10
  32.9 1.4 collective-permute-done.2
  34.3 2.1 %collective-permute-start.11 = (bf16[128,256]{1,0:T(8,128)(2,1)}, bf16[128,256]{1,0:T(8,128)(2,1)S(1)}, u32[]{:S(2)}, u32[]{:S(2)}) collective-permute-start(bf16[128,256]{1,0:T(8,128)(2,1)} %constant_dynamic-slice_fusion.6), channel_id=1, source_target_pairs={{0,1},{1,0},{2,3},{3,2},{4,5},{5,4},{6,7},{7,6},{8,9},{9,8},{10,11... | collective-permute-start | bytes 196616 | tf_op jit(solution)/shard_map/ppermute | solution.py:12
  39.1 4.2 %collective-permute-start.18 = (bf16[128,256]{1,0:T(8,128)(2,1)}, bf16[128,256]{1,0:T(8,128)(2,1)S(1)}, u32[]{:S(2)}, u32[]{:S(2)}) collective-permute-start(bf16[128,256]{1,0:T(8,128)(2,1)} %get-tuple-element.44), channel_id=1, source_target_pairs={{0,2},{1,3},{2,0},{3,1},{4,6},{5,7},{6,4},{7,5},{8,10},{9,11},{10,... | collective-permute-start | bytes 196616 | tf_op jit(solution)/shard_map/ppermute | solution.py:12
  43.3 1.6 pad_maximum_fusion.14
  45.4 1.5 collective-permute-start.26
  49.1 1.5 collective-permute-start.12
  51.9 1.5 collective-permute-start.20
  53.4 1.5 constant_dynamic-update-slice_fusion.9
  54.9 1.5 constant_dynamic-update-slice_fusion.8
  59.5 3.2 %collective-permute-done.7 = bf16[4,128,128]{2,1,0:T(8,128)(2,1)S(1)} collective-permute-done((bf16[4,128,128]{2,1,0:T(8,128)(2,1)S(1)}, bf16[4,128,128]{2,1,0:T(8,128)(2,1)S(1)}, u32[]{:S(2)}, u32[]{:S(2)}) %collective-permute-start.7) | collective-permute-done | bytes 131104 | tf_op jit(solution)/shard_map/ppermute | solution.py:12
  63.4 1.2 copy.62
  64.6 2.0 %reshape.177 = bf16[2,256,512]{2,1,0:T(8,128)(2,1)} reshape(bf16[512,4,128]{2,1,0:T(4,128)(2,1)} %copy.62) | data formatting | bytes 1048576 | tf_op jit(solution)/shard_map/reshape | solution.py:136
  66.6 1.7 dynamic-slice_bitcast_fusion
  68.8 1.7 constant_dynamic-update-slice_fusion.6
  70.5 1.8 %fusion.22 = bf16[1024,256]{1,0:T(8,128)(2,1)S(1)} fusion(bf16[1024,256]{1,0:T(8,128)(2,1)} %constant_dynamic-update-slice_fusion.6, s32[1024]{0:T(1024)S(1)} %copy-done.48, s32[1024]{0:T(1024)S(1)} %bitcast.213), kind=kOutput, calls=%fused_computation.35 | convolution fusion | flops 538181632 | bytes 1056768 | tf_op jit(solution)/shard_map/dot_general | solution.py:38
  74.6 1.7 fusion.76
  76.3 1.7 copy.117
  77.9 1.7 copy.115
  79.6 1.2 broadcast_select_fusion.11
  82.4 1.5 collective-permute-start.4
  90.5 1.5 collective-permute-start.21
  97.2 2.2 %reshape.182 = bf16[256,2,2,2,128]{4,3,2,1,0:T(2,128)(2,1)} reshape(bf16[256,1024]{1,0:T(8,128)(2,1)} %pad_maximum_fusion.5) | data formatting | bytes 1048576 | tf_op jit(solution)/shard_map/reshape | solution.py:179
  99.4 2.2 %constant_dynamic-slice_fusion.4 = (bf16[256,2,1,2,128]{4,3,2,1,0:T(2,128)(2,1)}, bf16[256,2,1,2,128]{4,3,2,1,0:T(2,128)(2,1)}) fusion(bf16[256,2,2,2,128]{4,3,2,1,0:T(2,128)(2,1)} %reshape.182, s32[]{:T(128)S(6)} %select_n.406, s32[]{:T(128)S(6)} %select_n.405), kind=kLoop, calls=%fused_computation.194 | loop fusion | bytes 1048584 | tf_op jit(solution)/shard_map/jit(dynamic_index_in_dim)/dynamic_slice | solution.py:30
  101.6 1.8 reshape.184
  103.3 1.8 reshape.183
  105.1 1.1 bitcast_select_fusion.3
  107.2 3.3 %collective-permute-done.21 = bf16[2,256,256]{1,2,0:T(8,128)(2,1)} collective-permute-done((bf16[2,256,256]{1,2,0:T(8,128)(2,1)}, bf16[2,256,256]{1,2,0:T(8,128)(2,1)}, u32[]{:S(2)}, u32[]{:S(2)}) %collective-permute-start.21) | collective-permute-done | bytes 262176 | tf_op jit(solution)/shard_map/ppermute | solution.py:12
  111.8 1.1 select_bitcast_fusion.1
  113.5 1.3 select_bitcast_fusion.3
  120.4 1.3 multiply_reduce_fusion
  123.2 1.5 convolution_convert_fusion
  124.8 6.4 %collective-permute-done.29 = bf16[256,512]{1,0:T(8,128)(2,1)S(1)} collective-permute-done((bf16[256,512]{1,0:T(8,128)(2,1)S(1)}, bf16[256,512]{1,0:T(8,128)(2,1)S(1)}, u32[]{:S(2)}, u32[]{:S(2)}) %collective-permute-start.29) | collective-permute-done | bytes 262176 | tf_op jit(solution)/shard_map/ppermute | solution.py:12
  132.6 2.0 %copy.121 = bf16[512,512]{0,1:T(8,128)(2,1)} copy(bf16[512,512]{1,0:T(8,128)(2,1)} %pad_maximum_fusion.7) | data formatting | bytes 1048576 | tf_op jit(solution)/shard_map/reshape | solution.py:176
  134.6 2.6 %fusion.80 = f32[4,128,512]{2,1,0:T(8,128)} fusion(bf16[512,4,128]{0,2,1:T(8,128)(2,1)} %bitcast.186, bf16[4,512,512]{2,1,0:T(8,128)(2,1)S(1)} %multiply_convert_fusion.1), kind=kOutput, calls=%fused_computation.220 | convolution fusion | flops 268435456 | bytes 3670016 | tf_op jit(solution)/shard_map/hts,the->she/dot_general | solution.py:215
  139.1 1.9 %convolution_bitcast_fusion = f32[512,4,128]{2,0,1:T(8,128)} fusion(bf16[4,512,512]{2,1,0:T(8,128)(2,1)S(1)} %multiply_convert_fusion, bf16[512,4,128]{2,1,0:T(4,128)(2,1)S(1)} %reshape_squeeze.9), kind=kOutput, calls=%fused_computation.14 | convolution fusion | flops 268435456 | bytes 3670016 | tf_op jit(solution)/shard_map/hts,thd->shd/dot_general | solution.py:211
  142.1 1.7 convert_add_fusion
  145.2 1.5 collective-permute-start.34
  146.8 1.4 collective-permute-start.35
  148.2 1.2 fusion.15
  149.4 1.2 copy.82
  152.6 1.6 collective-permute-start.31
  154.2 4.5 %collective-permute-done.34 = bf16[128,1024]{1,0:T(8,128)(2,1)} collective-permute-done((bf16[128,1024]{1,0:T(8,128)(2,1)}, bf16[128,1024]{1,0:T(8,128)(2,1)}, u32[]{:S(2)}, u32[]{:S(2)}) %collective-permute-start.34) | collective-permute-done | bytes 262176 | tf_op jit(solution)/shard_map/ppermute | solution.py:12
  158.7 1.7 collective-permute-done.35
  160.4 2.0 %fusion.33 = f32[128,1024]{1,0:T(8,128)} fusion(bf16[128,1024]{1,0:T(8,128)(2,1)} %collective-permute-done.35, bf16[128,1024]{1,0:T(8,128)(2,1)} %collective-permute-done.34, bf16[128,1024]{1,0:T(8,128)(2,1)} %collective-permute-done.33, f32[2,2,128,1024]{3,2,1,0:T(8,128)S(1)} %bitcast.194, s32[]{:T(128)S(6)} %select_n.407, s32[]{:T(128)S(6)} %select_n.409), kind=kLoop, calls=%fused_computation.73 | loop fusion | flops 786432 | bytes 1835016 | tf_op jit(solution)/shard_map/add | solution.py:194
  162.5 1.3 reshape.186
  164.7 3.9 %collective-permute-start.37 = (bf16[128,256]{1,0:T(8,128)(2,1)S(1)}, bf16[128,256]{1,0:T(8,128)(2,1)S(1)}, u32[]{:S(2)}, u32[]{:S(2)}) collective-permute-start(bf16[128,256]{1,0:T(8,128)(2,1)S(1)} %bitcast.210), channel_id=1, source_target_pairs={{0,2},{1,3},{2,0},{3,1},{4,6},{5,7},{6,4},{7,5},{8,10},{9,11},{10,... | collective-permute-start | bytes 196616 | tf_op jit(solution)/shard_map/ppermute | solution.py:12
  168.9 4.2 %collective-permute-done.37 = bf16[128,256]{1,0:T(8,128)(2,1)S(1)} collective-permute-done((bf16[128,256]{1,0:T(8,128)(2,1)S(1)}, bf16[128,256]{1,0:T(8,128)(2,1)S(1)}, u32[]{:S(2)}, u32[]{:S(2)}) %collective-permute-start.37) | collective-permute-done | bytes 65568 | tf_op jit(solution)/shard_map/ppermute | solution.py:12
  173.1 1.7 collective-permute-done.38
  175.8 1.6 fusion.17
  177.4 1.8 collective-permute-done.39
  (240 shorter events, 54.6 us)
Async XLA Ops:
  0.6 15.6 %copy-start.37 = (bf16[1,512,512]{2,1,0:T(8,128)(2,1)S(1)}, bf16[1,512,512]{2,1,0:T(8,128)(2,1)}, u32[]{:S(2)}) copy-start(bf16[1,512,512]{2,1,0:T(8,128)(2,1)} %param.10) | copy-start | bytes 1572868
  2.3 36.5 %collective-permute-start.23 = (bf16[128,256]{1,0:T(8,128)(2,1)}, bf16[128,256]{1,0:T(8,128)(2,1)S(1)}, u32[]{:S(2)}, u32[]{:S(2)}) collective-permute-start(bf16[128,256]{1,0:T(8,128)(2,1)} %get-tuple-element.16), channel_id=1, source_target_pairs={{0,1},{1,0},{2,3},{3,2},{4,5},{5,4},{6,7},{7,6},{8,9},{9,8},{10,11... | collective-permute-start | bytes 196616 | tf_op jit(solution)/shard_map/ppermute | solution.py:12
  5.3 33.6 %collective-permute-start.24 = (bf16[128,256]{1,0:T(8,128)(2,1)}, bf16[128,256]{1,0:T(8,128)(2,1)S(1)}, u32[]{:S(2)}, u32[]{:S(2)}) collective-permute-start(bf16[128,256]{1,0:T(8,128)(2,1)} %get-tuple-element.16), channel_id=1, source_target_pairs={{0,2},{1,3},{2,0},{3,1},{4,6},{5,7},{6,4},{7,5},{8,10},{9,11},{10,... | collective-permute-start | bytes 196616 | tf_op jit(solution)/shard_map/ppermute | solution.py:12
  9.4 22.0 %collective-permute-start = (bf16[256,128]{1,0:T(8,128)(2,1)}, bf16[256,128]{1,0:T(8,128)(2,1)}, u32[]{:S(2)}, u32[]{:S(2)}) collective-permute-start(bf16[256,128]{1,0:T(8,128)(2,1)} %constant_dynamic-slice_fusion.7), channel_id=1, source_target_pairs={{0,3},{1,2},{2,1},{3,0},{4,7},{5,6},{6,5},{7,4},{8,11},{9,10},{10,... | collective-permute-start | bytes 196616 | tf_op jit(solution)/shard_map/ppermute | solution.py:12
  9.4 22.3 %collective-permute-start.1 = (bf16[256,128]{1,0:T(8,128)(2,1)}, bf16[256,128]{1,0:T(8,128)(2,1)}, u32[]{:S(2)}, u32[]{:S(2)}) collective-permute-start(bf16[256,128]{1,0:T(8,128)(2,1)} %constant_dynamic-slice_fusion.7), channel_id=1, source_target_pairs={{0,2},{1,3},{2,0},{3,1},{4,6},{5,7},{6,4},{7,5},{8,10},{9,11},{10,... | collective-permute-start | bytes 196616 | tf_op jit(solution)/shard_map/ppermute | solution.py:12
  11.3 5.1 %copy-start.38 = (bf16[1,512,512]{2,1,0:T(8,128)(2,1)S(1)}, bf16[1,512,512]{2,1,0:T(8,128)(2,1)}, u32[]{:S(2)}) copy-start(bf16[1,512,512]{2,1,0:T(8,128)(2,1)} %param.8) | copy-start | bytes 1572868
  11.3 12.0 %collective-permute-start.15 = (s32[2,256]{1,0:T(2,128)}, s32[2,256]{1,0:T(2,128)S(1)}, u32[]{:S(2)}, u32[]{:S(2)}) collective-permute-start(s32[2,256]{1,0:T(2,128)} %bitcast.215), channel_id=1, source_target_pairs={{0,16},{8,24},{16,0},{24,8},{1,17},{9,25},{17,1},{25,9},{2,18},{10... | collective-permute-start | bytes 6152 | tf_op jit(solution)/shard_map/ppermute | solution.py:12
  23.9 4.9 %collective-permute-start.16 = (s32[2,2,256]{2,1,0:T(2,128)S(1)}, s32[2,2,256]{2,1,0:T(2,128)S(1)}, u32[]{:S(2)}, u32[]{:S(2)}) collective-permute-start(s32[2,2,256]{2,1,0:T(2,128)S(1)} %get-tuple-element.77), channel_id=1, source_target_pairs={{0,8},{8,0},{16,24},{24,16},{1,9},{9,1},{17,25},{25,17},{2,10},{10... | collective-permute-start | bytes 12296 | tf_op jit(solution)/shard_map/ppermute | solution.py:12
  28.8 22.3 %copy-start.44 = (bf16[128,256]{1,0:T(8,128)(2,1)S(1)}, bf16[128,256]{1,0:T(8,128)(2,1)}, u32[]{:S(2)}) copy-start(bf16[128,256]{1,0:T(8,128)(2,1)} %get-tuple-element.44) | copy-start | bytes 196612
  28.8 5.4 %collective-permute-start.2 = (bf16[256,128]{1,0:T(8,128)(2,1)}, bf16[256,128]{1,0:T(8,128)(2,1)S(1)}, u32[]{:S(2)}, u32[]{:S(2)}) collective-permute-start(bf16[256,128]{1,0:T(8,128)(2,1)} %constant_dynamic-slice_fusion.7), channel_id=1, source_target_pairs={{0,1},{1,0},{2,3},{3,2},{4,5},{5,4},{6,7},{7,6},{8,9},{9,8},{10,11... | collective-permute-start | bytes 196616 | tf_op jit(solution)/shard_map/ppermute | solution.py:12
  31.3 7.8 %collective-permute-start.25 = (bf16[128,256]{1,0:T(8,128)(2,1)}, bf16[128,256]{1,0:T(8,128)(2,1)S(1)}, u32[]{:S(2)}, u32[]{:S(2)}) collective-permute-start(bf16[128,256]{1,0:T(8,128)(2,1)} %get-tuple-element.16), channel_id=1, source_target_pairs={{0,3},{1,2},{2,1},{3,0},{4,7},{5,6},{6,5},{7,4},{8,11},{9,10},{10,... | collective-permute-start | bytes 196616 | tf_op jit(solution)/shard_map/ppermute | solution.py:12
  31.6 13.3 %collective-permute-start.10 = (bf16[128,256]{1,0:T(8,128)(2,1)}, bf16[128,256]{1,0:T(8,128)(2,1)S(1)}, u32[]{:S(2)}, u32[]{:S(2)}) collective-permute-start(bf16[128,256]{1,0:T(8,128)(2,1)} %constant_dynamic-slice_fusion.6), channel_id=1, source_target_pairs={{0,2},{1,3},{2,0},{3,1},{4,6},{5,7},{6,4},{7,5},{8,10},{9,11},{10,... | collective-permute-start | bytes 196616 | tf_op jit(solution)/shard_map/ppermute | solution.py:12
  34.3 10.6 %collective-permute-start.11 = (bf16[128,256]{1,0:T(8,128)(2,1)}, bf16[128,256]{1,0:T(8,128)(2,1)S(1)}, u32[]{:S(2)}, u32[]{:S(2)}) collective-permute-start(bf16[128,256]{1,0:T(8,128)(2,1)} %constant_dynamic-slice_fusion.6), channel_id=1, source_target_pairs={{0,1},{1,0},{2,3},{3,2},{4,5},{5,4},{6,7},{7,6},{8,9},{9,8},{10,11... | collective-permute-start | bytes 196616 | tf_op jit(solution)/shard_map/ppermute | solution.py:12
  37.4 25.2 %copy-start.8 = (f32[512,4,128]{2,0,1:T(8,128)S(1)}, f32[512,4,128]{2,0,1:T(8,128)}, u32[]{:S(2)}) copy-start(f32[512,4,128]{2,0,1:T(8,128)} %convolution_bitcast_fusion.2) | copy-start | bytes 3145732
  38.8 6.2 %copy-start.42 = (bf16[128,256]{1,0:T(8,128)(2,1)}, bf16[128,256]{1,0:T(8,128)(2,1)S(1)}, u32[]{:S(2)}) copy-start(bf16[128,256]{1,0:T(8,128)(2,1)S(1)} %collective-permute-done.23) | copy-start | bytes 196612
  38.8 6.6 %collective-permute-start.9 = (bf16[128,256]{1,0:T(8,128)(2,1)}, bf16[128,256]{1,0:T(8,128)(2,1)S(1)}, u32[]{:S(2)}, u32[]{:S(2)}) collective-permute-start(bf16[128,256]{1,0:T(8,128)(2,1)} %constant_dynamic-slice_fusion.6), channel_id=1, source_target_pairs={{0,3},{1,2},{2,1},{3,0},{4,7},{5,6},{6,5},{7,4},{8,11},{9,10},{10,... | collective-permute-start | bytes 196616 | tf_op jit(solution)/shard_map/ppermute | solution.py:12
  38.9 6.1 %copy-start.43 = (bf16[128,256]{1,0:T(8,128)(2,1)}, bf16[128,256]{1,0:T(8,128)(2,1)S(1)}, u32[]{:S(2)}) copy-start(bf16[128,256]{1,0:T(8,128)(2,1)S(1)} %collective-permute-done.24) | copy-start | bytes 196612
  38.9 9.7 %collective-permute-start.17 = (bf16[128,256]{1,0:T(8,128)(2,1)}, bf16[128,256]{1,0:T(8,128)(2,1)S(1)}, u32[]{:S(2)}, u32[]{:S(2)}) collective-permute-start(bf16[128,256]{1,0:T(8,128)(2,1)} %get-tuple-element.44), channel_id=1, source_target_pairs={{0,1},{1,0},{2,3},{3,2},{4,5},{5,4},{6,7},{7,6},{8,9},{9,8},{10,11... | collective-permute-start | bytes 196616 | tf_op jit(solution)/shard_map/ppermute | solution.py:12
  39.1 10.0 %collective-permute-start.18 = (bf16[128,256]{1,0:T(8,128)(2,1)}, bf16[128,256]{1,0:T(8,128)(2,1)S(1)}, u32[]{:S(2)}, u32[]{:S(2)}) collective-permute-start(bf16[128,256]{1,0:T(8,128)(2,1)} %get-tuple-element.44), channel_id=1, source_target_pairs={{0,2},{1,3},{2,0},{3,1},{4,6},{5,7},{6,4},{7,5},{8,10},{9,11},{10,... | collective-permute-start | bytes 196616 | tf_op jit(solution)/shard_map/ppermute | solution.py:12
  44.9 6.3 %collective-permute-start.19 = (bf16[128,256]{1,0:T(8,128)(2,1)}, bf16[128,256]{1,0:T(8,128)(2,1)S(1)}, u32[]{:S(2)}, u32[]{:S(2)}) collective-permute-start(bf16[128,256]{1,0:T(8,128)(2,1)} %get-tuple-element.44), channel_id=1, source_target_pairs={{0,3},{1,2},{2,1},{3,0},{4,7},{5,6},{6,5},{7,4},{8,11},{9,10},{10,... | collective-permute-start | bytes 196616 | tf_op jit(solution)/shard_map/ppermute | solution.py:12
  44.9 12.7 %collective-permute-start.6 = (bf16[4,128,128]{2,1,0:T(8,128)(2,1)}, bf16[4,128,128]{2,1,0:T(8,128)(2,1)S(1)}, u32[]{:S(2)}, u32[]{:S(2)}) collective-permute-start(bf16[4,128,128]{2,1,0:T(8,128)(2,1)} %get-tuple-element.81), channel_id=1, source_target_pairs={{0,8},{8,0},{16,24},{24,16},{1,9},{9,1},{17,25},{25,17},{2,10},{10... | collective-permute-start | bytes 393224 | tf_op jit(solution)/shard_map/ppermute | solution.py:12
  45.4 23.4 %collective-permute-start.26 = (bf16[512,256]{1,0:T(8,128)(2,1)}, bf16[512,256]{1,0:T(8,128)(2,1)}, u32[]{:S(2)}, u32[]{:S(2)}) collective-permute-start(bf16[512,256]{1,0:T(8,128)(2,1)} %pad_maximum_fusion.14), channel_id=1, source_target_pairs={{0,4},{4,0},{1,5},{5,1},{2,6},{6,2},{3,7},{7,3},{8,12},{12,8},{9,1... | collective-permute-start | bytes 786440 | tf_op jit(solution)/shard_map/ppermute | solution.py:12
  47.8 11.7 %copy-start.27 = (bf16[128,256]{1,0:T(8,128)(2,1)}, bf16[128,256]{1,0:T(8,128)(2,1)S(1)}, u32[]{:S(2)}) copy-start(bf16[128,256]{1,0:T(8,128)(2,1)S(1)} %get-tuple-element.66) | copy-start | bytes 196612
  47.8 11.7 %copy-start.29 = (bf16[128,256]{1,0:T(8,128)(2,1)}, bf16[128,256]{1,0:T(8,128)(2,1)S(1)}, u32[]{:S(2)}) copy-start(bf16[128,256]{1,0:T(8,128)(2,1)S(1)} %get-tuple-element.67) | copy-start | bytes 196612
  47.8 11.7 %copy-start.31 = (bf16[128,256]{1,0:T(8,128)(2,1)}, bf16[128,256]{1,0:T(8,128)(2,1)S(1)}, u32[]{:S(2)}) copy-start(bf16[128,256]{1,0:T(8,128)(2,1)S(1)} %get-tuple-element.68) | copy-start | bytes 196612
  47.8 11.7 %copy-start.33 = (bf16[128,256]{1,0:T(8,128)(2,1)}, bf16[128,256]{1,0:T(8,128)(2,1)S(1)}, u32[]{:S(2)}) copy-start(bf16[128,256]{1,0:T(8,128)(2,1)S(1)} %get-tuple-element.69) | copy-start | bytes 196612
  48.6 31.0 %collective-permute-start.3 = (bf16[256,512]{1,0:T(8,128)(2,1)}, bf16[256,512]{1,0:T(8,128)(2,1)}, u32[]{:S(2)}, u32[]{:S(2)}) collective-permute-start(bf16[256,512]{1,0:T(8,128)(2,1)} %pad_maximum_fusion.8), channel_id=1, source_target_pairs={{0,4},{4,0},{1,5},{5,1},{2,6},{6,2},{3,7},{7,3},{8,12},{12,8},{9,1... | collective-permute-start | bytes 786440 | tf_op jit(solution)/shard_map/ppermute | solution.py:12
  49.1 34.7 %collective-permute-start.12 = (bf16[128,1024]{1,0:T(8,128)(2,1)}, bf16[128,1024]{1,0:T(8,128)(2,1)}, u32[]{:S(2)}, u32[]{:S(2)}) collective-permute-start(bf16[128,1024]{1,0:T(8,128)(2,1)} %pad_maximum_fusion.9), channel_id=1, source_target_pairs={{0,4},{4,0},{1,5},{5,1},{2,6},{6,2},{3,7},{7,3},{8,12},{12,8},{9,1... | collective-permute-start | bytes 786440 | tf_op jit(solution)/shard_map/ppermute | solution.py:12
  51.9 35.1 %collective-permute-start.20 = (bf16[512,256]{1,0:T(8,128)(2,1)}, bf16[512,256]{1,0:T(8,128)(2,1)}, u32[]{:S(2)}, u32[]{:S(2)}) collective-permute-start(bf16[512,256]{1,0:T(8,128)(2,1)} %pad_maximum_fusion.10), channel_id=1, source_target_pairs={{0,4},{4,0},{1,5},{5,1},{2,6},{6,2},{3,7},{7,3},{8,12},{12,8},{9,1... | collective-permute-start | bytes 786440 | tf_op jit(solution)/shard_map/ppermute | solution.py:12
  57.6 5.0 %collective-permute-start.7 = (bf16[4,128,128]{2,1,0:T(8,128)(2,1)S(1)}, bf16[4,128,128]{2,1,0:T(8,128)(2,1)S(1)}, u32[]{:S(2)}, u32[]{:S(2)}) collective-permute-start(bf16[4,128,128]{2,1,0:T(8,128)(2,1)S(1)} %fusion.50), channel_id=1, source_target_pairs={{0,16},{8,24},{16,0},{24,8},{1,17},{9,25},{17,1},{25,9},{2,18},{10... | collective-permute-start | bytes 393224 | tf_op jit(solution)/shard_map/ppermute | solution.py:12
  63.4 7.1 %copy-start.48 = (s32[1024]{0:T(1024)S(1)}, s32[1024]{0:T(1024)}, u32[]{:S(2)}) copy-start(s32[1024]{0:T(1024)} %constant_dynamic-update-slice_fusion.15) | copy-start | bytes 12292
  68.3 26.3 %collective-permute-start.8 = (bf16[256,512]{1,0:T(8,128)(2,1)}, bf16[256,512]{1,0:T(8,128)(2,1)}, u32[]{:S(2)}, u32[]{:S(2)}) collective-permute-start(bf16[256,512]{1,0:T(8,128)(2,1)} %dynamic-slice_bitcast_fusion), channel_id=1, source_target_pairs={{0,4},{4,0},{1,5},{5,1},{2,6},{6,2},{3,7},{7,3},{8,12},{12,8},{9,1... | collective-permute-start | bytes 786440 | tf_op jit(solution)/shard_map/ppermute | solution.py:12
  74.0 9.9 %copy-start.28 = (bf16[128,256]{1,0:T(8,128)(2,1)S(1)}, bf16[128,256]{1,0:T(8,128)(2,1)}, u32[]{:S(2)}) copy-start(bf16[128,256]{1,0:T(8,128)(2,1)} %copy-done.27) | copy-start | bytes 196612
  74.0 9.9 %copy-start.30 = (bf16[128,256]{1,0:T(8,128)(2,1)S(1)}, bf16[128,256]{1,0:T(8,128)(2,1)}, u32[]{:S(2)}) copy-start(bf16[128,256]{1,0:T(8,128)(2,1)} %copy-done.29) | copy-start | bytes 196612
  74.0 9.9 %copy-start.32 = (bf16[128,256]{1,0:T(8,128)(2,1)S(1)}, bf16[128,256]{1,0:T(8,128)(2,1)}, u32[]{:S(2)}) copy-start(bf16[128,256]{1,0:T(8,128)(2,1)} %copy-done.31) | copy-start | bytes 196612
  74.0 9.9 %copy-start.34 = (bf16[128,256]{1,0:T(8,128)(2,1)S(1)}, bf16[128,256]{1,0:T(8,128)(2,1)}, u32[]{:S(2)}) copy-start(bf16[128,256]{1,0:T(8,128)(2,1)} %copy-done.33) | copy-start | bytes 196612
  74.0 31.1 %collective-permute-start.27 = (bf16[2,256,256]{1,2,0:T(8,128)(2,1)}, bf16[2,256,256]{1,2,0:T(8,128)(2,1)}, u32[]{:S(2)}, u32[]{:S(2)}) collective-permute-start(bf16[2,256,256]{1,2,0:T(8,128)(2,1)} %bitcast.207), channel_id=1, source_target_pairs={{0,16},{8,24},{16,0},{24,8},{1,17},{9,25},{17,1},{25,9},{2,18},{10... | collective-permute-start | bytes 786440 | tf_op jit(solution)/shard_map/ppermute | solution.py:12
  79.6 7.5 %copy-start.45 = (bf16[1024,256]{1,0:T(8,128)(2,1)S(1)}, bf16[1024,256]{1,0:T(8,128)(2,1)}, u32[]{:S(2)}) copy-start(bf16[1024,256]{1,0:T(8,128)(2,1)} %constant_dynamic-update-slice_fusion.2) | copy-start | bytes 1572868
  82.4 31.2 %collective-permute-start.4 = (bf16[256,1024]{1,0:T(8,128)(2,1)}, bf16[256,1024]{1,0:T(8,128)(2,1)}, u32[]{:S(2)}, u32[]{:S(2)}) collective-permute-start(bf16[256,1024]{1,0:T(8,128)(2,1)} %pad_maximum_fusion.4), channel_id=1, source_target_pairs={{0,16},{8,24},{16,0},{24,8},{1,17},{9,25},{17,1},{25,9},{2,18},{10... | collective-permute-start | bytes 1572872 | tf_op jit(solution)/shard_map/ppermute | solution.py:12
  86.5 25.2 %collective-permute-start.13 = (bf16[2,128,1024]{2,1,0:T(8,128)(2,1)}, bf16[2,128,1024]{2,1,0:T(8,128)(2,1)}, u32[]{:S(2)}, u32[]{:S(2)}) collective-permute-start(bf16[2,128,1024]{2,1,0:T(8,128)(2,1)} %pad_maximum_fusion.6), channel_id=1, source_target_pairs={{0,16},{8,24},{16,0},{24,8},{1,17},{9,25},{17,1},{25,9},{2,18},{10... | collective-permute-start | bytes 1572872 | tf_op jit(solution)/shard_map/ppermute | solution.py:12
  90.5 20.0 %collective-permute-start.21 = (bf16[2,256,256]{1,2,0:T(8,128)(2,1)}, bf16[2,256,256]{1,2,0:T(8,128)(2,1)}, u32[]{:S(2)}, u32[]{:S(2)}) collective-permute-start(bf16[2,256,256]{1,2,0:T(8,128)(2,1)} %bitcast.208), channel_id=1, source_target_pairs={{0,16},{8,24},{16,0},{24,8},{1,17},{9,25},{17,1},{25,9},{2,18},{10... | collective-permute-start | bytes 786440 | tf_op jit(solution)/shard_map/ppermute | solution.py:12
  105.1 6.5 %copy-start.41 = (bf16[1,1,256,256]{2,3,1,0:T(8,128)(2,1)S(1)}, bf16[1,1,256,256]{2,3,1,0:T(8,128)(2,1)}, u32[]{:S(2)}) copy-start(bf16[1,1,256,256]{2,3,1,0:T(8,128)(2,1)} %copy.112) | copy-start | bytes 393220
  105.1 6.7 %copy-start.17 = (bf16[1,128,1024]{2,1,0:T(8,128)(2,1)S(1)}, bf16[1,128,1024]{2,1,0:T(8,128)(2,1)}, u32[]{:S(2)}) copy-start(bf16[1,128,1024]{2,1,0:T(8,128)(2,1)} %copy-done.16) | copy-start | bytes 786436
  105.1 6.7 %copy-start.19 = (bf16[1,128,1024]{2,1,0:T(8,128)(2,1)S(1)}, bf16[1,128,1024]{2,1,0:T(8,128)(2,1)}, u32[]{:S(2)}) copy-start(bf16[1,128,1024]{2,1,0:T(8,128)(2,1)} %copy-done.18) | copy-start | bytes 786436
  107.2 7.9 %collective-permute-start.28 = (bf16[2,256,256]{1,2,0:T(8,128)(2,1)S(1)}, bf16[2,256,256]{1,2,0:T(8,128)(2,1)S(1)}, u32[]{:S(2)}, u32[]{:S(2)}) collective-permute-start(bf16[2,256,256]{1,2,0:T(8,128)(2,1)S(1)} %pad_maximum_fusion.15), channel_id=1, source_target_pairs={{0,8},{8,0},{16,24},{24,16},{1,9},{9,1},{17,25},{25,17},{2,10},{10... | collective-permute-start | bytes 786440 | tf_op jit(solution)/shard_map/ppermute | solution.py:12
  111.7 3.5 %collective-permute-start.22 = (bf16[2,256,256]{1,2,0:T(8,128)(2,1)S(1)}, bf16[2,256,256]{1,2,0:T(8,128)(2,1)S(1)}, u32[]{:S(2)}, u32[]{:S(2)}) collective-permute-start(bf16[2,256,256]{1,2,0:T(8,128)(2,1)S(1)} %pad_maximum_fusion.11), channel_id=1, source_target_pairs={{0,8},{8,0},{16,24},{24,16},{1,9},{9,1},{17,25},{25,17},{2,10},{10... | collective-permute-start | bytes 786440 | tf_op jit(solution)/shard_map/ppermute | solution.py:12
  113.0 2.8 %collective-permute-start.14 = (bf16[2,2,128,1024]{3,2,0,1:T(8,128)(2,1)S(1)}, bf16[2,2,128,1024]{3,2,0,1:T(8,128)(2,1)S(1)}, u32[]{:S(2)}, u32[]{:S(2)}) collective-permute-start(bf16[2,2,128,1024]{3,2,0,1:T(8,128)(2,1)S(1)} %pad_maximum_fusion.3), channel_id=1, source_target_pairs={{0,8},{8,0},{16,24},{24,16},{1,9},{9,1},{17,25},{25,17},{2,10},{10... | collective-permute-start | bytes 3145736 | tf_op jit(solution)/shard_map/ppermute | solution.py:12
  114.9 3.0 %collective-permute-start.5 = (bf16[2,256,1024]{2,1,0:T(8,128)(2,1)S(1)}, bf16[2,256,1024]{2,1,0:T(8,128)(2,1)S(1)}, u32[]{:S(2)}, u32[]{:S(2)}) collective-permute-start(bf16[2,256,1024]{2,1,0:T(8,128)(2,1)S(1)} %pad_maximum_fusion.2), channel_id=1, source_target_pairs={{0,8},{8,0},{16,24},{24,16},{1,9},{9,1},{17,25},{25,17},{2,10},{10... | collective-permute-start | bytes 3145736 | tf_op jit(solution)/shard_map/ppermute | solution.py:12
  122.1 9.7 %copy-start.2 = (bf16[256,1024]{0,1:T(8,128)(2,1)}, bf16[256,1024]{0,1:T(8,128)(2,1)S(1)}, u32[]{:S(2)}) copy-start(bf16[256,1024]{0,1:T(8,128)(2,1)S(1)} %add_convert_fusion) | copy-start | bytes 1572868
  122.6 8.7 %collective-permute-start.29 = (bf16[256,512]{1,0:T(8,128)(2,1)S(1)}, bf16[256,512]{1,0:T(8,128)(2,1)S(1)}, u32[]{:S(2)}, u32[]{:S(2)}) collective-permute-start(bf16[256,512]{1,0:T(8,128)(2,1)S(1)} %convolution_convert_fusion.2), channel_id=1, source_target_pairs={{0,4},{4,0},{1,5},{5,1},{2,6},{6,2},{3,7},{7,3},{8,12},{12,8},{9,1... | collective-permute-start | bytes 786440 | tf_op jit(solution)/shard_map/ppermute | solution.py:12
  124.7 17.0 %collective-permute-start.32 = (bf16[512,1024]{1,0:T(8,128)(2,1)}, bf16[512,1024]{1,0:T(8,128)(2,1)}, u32[]{:S(2)}, u32[]{:S(2)}) collective-permute-start(bf16[512,1024]{1,0:T(8,128)(2,1)} %convolution_convert_fusion), channel_id=1, source_target_pairs={{0,8},{8,0},{16,24},{24,16},{1,9},{9,1},{17,25},{25,17},{2,10},{10... | collective-permute-start | bytes 3145736 | tf_op jit(solution)/shard_map/ppermute | solution.py:12
  138.3 13.3 %collective-permute-start.30 = (bf16[4,128,128]{2,1,0:T(8,128)(2,1)}, bf16[4,128,128]{2,1,0:T(8,128)(2,1)S(1)}, u32[]{:S(2)}, u32[]{:S(2)}) collective-permute-start(bf16[4,128,128]{2,1,0:T(8,128)(2,1)} %get-tuple-element.88), channel_id=1, source_target_pairs={{0,8},{8,0},{16,24},{24,16},{1,9},{9,1},{17,25},{25,17},{2,10},{10... | collective-permute-start | bytes 393224 | tf_op jit(solution)/shard_map/ppermute | solution.py:12
  141.7 6.5 %copy-start.36 = (bf16[4,128,128]{2,1,0:T(8,128)(2,1)S(1)}, bf16[4,128,128]{2,1,0:T(8,128)(2,1)}, u32[]{:S(2)}) copy-start(bf16[4,128,128]{2,1,0:T(8,128)(2,1)} %copy-done.35) | copy-start | bytes 393220
  144.7 9.5 %collective-permute-start.33 = (bf16[128,1024]{1,0:T(8,128)(2,1)}, bf16[128,1024]{1,0:T(8,128)(2,1)}, u32[]{:S(2)}, u32[]{:S(2)}) collective-permute-start(bf16[128,1024]{1,0:T(8,128)(2,1)} %get-tuple-element.19), channel_id=1, source_target_pairs={{0,4},{4,0},{8,12},{12,8},{16,20},{20,16},{24,28},{28,24},{1,5},{5... | collective-permute-start | bytes 786440 | tf_op jit(solution)/shard_map/ppermute | solution.py:12
  145.2 13.4 %collective-permute-start.34 = (bf16[128,1024]{1,0:T(8,128)(2,1)}, bf16[128,1024]{1,0:T(8,128)(2,1)}, u32[]{:S(2)}, u32[]{:S(2)}) collective-permute-start(bf16[128,1024]{1,0:T(8,128)(2,1)} %get-tuple-element.21), channel_id=1, source_target_pairs={{0,16},{4,20},{8,24},{12,28},{16,0},{20,4},{24,8},{28,12},{1,17},{... | collective-permute-start | bytes 786440 | tf_op jit(solution)/shard_map/ppermute | solution.py:12
  146.8 13.7 %collective-permute-start.35 = (bf16[128,1024]{1,0:T(8,128)(2,1)}, bf16[128,1024]{1,0:T(8,128)(2,1)}, u32[]{:S(2)}, u32[]{:S(2)}) collective-permute-start(bf16[128,1024]{1,0:T(8,128)(2,1)} %get-tuple-element.20), channel_id=1, source_target_pairs={{0,20},{4,16},{8,28},{12,24},{16,4},{20,0},{24,12},{28,8},{1,21},{... | collective-permute-start | bytes 786440 | tf_op jit(solution)/shard_map/ppermute | solution.py:12
  152.6 23.2 %copy-start.5 = (bf16[512,4,128]{2,1,0:T(4,128)(2,1)S(1)}, bf16[512,4,128]{2,1,0:T(4,128)(2,1)}, u32[]{:S(2)}) copy-start(bf16[512,4,128]{2,1,0:T(4,128)(2,1)} %copy-done.4) | copy-start | bytes 1572868
  152.6 23.2 %collective-permute-start.31 = (bf16[4,128,128]{2,1,0:T(8,128)(2,1)S(1)}, bf16[4,128,128]{2,1,0:T(8,128)(2,1)S(1)}, u32[]{:S(2)}, u32[]{:S(2)}) collective-permute-start(bf16[4,128,128]{2,1,0:T(8,128)(2,1)S(1)} %fusion.53), channel_id=1, source_target_pairs={{0,16},{8,24},{16,0},{24,8},{1,17},{9,25},{17,1},{25,9},{2,18},{10... | collective-permute-start | bytes 393224 | tf_op jit(solution)/shard_map/ppermute | solution.py:12
  164.1 15.2 %copy-start.9 = (f32[512,4,128]{2,0,1:T(8,128)S(1)}, f32[512,4,128]{2,0,1:T(8,128)}, u32[]{:S(2)}) copy-start(f32[512,4,128]{2,0,1:T(8,128)} %convolution_bitcast_fusion) | copy-start | bytes 3145732
  164.1 4.7 %collective-permute-start.36 = (bf16[128,256]{1,0:T(8,128)(2,1)S(1)}, bf16[128,256]{1,0:T(8,128)(2,1)S(1)}, u32[]{:S(2)}, u32[]{:S(2)}) collective-permute-start(bf16[128,256]{1,0:T(8,128)(2,1)S(1)} %bitcast.209), channel_id=1, source_target_pairs={{0,1},{1,0},{2,3},{3,2},{4,5},{5,4},{6,7},{7,6},{8,9},{9,8},{10,11... | collective-permute-start | bytes 196616 | tf_op jit(solution)/shard_map/ppermute | solution.py:12
  164.7 8.3 %collective-permute-start.37 = (bf16[128,256]{1,0:T(8,128)(2,1)S(1)}, bf16[128,256]{1,0:T(8,128)(2,1)S(1)}, u32[]{:S(2)}, u32[]{:S(2)}) collective-permute-start(bf16[128,256]{1,0:T(8,128)(2,1)S(1)} %bitcast.210), channel_id=1, source_target_pairs={{0,2},{1,3},{2,0},{3,1},{4,6},{5,7},{6,4},{7,5},{8,10},{9,11},{10,... | collective-permute-start | bytes 196616 | tf_op jit(solution)/shard_map/ppermute | solution.py:12
  168.6 6.1 %collective-permute-start.38 = (bf16[128,256]{1,0:T(8,128)(2,1)S(1)}, bf16[128,256]{1,0:T(8,128)(2,1)S(1)}, u32[]{:S(2)}, u32[]{:S(2)}) collective-permute-start(bf16[128,256]{1,0:T(8,128)(2,1)S(1)} %bitcast.211), channel_id=1, source_target_pairs={{0,3},{1,2},{2,1},{3,0},{4,7},{5,6},{6,5},{7,4},{8,11},{9,10},{10,... | collective-permute-start | bytes 196616 | tf_op jit(solution)/shard_map/ppermute | solution.py:12
  174.8 4.3 %collective-permute-start.39 = (bf16[128,256]{1,0:T(8,128)(2,1)S(1)}, bf16[128,256]{1,0:T(8,128)(2,1)S(1)}, u32[]{:S(2)}, u32[]{:S(2)}) collective-permute-start(bf16[128,256]{1,0:T(8,128)(2,1)S(1)} %fusion.59), channel_id=1, source_target_pairs={{0,16},{8,24},{16,0},{24,8},{1,17},{9,25},{17,1},{25,9},{2,18},{10... | collective-permute-start | bytes 196616 | tf_op jit(solution)/shard_map/ppermute | solution.py:12
  179.2 2.6 %collective-permute-start.40 = (bf16[2,128,256]{2,1,0:T(8,128)(2,1)S(1)}, bf16[2,128,256]{2,1,0:T(8,128)(2,1)S(1)}, u32[]{:S(2)}, u32[]{:S(2)}) collective-permute-start(bf16[2,128,256]{2,1,0:T(8,128)(2,1)S(1)} %pad_maximum_fusion.19), channel_id=1, source_target_pairs={{0,8},{8,0},{16,24},{24,16},{1,9},{9,1},{17,25},{25,17},{2,10},{10... | collective-permute-start | bytes 393224 | tf_op jit(solution)/shard_map/ppermute | solution.py:12
  (26 other events, 36.1 us)

commit v2 on v1

--- a/solution.py
+++ b/solution.py
@@ -1,6 +1,8 @@
 import jax
 import jax.numpy as jnp
 from jax import lax
+from jax.experimental import pallas as pl
+from jax.experimental.pallas import tpu as pltpu
 from jax.sharding import PartitionSpec as P
 
 DH = 128
@@ -54,7 +56,7 @@
     return before.astype(BF16)
 
 
-def on_device(queries, keys, values, out_proj, depth_proj, code_table, code_ids, depth_cotangent):
+def on_device_any(queries, keys, values, out_proj, depth_proj, code_table, code_ids, depth_cotangent):
     n_seq, n_head, n_dp = (lax.axis_size(a) for a in ("seq", "head", "dp"))
     me_seq, me_head, me_dp = (lax.axis_index(a) for a in ("seq", "head", "dp"))
     group_len, width_dev = queries.shape[1:]
@@ -224,6 +226,423 @@
     )
 
 
+VMEM_BYTES = 48 * 1024 * 1024
+
+
+def run(body, outs, where, *args):
+    vmem = pl.BlockSpec(memory_space=pltpu.VMEM)
+    return pl.pallas_call(
+        body,
+        out_shape=outs,
+        in_specs=[pl.BlockSpec(memory_space=pltpu.SMEM)] + [vmem] * len(args),
+        out_specs=[vmem] * len(outs),
+        compiler_params=pltpu.CompilerParams(vmem_limit_bytes=VMEM_BYTES),
+    )(where, *args)
+
+
+def shaped(shape, dtype=BF16):
+    return jax.ShapeDtypeStruct(shape, dtype)
+
+
+def at(index, size):
+    return pl.ds(pl.multiple_of(index * size, size), size)
+
+
+HEAD, DP = 4, 5
+
+
+def prepare(where, out_proj, depth_proj, code_table):
+    rows, cols = out_proj.shape
+    d_rows, d_cols = depth_proj.shape
+    n_level, t_rows, t_cols = code_table.shape
+    rows, d_rows, t_cols = rows // 4, d_rows // 4, t_cols // 4
+
+    def body(where_ref, o_ref, d_ref, t_ref, o_out, d_out, *t_out):
+        o_out[...] = o_ref[...]
+        d_out[...] = d_ref[...]
+        for level, out in enumerate(t_out):
+            out[...] = t_ref[level]
+
+    def whole(shape):
+        return pl.BlockSpec(shape, lambda i, w: (0,) * len(shape))
+
+    return pl.pallas_call(
+        body,
+        out_shape=[shaped((rows, cols)), shaped((d_rows, d_cols))] + [shaped((t_rows, t_cols))] * n_level,
+        grid_spec=pltpu.PrefetchScalarGridSpec(
+            num_scalar_prefetch=1,
+            grid=(1,),
+            in_specs=[
+                pl.BlockSpec((rows, cols), lambda i, w: (w[0], 0)),
+                pl.BlockSpec((d_rows, d_cols), lambda i, w: (w[0], 0)),
+                pl.BlockSpec((n_level, t_rows, t_cols), lambda i, w: (0, 0, w[0])),
+            ],
+            out_specs=[whole((rows, cols)), whole((d_rows, d_cols))] + [whole((t_rows, t_cols))] * n_level,
+        ),
+    )(where, out_proj, depth_proj, code_table)
+
+
+def side_by_side(where, pieces):
+    rows, cols = pieces[0].shape
+
+    def body(where_ref, *refs):
+        out = refs[-1]
+        for k, ref in enumerate(refs[:-1]):
+            out[:, at(where_ref[DP] ^ k, cols)] = ref[...]
+
+    return run(body, [shaped((rows, cols * len(pieces)))], where, *pieces)[0]
+
+
+def stacked(where, pieces):
+    rows, cols = pieces[0].shape
+
+    def body(where_ref, *refs):
+        for k, ref in enumerate(refs[:-1]):
+            refs[-1][k * rows:(k + 1) * rows, :] = ref[...]
+
+    return run(body, [shaped((rows * len(pieces), cols))], where, *pieces)[0]
+
+
+def embed(where, ids, own, got, n_dp):
+    tokens = ids.shape[1]
+    half, cols = own.shape
+    rows_dev = half // n_dp
+
+    def body(where_ref, ids_ref, own_ref, got_ref, *outs):
+        place = lax.broadcasted_iota(jnp.int32, (tokens, half), 1)
+        piece = place // rows_dev
+        within = place % rows_dev
+        owner = jnp.bitwise_xor(piece, where_ref[DP])
+        base = owner * rows_dev + within
+        columns = ids_ref[...].T
+        for m, out in enumerate(outs):
+            col = columns[:, m:m + 1]
+            total = None
+            for k, ref in enumerate((own_ref, got_ref)):
+                start = (where_ref[HEAD] ^ k) * half
+                hot = (base == col - start).astype(F32).astype(BF16)
+                part = jnp.dot(hot, ref[...], preferred_element_type=F32)
+                total = part if total is None else total + part
+            out[...] = total.astype(BF16)
+
+    return run(body, [shaped((tokens, cols))] * 4, where, ids, own, got)
+
+
+def lanes_together(where, pieces):
+    rows, cols = pieces[0].shape
+
+    def body(where_ref, *refs):
+        for m, ref in enumerate(refs[:-1]):
+            refs[-1][:, at(where_ref[m], cols)] = ref[...]
+
+    return run(body, [shaped((rows, cols * 4))], where, *pieces)[0]
+
+
+def depth_together(where, blocks, cot):
+    rows, cols = blocks[0].shape
+    width = rows * 4
+    last = cot.shape[1] // width - 1
+
+    def body(where_ref, *refs):
+        cot_ref, full, grad = refs[8:]
+        for m in range(4):
+            for x in range(2):
+                full[at(where_ref[m], rows), at(where_ref[HEAD] ^ x, cols)] = refs[2 * m + x][...]
+        cot_last = cot_ref[:, last * width:(last + 1) * width]
+        grad[...] = dot(cot_last, full[...], ((1,), (1,)))
+
+    return run(body, [shaped((width, width)), shaped((cot.shape[0], width), F32)], where, *blocks, cot)
+
+
+def local_states(where, keys, values, dtype=BF16):
+    heads = keys.shape[1] // DH
+
+    def body(where_ref, k_ref, v_ref, out):
+        for i in range(heads):
+            cut = slice(i * DH, (i + 1) * DH)
+            out[i] = dot(k_ref[:, cut], v_ref[:, cut], ((0,), (0,))).astype(dtype)
+
+    return run(body, [shaped((heads, DH, DH), dtype)], where, keys, values)[0]
+
+
+def lower(size):
+    rows = lax.broadcasted_iota(jnp.int32, (size, size), 0)
+    cols = lax.broadcasted_iota(jnp.int32, (size, size), 1)
+    return rows >= cols
+
+
+def upper(size):
+    rows = lax.broadcasted_iota(jnp.int32, (size, size), 0)
+    cols = lax.broadcasted_iota(jnp.int32, (size, size), 1)
+    return rows <= cols
+
+
+def attend(where, queries, keys, values, from_core, from_far, att_scale):
+    length, width_dev = queries.shape
+    heads = width_dev // DH
+
+    def body(where_ref, q_ref, k_ref, v_ref, core_ref, far_ref, att, state):
+        near = (where_ref[0] // 2).astype(F32)
+        far = (where_ref[0] % 2).astype(F32)
+        keep = lower(length)
+        for i in range(heads):
+            cut = slice(i * DH, (i + 1) * DH)
+            state[i] = (core_ref[i].astype(F32) * near + far_ref[i].astype(F32) * far).astype(BF16)
+            q = q_ref[:, cut]
+            scores = jnp.where(keep, dot(q, k_ref[:, cut], ((1,), (1,))), 0.0).astype(BF16)
+            both = jnp.dot(scores, v_ref[:, cut], preferred_element_type=F32)
+            both += jnp.dot(q, state[i], preferred_element_type=F32)
+            att[:, cut] = (att_scale * both).astype(BF16)
+
+    return run(
+        body, [shaped((length, width_dev)), shaped((heads, DH, DH))], where, queries, keys, values, from_core, from_far
+    )
+
+
+def mix(where, attended, blocks, other):
+    length = attended.shape[0] // 2
+    width = blocks[0].shape[1]
+    dtype = BF16 if other else F32
+
+    def body(where_ref, att, *refs):
+        rows = at(where_ref[HEAD] ^ (1 if other else 0), length)
+        total = None
+        for m in range(4):
+            part = jnp.dot(att[rows, at(where_ref[m], DH)], refs[m][...], preferred_element_type=F32)
+            total = part if total is None else total + part
+        refs[-1][...] = total.astype(dtype)
+
+    return run(body, [shaped((length, width), dtype)], where, attended, *blocks)[0]
+
+
+def weight_terms(where, attended, grad_own, grad_got):
+    tokens, width = grad_own.shape
+
+    def body(where_ref, att, own, got, send, keep):
+        def term(m):
+            total = None
+            for k, ref in enumerate((own, got)):
+                a = att[at(where_ref[HEAD] ^ k, tokens), at(where_ref[m], DH)]
+                part = dot(a, ref[...], ((0,), (0,)))
+                total = part if total is None else total + part
+            return total
+
+        send[0] = term(2).astype(BF16)
+        send[1] = term(3).astype(BF16)
+        keep[0] = term(0)
+        keep[1] = term(1)
+
+    return run(
+        body, [shaped((2, DH, width)), shaped((2, DH, width), F32)], where, attended, grad_own, grad_got
+    )
+
+
+def add_core(where, keep, got):
+    shape = keep.shape[1:]
+
+    def body(where_ref, keep_ref, got_ref, send, rest):
+        rest[...] = keep_ref[0] + got_ref[0].astype(F32)
+        send[...] = (keep_ref[1] + got_ref[1].astype(F32)).astype(BF16)
+
+    return run(body, [shaped(shape), shaped(shape, F32)], where, keep, got)
+
+
+def add_far(where, keep, got, n_dp):
+    rows, width = keep.shape
+    cols = width // n_dp
+
+    def body(where_ref, keep_ref, got_ref, rest, *send):
+        for k in range(n_dp):
+            cut = at(where_ref[DP] ^ k, cols)
+            total = keep_ref[:, cut] + got_ref[:, cut].astype(F32)
+            if k:
+                send[k - 1][...] = total.astype(BF16)
+            else:
+                rest[...] = total
+
+    return run(body, [shaped((rows, cols), F32)] + [shaped((rows, cols))] * (n_dp - 1), where, keep, got)
+
+
+def add_all(where, keep, got):
+    def body(where_ref, keep_ref, *refs):
+        total = keep_ref[...]
+        for ref in refs[:-1]:
+            total = total + ref[...].astype(F32)
+        refs[-1][...] = total.astype(BF16)
+
+    return run(body, [shaped(keep.shape)], where, keep, *got)[0]
+
+
+def rows_together(where, pieces):
+    rows, cols = pieces[0].shape
+
+    def body(where_ref, *refs):
+        for m, ref in enumerate(refs[:-1]):
+            refs[-1][at(where_ref[m], rows), :] = ref[...].astype(F32)
+
+    return run(body, [shaped((rows * 4, cols), F32)], where, *pieces)[0]
+
+
+def grad_attend(where, grad_own, grad_got, blocks, queries):
+    tokens, width = grad_own.shape
+    length, width_dev = queries.shape
+
+    def body(where_ref, own, got, o0, o1, o2, o3, q_ref, rows, back):
+        for m, block in enumerate((o0, o1, o2, o3)):
+            for k, ref in enumerate((own, got)):
+                part = dot(ref[...], block[...], ((1,), (1,))).astype(BF16)
+                rows[at(where_ref[HEAD] ^ k, tokens), at(where_ref[m], DH)] = part
+        for i in range(width_dev // DH):
+            cut = slice(i * DH, (i + 1) * DH)
+            back[i] = dot(q_ref[:, cut], rows[:, cut], ((0,), (0,))).astype(BF16)
+
+    outs = [shaped((length, width_dev)), shaped((width_dev // DH, DH, DH))]
+    return run(body, outs, where, grad_own, grad_got, *blocks, queries)
+
+
+def query_grads(where, grad_rows, keys, values, state, att_scale):
+    length, width_dev = keys.shape
+
+    def body(where_ref, g_ref, k_ref, v_ref, s_ref, out):
+        keep = lower(length)
+        for i in range(width_dev // DH):
+            cut = slice(i * DH, (i + 1) * DH)
+            g = g_ref[:, cut]
+            scores = jnp.where(keep, dot(g, v_ref[:, cut], ((1,), (1,))), 0.0).astype(BF16)
+            both = jnp.dot(scores, k_ref[:, cut], preferred_element_type=F32)
+            both += dot(g, s_ref[i], ((1,), (1,)))
+            out[:, cut] = (att_scale * both).astype(BF16)
+
+    return run(body, [shaped((length, width_dev))], where, grad_rows, keys, values, state)[0]
+
+
+def key_value_grads(where, grad_rows, queries, keys, values, from_core, from_far, att_scale):
+    length, width_dev = keys.shape
+
+    def body(where_ref, g_ref, q_ref, k_ref, v_ref, core_ref, far_ref, dk, dv):
+        near = 1.0 - (where_ref[0] // 2).astype(F32)
+        far = 1.0 - (where_ref[0] % 2).astype(F32)
+        keep = upper(length)
+        for i in range(width_dev // DH):
+            cut = slice(i * DH, (i + 1) * DH)
+            g, q, k, v = g_ref[:, cut], q_ref[:, cut], k_ref[:, cut], v_ref[:, cut]
+            back = (core_ref[i].astype(F32) * near + far_ref[i].astype(F32) * far).astype(BF16)
+            grad_scores = jnp.where(keep, dot(v, g, ((1,), (1,))), 0.0).astype(BF16)
+            both = jnp.dot(grad_scores, q, preferred_element_type=F32)
+            both += dot(v, back, ((1,), (1,)))
+            dk[:, cut] = (att_scale * both).astype(BF16)
+            scores = jnp.where(keep, dot(k, q, ((1,), (1,))), 0.0).astype(BF16)
+            both = jnp.dot(scores, g, preferred_element_type=F32)
+            both += jnp.dot(k, back, preferred_element_type=F32)
+            dv[:, cut] = (att_scale * both).astype(BF16)
+
+    outs = [shaped((length, width_dev))] * 2
+    return run(body, outs, where, grad_rows, queries, keys, values, from_core, from_far)
+
+
+def fits(queries, out_proj, depth_proj, code_table):
+    n_seq, n_head = lax.axis_size("seq"), lax.axis_size("head")
+    return (
+        n_seq == 4
+        and n_head == 2
+        and queries.shape[2] == 4 * DH
+        and code_table.shape[0] == 2
+        and out_proj.shape[1] % 128 == 0
+        and depth_proj.shape[1] % 128 == 0
+        and code_table.shape[1] % 128 == 0
+    )
+
+
+def on_device(queries, keys, values, out_proj, depth_proj, code_table, code_ids, depth_cotangent):
+    if not fits(queries, out_proj, depth_proj, code_table):
+        return on_device_any(
+            queries, keys, values, out_proj, depth_proj, code_table, code_ids, depth_cotangent
+        )
+    n_dp = lax.axis_size("dp")
+    me_seq, me_head, me_dp = (lax.axis_index(a) for a in ("seq", "head", "dp"))
+    group_len = queries.shape[1]
+    width = code_table.shape[2]
+    att_scale = float(group_len * lax.axis_size("seq")) ** (-0.5)
+    core, far = me_seq % 2, me_seq // 2
+    lane = 2 * core + far
+    where = jnp.stack([lane, lane ^ 1, lane ^ 2, lane ^ 3, me_head, me_dp]).astype(jnp.int32)
+    queries, keys, values = queries[0], keys[0], values[0]
+
+    def far_swap(block):
+        return swap(block, "seq", 2)
+
+    def core_swap(block):
+        return swap(block, "seq", 1)
+
+    def all_lanes(block):
+        got = far_swap(block)
+        return [block, got, core_swap(block), core_swap(got)]
+
+    out_lane, depth_lane, *table_lanes = prepare(where, out_proj, depth_proj, code_table)
+    ids = code_ids[0].T
+    ids_rel = all_lanes(ids)
+
+    out_part = side_by_side(where, exchange(out_lane, "dp"))
+    out_blocks = all_lanes(out_part)
+
+    depth_part = side_by_side(where, exchange(depth_lane, "dp"))
+    depth_got = swap(depth_part, "head", 1)
+    own_lanes, got_lanes = all_lanes(depth_part), all_lanes(depth_got)
+    depth_blocks = [block for pair in zip(own_lanes, got_lanes) for block in pair]
+
+    embedded = []
+    for level, table in enumerate(table_lanes):
+        part = stacked(where, exchange(table, "dp"))
+        got = swap(part, "head", 1)
+        level_ids = jnp.stack([i[level] for i in ids_rel])
+        for_own, for_far, for_core, for_core_far = embed(where, level_ids, part, got, n_dp)
+        from_far, pass_on = far_swap(for_far), far_swap(for_core_far)
+        pieces = [for_own, from_far, core_swap(for_core), core_swap(pass_on)]
+        embedded.append(lanes_together(where, pieces))
+
+    state = local_states(where, keys, values)
+    state_core = core_swap(state)
+    chip = (state.astype(F32) + state_core.astype(F32)).astype(BF16)
+    state_far = far_swap(chip)
+    attended, state_in = attend(where, queries, keys, values, state_core, state_far, att_scale)
+
+    mixed_got = swap(mix(where, attended, out_blocks, True), "head", 1)
+    mixed = mix(where, attended, out_blocks, False) + mixed_got.astype(F32)
+
+    cot = depth_cotangent[0].reshape(depth_cotangent.shape[1], -1)
+    proj_mat, grad_last = depth_together(where, depth_blocks, cot)
+    sum_0 = mixed + embedded[0].astype(F32)
+    inv_0 = lax.rsqrt(jnp.mean(sum_0 * sum_0, axis=-1, keepdims=True) + 1e-05)
+    projected = dot((sum_0 * inv_0).astype(BF16), proj_mat, ((1,), (0,)))
+    gate = jax.nn.sigmoid(projected)
+    sum_1 = sum_0 + projected * gate + embedded[1].astype(F32)
+    inv_1 = lax.rsqrt(jnp.mean(sum_1 * sum_1, axis=-1, keepdims=True) + 1e-05)
+    along = jnp.mean(grad_last * sum_1, axis=-1, keepdims=True)
+    grad = grad_last * inv_1 - sum_1 * (along * inv_1 * inv_1 * inv_1)
+    slope = gate * (1.0 + projected * (1.0 - gate))
+    grad_proj = (cot[:, :width].astype(F32) + grad * slope).astype(BF16)
+    grad_normed = dot(grad_proj, proj_mat, ((1,), (1,)))
+    along = jnp.mean(grad_normed * sum_0, axis=-1, keepdims=True)
+    grad = grad + grad_normed * inv_0 - sum_0 * (along * inv_0 * inv_0 * inv_0)
+    grad_mixed = grad.astype(BF16)
+
+    grad_got = swap(grad_mixed, "head", 1)
+    send, keep = weight_terms(where, attended, grad_mixed, grad_got)
+    send, keep = add_core(where, keep, core_swap(send))
+    keep, *send = add_far(where, keep, far_swap(send), n_dp)
+    block = add_all(where, keep, [swap(s, "dp", k + 1) for k, s in enumerate(send)])
+    grad_out_proj = rows_together(where, all_lanes(block))
+
+    grad_rows, back = grad_attend(where, grad_mixed, grad_got, out_blocks, queries)
+    back_core = core_swap(back)
+    back_far = far_swap((back.astype(F32) + back_core.astype(F32)).astype(BF16))
+    grad_query = query_grads(where, grad_rows, keys, values, state_in, att_scale)
+    grad_key, grad_value = key_value_grads(
+        where, grad_rows, queries, keys, values, back_core, back_far, att_scale
+    )
+    return grad_query[None], grad_key[None], grad_value[None], grad_out_proj
+
+
 def solution(mesh):
     in_specs = (
         P("dp", "seq", "head"),

time: 184 us -> 137 us (0.74)
  local copies, waits for them, and re-layouts: 57.4 us -> 7.37 us
  Pallas kernels: 0 us -> 29.6 us
  other arithmetic: 25.9 us -> 1.35 us
  matrix products: 26.1 us -> 1.92 us
  waiting for transfers between devices: 29.6 us -> 50.1 us
  starting transfers between devices: 42.2 us -> 44.8 us
    pallas_call x0 -> x22, Pallas kernels: none -> 29.6 us  [the longest x21 27.2 us: run(): pl.pallas_call(body, out_shape=outs, in_specs=[pl.BlockSpec(memory_space=...]
    unnamed x118 -> x27, local copies, waits for them, and re-layouts: 28.4 us -> 5.97 us
    ppermute x41 -> x49, waiting for transfers between devices: 29.6 us -> 50.1 us  [swap(): lax.ppermute(block, axis, [(i, i ^ mask) for i in range(lax.axis_size(axi...]
    dot_general x12 -> x0, matrix products: 15.1 us -> none  [the longest x1 2.57 us: on_device(): jnp.einsum('hts,the->she', scores, grad_rows, preferred_element_type=F32)]
    reshape x6 -> x0, local copies, waits for them, and re-layouts: 11.1 us -> none  [the longest x2 3.52 us: term(): part = pick(att_lanes, core, 2).reshape(tokens, n_head * n_far * rows)]
    dot_general x10 -> x2, matrix products: 11 us -> 1.92 us  [dot(): lax.dot_general(a, b, ((dims[0], dims[1]), ((), ())), preferred_element_t...]
    concatenate x11 -> x0, other arithmetic: 8.03 us -> none  [the longest x2 2.32 us: on_device(): part = jnp.concatenate(exchange(table[level], 'dp'), axis=0)]
    select_n x13 -> x0, other arithmetic: 6.78 us -> none  [in_order(): jnp.where(odd, pieces[j ^ bit], pieces[j])]
  transfers between devices with their start and end apart: 41 -> 49, of which waited for: 12 -> 15; matrix products, arithmetic and copies ran while one was open for 52% -> 1% of each run, Pallas kernels for 0% -> 19%
where the time goes in v2:
time: 137 us; the launch traced here: 136 us
  waiting for transfers between devices  50.1 us (37%)
  starting transfers between devices  44.8 us (33%)
  Pallas kernels  29.6 us (22%)
  local copies, waits for them, and re-layouts  7.37 us (5%)
  matrix products  1.92 us (1%)
    ppermute x49, waiting for transfers between devices, swap(): lax.ppermute(block, axis, [(i, i ^ mask) for i in range(lax.axis_size(axi...  50.1 us
    ppermute x49, starting transfers between devices, swap(): lax.ppermute(block, axis, [(i, i ^ mask) for i in range(lax.axis_size(axi...  44.8 us
    pallas_call x21, Pallas kernels, run(): pl.pallas_call(body, out_shape=outs, in_specs=[pl.BlockSpec(memory_space=...  27.2 us
    unnamed x27, local copies, waits for them, and re-layouts  5.97 us
  transfers between devices with their start and end apart: 49, of which 15 were waited for; matrix products, arithmetic and copies ran while one was open for 1% of the time, Pallas kernels for 19%

profile of v2, /device:TPU:0, one launch (start us, length us, event | category | flops | bytes accessed | tf_op | source)
XLA Modules:
  0.0 136.1 jit_solution(14354175977898053606)
XLA Ops:
  0.6 3.0 %collective-permute-start.19 = (s32[2,256]{1,0:T(2,128)}, s32[2,256]{1,0:T(2,128)S(1)}, u32[]{:S(2)}, u32[]{:S(2)}) collective-permute-start(s32[2,256]{1,0:T(2,128)} %bitcast.35), channel_id=1, source_target_pairs={{0,16},{8,24},{16,0},{24,8},{1,17},{9,25},{17,1},{25,9},{2,18},{10... | collective-permute-start | bytes 6152 | tf_op jit(solution)/shard_map/ppermute | solution.py:14
  3.7 0.6 stack.33.where_ref
  4.3 2.3 %shard_map.111 = (bf16[128,256]{1,0:T(8,128)(2,1)}, bf16[256,128]{1,0:T(8,128)(2,1)}, bf16[128,256]{1,0:T(8,128)(2,1)}, bf16[128,256]{1,0:T(8,128)(2,1)}) custom-call(s32[6]{0:T(128)} %stack.33.where_ref, bf16[512,256]{1,0:T(8,128)(2,1)} %o_ref.1, bf16[1024,128]{1,0:T(8,128)(2,1)} %d_ref.1, bf16[2,128,1024]{2,1,0:T(8,128)(2,1)} %t_ref.1), custom_call_target="tpu_custom_call" | custom-call | tf_op jit(solution)/shard_map/pallas_call | solution.py:269
  6.6 3.6 %collective-permute-start.14 = (bf16[128,256]{1,0:T(8,128)(2,1)}, bf16[128,256]{1,0:T(8,128)(2,1)S(1)}, u32[]{:S(2)}, u32[]{:S(2)}) collective-permute-start(bf16[128,256]{1,0:T(8,128)(2,1)} %get-tuple-element.35.refs_0_), channel_id=1, source_target_pairs={{0,3},{1,2},{2,1},{3,0},{4,7},{5,6},{6,5},{7,4},{8,11},{9,10},{10,... | collective-permute-start | bytes 196616 | tf_op jit(solution)/shard_map/ppermute | solution.py:14
  10.2 0.8 collective-permute-start.12
  11.0 3.6 %collective-permute-start.32 = (bf16[128,256]{1,0:T(8,128)(2,1)}, bf16[128,256]{1,0:T(8,128)(2,1)S(1)}, u32[]{:S(2)}, u32[]{:S(2)}) collective-permute-start(bf16[128,256]{1,0:T(8,128)(2,1)} %get-tuple-element.42.refs_0_), channel_id=1, source_target_pairs={{0,3},{1,2},{2,1},{3,0},{4,7},{5,6},{6,5},{7,4},{8,11},{9,10},{10,... | collective-permute-start | bytes 196616 | tf_op jit(solution)/shard_map/ppermute | solution.py:14
  14.6 0.8 fusion.4
  15.4 1.0 copy-done
  16.4 1.0 copy-done.2
  17.5 0.6 copy-done.5
  18.1 0.9 shard_map.114
  19.2 3.0 %collective-permute-start.2 = (bf16[256,128]{1,0:T(8,128)(2,1)}, bf16[256,128]{1,0:T(8,128)(2,1)S(1)}, u32[]{:S(2)}, u32[]{:S(2)}) collective-permute-start(bf16[256,128]{1,0:T(8,128)(2,1)} %get-tuple-element.32.refs_0_), channel_id=1, source_target_pairs={{0,3},{1,2},{2,1},{3,0},{4,7},{5,6},{6,5},{7,4},{8,11},{9,10},{10,... | collective-permute-start | bytes 196616 | tf_op jit(solution)/shard_map/ppermute | solution.py:14
  22.2 1.4 collective-permute-start.30
  23.6 0.8 copy-done.9
  25.0 2.2 %collective-permute-done.30.refs_1_ = bf16[128,256]{1,0:T(8,128)(2,1)S(1)} collective-permute-done((bf16[128,256]{1,0:T(8,128)(2,1)}, bf16[128,256]{1,0:T(8,128)(2,1)S(1)}, u32[]{:S(2)}, u32[]{:S(2)}) %collective-permute-start.30) | collective-permute-done | bytes 65568 | tf_op jit(solution)/shard_map/ppermute | solution.py:14
  27.2 1.7 %collective-permute-start = (bf16[256,128]{1,0:T(8,128)(2,1)}, bf16[256,128]{1,0:T(8,128)(2,1)S(1)}, u32[]{:S(2)}, u32[]{:S(2)}) collective-permute-start(bf16[256,128]{1,0:T(8,128)(2,1)} %get-tuple-element.32.refs_0_), channel_id=1, source_target_pairs={{0,1},{1,0},{2,3},{3,2},{4,5},{5,4},{6,7},{7,6},{8,9},{9,8},{10,11... | collective-permute-start | bytes 196616 | tf_op jit(solution)/shard_map/ppermute | solution.py:14
  29.0 0.8 copy-done.8
  30.4 2.2 %collective-permute-start.24 = (bf16[128,256]{1,0:T(8,128)(2,1)S(1)}, bf16[128,256]{1,0:T(8,128)(2,1)S(1)}, u32[]{:S(2)}, u32[]{:S(2)}) collective-permute-start(bf16[128,256]{1,0:T(8,128)(2,1)S(1)} %copy-done.6), channel_id=1, source_target_pairs={{0,3},{1,2},{2,1},{3,0},{4,7},{5,6},{6,5},{7,4},{8,11},{9,10},{10,... | collective-permute-start | bytes 196616 | tf_op jit(solution)/shard_map/ppermute | solution.py:14
  32.6 1.6 %collective-permute-start.33 = (bf16[512,256]{1,0:T(8,128)(2,1)S(1)}, bf16[512,256]{1,0:T(8,128)(2,1)S(1)}, u32[]{:S(2)}, u32[]{:S(2)}) collective-permute-start(bf16[512,256]{1,0:T(8,128)(2,1)S(1)} %shard_map.122.own_ref), channel_id=1, source_target_pairs={{0,4},{4,0},{1,5},{5,1},{2,6},{6,2},{3,7},{7,3},{8,12},{12,8},{9,1... | collective-permute-start | bytes 786440 | tf_op jit(solution)/shard_map/ppermute | solution.py:14
  34.7 2.2 %collective-permute-start.22 = (bf16[128,256]{1,0:T(8,128)(2,1)S(1)}, bf16[128,256]{1,0:T(8,128)(2,1)S(1)}, u32[]{:S(2)}, u32[]{:S(2)}) collective-permute-start(bf16[128,256]{1,0:T(8,128)(2,1)S(1)} %copy-done.6), channel_id=1, source_target_pairs={{0,1},{1,0},{2,3},{3,2},{4,5},{5,4},{6,7},{7,6},{8,9},{9,8},{10,11... | collective-permute-start | bytes 196616 | tf_op jit(solution)/shard_map/ppermute | solution.py:14
  37.0 1.5 %collective-permute-done.23.refs_2_ = bf16[128,256]{1,0:T(8,128)(2,1)S(1)} collective-permute-done((bf16[128,256]{1,0:T(8,128)(2,1)S(1)}, bf16[128,256]{1,0:T(8,128)(2,1)S(1)}, u32[]{:S(2)}, u32[]{:S(2)}) %collective-permute-start.23) | collective-permute-done | bytes 65568 | tf_op jit(solution)/shard_map/ppermute | solution.py:14
  40.2 1.6 %collective-permute-start.4 = (bf16[256,512]{1,0:T(8,128)(2,1)S(1)}, bf16[256,512]{1,0:T(8,128)(2,1)S(1)}, u32[]{:S(2)}, u32[]{:S(2)}) collective-permute-start(bf16[256,512]{1,0:T(8,128)(2,1)S(1)} %shard_map.112.refs_0_), channel_id=1, source_target_pairs={{0,16},{8,24},{16,0},{24,8},{1,17},{9,25},{17,1},{25,9},{2,18},{10... | collective-permute-start | bytes 786440 | tf_op jit(solution)/shard_map/ppermute | solution.py:14
  41.8 1.9 %collective-permute-done.11.far_ref = bf16[4,128,128]{2,1,0:T(8,128)(2,1)S(1)} collective-permute-done((bf16[4,128,128]{2,1,0:T(8,128)(2,1)S(1)}, bf16[4,128,128]{2,1,0:T(8,128)(2,1)S(1)}, u32[]{:S(2)}, u32[]{:S(2)}) %collective-permute-start.11) | collective-permute-done | bytes 131104 | tf_op jit(solution)/shard_map/ppermute | solution.py:14
  43.8 1.4 %collective-permute-start.3 = (bf16[256,512]{1,0:T(8,128)(2,1)S(1)}, bf16[256,512]{1,0:T(8,128)(2,1)S(1)}, u32[]{:S(2)}, u32[]{:S(2)}) collective-permute-start(bf16[256,512]{1,0:T(8,128)(2,1)S(1)} %shard_map.112.refs_0_), channel_id=1, source_target_pairs={{0,4},{4,0},{1,5},{5,1},{2,6},{6,2},{3,7},{7,3},{8,12},{12,8},{9,1... | collective-permute-start | bytes 786440 | tf_op jit(solution)/shard_map/ppermute | solution.py:14
  45.1 0.7 collective-permute-start.25
  45.8 1.5 %shard_map.123 = (bf16[256,256]{1,0:T(8,128)(2,1)S(1)}, bf16[256,256]{1,0:T(8,128)(2,1)S(1)}, bf16[256,256]{1,0:T(8,128)(2,1)S(1)}, bf16[256,256]{1,0:T(8,128)(2,1)S(1)}) custom-call(s32[6]{0:T(128)S(1)} %copy-done.5, s32[4,256]{1,0:T(4,128)S(1)} %pad_add_fusion.1.ids_ref, bf16[512,256]{1,0:T(8,128)(2,1)S(1)} %shard_map.122.own_ref, ...), custom_call_target="tpu_custom_call" | custom-call | tf_op jit(solution)/shard_map/pallas_call | solution.py:234
  47.3 9.0 %collective-permute-done.25.got_ref = bf16[512,256]{1,0:T(8,128)(2,1)S(1)} collective-permute-done((bf16[512,256]{1,0:T(8,128)(2,1)S(1)}, bf16[512,256]{1,0:T(8,128)(2,1)S(1)}, u32[]{:S(2)}, u32[]{:S(2)}) %collective-permute-start.25) | collective-permute-done | bytes 262176 | tf_op jit(solution)/shard_map/ppermute | solution.py:14
  56.3 1.1 collective-permute-start.34
  57.4 1.5 %shard_map.120 = (bf16[256,256]{1,0:T(8,128)(2,1)S(1)}, bf16[256,256]{1,0:T(8,128)(2,1)S(1)}, bf16[256,256]{1,0:T(8,128)(2,1)S(1)}, bf16[256,256]{1,0:T(8,128)(2,1)S(1)}) custom-call(s32[6]{0:T(128)S(1)} %copy-done.5, s32[4,256]{1,0:T(4,128)S(1)} %pad_add_fusion.ids_ref, bf16[512,256]{1,0:T(8,128)(2,1)S(1)} %shard_map.119.own_ref, ...), custom_call_target="tpu_custom_call" | custom-call | tf_op jit(solution)/shard_map/pallas_call | solution.py:234
  59.0 1.0 collective-permute-start.36
  59.9 1.1 collective-permute-start.26
  61.3 1.1 collective-permute-start.5
  62.4 0.9 collective-permute-start.28
  63.3 2.0 %shard_map.115 = (bf16[512,512]{1,0:T(8,128)(2,1)S(1)}, bf16[4,128,128]{2,1,0:T(8,128)(2,1)S(1)}) custom-call(s32[6]{0:T(128)S(1)} %copy-done.5, bf16[512,512]{1,0:T(8,128)(2,1)S(1)} %bitcast.28, bf16[512,512]{1,0:T(8,128)(2,1)S(1)} %bitcast.21, bf16[512,512]{1,0:T(8,128)(2,1)S(1)} %bitcast.25, bf16[4,128,128]{2,1,0:T(8,128)(2,1)S(1)} %collective-permute-done.10.core_ref, ...), custom_call_target="tpu_custom_call" | custom-call | tf_op jit(solution)/shard_map/pallas_call | solution.py:234
  65.3 1.2 shard_map.118
  66.5 1.3 collective-permute-start.18
  68.3 7.9 %collective-permute-done.28 = bf16[256,256]{1,0:T(8,128)(2,1)S(1)} collective-permute-done((bf16[256,256]{1,0:T(8,128)(2,1)S(1)}, bf16[256,256]{1,0:T(8,128)(2,1)S(1)}, u32[]{:S(2)}, u32[]{:S(2)}) %collective-permute-start.28) | collective-permute-done | bytes 131104 | tf_op jit(solution)/shard_map/ppermute | solution.py:14
  77.9 1.2 shard_map.117
  79.2 0.6 shard_map.124
  79.8 0.6 shard_map.121
  80.4 2.0 %shard_map.113 = (bf16[1024,1024]{1,0:T(8,128)(2,1)}, f32[256,1024]{1,0:T(8,128)S(1)}) custom-call(s32[6]{0:T(128)S(1)} %copy-done.5, bf16[256,512]{1,0:T(8,128)(2,1)S(1)} %shard_map.112.refs_0_, bf16[256,512]{1,0:T(8,128)(2,1)S(1)} %collective-permute-done.3.refs_1_, bf16[256,512]{1,0:T(8,128)(2,1)S(1)} %collective-permute-done.4.refs_2_, ...), custom_call_target="tpu_custom_call" | custom-call | tf_op jit(solution)/shard_map/pallas_call | solution.py:234
  82.8 1.3 copy-done.10
  84.1 0.8 fusion
  85.4 1.2 multiply_reduce_fusion
  86.9 0.9 collective-permute-start.38
  87.9 13.3 %collective-permute-done.38.got = bf16[256,1024]{1,0:T(8,128)(2,1)S(1)} collective-permute-done((bf16[256,1024]{1,0:T(8,128)(2,1)S(1)}, bf16[256,1024]{1,0:T(8,128)(2,1)S(1)}, u32[]{:S(2)}, u32[]{:S(2)}) %collective-permute-start.38) | collective-permute-done | bytes 524320 | tf_op jit(solution)/shard_map/ppermute | solution.py:14
  101.2 1.3 shard_map.128
  102.6 1.9 %collective-permute-done.41.got_ref = bf16[2,128,1024]{2,1,0:T(8,128)(2,1)S(1)} collective-permute-done((bf16[2,128,1024]{2,1,0:T(8,128)(2,1)S(1)}, bf16[2,128,1024]{2,1,0:T(8,128)(2,1)S(1)}, u32[]{:S(2)}, u32[]{:S(2)}) %collective-permute-start.41) | collective-permute-done | bytes 524320 | tf_op jit(solution)/shard_map/ppermute | solution.py:14
  104.5 0.6 shard_map.129
  105.1 1.0 collective-permute-start.42
  106.1 2.3 %shard_map.125 = (bf16[512,512]{1,0:T(8,128)(2,1)S(1)}, bf16[4,128,128]{2,1,0:T(8,128)(2,1)S(1)}) custom-call(s32[6]{0:T(128)S(1)} %copy-done.5, bf16[256,1024]{1,0:T(8,128)(2,1)S(1)} %subtract_convert_fusion.own, bf16[256,1024]{1,0:T(8,128)(2,1)S(1)} %collective-permute-done.38.got, bf16[128,1024]{1,0:T(8,128)(2,1)S(1)} %shard_map.116.refs_0_.o0, ...), custom_call_target="tpu_custom_call" | custom-call | tf_op jit(solution)/shard_map/pallas_call | solution.py:234
  108.4 5.1 %collective-permute-done.42.got_ref = bf16[128,1024]{1,0:T(8,128)(2,1)S(1)} collective-permute-done((bf16[128,1024]{1,0:T(8,128)(2,1)S(1)}, bf16[128,1024]{1,0:T(8,128)(2,1)S(1)}, u32[]{:S(2)}, u32[]{:S(2)}) %collective-permute-start.42) | collective-permute-done | bytes 262176 | tf_op jit(solution)/shard_map/ppermute | solution.py:14
  113.5 0.6 shard_map.130
  114.1 1.1 collective-permute-start.43
  115.3 1.7 %collective-permute-start.44 = (bf16[128,256]{1,0:T(8,128)(2,1)S(1)}, bf16[128,256]{1,0:T(8,128)(2,1)S(1)}, u32[]{:S(2)}, u32[]{:S(2)}) collective-permute-start(bf16[128,256]{1,0:T(8,128)(2,1)S(1)} %get-tuple-element.58), channel_id=1, source_target_pairs={{0,2},{1,3},{2,0},{3,1},{4,6},{5,7},{6,4},{7,5},{8,10},{9,11},{10,... | collective-permute-start | bytes 196616 | tf_op jit(solution)/shard_map/ppermute | solution.py:14
  116.9 1.7 %collective-permute-start.45 = (bf16[128,256]{1,0:T(8,128)(2,1)S(1)}, bf16[128,256]{1,0:T(8,128)(2,1)S(1)}, u32[]{:S(2)}, u32[]{:S(2)}) collective-permute-start(bf16[128,256]{1,0:T(8,128)(2,1)S(1)} %get-tuple-element.59), channel_id=1, source_target_pairs={{0,3},{1,2},{2,1},{3,0},{4,7},{5,6},{6,5},{7,4},{8,11},{9,10},{10,... | collective-permute-start | bytes 196616 | tf_op jit(solution)/shard_map/ppermute | solution.py:14
  118.6 1.0 collective-permute-start.40
  119.6 2.4 %collective-permute-done.44.refs_1_ = bf16[128,256]{1,0:T(8,128)(2,1)S(1)} collective-permute-done((bf16[128,256]{1,0:T(8,128)(2,1)S(1)}, bf16[128,256]{1,0:T(8,128)(2,1)S(1)}, u32[]{:S(2)}, u32[]{:S(2)}) %collective-permute-start.44) | collective-permute-done | bytes 65568 | tf_op jit(solution)/shard_map/ppermute | solution.py:14
  122.0 1.1 collective-permute-done.45.refs_2_
  123.7 1.5 %collective-permute-start.46 = (bf16[128,256]{1,0:T(8,128)(2,1)S(1)}, bf16[128,256]{1,0:T(8,128)(2,1)S(1)}, u32[]{:S(2)}, u32[]{:S(2)}) collective-permute-start(bf16[128,256]{1,0:T(8,128)(2,1)S(1)} %shard_map.131.refs_0_), channel_id=1, source_target_pairs={{0,16},{8,24},{16,0},{24,8},{1,17},{9,25},{17,1},{25,9},{2,18},{10... | collective-permute-start | bytes 196616 | tf_op jit(solution)/shard_map/ppermute | solution.py:14
  125.2 2.8 %collective-permute-done.46.refs_1_ = bf16[128,256]{1,0:T(8,128)(2,1)S(1)} collective-permute-done((bf16[128,256]{1,0:T(8,128)(2,1)S(1)}, bf16[128,256]{1,0:T(8,128)(2,1)S(1)}, u32[]{:S(2)}, u32[]{:S(2)}) %collective-permute-start.46) | collective-permute-done | bytes 65568 | tf_op jit(solution)/shard_map/ppermute | solution.py:14
  128.0 2.7 %shard_map.126 = bf16[512,512]{1,0:T(8,128)(2,1)} custom-call(s32[6]{0:T(128)S(1)} %copy-done.5, bf16[512,512]{1,0:T(8,128)(2,1)S(1)} %get-tuple-element.47.g_ref, bf16[512,512]{1,0:T(8,128)(2,1)S(1)} %bitcast.22, bf16[512,512]{1,0:T(8,128)(2,1)S(1)} %bitcast.26, bf16[4,128,128]{2,1,0:T(8,128)(2,1)S(1)} %get-tuple-element.48.s_ref), custom_call_target="tpu_custom_call" | custom-call | tf_op jit(solution)/shard_map/pallas_call | solution.py:234
  130.8 4.0 %shard_map.127 = (bf16[512,512]{1,0:T(8,128)(2,1)}, bf16[512,512]{1,0:T(8,128)(2,1)}) custom-call(s32[6]{0:T(128)S(1)} %copy-done.5, bf16[512,512]{1,0:T(8,128)(2,1)S(1)} %get-tuple-element.47.g_ref, bf16[512,512]{1,0:T(8,128)(2,1)S(1)} %bitcast.30, bf16[512,512]{1,0:T(8,128)(2,1)S(1)} %bitcast.23, bf16[512,512]{1,0:T(8,128)(2,1)S(1)} %bitcast.27, ...), custom_call_target="tpu_custom_call" | custom-call | tf_op jit(solution)/shard_map/pallas_call | solution.py:234
  134.7 1.4 %shard_map.132 = f32[512,256]{1,0:T(8,128)} custom-call(s32[6]{0:T(128)S(1)} %copy-done.5, bf16[128,256]{1,0:T(8,128)(2,1)S(1)} %shard_map.131.refs_0_, bf16[128,256]{1,0:T(8,128)(2,1)S(1)} %collective-permute-done.46.refs_1_, bf16[128,256]{1,0:T(8,128)(2,1)S(1)} %collective-permute-done.47.refs_2_, bf16[128,256]{1,0:T(8,128)(2,1)S(1)} %collective-permute-done.48.refs_3_), custom_call_target="tpu_custom_call" | custom-call | tf_op jit(solution)/shard_map/pallas_call | solution.py:234
  (100 shorter events, 8.2 us)
Async XLA Ops:
  0.6 18.4 %copy-start.12 = (s32[1,256,2]{1,2,0:T(2,128)S(1)}, s32[1,256,2]{1,2,0:T(2,128)}, u32[]{:S(2)}) copy-start(s32[1,256,2]{1,2,0:T(2,128)} %param.14) | copy-start | bytes 6148
  0.6 14.0 %collective-permute-start.19 = (s32[2,256]{1,0:T(2,128)}, s32[2,256]{1,0:T(2,128)S(1)}, u32[]{:S(2)}, u32[]{:S(2)}) collective-permute-start(s32[2,256]{1,0:T(2,128)} %bitcast.35), channel_id=1, source_target_pairs={{0,16},{8,24},{16,0},{24,8},{1,17},{9,25},{17,1},{25,9},{2,18},{10... | collective-permute-start | bytes 6152 | tf_op jit(solution)/shard_map/ppermute | solution.py:14
  6.6 12.4 %collective-permute-start.14 = (bf16[128,256]{1,0:T(8,128)(2,1)}, bf16[128,256]{1,0:T(8,128)(2,1)S(1)}, u32[]{:S(2)}, u32[]{:S(2)}) collective-permute-start(bf16[128,256]{1,0:T(8,128)(2,1)} %get-tuple-element.35.refs_0_), channel_id=1, source_target_pairs={{0,3},{1,2},{2,1},{3,0},{4,7},{5,6},{6,5},{7,4},{8,11},{9,10},{10,... | collective-permute-start | bytes 196616 | tf_op jit(solution)/shard_map/ppermute | solution.py:14
  10.2 8.9 %collective-permute-start.13 = (bf16[128,256]{1,0:T(8,128)(2,1)}, bf16[128,256]{1,0:T(8,128)(2,1)S(1)}, u32[]{:S(2)}, u32[]{:S(2)}) collective-permute-start(bf16[128,256]{1,0:T(8,128)(2,1)} %get-tuple-element.35.refs_0_), channel_id=1, source_target_pairs={{0,2},{1,3},{2,0},{3,1},{4,6},{5,7},{6,4},{7,5},{8,10},{9,11},{10,... | collective-permute-start | bytes 196616 | tf_op jit(solution)/shard_map/ppermute | solution.py:14
  10.2 12.0 %collective-permute-start.12 = (bf16[128,256]{1,0:T(8,128)(2,1)}, bf16[128,256]{1,0:T(8,128)(2,1)S(1)}, u32[]{:S(2)}, u32[]{:S(2)}) collective-permute-start(bf16[128,256]{1,0:T(8,128)(2,1)} %get-tuple-element.35.refs_0_), channel_id=1, source_target_pairs={{0,1},{1,0},{2,3},{3,2},{4,5},{5,4},{6,7},{7,6},{8,9},{9,8},{10,11... | collective-permute-start | bytes 196616 | tf_op jit(solution)/shard_map/ppermute | solution.py:14
  11.0 11.2 %collective-permute-start.32 = (bf16[128,256]{1,0:T(8,128)(2,1)}, bf16[128,256]{1,0:T(8,128)(2,1)S(1)}, u32[]{:S(2)}, u32[]{:S(2)}) collective-permute-start(bf16[128,256]{1,0:T(8,128)(2,1)} %get-tuple-element.42.refs_0_), channel_id=1, source_target_pairs={{0,3},{1,2},{2,1},{3,0},{4,7},{5,6},{6,5},{7,4},{8,11},{9,10},{10,... | collective-permute-start | bytes 196616 | tf_op jit(solution)/shard_map/ppermute | solution.py:14
  14.6 9.0 %collective-permute-start.31 = (bf16[128,256]{1,0:T(8,128)(2,1)}, bf16[128,256]{1,0:T(8,128)(2,1)S(1)}, u32[]{:S(2)}, u32[]{:S(2)}) collective-permute-start(bf16[128,256]{1,0:T(8,128)(2,1)} %get-tuple-element.42.refs_0_), channel_id=1, source_target_pairs={{0,2},{1,3},{2,0},{3,1},{4,6},{5,7},{6,4},{7,5},{8,10},{9,11},{10,... | collective-permute-start | bytes 196616 | tf_op jit(solution)/shard_map/ppermute | solution.py:14
  15.4 1.0 copy-start
  16.4 1.0 copy-start.2
  17.5 0.6 copy-start.5
  18.1 12.3 %copy-start.6 = (bf16[128,256]{1,0:T(8,128)(2,1)S(1)}, bf16[128,256]{1,0:T(8,128)(2,1)}, u32[]{:S(2)}) copy-start(bf16[128,256]{1,0:T(8,128)(2,1)} %get-tuple-element.36.refs_0_) | copy-start | bytes 196612
  18.1 20.9 %copy-start.7 = (bf16[256,128]{1,0:T(8,128)(2,1)S(1)}, bf16[256,128]{1,0:T(8,128)(2,1)}, u32[]{:S(2)}) copy-start(bf16[256,128]{1,0:T(8,128)(2,1)} %get-tuple-element.32.refs_0_) | copy-start | bytes 196612
  19.0 44.3 %copy-start.1 = (bf16[1,512,512]{2,1,0:T(8,128)(2,1)S(1)}, bf16[1,512,512]{2,1,0:T(8,128)(2,1)}, u32[]{:S(2)}) copy-start(bf16[1,512,512]{2,1,0:T(8,128)(2,1)} %param.9) | copy-start | bytes 1572868
  19.0 44.3 %copy-start.3 = (bf16[1,512,512]{2,1,0:T(8,128)(2,1)S(1)}, bf16[1,512,512]{2,1,0:T(8,128)(2,1)}, u32[]{:S(2)}) copy-start(bf16[1,512,512]{2,1,0:T(8,128)(2,1)} %param.10) | copy-start | bytes 1572868
  19.0 44.3 %copy-start.4 = (bf16[1,512,512]{2,1,0:T(8,128)(2,1)S(1)}, bf16[1,512,512]{2,1,0:T(8,128)(2,1)}, u32[]{:S(2)}) copy-start(bf16[1,512,512]{2,1,0:T(8,128)(2,1)} %param.8) | copy-start | bytes 1572868
  19.1 11.3 %collective-permute-start.20 = (s32[2,256]{1,0:T(2,128)S(1)}, s32[2,256]{1,0:T(2,128)S(1)}, u32[]{:S(2)}, u32[]{:S(2)}) collective-permute-start(s32[2,256]{1,0:T(2,128)S(1)} %bitcast.37), channel_id=1, source_target_pairs={{0,8},{8,0},{16,24},{24,16},{1,9},{9,1},{17,25},{25,17},{2,10},{10... | collective-permute-start | bytes 6152 | tf_op jit(solution)/shard_map/ppermute | solution.py:14
  19.2 13.4 %collective-permute-start.2 = (bf16[256,128]{1,0:T(8,128)(2,1)}, bf16[256,128]{1,0:T(8,128)(2,1)S(1)}, u32[]{:S(2)}, u32[]{:S(2)}) collective-permute-start(bf16[256,128]{1,0:T(8,128)(2,1)} %get-tuple-element.32.refs_0_), channel_id=1, source_target_pairs={{0,3},{1,2},{2,1},{3,0},{4,7},{5,6},{6,5},{7,4},{8,11},{9,10},{10,... | collective-permute-start | bytes 196616 | tf_op jit(solution)/shard_map/ppermute | solution.py:14
  22.2 10.4 %collective-permute-start.1 = (bf16[256,128]{1,0:T(8,128)(2,1)}, bf16[256,128]{1,0:T(8,128)(2,1)S(1)}, u32[]{:S(2)}, u32[]{:S(2)}) collective-permute-start(bf16[256,128]{1,0:T(8,128)(2,1)} %get-tuple-element.32.refs_0_), channel_id=1, source_target_pairs={{0,2},{1,3},{2,0},{3,1},{4,6},{5,7},{6,4},{7,5},{8,10},{9,11},{10,... | collective-permute-start | bytes 196616 | tf_op jit(solution)/shard_map/ppermute | solution.py:14
  22.2 5.0 %collective-permute-start.30 = (bf16[128,256]{1,0:T(8,128)(2,1)}, bf16[128,256]{1,0:T(8,128)(2,1)S(1)}, u32[]{:S(2)}, u32[]{:S(2)}) collective-permute-start(bf16[128,256]{1,0:T(8,128)(2,1)} %get-tuple-element.42.refs_0_), channel_id=1, source_target_pairs={{0,1},{1,0},{2,3},{3,2},{4,5},{5,4},{6,7},{7,6},{8,9},{9,8},{10,11... | collective-permute-start | bytes 196616 | tf_op jit(solution)/shard_map/ppermute | solution.py:14
  23.6 10.6 %collective-permute-start.10 = (bf16[4,128,128]{2,1,0:T(8,128)(2,1)S(1)}, bf16[4,128,128]{2,1,0:T(8,128)(2,1)S(1)}, u32[]{:S(2)}, u32[]{:S(2)}) collective-permute-start(bf16[4,128,128]{2,1,0:T(8,128)(2,1)S(1)} %shard_map.114), channel_id=1, source_target_pairs={{0,8},{8,0},{16,24},{24,16},{1,9},{9,1},{17,25},{25,17},{2,10},{10... | collective-permute-start | bytes 393224 | tf_op jit(solution)/shard_map/ppermute | solution.py:14
  23.6 0.8 copy-start.9
  27.2 7.5 %collective-permute-start = (bf16[256,128]{1,0:T(8,128)(2,1)}, bf16[256,128]{1,0:T(8,128)(2,1)S(1)}, u32[]{:S(2)}, u32[]{:S(2)}) collective-permute-start(bf16[256,128]{1,0:T(8,128)(2,1)} %get-tuple-element.32.refs_0_), channel_id=1, source_target_pairs={{0,1},{1,0},{2,3},{3,2},{4,5},{5,4},{6,7},{7,6},{8,9},{9,8},{10,11... | collective-permute-start | bytes 196616 | tf_op jit(solution)/shard_map/ppermute | solution.py:14
  29.0 0.8 copy-start.8
  30.4 6.6 %collective-permute-start.24 = (bf16[128,256]{1,0:T(8,128)(2,1)S(1)}, bf16[128,256]{1,0:T(8,128)(2,1)S(1)}, u32[]{:S(2)}, u32[]{:S(2)}) collective-permute-start(bf16[128,256]{1,0:T(8,128)(2,1)S(1)} %copy-done.6), channel_id=1, source_target_pairs={{0,3},{1,2},{2,1},{3,0},{4,7},{5,6},{6,5},{7,4},{8,11},{9,10},{10,... | collective-permute-start | bytes 196616 | tf_op jit(solution)/shard_map/ppermute | solution.py:14
  32.6 5.9 %collective-permute-start.23 = (bf16[128,256]{1,0:T(8,128)(2,1)S(1)}, bf16[128,256]{1,0:T(8,128)(2,1)S(1)}, u32[]{:S(2)}, u32[]{:S(2)}) collective-permute-start(bf16[128,256]{1,0:T(8,128)(2,1)S(1)} %copy-done.6), channel_id=1, source_target_pairs={{0,2},{1,3},{2,0},{3,1},{4,6},{5,7},{6,4},{7,5},{8,10},{9,11},{10,... | collective-permute-start | bytes 196616 | tf_op jit(solution)/shard_map/ppermute | solution.py:14
  32.6 12.5 %collective-permute-start.33 = (bf16[512,256]{1,0:T(8,128)(2,1)S(1)}, bf16[512,256]{1,0:T(8,128)(2,1)S(1)}, u32[]{:S(2)}, u32[]{:S(2)}) collective-permute-start(bf16[512,256]{1,0:T(8,128)(2,1)S(1)} %shard_map.122.own_ref), channel_id=1, source_target_pairs={{0,4},{4,0},{1,5},{5,1},{2,6},{6,2},{3,7},{7,3},{8,12},{12,8},{9,1... | collective-permute-start | bytes 786440 | tf_op jit(solution)/shard_map/ppermute | solution.py:14
  34.2 11.6 %collective-permute-start.15 = (bf16[128,1024]{1,0:T(8,128)(2,1)S(1)}, bf16[128,1024]{1,0:T(8,128)(2,1)S(1)}, u32[]{:S(2)}, u32[]{:S(2)}) collective-permute-start(bf16[128,1024]{1,0:T(8,128)(2,1)S(1)} %shard_map.116.refs_0_.o0), channel_id=1, source_target_pairs={{0,16},{8,24},{16,0},{24,8},{1,17},{9,25},{17,1},{25,9},{2,18},{10... | collective-permute-start | bytes 786440 | tf_op jit(solution)/shard_map/ppermute | solution.py:14
  34.7 4.9 %collective-permute-start.22 = (bf16[128,256]{1,0:T(8,128)(2,1)S(1)}, bf16[128,256]{1,0:T(8,128)(2,1)S(1)}, u32[]{:S(2)}, u32[]{:S(2)}) collective-permute-start(bf16[128,256]{1,0:T(8,128)(2,1)S(1)} %copy-done.6), channel_id=1, source_target_pairs={{0,1},{1,0},{2,3},{3,2},{4,5},{5,4},{6,7},{7,6},{8,9},{9,8},{10,11... | collective-permute-start | bytes 196616 | tf_op jit(solution)/shard_map/ppermute | solution.py:14
  37.0 3.3 %collective-permute-start.21 = (s32[2,256]{1,0:T(2,128)S(1)}, s32[2,256]{1,0:T(2,128)S(1)}, u32[]{:S(2)}, u32[]{:S(2)}) collective-permute-start(s32[2,256]{1,0:T(2,128)S(1)} %collective-permute-done.19), channel_id=1, source_target_pairs={{0,8},{8,0},{16,24},{24,16},{1,9},{9,1},{17,25},{25,17},{2,10},{10... | collective-permute-start | bytes 6152 | tf_op jit(solution)/shard_map/ppermute | solution.py:14
  38.5 5.3 %collective-permute-start.11 = (bf16[4,128,128]{2,1,0:T(8,128)(2,1)S(1)}, bf16[4,128,128]{2,1,0:T(8,128)(2,1)S(1)}, u32[]{:S(2)}, u32[]{:S(2)}) collective-permute-start(bf16[4,128,128]{2,1,0:T(8,128)(2,1)S(1)} %add_convert_fusion.3), channel_id=1, source_target_pairs={{0,16},{8,24},{16,0},{24,8},{1,17},{9,25},{17,1},{25,9},{2,18},{10... | collective-permute-start | bytes 393224 | tf_op jit(solution)/shard_map/ppermute | solution.py:14
  39.6 17.8 %collective-permute-start.16 = (bf16[128,1024]{1,0:T(8,128)(2,1)S(1)}, bf16[128,1024]{1,0:T(8,128)(2,1)S(1)}, u32[]{:S(2)}, u32[]{:S(2)}) collective-permute-start(bf16[128,1024]{1,0:T(8,128)(2,1)S(1)} %shard_map.116.refs_0_.o0), channel_id=1, source_target_pairs={{0,8},{8,0},{16,24},{24,16},{1,9},{9,1},{17,25},{25,17},{2,10},{10... | collective-permute-start | bytes 786440 | tf_op jit(solution)/shard_map/ppermute | solution.py:14
  40.2 18.7 %collective-permute-start.4 = (bf16[256,512]{1,0:T(8,128)(2,1)S(1)}, bf16[256,512]{1,0:T(8,128)(2,1)S(1)}, u32[]{:S(2)}, u32[]{:S(2)}) collective-permute-start(bf16[256,512]{1,0:T(8,128)(2,1)S(1)} %shard_map.112.refs_0_), channel_id=1, source_target_pairs={{0,16},{8,24},{16,0},{24,8},{1,17},{9,25},{17,1},{25,9},{2,18},{10... | collective-permute-start | bytes 786440 | tf_op jit(solution)/shard_map/ppermute | solution.py:14
  43.8 16.2 %collective-permute-start.3 = (bf16[256,512]{1,0:T(8,128)(2,1)S(1)}, bf16[256,512]{1,0:T(8,128)(2,1)S(1)}, u32[]{:S(2)}, u32[]{:S(2)}) collective-permute-start(bf16[256,512]{1,0:T(8,128)(2,1)S(1)} %shard_map.112.refs_0_), channel_id=1, source_target_pairs={{0,4},{4,0},{1,5},{5,1},{2,6},{6,2},{3,7},{7,3},{8,12},{12,8},{9,1... | collective-permute-start | bytes 786440 | tf_op jit(solution)/shard_map/ppermute | solution.py:14
  45.1 11.1 %collective-permute-start.25 = (bf16[512,256]{1,0:T(8,128)(2,1)S(1)}, bf16[512,256]{1,0:T(8,128)(2,1)S(1)}, u32[]{:S(2)}, u32[]{:S(2)}) collective-permute-start(bf16[512,256]{1,0:T(8,128)(2,1)S(1)} %shard_map.119.own_ref), channel_id=1, source_target_pairs={{0,4},{4,0},{1,5},{5,1},{2,6},{6,2},{3,7},{7,3},{8,12},{12,8},{9,1... | collective-permute-start | bytes 786440 | tf_op jit(solution)/shard_map/ppermute | solution.py:14
  45.8 16.6 %collective-permute-start.17 = (bf16[128,1024]{1,0:T(8,128)(2,1)S(1)}, bf16[128,1024]{1,0:T(8,128)(2,1)S(1)}, u32[]{:S(2)}, u32[]{:S(2)}) collective-permute-start(bf16[128,1024]{1,0:T(8,128)(2,1)S(1)} %collective-permute-done.15.refs_1_.o1), channel_id=1, source_target_pairs={{0,8},{8,0},{16,24},{24,16},{1,9},{9,1},{17,25},{25,17},{2,10},{10... | collective-permute-start | bytes 786440 | tf_op jit(solution)/shard_map/ppermute | solution.py:14
  56.3 5.0 %collective-permute-start.34 = (bf16[256,256]{1,0:T(8,128)(2,1)S(1)}, bf16[256,256]{1,0:T(8,128)(2,1)S(1)}, u32[]{:S(2)}, u32[]{:S(2)}) collective-permute-start(bf16[256,256]{1,0:T(8,128)(2,1)S(1)} %get-tuple-element.44), channel_id=1, source_target_pairs={{0,16},{8,24},{16,0},{24,8},{1,17},{9,25},{17,1},{25,9},{2,18},{10... | collective-permute-start | bytes 393224 | tf_op jit(solution)/shard_map/ppermute | solution.py:14
  57.4 9.1 %collective-permute-start.35 = (bf16[256,256]{1,0:T(8,128)(2,1)S(1)}, bf16[256,256]{1,0:T(8,128)(2,1)S(1)}, u32[]{:S(2)}, u32[]{:S(2)}) collective-permute-start(bf16[256,256]{1,0:T(8,128)(2,1)S(1)} %get-tuple-element.45), channel_id=1, source_target_pairs={{0,8},{8,0},{16,24},{24,16},{1,9},{9,1},{17,25},{25,17},{2,10},{10... | collective-permute-start | bytes 393224 | tf_op jit(solution)/shard_map/ppermute | solution.py:14
  58.9 18.7 %copy-start.11 = (bf16[1,256,2,1024]{3,2,1,0:T(2,128)(2,1)S(1)}, bf16[1,256,2,1024]{3,2,1,0:T(2,128)(2,1)}, u32[]{:S(2)}) copy-start(bf16[1,256,2,1024]{3,2,1,0:T(2,128)(2,1)} %param.15) | copy-start | bytes 3145732
  59.0 8.8 %collective-permute-start.36 = (bf16[256,256]{1,0:T(8,128)(2,1)S(1)}, bf16[256,256]{1,0:T(8,128)(2,1)S(1)}, u32[]{:S(2)}, u32[]{:S(2)}) collective-permute-start(bf16[256,256]{1,0:T(8,128)(2,1)S(1)} %get-tuple-element.46), channel_id=1, source_target_pairs={{0,16},{8,24},{16,0},{24,8},{1,17},{9,25},{17,1},{25,9},{2,18},{10... | collective-permute-start | bytes 393224 | tf_op jit(solution)/shard_map/ppermute | solution.py:14
  59.9 8.2 %collective-permute-start.26 = (bf16[256,256]{1,0:T(8,128)(2,1)S(1)}, bf16[256,256]{1,0:T(8,128)(2,1)S(1)}, u32[]{:S(2)}, u32[]{:S(2)}) collective-permute-start(bf16[256,256]{1,0:T(8,128)(2,1)S(1)} %get-tuple-element.38), channel_id=1, source_target_pairs={{0,16},{8,24},{16,0},{24,8},{1,17},{9,25},{17,1},{25,9},{2,18},{10... | collective-permute-start | bytes 393224 | tf_op jit(solution)/shard_map/ppermute | solution.py:14
  61.3 15.4 %collective-permute-start.5 = (bf16[256,512]{1,0:T(8,128)(2,1)S(1)}, bf16[256,512]{1,0:T(8,128)(2,1)S(1)}, u32[]{:S(2)}, u32[]{:S(2)}) collective-permute-start(bf16[256,512]{1,0:T(8,128)(2,1)S(1)} %collective-permute-done.3.refs_1_), channel_id=1, source_target_pairs={{0,16},{8,24},{16,0},{24,8},{1,17},{9,25},{17,1},{25,9},{2,18},{10... | collective-permute-start | bytes 786440 | tf_op jit(solution)/shard_map/ppermute | solution.py:14
  62.4 13.8 %collective-permute-start.28 = (bf16[256,256]{1,0:T(8,128)(2,1)S(1)}, bf16[256,256]{1,0:T(8,128)(2,1)S(1)}, u32[]{:S(2)}, u32[]{:S(2)}) collective-permute-start(bf16[256,256]{1,0:T(8,128)(2,1)S(1)} %get-tuple-element.40), channel_id=1, source_target_pairs={{0,16},{8,24},{16,0},{24,8},{1,17},{9,25},{17,1},{25,9},{2,18},{10... | collective-permute-start | bytes 393224 | tf_op jit(solution)/shard_map/ppermute | solution.py:14
  66.5 15.9 %collective-permute-start.18 = (bf16[256,1024]{1,0:T(8,128)(2,1)S(1)}, bf16[256,1024]{1,0:T(8,128)(2,1)S(1)}, u32[]{:S(2)}, u32[]{:S(2)}) collective-permute-start(bf16[256,1024]{1,0:T(8,128)(2,1)S(1)} %shard_map.118), channel_id=1, source_target_pairs={{0,4},{4,0},{1,5},{5,1},{2,6},{6,2},{3,7},{7,3},{8,12},{12,8},{9,1... | collective-permute-start | bytes 1572872 | tf_op jit(solution)/shard_map/ppermute | solution.py:14
  67.8 8.4 %collective-permute-start.27 = (bf16[256,256]{1,0:T(8,128)(2,1)S(1)}, bf16[256,256]{1,0:T(8,128)(2,1)S(1)}, u32[]{:S(2)}, u32[]{:S(2)}) collective-permute-start(bf16[256,256]{1,0:T(8,128)(2,1)S(1)} %get-tuple-element.39), channel_id=1, source_target_pairs={{0,8},{8,0},{16,24},{24,16},{1,9},{9,1},{17,25},{25,17},{2,10},{10... | collective-permute-start | bytes 393224 | tf_op jit(solution)/shard_map/ppermute | solution.py:14
  68.1 8.6 %collective-permute-start.37 = (bf16[256,256]{1,0:T(8,128)(2,1)S(1)}, bf16[256,256]{1,0:T(8,128)(2,1)S(1)}, u32[]{:S(2)}, u32[]{:S(2)}) collective-permute-start(bf16[256,256]{1,0:T(8,128)(2,1)S(1)} %collective-permute-done.36), channel_id=1, source_target_pairs={{0,8},{8,0},{16,24},{24,16},{1,9},{9,1},{17,25},{25,17},{2,10},{10... | collective-permute-start | bytes 393224 | tf_op jit(solution)/shard_map/ppermute | solution.py:14
  76.2 1.3 collective-permute-start.29
  76.2 4.2 %collective-permute-start.6 = (bf16[256,512]{1,0:T(8,128)(2,1)S(1)}, bf16[256,512]{1,0:T(8,128)(2,1)S(1)}, u32[]{:S(2)}, u32[]{:S(2)}) collective-permute-start(bf16[256,512]{1,0:T(8,128)(2,1)S(1)} %shard_map.112.refs_0_), channel_id=1, source_target_pairs={{0,8},{8,0},{16,24},{24,16},{1,9},{9,1},{17,25},{25,17},{2,10},{10... | collective-permute-start | bytes 786440 | tf_op jit(solution)/shard_map/ppermute | solution.py:14
  76.7 3.7 %collective-permute-start.7 = (bf16[256,512]{1,0:T(8,128)(2,1)S(1)}, bf16[256,512]{1,0:T(8,128)(2,1)S(1)}, u32[]{:S(2)}, u32[]{:S(2)}) collective-permute-start(bf16[256,512]{1,0:T(8,128)(2,1)S(1)} %collective-permute-done.3.refs_1_), channel_id=1, source_target_pairs={{0,8},{8,0},{16,24},{24,16},{1,9},{9,1},{17,25},{25,17},{2,10},{10... | collective-permute-start | bytes 786440 | tf_op jit(solution)/shard_map/ppermute | solution.py:14
  76.8 3.6 %collective-permute-start.8 = (bf16[256,512]{1,0:T(8,128)(2,1)S(1)}, bf16[256,512]{1,0:T(8,128)(2,1)S(1)}, u32[]{:S(2)}, u32[]{:S(2)}) collective-permute-start(bf16[256,512]{1,0:T(8,128)(2,1)S(1)} %collective-permute-done.4.refs_2_), channel_id=1, source_target_pairs={{0,8},{8,0},{16,24},{24,16},{1,9},{9,1},{17,25},{25,17},{2,10},{10... | collective-permute-start | bytes 786440 | tf_op jit(solution)/shard_map/ppermute | solution.py:14
  77.5 2.9 %collective-permute-start.9 = (bf16[256,512]{1,0:T(8,128)(2,1)S(1)}, bf16[256,512]{1,0:T(8,128)(2,1)S(1)}, u32[]{:S(2)}, u32[]{:S(2)}) collective-permute-start(bf16[256,512]{1,0:T(8,128)(2,1)S(1)} %collective-permute-done.5.refs_3_), channel_id=1, source_target_pairs={{0,8},{8,0},{16,24},{24,16},{1,9},{9,1},{17,25},{25,17},{2,10},{10... | collective-permute-start | bytes 786440 | tf_op jit(solution)/shard_map/ppermute | solution.py:14
  82.5 1.6 %copy-start.10 = (bf16[1024,1024]{1,0:T(8,128)(2,1)S(1)}, bf16[1024,1024]{1,0:T(8,128)(2,1)}, u32[]{:S(2)}) copy-start(bf16[1024,1024]{1,0:T(8,128)(2,1)} %get-tuple-element.41) | copy-start | bytes 6291460
  86.9 14.3 %collective-permute-start.38 = (bf16[256,1024]{1,0:T(8,128)(2,1)S(1)}, bf16[256,1024]{1,0:T(8,128)(2,1)S(1)}, u32[]{:S(2)}, u32[]{:S(2)}) collective-permute-start(bf16[256,1024]{1,0:T(8,128)(2,1)S(1)} %subtract_convert_fusion.own), channel_id=1, source_target_pairs={{0,4},{4,0},{1,5},{5,1},{2,6},{6,2},{3,7},{7,3},{8,12},{12,8},{9,1... | collective-permute-start | bytes 1572872 | tf_op jit(solution)/shard_map/ppermute | solution.py:14
  102.5 2.0 %collective-permute-start.41 = (bf16[2,128,1024]{2,1,0:T(8,128)(2,1)S(1)}, bf16[2,128,1024]{2,1,0:T(8,128)(2,1)S(1)}, u32[]{:S(2)}, u32[]{:S(2)}) collective-permute-start(bf16[2,128,1024]{2,1,0:T(8,128)(2,1)S(1)} %get-tuple-element.53), channel_id=1, source_target_pairs={{0,8},{8,0},{16,24},{24,16},{1,9},{9,1},{17,25},{25,17},{2,10},{10... | collective-permute-start | bytes 1572872 | tf_op jit(solution)/shard_map/ppermute | solution.py:14
  105.1 8.4 %collective-permute-start.42 = (bf16[128,1024]{1,0:T(8,128)(2,1)S(1)}, bf16[128,1024]{1,0:T(8,128)(2,1)S(1)}, u32[]{:S(2)}, u32[]{:S(2)}) collective-permute-start(bf16[128,1024]{1,0:T(8,128)(2,1)S(1)} %get-tuple-element.55), channel_id=1, source_target_pairs={{0,16},{8,24},{16,0},{24,8},{1,17},{9,25},{17,1},{25,9},{2,18},{10... | collective-permute-start | bytes 786440 | tf_op jit(solution)/shard_map/ppermute | solution.py:14
  108.3 10.3 %collective-permute-start.39 = (bf16[4,128,128]{2,1,0:T(8,128)(2,1)S(1)}, bf16[4,128,128]{2,1,0:T(8,128)(2,1)S(1)}, u32[]{:S(2)}, u32[]{:S(2)}) collective-permute-start(bf16[4,128,128]{2,1,0:T(8,128)(2,1)S(1)} %get-tuple-element.49), channel_id=1, source_target_pairs={{0,8},{8,0},{16,24},{24,16},{1,9},{9,1},{17,25},{25,17},{2,10},{10... | collective-permute-start | bytes 393224 | tf_op jit(solution)/shard_map/ppermute | solution.py:14
  114.1 5.5 %collective-permute-start.43 = (bf16[128,256]{1,0:T(8,128)(2,1)S(1)}, bf16[128,256]{1,0:T(8,128)(2,1)S(1)}, u32[]{:S(2)}, u32[]{:S(2)}) collective-permute-start(bf16[128,256]{1,0:T(8,128)(2,1)S(1)} %get-tuple-element.57), channel_id=1, source_target_pairs={{0,1},{1,0},{2,3},{3,2},{4,5},{5,4},{6,7},{7,6},{8,9},{9,8},{10,11... | collective-permute-start | bytes 196616 | tf_op jit(solution)/shard_map/ppermute | solution.py:14
  115.3 6.7 %collective-permute-start.44 = (bf16[128,256]{1,0:T(8,128)(2,1)S(1)}, bf16[128,256]{1,0:T(8,128)(2,1)S(1)}, u32[]{:S(2)}, u32[]{:S(2)}) collective-permute-start(bf16[128,256]{1,0:T(8,128)(2,1)S(1)} %get-tuple-element.58), channel_id=1, source_target_pairs={{0,2},{1,3},{2,0},{3,1},{4,6},{5,7},{6,4},{7,5},{8,10},{9,11},{10,... | collective-permute-start | bytes 196616 | tf_op jit(solution)/shard_map/ppermute | solution.py:14
  116.9 6.2 %collective-permute-start.45 = (bf16[128,256]{1,0:T(8,128)(2,1)S(1)}, bf16[128,256]{1,0:T(8,128)(2,1)S(1)}, u32[]{:S(2)}, u32[]{:S(2)}) collective-permute-start(bf16[128,256]{1,0:T(8,128)(2,1)S(1)} %get-tuple-element.59), channel_id=1, source_target_pairs={{0,3},{1,2},{2,1},{3,0},{4,7},{5,6},{6,5},{7,4},{8,11},{9,10},{10,... | collective-permute-start | bytes 196616 | tf_op jit(solution)/shard_map/ppermute | solution.py:14
  118.6 12.1 %collective-permute-start.40 = (bf16[4,128,128]{2,1,0:T(8,128)(2,1)S(1)}, bf16[4,128,128]{2,1,0:T(8,128)(2,1)S(1)}, u32[]{:S(2)}, u32[]{:S(2)}) collective-permute-start(bf16[4,128,128]{2,1,0:T(8,128)(2,1)S(1)} %add_convert_fusion.2), channel_id=1, source_target_pairs={{0,16},{8,24},{16,0},{24,8},{1,17},{9,25},{17,1},{25,9},{2,18},{10... | collective-permute-start | bytes 393224 | tf_op jit(solution)/shard_map/ppermute | solution.py:14
  123.7 4.3 %collective-permute-start.46 = (bf16[128,256]{1,0:T(8,128)(2,1)S(1)}, bf16[128,256]{1,0:T(8,128)(2,1)S(1)}, u32[]{:S(2)}, u32[]{:S(2)}) collective-permute-start(bf16[128,256]{1,0:T(8,128)(2,1)S(1)} %shard_map.131.refs_0_), channel_id=1, source_target_pairs={{0,16},{8,24},{16,0},{24,8},{1,17},{9,25},{17,1},{25,9},{2,18},{10... | collective-permute-start | bytes 196616 | tf_op jit(solution)/shard_map/ppermute | solution.py:14
  125.2 9.5 %collective-permute-start.47 = (bf16[128,256]{1,0:T(8,128)(2,1)S(1)}, bf16[128,256]{1,0:T(8,128)(2,1)S(1)}, u32[]{:S(2)}, u32[]{:S(2)}) collective-permute-start(bf16[128,256]{1,0:T(8,128)(2,1)S(1)} %shard_map.131.refs_0_), channel_id=1, source_target_pairs={{0,8},{8,0},{16,24},{24,16},{1,9},{9,1},{17,25},{25,17},{2,10},{10... | collective-permute-start | bytes 196616 | tf_op jit(solution)/shard_map/ppermute | solution.py:14
  128.0 6.7 %collective-permute-start.48 = (bf16[128,256]{1,0:T(8,128)(2,1)S(1)}, bf16[128,256]{1,0:T(8,128)(2,1)S(1)}, u32[]{:S(2)}, u32[]{:S(2)}) collective-permute-start(bf16[128,256]{1,0:T(8,128)(2,1)S(1)} %collective-permute-done.46.refs_1_), channel_id=1, source_target_pairs={{0,8},{8,0},{16,24},{24,16},{1,9},{9,1},{17,25},{25,17},{2,10},{10... | collective-permute-start | bytes 196616 | tf_op jit(solution)/shard_map/ppermute | solution.py:14

commit v3 on v2

--- a/solution.py
+++ b/solution.py
@@ -248,121 +248,291 @@
     return pl.ds(pl.multiple_of(index * size, size), size)
 
 
-HEAD, DP = 4, 5
-
-
-def prepare(where, out_proj, depth_proj, code_table):
-    rows, cols = out_proj.shape
-    d_rows, d_cols = depth_proj.shape
-    n_level, t_rows, t_cols = code_table.shape
-    rows, d_rows, t_cols = rows // 4, d_rows // 4, t_cols // 4
-
-    def body(where_ref, o_ref, d_ref, t_ref, o_out, d_out, *t_out):
-        o_out[...] = o_ref[...]
-        d_out[...] = d_ref[...]
-        for level, out in enumerate(t_out):
-            out[...] = t_ref[level]
-
-    def whole(shape):
-        return pl.BlockSpec(shape, lambda i, w: (0,) * len(shape))
-
+HEAD, DP, SEQ = 4, 5, 6
+
+
+def own_lane():
+    me = lax.axis_index("seq")
+    return 2 * (me % 2) + me // 2
+
+
+def copies(body_of, outs, args):
+    n_copies = len(body_of(None))
+
+    def body(*refs):
+        sems = refs[-1]
+        going = [pltpu.make_async_copy(src, dst, sems.at[i]) for i, (src, dst) in enumerate(body_of(refs[:-1]))]
+        for copy in going:
+            copy.start()
+        for copy in going:
+            copy.wait()
+
+    anywhere = pl.BlockSpec(memory_space=pl.ANY)
     return pl.pallas_call(
         body,
-        out_shape=[shaped((rows, cols)), shaped((d_rows, d_cols))] + [shaped((t_rows, t_cols))] * n_level,
-        grid_spec=pltpu.PrefetchScalarGridSpec(
-            num_scalar_prefetch=1,
-            grid=(1,),
-            in_specs=[
-                pl.BlockSpec((rows, cols), lambda i, w: (w[0], 0)),
-                pl.BlockSpec((d_rows, d_cols), lambda i, w: (w[0], 0)),
-                pl.BlockSpec((n_level, t_rows, t_cols), lambda i, w: (0, 0, w[0])),
-            ],
-            out_specs=[whole((rows, cols)), whole((d_rows, d_cols))] + [whole((t_rows, t_cols))] * n_level,
-        ),
-    )(where, out_proj, depth_proj, code_table)
-
-
-def side_by_side(where, pieces):
-    rows, cols = pieces[0].shape
+        out_shape=outs,
+        in_specs=[anywhere] * len(args),
+        out_specs=pl.BlockSpec(memory_space=pltpu.VMEM),
+        scratch_shapes=[pltpu.SemaphoreType.DMA((n_copies,))],
+    )(*args)
+
+
+def first_lanes(code_table, depth_proj, n_dp):
+    t_rows, t_cols = code_table.shape[1], code_table.shape[2] // 4
+    d_half, d_cols = depth_proj.shape[0] // 8, depth_proj.shape[1]
+
+    def views(refs):
+        if refs is None:
+            return [0] * (3 * n_dp)
+        table, depth, lanes = refs
+        found = []
+        for k in range(n_dp):
+            found.append((table.at[0, :, at(own_lane(), t_cols)], lanes.at[k, 0:t_rows]))
+            for half in range(2):
+                found.append(
+                    (
+                        depth.at[at(2 * own_lane() + half, d_half)],
+                        lanes.at[k, t_rows:t_rows + d_half, half * d_cols:(half + 1) * d_cols],
+                    )
+                )
+        return found
+
+    return copies(views, shaped((n_dp, t_rows + d_half, t_cols)), [code_table, depth_proj])
+
+
+def second_lanes(code_table, out_proj, after):
+    t_rows, t_cols = code_table.shape[1], code_table.shape[2] // 4
+    rows, cols = out_proj.shape[0] // 2, out_proj.shape[1]
+
+    def views(refs):
+        if refs is None:
+            return [0, 1]
+        table, out, _, lanes = refs
+        return [
+            (table.at[1, :, at(own_lane(), t_cols)], lanes.at[0:t_rows]),
+            (out.at[at(own_lane() // 2, rows)], lanes.at[t_rows:t_rows + rows]),
+        ]
+
+    return copies(views, shaped((t_rows + rows, cols)), [code_table, out_proj, after])
+
+
+def first_parts(where, pieces, t_rows):
+    n, d_half, t_cols = pieces.shape
+    d_half, d_cols = d_half - t_rows, t_cols // 2
+    top, fold = n * t_rows, 2 * d_half
+
+    def body(where_ref, ref, both, depth, top_fold):
+        for k in range(n):
+            both[k * t_rows:(k + 1) * t_rows, :] = ref[where_ref[DP] ^ k, :t_rows]
+            place = where_ref[DP] ^ k
+            cols = at(place % 2, d_cols)
+            for half in range(2):
+                part = ref[place, t_rows:, half * d_cols:(half + 1) * d_cols]
+                row = pl.multiple_of((place // 2) * fold + half * d_half, d_half)
+                both[pl.ds(pl.multiple_of(top + row, d_half), d_half), cols] = part
+                depth[pl.ds(row, d_half), cols] = part
+        top_fold[...] = depth[:fold]
+
+    rows = fold * n // 2
+    return run(body, [shaped((top + rows, t_cols)), shaped((rows, t_cols)), shaped((fold, t_cols))], where, pieces)
+
+
+def table_part(where, pieces, t_rows):
+    n, cols = len(pieces), pieces[0].shape[1]
 
     def body(where_ref, *refs):
-        out = refs[-1]
-        for k, ref in enumerate(refs[:-1]):
-            out[:, at(where_ref[DP] ^ k, cols)] = ref[...]
-
-    return run(body, [shaped((rows, cols * len(pieces)))], where, *pieces)[0]
-
-
-def stacked(where, pieces):
-    rows, cols = pieces[0].shape
+        for k in range(n):
+            refs[n][k * t_rows:(k + 1) * t_rows, :] = refs[k][:t_rows]
+
+    return run(body, [shaped((n * t_rows, cols))], where, *pieces)[0]
+
+
+def out_part(where, pieces, t_rows):
+    rows, cols = pieces[0].shape[0] - t_rows, pieces[0].shape[1]
+    n = len(pieces)
+    first = 160
 
     def body(where_ref, *refs):
-        for k, ref in enumerate(refs[:-1]):
-            refs[-1][k * rows:(k + 1) * rows, :] = ref[...]
-
-    return run(body, [shaped((rows * len(pieces), cols))], where, *pieces)[0]
-
-
-def embed(where, ids, own, got, n_dp):
-    tokens = ids.shape[1]
-    half, cols = own.shape
-    rows_dev = half // n_dp
-
-    def body(where_ref, ids_ref, own_ref, got_ref, *outs):
+        out, head, tail = refs[n:]
+        for k in range(n):
+            cut = at(where_ref[DP] ^ k, cols)
+            out[:, cut] = refs[k][t_rows:]
+            head[:, cut] = refs[k][t_rows:t_rows + first]
+            tail[:, cut] = refs[k][t_rows + first:]
+
+    outs = [shaped((rows, n * cols)), shaped((first, n * cols)), shaped((rows - first, n * cols))]
+    return run(body, outs, where, *pieces)
+
+
+def embed(where, packed, top, level, n_level, tokens, own, got, half, n_dp):
+    folds = tokens // DH
+    n_rows = id_rows(n_level, tokens)
+    rows, cols = own.shape
+    rows_dev, extra = half // n_dp, rows - half
+    late = extra // 2
+
+    def body(where_ref, mine_ref, core_ref, far_ref, own_ref, got_ref, *outs):
+        def ids_of(ref, start):
+            all_ids = ref[start:start + 2 * n_level * folds].astype(F32)
+            mine = level * folds
+            high = all_ids[mine:mine + folds]
+            low = all_ids[(n_level * folds) + mine:(n_level * folds) + mine + folds]
+            ids = high * 32.0 + low
+            return jnp.concatenate([ids[f:f + 1] for f in range(folds)], axis=1)
+
         place = lax.broadcasted_iota(jnp.int32, (tokens, half), 1)
-        piece = place // rows_dev
-        within = place % rows_dev
-        owner = jnp.bitwise_xor(piece, where_ref[DP])
-        base = owner * rows_dev + within
-        columns = ids_ref[...].T
-        for m, out in enumerate(outs):
+        owner = jnp.bitwise_xor(place // rows_dev, where_ref[DP])
+        base = owner * rows_dev + place % rows_dev
+        rows_of = [(mine_ref, top), (core_ref, top), (far_ref, top), (far_ref, top + n_rows)]
+        columns = jnp.concatenate([ids_of(*r) for r in rows_of], axis=0).T.astype(jnp.int32)
+        for m in (2, 3, 1, 0):
             col = columns[:, m:m + 1]
             total = None
             for k, ref in enumerate((own_ref, got_ref)):
                 start = (where_ref[HEAD] ^ k) * half
                 hot = (base == col - start).astype(F32).astype(BF16)
-                part = jnp.dot(hot, ref[...], preferred_element_type=F32)
+                part = jnp.dot(hot, ref[:half], preferred_element_type=F32)
                 total = part if total is None else total + part
-            out[...] = total.astype(BF16)
-
-    return run(body, [shaped((tokens, cols))] * 4, where, ids, own, got)
-
-
-def lanes_together(where, pieces):
-    rows, cols = pieces[0].shape
+            total = total.astype(BF16)
+            if m < 2:
+                outs[m][:tokens] = total
+            else:
+                outs[2][(m - 2) * tokens:(m - 1) * tokens, :] = total
+        if extra:
+            outs[1][tokens:] = got_ref[half:]
+            outs[2][2 * tokens:2 * tokens + extra] = got_ref[half:]
+            outs[2][2 * tokens + extra:] = own_ref[rows - late:]
+
+    outs = [shaped((tokens, cols)), shaped((tokens + extra, cols)), shaped((2 * tokens + extra + late, cols))]
+    return run(body, outs, where, *packed, own, got)
+
+
+def depth_grad(where, folds, first, second, mixed, mixed_got, cot):
+    arrays, which = [], []
+    for array, _ in folds + first + second:
+        found = [i for i, other in enumerate(arrays) if other is array]
+        if not found:
+            arrays.append(array)
+        which.append(found[0] if found else len(arrays) - 1)
+    starts = [start for _, start in folds + first + second]
+    tokens, width = mixed.shape
+    cols = width // 4
+    chunk = 32
 
     def body(where_ref, *refs):
-        for m, ref in enumerate(refs[:-1]):
-            refs[-1][:, at(where_ref[m], cols)] = ref[...]
-
-    return run(body, [shaped((rows, cols * 4))], where, *pieces)[0]
-
-
-def depth_together(where, blocks, cot):
-    rows, cols = blocks[0].shape
-    width = rows * 4
-    last = cot.shape[1] // width - 1
-
-    def body(where_ref, *refs):
-        cot_ref, full, grad = refs[8:]
-        for m in range(4):
-            for x in range(2):
-                full[at(where_ref[m], rows), at(where_ref[HEAD] ^ x, cols)] = refs[2 * m + x][...]
-        cot_last = cot_ref[:, last * width:(last + 1) * width]
-        grad[...] = dot(cot_last, full[...], ((1,), (1,)))
-
-    return run(body, [shaped((width, width)), shaped((cot.shape[0], width), F32)], where, *blocks, cot)
-
-
-def local_states(where, keys, values, dtype=BF16):
+        parts = refs[:len(arrays)]
+        mixed_ref, got_ref, cot_ref, out, full, sum_ref, mid_ref, last_ref, row_ref = refs[len(arrays):]
+        for n in range(16):
+            m, x, j = n // 4, n // 2 % 2, n % 2
+            place = (where_ref[HEAD] ^ x) * 2 + j
+            full[at(where_ref[m], cols), at(place, cols)] = parts[which[n]][starts[n]:starts[n] + cols]
+
+        def rows_of(i):
+            return pl.ds(pl.multiple_of(i * chunk, chunk), chunk)
+
+        def lane_rows(i, n):
+            return parts[which[n]][pl.ds(pl.multiple_of(starts[n] + i * chunk, chunk), chunk), :].astype(F32)
+
+        def inverse(total):
+            return lax.rsqrt(jnp.mean(total * total, axis=-1, keepdims=True) + 1e-05)
+
+        def enter(i, carry):
+            rows = rows_of(i)
+            for m in range(4):
+                cut = at(where_ref[m], cols)
+                sum_ref[rows, cut] = mixed_ref[rows, cut] + got_ref[rows, cut].astype(F32) + lane_rows(i, 16 + m)
+            total = sum_ref[rows, :]
+            row_ref[rows, :] = (total * inverse(total)).astype(BF16)
+            return carry
+
+        lax.fori_loop(0, tokens // chunk, enter, 0, unroll=True)
+        mid_ref[...] = jnp.dot(row_ref[...], full[...], preferred_element_type=F32)
+        last_ref[...] = dot(cot_ref[:, width:], full[...], ((1,), (1,)))
+
+        def middle(i, carry):
+            rows = rows_of(i)
+            projected = mid_ref[rows, :]
+            gate = jax.nn.sigmoid(projected)
+            mid_ref[rows, :] = sum_ref[rows, :] + projected * gate
+            for m in range(4):
+                cut = at(where_ref[m], cols)
+                mid_ref[rows, cut] += lane_rows(i, 20 + m)
+            total = mid_ref[rows, :]
+            inv = inverse(total)
+            grad = last_ref[rows, :]
+            along = jnp.mean(grad * total, axis=-1, keepdims=True)
+            grad = grad * inv - total * (along * inv * inv * inv)
+            last_ref[rows, :] = grad
+            slope = gate * (1.0 + projected * (1.0 - gate))
+            row_ref[rows, :] = (cot_ref[rows, :width].astype(F32) + grad * slope).astype(BF16)
+            return carry
+
+        lax.fori_loop(0, tokens // chunk, middle, 0, unroll=True)
+        mid_ref[...] = dot(row_ref[...], full[...], ((1,), (1,)))
+
+        def leave(i, carry):
+            rows = rows_of(i)
+            total = sum_ref[rows, :]
+            inv = inverse(total)
+            grad = mid_ref[rows, :]
+            along = jnp.mean(grad * total, axis=-1, keepdims=True)
+            grad = last_ref[rows, :] + grad * inv - total * (along * inv * inv * inv)
+            out[rows, :] = grad.astype(BF16)
+            return carry
+
+        lax.fori_loop(0, tokens // chunk, leave, 0, unroll=True)
+
+    vmem = pl.BlockSpec(memory_space=pltpu.VMEM)
+    return pl.pallas_call(
+        body,
+        out_shape=shaped((tokens, width)),
+        in_specs=[pl.BlockSpec(memory_space=pltpu.SMEM)] + [vmem] * (len(arrays) + 3),
+        out_specs=vmem,
+        scratch_shapes=[
+            pltpu.VMEM((width, width), BF16),
+            pltpu.VMEM((tokens, width), F32),
+            pltpu.VMEM((tokens, width), F32),
+            pltpu.VMEM((tokens, width), F32),
+            pltpu.VMEM((tokens, width), BF16),
+        ],
+        compiler_params=pltpu.CompilerParams(vmem_limit_bytes=VMEM_BYTES),
+    )(where, *arrays, mixed, mixed_got, cot)
+
+
+def id_rows(n_level, tokens):
+    return -(-2 * n_level * (tokens // DH) // 16) * 16
+
+
+def pack(where, keys, values, ids):
     heads = keys.shape[1] // DH
-
-    def body(where_ref, k_ref, v_ref, out):
+    n_level, tokens = ids.shape
+    folds = tokens // DH
+    top = heads * DH
+
+    def body(where_ref, k_ref, v_ref, ids_ref, out):
+        parts = []
+        for level in range(n_level):
+            for fold in range(folds):
+                parts.append(ids_ref[level:level + 1, fold * DH:(fold + 1) * DH])
+        whole = jnp.concatenate(parts, axis=0)
+        both = jnp.concatenate([whole // 32, whole % 32], axis=0).astype(F32).astype(BF16)
+        out[top:top + 2 * n_level * folds] = both
         for i in range(heads):
             cut = slice(i * DH, (i + 1) * DH)
-            out[i] = dot(k_ref[:, cut], v_ref[:, cut], ((0,), (0,))).astype(dtype)
-
-    return run(body, [shaped((heads, DH, DH), dtype)], where, keys, values)[0]
+            out[cut] = dot(k_ref[:, cut], v_ref[:, cut], ((0,), (0,))).astype(BF16)
+
+    return run(body, [shaped((top + id_rows(n_level, tokens), DH))], where, keys, values, ids)[0]
+
+
+def pack_chip(where, own, core, top):
+    rows = own.shape[0] - top
+
+    def body(where_ref, own_ref, core_ref, out):
+        out[:top] = (own_ref[:top].astype(F32) + core_ref[:top].astype(F32)).astype(BF16)
+        out[top:top + rows] = own_ref[top:]
+        out[top + rows:] = core_ref[top:]
+
+    return run(body, [shaped((top + 2 * rows, DH))], where, own, core)[0]
 
 
 def lower(size):
@@ -387,7 +557,7 @@
         keep = lower(length)
         for i in range(heads):
             cut = slice(i * DH, (i + 1) * DH)
-            state[i] = (core_ref[i].astype(F32) * near + far_ref[i].astype(F32) * far).astype(BF16)
+            state[i] = (core_ref[cut].astype(F32) * near + far_ref[cut].astype(F32) * far).astype(BF16)
             q = q_ref[:, cut]
             scores = jnp.where(keep, dot(q, k_ref[:, cut], ((1,), (1,))), 0.0).astype(BF16)
             both = jnp.dot(scores, v_ref[:, cut], preferred_element_type=F32)
@@ -399,20 +569,34 @@
     )
 
 
-def mix(where, attended, blocks, other):
+def mix_own(where, attended, own_rows):
     length = attended.shape[0] // 2
-    width = blocks[0].shape[1]
+    half, width = own_rows.shape
+
+    def body(where_ref, att, own, out):
+        core = where_ref[0] // 2
+        for k in range(2):
+            rows = at(where_ref[HEAD] ^ (1 - k), length)
+            out[k] = jnp.dot(att[rows, at(core, half)], own[...], preferred_element_type=F32)
+
+    return run(body, [shaped((2, length, width), F32)], where, attended, own_rows)[0]
+
+
+def mix(where, attended, part, got_head, got_tail, other):
+    length = attended.shape[0] // 2
+    width = part.shape[2]
+    half = got_head.shape[0] + got_tail.shape[0]
     dtype = BF16 if other else F32
 
-    def body(where_ref, att, *refs):
+    def body(where_ref, att, part_ref, head, tail, out):
         rows = at(where_ref[HEAD] ^ (1 if other else 0), length)
-        total = None
-        for m in range(4):
-            part = jnp.dot(att[rows, at(where_ref[m], DH)], refs[m][...], preferred_element_type=F32)
-            total = part if total is None else total + part
-        refs[-1][...] = total.astype(dtype)
-
-    return run(body, [shaped((length, width), dtype)], where, attended, *blocks)[0]
+        core = where_ref[0] // 2
+        got = jnp.concatenate([head[...], tail[...]], axis=0)
+        total = part_ref[0 if other else 1]
+        total += jnp.dot(att[rows, at(1 - core, half)], got, preferred_element_type=F32)
+        out[...] = total.astype(dtype)
+
+    return run(body, [shaped((length, width), dtype)], where, attended, part, got_head, got_tail)[0]
 
 
 def weight_terms(where, attended, grad_own, grad_got):
@@ -483,21 +667,23 @@
     return run(body, [shaped((rows * 4, cols), F32)], where, *pieces)[0]
 
 
-def grad_attend(where, grad_own, grad_got, blocks, queries):
+def grad_attend(where, grad_own, grad_got, own_rows, got_head, got_tail, queries):
     tokens, width = grad_own.shape
     length, width_dev = queries.shape
-
-    def body(where_ref, own, got, o0, o1, o2, o3, q_ref, rows, back):
-        for m, block in enumerate((o0, o1, o2, o3)):
+    half = width_dev // 2
+
+    def body(where_ref, own, got, o_own, head, tail, q_ref, rows, back):
+        for c in range(2):
+            block = o_own[...] if c == 0 else jnp.concatenate([head[...], tail[...]], axis=0)
             for k, ref in enumerate((own, got)):
-                part = dot(ref[...], block[...], ((1,), (1,))).astype(BF16)
-                rows[at(where_ref[HEAD] ^ k, tokens), at(where_ref[m], DH)] = part
+                part = dot(ref[...], block, ((1,), (1,))).astype(BF16)
+                rows[at(where_ref[HEAD] ^ k, tokens), at((where_ref[0] // 2) ^ c, half)] = part
         for i in range(width_dev // DH):
             cut = slice(i * DH, (i + 1) * DH)
             back[i] = dot(q_ref[:, cut], rows[:, cut], ((0,), (0,))).astype(BF16)
 
     outs = [shaped((length, width_dev)), shaped((width_dev // DH, DH, DH))]
-    return run(body, outs, where, grad_own, grad_got, *blocks, queries)
+    return run(body, outs, where, grad_own, grad_got, own_rows, got_head, got_tail, queries)
 
 
 def query_grads(where, grad_rows, keys, values, state, att_scale):
@@ -540,7 +726,7 @@
     return run(body, outs, where, grad_rows, queries, keys, values, from_core, from_far)
 
 
-def fits(queries, out_proj, depth_proj, code_table):
+def fits(queries, out_proj, depth_proj, code_table, code_ids):
     n_seq, n_head = lax.axis_size("seq"), lax.axis_size("head")
     return (
         n_seq == 4
@@ -550,11 +736,13 @@
         and out_proj.shape[1] % 128 == 0
         and depth_proj.shape[1] % 128 == 0
         and code_table.shape[1] % 128 == 0
+        and code_ids.shape[1] % DH == 0
+        and code_table.shape[1] * n_head * lax.axis_size("dp") <= 32 * 256
     )
 
 
 def on_device(queries, keys, values, out_proj, depth_proj, code_table, code_ids, depth_cotangent):
-    if not fits(queries, out_proj, depth_proj, code_table):
+    if not fits(queries, out_proj, depth_proj, code_table, code_ids):
         return on_device_any(
             queries, keys, values, out_proj, depth_proj, code_table, code_ids, depth_cotangent
         )
@@ -565,7 +753,7 @@
     att_scale = float(group_len * lax.axis_size("seq")) ** (-0.5)
     core, far = me_seq % 2, me_seq // 2
     lane = 2 * core + far
-    where = jnp.stack([lane, lane ^ 1, lane ^ 2, lane ^ 3, me_head, me_dp]).astype(jnp.int32)
+    where = jnp.stack([lane, lane ^ 1, lane ^ 2, lane ^ 3, me_head, me_dp, me_seq]).astype(jnp.int32)
     queries, keys, values = queries[0], keys[0], values[0]
 
     def far_swap(block):
@@ -578,68 +766,82 @@
         got = far_swap(block)
         return [block, got, core_swap(block), core_swap(got)]
 
-    out_lane, depth_lane, *table_lanes = prepare(where, out_proj, depth_proj, code_table)
-    ids = code_ids[0].T
-    ids_rel = all_lanes(ids)
-
-    out_part = side_by_side(where, exchange(out_lane, "dp"))
-    out_blocks = all_lanes(out_part)
-
-    depth_part = side_by_side(where, exchange(depth_lane, "dp"))
-    depth_got = swap(depth_part, "head", 1)
-    own_lanes, got_lanes = all_lanes(depth_part), all_lanes(depth_got)
-    depth_blocks = [block for pair in zip(own_lanes, got_lanes) for block in pair]
-
-    embedded = []
-    for level, table in enumerate(table_lanes):
-        part = stacked(where, exchange(table, "dp"))
-        got = swap(part, "head", 1)
-        level_ids = jnp.stack([i[level] for i in ids_rel])
-        for_own, for_far, for_core, for_core_far = embed(where, level_ids, part, got, n_dp)
-        from_far, pass_on = far_swap(for_far), far_swap(for_core_far)
-        pieces = [for_own, from_far, core_swap(for_core), core_swap(pass_on)]
-        embedded.append(lanes_together(where, pieces))
-
-    state = local_states(where, keys, values)
-    state_core = core_swap(state)
-    chip = (state.astype(F32) + state_core.astype(F32)).astype(BF16)
-    state_far = far_swap(chip)
-    attended, state_in = attend(where, queries, keys, values, state_core, state_far, att_scale)
-
-    mixed_got = swap(mix(where, attended, out_blocks, True), "head", 1)
-    mixed = mix(where, attended, out_blocks, False) + mixed_got.astype(F32)
-
-    cot = depth_cotangent[0].reshape(depth_cotangent.shape[1], -1)
-    proj_mat, grad_last = depth_together(where, depth_blocks, cot)
-    sum_0 = mixed + embedded[0].astype(F32)
-    inv_0 = lax.rsqrt(jnp.mean(sum_0 * sum_0, axis=-1, keepdims=True) + 1e-05)
-    projected = dot((sum_0 * inv_0).astype(BF16), proj_mat, ((1,), (0,)))
-    gate = jax.nn.sigmoid(projected)
-    sum_1 = sum_0 + projected * gate + embedded[1].astype(F32)
-    inv_1 = lax.rsqrt(jnp.mean(sum_1 * sum_1, axis=-1, keepdims=True) + 1e-05)
-    along = jnp.mean(grad_last * sum_1, axis=-1, keepdims=True)
-    grad = grad_last * inv_1 - sum_1 * (along * inv_1 * inv_1 * inv_1)
-    slope = gate * (1.0 + projected * (1.0 - gate))
-    grad_proj = (cot[:, :width].astype(F32) + grad * slope).astype(BF16)
-    grad_normed = dot(grad_proj, proj_mat, ((1,), (1,)))
-    along = jnp.mean(grad_normed * sum_0, axis=-1, keepdims=True)
-    grad = grad + grad_normed * inv_0 - sum_0 * (along * inv_0 * inv_0 * inv_0)
-    grad_mixed = grad.astype(BF16)
+    t_rows, tokens = code_table.shape[1], code_ids.shape[1]
+    half = t_rows * n_dp
+    lanes_0 = first_lanes(code_table, depth_proj, n_dp)
+    pieces_0 = lax.all_to_all(lanes_0, "dp", 0, 0)
+    lanes_1 = second_lanes(code_table, out_proj, lanes_0)
+    pieces_1 = exchange(lanes_1, "dp")
+
+    top = keys.shape[1]
+    keys, values, _ = lax.optimization_barrier((keys, values, lanes_1))
+    mine = pack(where, keys, values, code_ids[0].T)
+    from_core = core_swap(mine)
+    chip = pack_chip(where, mine, from_core, top)
+    from_far = far_swap(chip)
+    packed = (mine, from_core, from_far)
+
+    attended, state_in = attend(where, queries, keys, values, from_core, from_far, att_scale)
+
+    pieces_0, _ = lax.optimization_barrier((pieces_0, attended))
+    part_0, depth_part, depth_top = first_parts(where, pieces_0, t_rows)
+    got_0 = swap(part_0, "head", 1)
+    depth_far = far_swap(depth_top)
+
+    pieces_1, depth_far = lax.optimization_barrier((pieces_1, depth_far))
+    out_rows, out_head, out_tail = out_part(where, pieces_1, t_rows)
+    got_head, got_tail = core_swap(out_head), core_swap(out_tail)
+    part_1 = table_part(where, pieces_1, t_rows)
+    got_1 = swap(part_1, "head", 1)
+
+    mixed_part = mix_own(where, attended, out_rows)
+    got_0, got_head, _, _ = lax.optimization_barrier((got_0, got_head, part_1, mixed_part))
+    own_0, to_core, to_far = embed(where, packed, top, 0, 2, tokens, part_0, got_0, half, n_dp)
+    far_0 = far_swap(to_far)
+
+    got_tail, _ = lax.optimization_barrier((got_tail, to_far))
+    mixed_send = mix(where, attended, mixed_part, got_head, got_tail, True)
+    mixed_got = swap(mixed_send, "head", 1)
+    mixed = mix(where, attended, mixed_part, got_head, got_tail, False)
+    core_0 = core_swap(to_core)
+
+    got_1, _, _ = lax.optimization_barrier((got_1, mixed, mixed_send))
+    own_1, to_core, to_far = embed(where, packed, top, 1, 2, tokens, part_1, got_1, half, n_dp)
+    far_1 = far_swap(to_far)
+    depth_core, depth_core_far = core_swap(depth_part), core_swap(depth_far)
+    far_0, far_1, mixed_got, depth_core, depth_core_far, core_0 = lax.optimization_barrier(
+        (far_0, far_1, mixed_got, depth_core, depth_core_far, core_0)
+    )
+    core_far_0, core_1, core_far_1 = core_swap(far_0), core_swap(to_core), core_swap(far_1)
+
+    fold, end = depth_top.shape[0], 2 * tokens
+    folds = [(depth_part, 0), (depth_part, fold), (got_0, half), (got_0, half + fold)]
+    folds += [(depth_far, 0), (far_0, end + 2 * fold), (far_0, end), (far_0, end + fold)]
+    folds += [(depth_core, 0), (depth_core, fold), (core_0, tokens), (core_0, tokens + fold)]
+    folds += [(depth_core_far, 0), (core_far_0, end + 2 * fold), (core_far_0, end), (core_far_0, end + fold)]
+    first = [(own_0, 0), (far_0, 0), (core_0, 0), (core_far_0, tokens)]
+    second = [(own_1, 0), (far_1, 0), (core_1, 0), (core_far_1, tokens)]
+    cot = depth_cotangent[0].reshape(tokens, -1)
+    grad_mixed = depth_grad(where, folds, first, second, mixed, mixed_got, cot)
 
     grad_got = swap(grad_mixed, "head", 1)
     send, keep = weight_terms(where, attended, grad_mixed, grad_got)
     send, keep = add_core(where, keep, core_swap(send))
-    keep, *send = add_far(where, keep, far_swap(send), n_dp)
-    block = add_all(where, keep, [swap(s, "dp", k + 1) for k, s in enumerate(send)])
-    grad_out_proj = rows_together(where, all_lanes(block))
-
-    grad_rows, back = grad_attend(where, grad_mixed, grad_got, out_blocks, queries)
+    from_far = far_swap(send)
+    grad_rows, back = grad_attend(where, grad_mixed, grad_got, out_rows, got_head, got_tail, queries)
     back_core = core_swap(back)
-    back_far = far_swap((back.astype(F32) + back_core.astype(F32)).astype(BF16))
     grad_query = query_grads(where, grad_rows, keys, values, state_in, att_scale)
+    back_chip = (back.astype(F32) + back_core.astype(F32)).astype(BF16)
+    back_far = far_swap(back_chip)
+    from_far, grad_query, _ = lax.optimization_barrier((from_far, grad_query, back_chip))
+    keep, *send = add_far(where, keep, from_far, n_dp)
+    got = [swap(s, "dp", k + 1) for k, s in enumerate(send)]
     grad_key, grad_value = key_value_grads(
         where, grad_rows, queries, keys, values, back_core, back_far, att_scale
     )
+    got, grad_key, grad_value = lax.optimization_barrier((got, grad_key, grad_value))
+    block = add_all(where, keep, got)
+    grad_out_proj = rows_together(where, all_lanes(block))
     return grad_query[None], grad_key[None], grad_value[None], grad_out_proj
 
 

time: 137 us -> 120 us (0.88)
  starting transfers between devices: 44.8 us -> 33.9 us
  local copies, waits for them, and re-layouts: 7.37 us -> 2.05 us
  Pallas kernels: 29.6 us -> 32.8 us
  matrix products: 1.92 us -> 0 us
    ppermute x49 -> x30, starting transfers between devices: 44.8 us -> 27.4 us  [swap(): lax.ppermute(block, axis, [(i, i ^ mask) for i in range(lax.axis_size(axi...]
    all_to_all x0 -> x1, starting transfers between devices: none -> 6.46 us  [on_device(): pieces_0 = lax.all_to_all(lanes_0, 'dp', 0, 0)]
    pallas_call x1 -> x3, Pallas kernels: 2.34 us -> 8.13 us  [the longest x1 4.25 us: depth_grad(): pl.pallas_call(body, out_shape=shaped((tokens, width)), in_specs=[pl.Bloc...]
    unnamed x27 -> x17, local copies, waits for them, and re-layouts: 5.97 us -> 1.96 us
    ppermute x49 -> x30, waiting for transfers between devices: 50.1 us -> 47.3 us  [swap(): lax.ppermute(block, axis, [(i, i ^ mask) for i in range(lax.axis_size(axi...]
    pallas_call x21 -> x19, Pallas kernels: 27.2 us -> 24.7 us  [run(): pl.pallas_call(body, out_shape=outs, in_specs=[pl.BlockSpec(memory_space=...]
    all_to_all x0 -> x1, waiting for transfers between devices: none -> 2.23 us  [on_device(): pieces_0 = lax.all_to_all(lanes_0, 'dp', 0, 0)]
    dot_general x2 -> x0, matrix products: 1.92 us -> none  [dot(): lax.dot_general(a, b, ((dims[0], dims[1]), ((), ())), preferred_element_t...]
  transfers between devices with their start and end apart: 49 -> 31, of which waited for: 15 -> 11; matrix products, arithmetic and copies ran while one was open for 1% -> 1% of each run, Pallas kernels for 19% -> 19%
where the time goes in v3:
time: 120 us; the launch traced here: 119 us
  waiting for transfers between devices  49.5 us (41%)
  starting transfers between devices  33.9 us (28%)
  Pallas kernels  32.8 us (27%)
  local copies, waits for them, and re-layouts  2.05 us (2%)
    ppermute x30, waiting for transfers between devices, swap(): lax.ppermute(block, axis, [(i, i ^ mask) for i in range(lax.axis_size(axi...  47.3 us
    ppermute x30, starting transfers between devices, swap(): lax.ppermute(block, axis, [(i, i ^ mask) for i in range(lax.axis_size(axi...  27.4 us
    pallas_call x19, Pallas kernels, run(): pl.pallas_call(body, out_shape=outs, in_specs=[pl.BlockSpec(memory_space=...  24.7 us
    all_to_all x1, starting transfers between devices, on_device(): pieces_0 = lax.all_to_all(lanes_0, 'dp', 0, 0)  6.46 us
    pallas_call x1, Pallas kernels, depth_grad(): pl.pallas_call(body, out_shape=shaped((tokens, width)), in_specs=[pl.Bloc...  4.25 us
    pallas_call x2, Pallas kernels, copies(): pl.pallas_call(body, out_shape=outs, in_specs=[anywhere] * len(args), out...  3.88 us
  transfers between devices with their start and end apart: 31, of which 11 were waited for; matrix products, arithmetic and copies ran while one was open for 1% of the time, Pallas kernels for 19%

profile of v3, /device:TPU:0, one launch (start us, length us, event | category | flops | bytes accessed | tf_op | source)
XLA Modules:
  0.0 119.3 jit_solution(2815748590476848176)
XLA Ops:
  0.7 2.2 %shard_map.111.refs_2_ = bf16[4,256,256]{2,1,0:T(8,128)(2,1)} custom-call(bf16[2,128,1024]{2,1,0:T(8,128)(2,1)} %refs_0_.3, bf16[1024,128]{1,0:T(8,128)(2,1)} %refs_1_.2), custom_call_target="tpu_custom_call" | custom-call | tf_op jit(solution)/shard_map/pallas_call | solution.py:271
  2.9 6.5 %all-to-all-start = ((bf16[4,256,256]{2,1,0:T(8,128)(2,1)}), bf16[4,256,256]{2,1,0:T(8,128)(2,1)S(1)}, u32[]{:S(2)}, u32[]{:S(2)}) async-start(bf16[4,256,256]{2,1,0:T(8,128)(2,1)} %shard_map.111.refs_2_), calls=%async_computation | async-start | bytes 1048576 | tf_op jit(solution)/shard_map/all_to_all | solution.py:772
  9.4 1.6 %shard_map.112.refs_0_ = bf16[384,256]{1,0:T(8,128)(2,1)} custom-call(bf16[2,128,1024]{2,1,0:T(8,128)(2,1)} %refs_0_.3, bf16[512,256]{1,0:T(8,128)(2,1)} %refs_1_.3, bf16[4,256,256]{2,1,0:T(8,128)(2,1)} %shard_map.111.refs_2_), custom_call_target="tpu_custom_call" | custom-call | tf_op jit(solution)/shard_map/pallas_call | solution.py:271
  11.0 0.0 copy-start.3
  11.0 0.1 stack.31.where_ref
  11.1 0.9 shard_map.113.own_ref.mine_ref
  12.0 0.1 collective-permute-start
  12.1 1.3 %collective-permute-done.core_ref = bf16[528,128]{1,0:T(8,128)(2,1)S(1)} collective-permute-done((bf16[528,128]{1,0:T(8,128)(2,1)S(1)}, bf16[528,128]{1,0:T(8,128)(2,1)S(1)}, u32[]{:S(2)}, u32[]{:S(2)}) %collective-permute-start) | collective-permute-done | bytes 135200 | tf_op jit(solution)/shard_map/ppermute | solution.py:14
  13.5 0.6 shard_map.114
  14.0 1.6 %collective-permute-start.1 = (bf16[544,128]{1,0:T(8,128)(2,1)S(1)}, bf16[544,128]{1,0:T(8,128)(2,1)S(1)}, u32[]{:S(2)}, u32[]{:S(2)}) collective-permute-start(bf16[544,128]{1,0:T(8,128)(2,1)S(1)} %shard_map.114), channel_id=1, source_target_pairs={{0,16},{8,24},{16,0},{24,8},{1,17},{9,25},{17,1},{25,9},{2,18},{10... | collective-permute-start | bytes 417800 | tf_op jit(solution)/shard_map/ppermute | solution.py:14
  15.6 2.0 %collective-permute-start.3 = (bf16[384,256]{1,0:T(8,128)(2,1)}, bf16[384,256]{1,0:T(8,128)(2,1)S(1)}, u32[]{:S(2)}, u32[]{:S(2)}) collective-permute-start(bf16[384,256]{1,0:T(8,128)(2,1)} %shard_map.112.refs_0_), channel_id=1, source_target_pairs={{0,1},{1,0},{2,3},{3,2},{4,5},{5,4},{6,7},{7,6},{8,9},{9,8},{10,11... | collective-permute-start | bytes 589832 | tf_op jit(solution)/shard_map/ppermute | solution.py:14
  17.6 2.4 %collective-permute-start.4 = (bf16[384,256]{1,0:T(8,128)(2,1)}, bf16[384,256]{1,0:T(8,128)(2,1)}, u32[]{:S(2)}, u32[]{:S(2)}) collective-permute-start(bf16[384,256]{1,0:T(8,128)(2,1)} %shard_map.112.refs_0_), channel_id=1, source_target_pairs={{0,2},{1,3},{2,0},{3,1},{4,6},{5,7},{6,4},{7,5},{8,10},{9,11},{10,... | collective-permute-start | bytes 589832 | tf_op jit(solution)/shard_map/ppermute | solution.py:14
  20.0 2.0 %shard_map.115 = (bf16[512,512]{1,0:T(8,128)(2,1)S(1)}, bf16[4,128,128]{2,1,0:T(8,128)(2,1)S(1)}) custom-call(s32[7]{0:T(128)S(1)} %stack.31.where_ref, bf16[512,512]{1,0:T(8,128)(2,1)S(1)} %bitcast.27, bf16[512,512]{1,0:T(8,128)(2,1)S(1)} %bitcast.20, bf16[512,512]{1,0:T(8,128)(2,1)S(1)} %bitcast.24, bf16[528,128]{1,0:T(8,128)(2,1)S(1)} %collective-permute-done.core_ref, ...), custom_call_target="tpu_custom_call" | custom-call | tf_op jit(solution)/shard_map/pallas_call | solution.py:234
  22.0 0.0 copy-start.4
  22.0 0.6 copy-done.4
  22.7 2.2 %all-to-all-done.ref = bf16[4,256,256]{2,1,0:T(8,128)(2,1)S(1)} async-done(((bf16[4,256,256]{2,1,0:T(8,128)(2,1)}), bf16[4,256,256]{2,1,0:T(8,128)(2,1)S(1)}, u32[]{:S(2)}, u32[]{:S(2)}) %all-to-all-start) | async-done | bytes 524320 | tf_op jit(solution)/shard_map/all_to_all | solution.py:772
  24.9 0.6 shard_map.116
  25.5 1.6 %collective-permute-start.2 = (bf16[1024,256]{1,0:T(8,128)(2,1)S(1)}, bf16[1024,256]{1,0:T(8,128)(2,1)S(1)}, u32[]{:S(2)}, u32[]{:S(2)}) collective-permute-start(bf16[1024,256]{1,0:T(8,128)(2,1)S(1)} %get-tuple-element.60.own_ref), channel_id=1, source_target_pairs={{0,4},{4,0},{1,5},{5,1},{2,6},{6,2},{3,7},{7,3},{8,12},{12,8},{9,1... | collective-permute-start | bytes 1572872 | tf_op jit(solution)/shard_map/ppermute | solution.py:14
  27.1 1.7 %collective-permute-start.6 = (bf16[256,256]{1,0:T(8,128)(2,1)S(1)}, bf16[256,256]{1,0:T(8,128)(2,1)S(1)}, u32[]{:S(2)}, u32[]{:S(2)}) collective-permute-start(bf16[256,256]{1,0:T(8,128)(2,1)S(1)} %get-tuple-element.61), channel_id=1, source_target_pairs={{0,16},{8,24},{16,0},{24,8},{1,17},{9,25},{17,1},{25,9},{2,18},{10... | collective-permute-start | bytes 393224 | tf_op jit(solution)/shard_map/ppermute | solution.py:14
  28.8 8.8 %collective-permute-done.4.refs_2_ = bf16[384,256]{1,0:T(8,128)(2,1)} collective-permute-done((bf16[384,256]{1,0:T(8,128)(2,1)}, bf16[384,256]{1,0:T(8,128)(2,1)}, u32[]{:S(2)}, u32[]{:S(2)}) %collective-permute-start.4) | collective-permute-done | bytes 196640 | tf_op jit(solution)/shard_map/ppermute | solution.py:14
  37.6 1.2 shard_map.117
  38.7 0.1 collective-permute-start.7
  38.8 0.5 collective-permute-start.10
  39.3 1.0 shard_map.118.own_ref
  40.4 1.0 shard_map.119.part_ref
  41.4 1.4 %shard_map.120 = (bf16[256,256]{1,0:T(8,128)(2,1)S(1)}, bf16[768,256]{1,0:T(8,128)(2,1)S(1)}, bf16[1280,256]{1,0:T(8,128)(2,1)S(1)}) custom-call(s32[7]{0:T(128)S(1)} %stack.31.where_ref, bf16[528,128]{1,0:T(8,128)(2,1)S(1)} %shard_map.113.own_ref.mine_ref, bf16[528,128]{1,0:T(8,128)(2,1)S(1)} %collective-permute-done.core_ref, ...), custom_call_target="tpu_custom_call" | custom-call | tf_op jit(solution)/shard_map/pallas_call | solution.py:234
  42.8 1.6 %collective-permute-start.8 = (bf16[1280,256]{1,0:T(8,128)(2,1)S(1)}, bf16[1280,256]{1,0:T(8,128)(2,1)S(1)}, u32[]{:S(2)}, u32[]{:S(2)}) collective-permute-start(bf16[1280,256]{1,0:T(8,128)(2,1)S(1)} %get-tuple-element.70), channel_id=1, source_target_pairs={{0,16},{8,24},{16,0},{24,8},{1,17},{9,25},{17,1},{25,9},{2,18},{10... | collective-permute-start | bytes 1966088 | tf_op jit(solution)/shard_map/ppermute | solution.py:14
  44.4 1.5 %collective-permute-start.9 = (bf16[512,256]{1,0:T(8,128)(2,1)S(1)}, bf16[512,256]{1,0:T(8,128)(2,1)S(1)}, u32[]{:S(2)}, u32[]{:S(2)}) collective-permute-start(bf16[512,256]{1,0:T(8,128)(2,1)S(1)} %shard_map.118.own_ref), channel_id=1, source_target_pairs={{0,4},{4,0},{1,5},{5,1},{2,6},{6,2},{3,7},{7,3},{8,12},{12,8},{9,1... | collective-permute-start | bytes 786440 | tf_op jit(solution)/shard_map/ppermute | solution.py:14
  45.9 0.8 shard_map.122
  46.7 0.6 collective-permute-start.12
  47.3 0.5 collective-permute-start.15
  47.8 0.8 shard_map.121.refs_13_
  48.7 4.9 %collective-permute-done.9.got_ref = bf16[512,256]{1,0:T(8,128)(2,1)S(1)} collective-permute-done((bf16[512,256]{1,0:T(8,128)(2,1)S(1)}, bf16[512,256]{1,0:T(8,128)(2,1)S(1)}, u32[]{:S(2)}, u32[]{:S(2)}) %collective-permute-start.9) | collective-permute-done | bytes 262176 | tf_op jit(solution)/shard_map/ppermute | solution.py:14
  53.6 1.4 %shard_map.123 = (bf16[256,256]{1,0:T(8,128)(2,1)S(1)}, bf16[256,256]{1,0:T(8,128)(2,1)S(1)}, bf16[512,256]{1,0:T(8,128)(2,1)S(1)}) custom-call(s32[7]{0:T(128)S(1)} %stack.31.where_ref, bf16[528,128]{1,0:T(8,128)(2,1)S(1)} %shard_map.113.own_ref.mine_ref, bf16[528,128]{1,0:T(8,128)(2,1)S(1)} %collective-permute-done.core_ref, ...), custom_call_target="tpu_custom_call" | custom-call | tf_op jit(solution)/shard_map/pallas_call | solution.py:234
  55.0 0.6 collective-permute-start.11
  55.6 9.6 %collective-permute-done.11.refs_10_ = bf16[512,256]{1,0:T(8,128)(2,1)S(1)} collective-permute-done((bf16[512,256]{1,0:T(8,128)(2,1)S(1)}, bf16[512,256]{1,0:T(8,128)(2,1)S(1)}, u32[]{:S(2)}, u32[]{:S(2)}) %collective-permute-start.11) | collective-permute-done | bytes 262176 | tf_op jit(solution)/shard_map/ppermute | solution.py:14
  65.2 0.1 collective-permute-start.16
  65.3 0.5 collective-permute-start.18
  65.8 0.1 collective-permute-start.17
  65.8 1.3 %copy.12 = bf16[32,8,2,1024]{3,1,2,0:T(8,128)(2,1)} copy(bf16[32,8,2,1024]{3,2,1,0:T(2,128)(2,1)S(1)} %bitcast.32) | data formatting | bytes 2097152
  67.1 0.8 collective-permute-done.17.refs_11_
  67.9 4.3 %shard_map.124.own = bf16[256,1024]{1,0:T(8,128)(2,1)S(1)} custom-call(s32[7]{0:T(128)S(1)} %stack.31.where_ref, bf16[512,256]{1,0:T(8,128)(2,1)S(1)} %get-tuple-element.59.refs_0_, bf16[1024,256]{1,0:T(8,128)(2,1)S(1)} %collective-permute-done.2.got_ref.refs_1_, bf16[256,256]{1,0:T(8,128)(2,1)S(1)} %collective-permute-done.6.refs_2_, ...), custom_call_target="tpu_custom_call" | custom-call | tf_op jit(solution)/shard_map/pallas_call | solution.py:486
  72.2 1.6 %collective-permute-start.19 = (bf16[256,1024]{1,0:T(8,128)(2,1)S(1)}, bf16[256,1024]{1,0:T(8,128)(2,1)S(1)}, u32[]{:S(2)}, u32[]{:S(2)}) collective-permute-start(bf16[256,1024]{1,0:T(8,128)(2,1)S(1)} %shard_map.124.own), channel_id=1, source_target_pairs={{0,4},{4,0},{1,5},{5,1},{2,6},{6,2},{3,7},{7,3},{8,12},{12,8},{9,1... | collective-permute-start | bytes 1572872 | tf_op jit(solution)/shard_map/ppermute | solution.py:14
  73.7 12.5 %collective-permute-done.19.got = bf16[256,1024]{1,0:T(8,128)(2,1)S(1)} collective-permute-done((bf16[256,1024]{1,0:T(8,128)(2,1)S(1)}, bf16[256,1024]{1,0:T(8,128)(2,1)S(1)}, u32[]{:S(2)}, u32[]{:S(2)}) %collective-permute-start.19) | collective-permute-done | bytes 524320 | tf_op jit(solution)/shard_map/ppermute | solution.py:14
  86.2 1.3 %shard_map.125 = (bf16[2,128,1024]{2,1,0:T(8,128)(2,1)S(1)}, f32[2,128,1024]{2,1,0:T(8,128)S(1)}) custom-call(s32[7]{0:T(128)S(1)} %stack.31.where_ref, bf16[512,512]{1,0:T(8,128)(2,1)S(1)} %get-tuple-element.57.att, bf16[256,1024]{1,0:T(8,128)(2,1)S(1)} %shard_map.124.own, bf16[256,1024]{1,0:T(8,128)(2,1)S(1)} %collective-permute-done.19.got), custom_call_target="tpu_custom_call" | custom-call | tf_op jit(solution)/shard_map/pallas_call | solution.py:234
  87.5 0.1 collective-permute-start.20
  87.6 1.6 %shard_map.127 = (bf16[512,512]{1,0:T(8,128)(2,1)S(1)}, bf16[4,128,128]{2,1,0:T(8,128)(2,1)S(1)}) custom-call(s32[7]{0:T(128)S(1)} %stack.31.where_ref, bf16[256,1024]{1,0:T(8,128)(2,1)S(1)} %shard_map.124.own, bf16[256,1024]{1,0:T(8,128)(2,1)S(1)} %collective-permute-done.19.got, bf16[256,1024]{1,0:T(8,128)(2,1)S(1)} %get-tuple-element.67.own.o_own, ...), custom_call_target="tpu_custom_call" | custom-call | tf_op jit(solution)/shard_map/pallas_call | solution.py:234
  89.2 0.6 collective-permute-start.22
  89.8 0.6 shard_map.126
  90.4 1.6 %collective-permute-start.21 = (bf16[128,1024]{1,0:T(8,128)(2,1)S(1)}, bf16[128,1024]{1,0:T(8,128)(2,1)S(1)}, u32[]{:S(2)}, u32[]{:S(2)}) collective-permute-start(bf16[128,1024]{1,0:T(8,128)(2,1)S(1)} %get-tuple-element.88), channel_id=1, source_target_pairs={{0,16},{8,24},{16,0},{24,8},{1,17},{9,25},{17,1},{25,9},{2,18},{10... | collective-permute-start | bytes 786440 | tf_op jit(solution)/shard_map/ppermute | solution.py:14
  92.1 0.6 collective-permute-start.26
  92.6 2.9 %shard_map.128 = bf16[512,512]{1,0:T(8,128)(2,1)} custom-call(s32[7]{0:T(128)S(1)} %stack.31.where_ref, bf16[512,512]{1,0:T(8,128)(2,1)S(1)} %get-tuple-element.89.g_ref, bf16[512,512]{1,0:T(8,128)(2,1)S(1)} %bitcast.21, bf16[512,512]{1,0:T(8,128)(2,1)S(1)} %bitcast.25, bf16[4,128,128]{2,1,0:T(8,128)(2,1)S(1)} %copy-done.5), custom_call_target="tpu_custom_call" | custom-call | tf_op jit(solution)/shard_map/pallas_call | solution.py:234
  95.5 4.1 %collective-permute-done.21.got_ref = bf16[128,1024]{1,0:T(8,128)(2,1)S(1)} collective-permute-done((bf16[128,1024]{1,0:T(8,128)(2,1)S(1)}, bf16[128,1024]{1,0:T(8,128)(2,1)S(1)}, u32[]{:S(2)}, u32[]{:S(2)}) %collective-permute-start.21) | collective-permute-done | bytes 262176 | tf_op jit(solution)/shard_map/ppermute | solution.py:14
  99.7 0.6 shard_map.129
  100.3 3.8 %collective-permute-start.23 = (bf16[128,256]{1,0:T(8,128)(2,1)S(1)}, bf16[128,256]{1,0:T(8,128)(2,1)S(1)}, u32[]{:S(2)}, u32[]{:S(2)}) collective-permute-start(bf16[128,256]{1,0:T(8,128)(2,1)S(1)} %get-tuple-element.95), channel_id=1, source_target_pairs={{0,1},{1,0},{2,3},{3,2},{4,5},{5,4},{6,7},{7,6},{8,9},{9,8},{10,11... | collective-permute-start | bytes 196616 | tf_op jit(solution)/shard_map/ppermute | solution.py:14
  104.0 1.6 %collective-permute-start.24 = (bf16[128,256]{1,0:T(8,128)(2,1)S(1)}, bf16[128,256]{1,0:T(8,128)(2,1)S(1)}, u32[]{:S(2)}, u32[]{:S(2)}) collective-permute-start(bf16[128,256]{1,0:T(8,128)(2,1)S(1)} %get-tuple-element.96), channel_id=1, source_target_pairs={{0,2},{1,3},{2,0},{3,1},{4,6},{5,7},{6,4},{7,5},{8,10},{9,11},{10,... | collective-permute-start | bytes 196616 | tf_op jit(solution)/shard_map/ppermute | solution.py:14
  105.7 0.8 collective-permute-start.25
  106.5 4.0 %shard_map.130 = (bf16[512,512]{1,0:T(8,128)(2,1)}, bf16[512,512]{1,0:T(8,128)(2,1)}) custom-call(s32[7]{0:T(128)S(1)} %stack.31.where_ref, bf16[512,512]{1,0:T(8,128)(2,1)S(1)} %get-tuple-element.89.g_ref, bf16[512,512]{1,0:T(8,128)(2,1)S(1)} %bitcast.29, bf16[512,512]{1,0:T(8,128)(2,1)S(1)} %bitcast.22, bf16[512,512]{1,0:T(8,128)(2,1)S(1)} %bitcast.26, ...), custom_call_target="tpu_custom_call" | custom-call | tf_op jit(solution)/shard_map/pallas_call | solution.py:234
  110.5 1.3 %collective-permute-done.25.refs_2_ = bf16[128,256]{1,0:T(8,128)(2,1)S(1)} collective-permute-done((bf16[128,256]{1,0:T(8,128)(2,1)S(1)}, bf16[128,256]{1,0:T(8,128)(2,1)S(1)}, u32[]{:S(2)}, u32[]{:S(2)}) %collective-permute-start.25) | collective-permute-done | bytes 65568 | tf_op jit(solution)/shard_map/ppermute | solution.py:14
  111.7 0.6 shard_map.131.refs_0_
  112.3 1.6 %collective-permute-start.27 = (bf16[128,256]{1,0:T(8,128)(2,1)S(1)}, bf16[128,256]{1,0:T(8,128)(2,1)S(1)}, u32[]{:S(2)}, u32[]{:S(2)}) collective-permute-start(bf16[128,256]{1,0:T(8,128)(2,1)S(1)} %shard_map.131.refs_0_), channel_id=1, source_target_pairs={{0,16},{8,24},{16,0},{24,8},{1,17},{9,25},{17,1},{25,9},{2,18},{10... | collective-permute-start | bytes 196616 | tf_op jit(solution)/shard_map/ppermute | solution.py:14
  113.9 2.7 %collective-permute-done.27.refs_1_ = bf16[128,256]{1,0:T(8,128)(2,1)S(1)} collective-permute-done((bf16[128,256]{1,0:T(8,128)(2,1)S(1)}, bf16[128,256]{1,0:T(8,128)(2,1)S(1)}, u32[]{:S(2)}, u32[]{:S(2)}) %collective-permute-start.27) | collective-permute-done | bytes 65568 | tf_op jit(solution)/shard_map/ppermute | solution.py:14
  116.6 1.2 %collective-permute-done.29.refs_3_ = bf16[128,256]{1,0:T(8,128)(2,1)S(1)} collective-permute-done((bf16[128,256]{1,0:T(8,128)(2,1)S(1)}, bf16[128,256]{1,0:T(8,128)(2,1)S(1)}, u32[]{:S(2)}, u32[]{:S(2)}) %collective-permute-start.29) | collective-permute-done | bytes 65568 | tf_op jit(solution)/shard_map/ppermute | solution.py:14
  117.9 1.4 %shard_map.132 = f32[512,256]{1,0:T(8,128)} custom-call(s32[7]{0:T(128)S(1)} %stack.31.where_ref, bf16[128,256]{1,0:T(8,128)(2,1)S(1)} %shard_map.131.refs_0_, bf16[128,256]{1,0:T(8,128)(2,1)S(1)} %collective-permute-done.27.refs_1_, bf16[128,256]{1,0:T(8,128)(2,1)S(1)} %collective-permute-done.28.refs_2_, bf16[128,256]{1,0:T(8,128)(2,1)S(1)} %collective-permute-done.29.refs_3_), custom_call_target="tpu_custom_call" | custom-call | tf_op jit(solution)/shard_map/pallas_call | solution.py:234
  (39 shorter events, 0.1 us)
Async XLA Ops:
  0.6 10.5 %copy-start = (bf16[1,512,512]{2,1,0:T(8,128)(2,1)S(1)}, bf16[1,512,512]{2,1,0:T(8,128)(2,1)}, u32[]{:S(2)}) copy-start(bf16[1,512,512]{2,1,0:T(8,128)(2,1)} %param.9) | copy-start | bytes 1572868
  0.6 10.5 %copy-start.1 = (bf16[1,512,512]{2,1,0:T(8,128)(2,1)S(1)}, bf16[1,512,512]{2,1,0:T(8,128)(2,1)}, u32[]{:S(2)}) copy-start(bf16[1,512,512]{2,1,0:T(8,128)(2,1)} %param.10) | copy-start | bytes 1572868
  0.7 10.5 %copy-start.6 = (s32[1,256,2]{1,2,0:T(2,128)S(1)}, s32[1,256,2]{1,2,0:T(2,128)}, u32[]{:S(2)}) copy-start(s32[1,256,2]{1,2,0:T(2,128)} %param.14) | copy-start | bytes 6148
  2.9 17.1 %copy-start.2 = (bf16[1,512,512]{2,1,0:T(8,128)(2,1)S(1)}, bf16[1,512,512]{2,1,0:T(8,128)(2,1)}, u32[]{:S(2)}) copy-start(bf16[1,512,512]{2,1,0:T(8,128)(2,1)} %param.8) | copy-start | bytes 1572868
  2.9 22.0 %all-to-all-start = ((bf16[4,256,256]{2,1,0:T(8,128)(2,1)}), bf16[4,256,256]{2,1,0:T(8,128)(2,1)S(1)}, u32[]{:S(2)}, u32[]{:S(2)}) async-start(bf16[4,256,256]{2,1,0:T(8,128)(2,1)} %shard_map.111.refs_2_), calls=%async_computation | async-start | bytes 1048576 | tf_op jit(solution)/shard_map/all_to_all | solution.py:772
  11.0 26.6 %copy-start.3 = (bf16[384,256]{1,0:T(8,128)(2,1)S(1)}, bf16[384,256]{1,0:T(8,128)(2,1)}, u32[]{:S(2)}) copy-start(bf16[384,256]{1,0:T(8,128)(2,1)} %shard_map.112.refs_0_) | copy-start | bytes 589828
  12.0 1.4 %collective-permute-start = (bf16[528,128]{1,0:T(8,128)(2,1)S(1)}, bf16[528,128]{1,0:T(8,128)(2,1)S(1)}, u32[]{:S(2)}, u32[]{:S(2)}) collective-permute-start(bf16[528,128]{1,0:T(8,128)(2,1)S(1)} %shard_map.113.own_ref.mine_ref), channel_id=1, source_target_pairs={{0,8},{8,0},{16,24},{24,16},{1,9},{9,1},{17,25},{25,17},{2,10},{10... | collective-permute-start | bytes 405512 | tf_op jit(solution)/shard_map/ppermute | solution.py:14
  14.0 6.0 %collective-permute-start.1 = (bf16[544,128]{1,0:T(8,128)(2,1)S(1)}, bf16[544,128]{1,0:T(8,128)(2,1)S(1)}, u32[]{:S(2)}, u32[]{:S(2)}) collective-permute-start(bf16[544,128]{1,0:T(8,128)(2,1)S(1)} %shard_map.114), channel_id=1, source_target_pairs={{0,16},{8,24},{16,0},{24,8},{1,17},{9,25},{17,1},{25,9},{2,18},{10... | collective-permute-start | bytes 417800 | tf_op jit(solution)/shard_map/ppermute | solution.py:14
  15.6 13.2 %collective-permute-start.3 = (bf16[384,256]{1,0:T(8,128)(2,1)}, bf16[384,256]{1,0:T(8,128)(2,1)S(1)}, u32[]{:S(2)}, u32[]{:S(2)}) collective-permute-start(bf16[384,256]{1,0:T(8,128)(2,1)} %shard_map.112.refs_0_), channel_id=1, source_target_pairs={{0,1},{1,0},{2,3},{3,2},{4,5},{5,4},{6,7},{7,6},{8,9},{9,8},{10,11... | collective-permute-start | bytes 589832 | tf_op jit(solution)/shard_map/ppermute | solution.py:14
  17.6 19.9 %collective-permute-start.4 = (bf16[384,256]{1,0:T(8,128)(2,1)}, bf16[384,256]{1,0:T(8,128)(2,1)}, u32[]{:S(2)}, u32[]{:S(2)}) collective-permute-start(bf16[384,256]{1,0:T(8,128)(2,1)} %shard_map.112.refs_0_), channel_id=1, source_target_pairs={{0,2},{1,3},{2,0},{3,1},{4,6},{5,7},{6,4},{7,5},{8,10},{9,11},{10,... | collective-permute-start | bytes 589832 | tf_op jit(solution)/shard_map/ppermute | solution.py:14
  20.0 17.6 %collective-permute-start.5 = (bf16[384,256]{1,0:T(8,128)(2,1)}, bf16[384,256]{1,0:T(8,128)(2,1)}, u32[]{:S(2)}, u32[]{:S(2)}) collective-permute-start(bf16[384,256]{1,0:T(8,128)(2,1)} %shard_map.112.refs_0_), channel_id=1, source_target_pairs={{0,3},{1,2},{2,1},{3,0},{4,7},{5,6},{6,5},{7,4},{8,11},{9,10},{10,... | collective-permute-start | bytes 589832 | tf_op jit(solution)/shard_map/ppermute | solution.py:14
  22.0 0.7 copy-start.4
  25.5 15.9 %collective-permute-start.2 = (bf16[1024,256]{1,0:T(8,128)(2,1)S(1)}, bf16[1024,256]{1,0:T(8,128)(2,1)S(1)}, u32[]{:S(2)}, u32[]{:S(2)}) collective-permute-start(bf16[1024,256]{1,0:T(8,128)(2,1)S(1)} %get-tuple-element.60.own_ref), channel_id=1, source_target_pairs={{0,4},{4,0},{1,5},{5,1},{2,6},{6,2},{3,7},{7,3},{8,12},{12,8},{9,1... | collective-permute-start | bytes 1572872 | tf_op jit(solution)/shard_map/ppermute | solution.py:14
  27.1 10.5 %collective-permute-start.6 = (bf16[256,256]{1,0:T(8,128)(2,1)S(1)}, bf16[256,256]{1,0:T(8,128)(2,1)S(1)}, u32[]{:S(2)}, u32[]{:S(2)}) collective-permute-start(bf16[256,256]{1,0:T(8,128)(2,1)S(1)} %get-tuple-element.61), channel_id=1, source_target_pairs={{0,16},{8,24},{16,0},{24,8},{1,17},{9,25},{17,1},{25,9},{2,18},{10... | collective-permute-start | bytes 393224 | tf_op jit(solution)/shard_map/ppermute | solution.py:14
  38.7 2.6 %collective-permute-start.7 = (bf16[160,1024]{1,0:T(8,128)(2,1)S(1)}, bf16[160,1024]{1,0:T(8,128)(2,1)S(1)}, u32[]{:S(2)}, u32[]{:S(2)}) collective-permute-start(bf16[160,1024]{1,0:T(8,128)(2,1)S(1)} %get-tuple-element.66), channel_id=1, source_target_pairs={{0,8},{8,0},{16,24},{24,16},{1,9},{9,1},{17,25},{25,17},{2,10},{10... | collective-permute-start | bytes 983048 | tf_op jit(solution)/shard_map/ppermute | solution.py:14
  38.8 7.0 %collective-permute-start.10 = (bf16[96,1024]{1,0:T(8,128)(2,1)S(1)}, bf16[96,1024]{1,0:T(8,128)(2,1)S(1)}, u32[]{:S(2)}, u32[]{:S(2)}) collective-permute-start(bf16[96,1024]{1,0:T(8,128)(2,1)S(1)} %get-tuple-element.72), channel_id=1, source_target_pairs={{0,8},{8,0},{16,24},{24,16},{1,9},{9,1},{17,25},{25,17},{2,10},{10... | collective-permute-start | bytes 589832 | tf_op jit(solution)/shard_map/ppermute | solution.py:14
  42.8 22.4 %collective-permute-start.8 = (bf16[1280,256]{1,0:T(8,128)(2,1)S(1)}, bf16[1280,256]{1,0:T(8,128)(2,1)S(1)}, u32[]{:S(2)}, u32[]{:S(2)}) collective-permute-start(bf16[1280,256]{1,0:T(8,128)(2,1)S(1)} %get-tuple-element.70), channel_id=1, source_target_pairs={{0,16},{8,24},{16,0},{24,8},{1,17},{9,25},{17,1},{25,9},{2,18},{10... | collective-permute-start | bytes 1966088 | tf_op jit(solution)/shard_map/ppermute | solution.py:14
  44.4 9.2 %collective-permute-start.9 = (bf16[512,256]{1,0:T(8,128)(2,1)S(1)}, bf16[512,256]{1,0:T(8,128)(2,1)S(1)}, u32[]{:S(2)}, u32[]{:S(2)}) collective-permute-start(bf16[512,256]{1,0:T(8,128)(2,1)S(1)} %shard_map.118.own_ref), channel_id=1, source_target_pairs={{0,4},{4,0},{1,5},{5,1},{2,6},{6,2},{3,7},{7,3},{8,12},{12,8},{9,1... | collective-permute-start | bytes 786440 | tf_op jit(solution)/shard_map/ppermute | solution.py:14
  46.7 18.5 %collective-permute-start.12 = (bf16[256,1024]{1,0:T(8,128)(2,1)S(1)}, bf16[256,1024]{1,0:T(8,128)(2,1)S(1)}, u32[]{:S(2)}, u32[]{:S(2)}) collective-permute-start(bf16[256,1024]{1,0:T(8,128)(2,1)S(1)} %shard_map.122), channel_id=1, source_target_pairs={{0,4},{4,0},{1,5},{5,1},{2,6},{6,2},{3,7},{7,3},{8,12},{12,8},{9,1... | collective-permute-start | bytes 1572872 | tf_op jit(solution)/shard_map/ppermute | solution.py:14
  47.3 7.7 %collective-permute-start.14 = (bf16[256,256]{1,0:T(8,128)(2,1)S(1)}, bf16[256,256]{1,0:T(8,128)(2,1)S(1)}, u32[]{:S(2)}, u32[]{:S(2)}) collective-permute-start(bf16[256,256]{1,0:T(8,128)(2,1)S(1)} %collective-permute-done.6.refs_2_), channel_id=1, source_target_pairs={{0,8},{8,0},{16,24},{24,16},{1,9},{9,1},{17,25},{25,17},{2,10},{10... | collective-permute-start | bytes 393224 | tf_op jit(solution)/shard_map/ppermute | solution.py:14
  47.3 18.5 %copy-start.7 = (bf16[1,256,2,1024]{3,2,1,0:T(2,128)(2,1)S(1)}, bf16[1,256,2,1024]{3,2,1,0:T(2,128)(2,1)}, u32[]{:S(2)}) copy-start(bf16[1,256,2,1024]{3,2,1,0:T(2,128)(2,1)} %param.15) | copy-start | bytes 3145732
  47.3 17.9 %collective-permute-start.15 = (bf16[768,256]{1,0:T(8,128)(2,1)S(1)}, bf16[768,256]{1,0:T(8,128)(2,1)S(1)}, u32[]{:S(2)}, u32[]{:S(2)}) collective-permute-start(bf16[768,256]{1,0:T(8,128)(2,1)S(1)} %get-tuple-element.76), channel_id=1, source_target_pairs={{0,8},{8,0},{16,24},{24,16},{1,9},{9,1},{17,25},{25,17},{2,10},{10... | collective-permute-start | bytes 1179656 | tf_op jit(solution)/shard_map/ppermute | solution.py:14
  53.6 2.0 %collective-permute-start.13 = (bf16[512,256]{1,0:T(8,128)(2,1)S(1)}, bf16[512,256]{1,0:T(8,128)(2,1)S(1)}, u32[]{:S(2)}, u32[]{:S(2)}) collective-permute-start(bf16[512,256]{1,0:T(8,128)(2,1)S(1)} %get-tuple-element.59.refs_0_), channel_id=1, source_target_pairs={{0,8},{8,0},{16,24},{24,16},{1,9},{9,1},{17,25},{25,17},{2,10},{10... | collective-permute-start | bytes 786440 | tf_op jit(solution)/shard_map/ppermute | solution.py:14
  55.0 10.2 %collective-permute-start.11 = (bf16[512,256]{1,0:T(8,128)(2,1)S(1)}, bf16[512,256]{1,0:T(8,128)(2,1)S(1)}, u32[]{:S(2)}, u32[]{:S(2)}) collective-permute-start(bf16[512,256]{1,0:T(8,128)(2,1)S(1)} %get-tuple-element.75), channel_id=1, source_target_pairs={{0,16},{8,24},{16,0},{24,8},{1,17},{9,25},{17,1},{25,9},{2,18},{10... | collective-permute-start | bytes 786440 | tf_op jit(solution)/shard_map/ppermute | solution.py:14
  65.2 2.7 %collective-permute-start.16 = (bf16[1280,256]{1,0:T(8,128)(2,1)S(1)}, bf16[1280,256]{1,0:T(8,128)(2,1)S(1)}, u32[]{:S(2)}, u32[]{:S(2)}) collective-permute-start(bf16[1280,256]{1,0:T(8,128)(2,1)S(1)} %collective-permute-done.8.refs_3_), channel_id=1, source_target_pairs={{0,8},{8,0},{16,24},{24,16},{1,9},{9,1},{17,25},{25,17},{2,10},{10... | collective-permute-start | bytes 1966088 | tf_op jit(solution)/shard_map/ppermute | solution.py:14
  65.3 2.6 %collective-permute-start.18 = (bf16[512,256]{1,0:T(8,128)(2,1)S(1)}, bf16[512,256]{1,0:T(8,128)(2,1)S(1)}, u32[]{:S(2)}, u32[]{:S(2)}) collective-permute-start(bf16[512,256]{1,0:T(8,128)(2,1)S(1)} %collective-permute-done.11.refs_10_), channel_id=1, source_target_pairs={{0,8},{8,0},{16,24},{24,16},{1,9},{9,1},{17,25},{25,17},{2,10},{10... | collective-permute-start | bytes 786440 | tf_op jit(solution)/shard_map/ppermute | solution.py:14
  65.8 2.1 %collective-permute-start.17 = (bf16[256,256]{1,0:T(8,128)(2,1)S(1)}, bf16[256,256]{1,0:T(8,128)(2,1)S(1)}, u32[]{:S(2)}, u32[]{:S(2)}) collective-permute-start(bf16[256,256]{1,0:T(8,128)(2,1)S(1)} %get-tuple-element.84), channel_id=1, source_target_pairs={{0,8},{8,0},{16,24},{24,16},{1,9},{9,1},{17,25},{25,17},{2,10},{10... | collective-permute-start | bytes 393224 | tf_op jit(solution)/shard_map/ppermute | solution.py:14
  72.2 14.0 %collective-permute-start.19 = (bf16[256,1024]{1,0:T(8,128)(2,1)S(1)}, bf16[256,1024]{1,0:T(8,128)(2,1)S(1)}, u32[]{:S(2)}, u32[]{:S(2)}) collective-permute-start(bf16[256,1024]{1,0:T(8,128)(2,1)S(1)} %shard_map.124.own), channel_id=1, source_target_pairs={{0,4},{4,0},{1,5},{5,1},{2,6},{6,2},{3,7},{7,3},{8,12},{12,8},{9,1... | collective-permute-start | bytes 1572872 | tf_op jit(solution)/shard_map/ppermute | solution.py:14
  87.5 5.1 %copy-start.5 = (bf16[4,128,128]{2,1,0:T(8,128)(2,1)S(1)}, bf16[4,128,128]{2,1,0:T(8,128)(2,1)}, u32[]{:S(2)}) copy-start(bf16[4,128,128]{2,1,0:T(8,128)(2,1)} %copy-done.4) | copy-start | bytes 393220
  87.5 2.3 %collective-permute-start.20 = (bf16[2,128,1024]{2,1,0:T(8,128)(2,1)S(1)}, bf16[2,128,1024]{2,1,0:T(8,128)(2,1)S(1)}, u32[]{:S(2)}, u32[]{:S(2)}) collective-permute-start(bf16[2,128,1024]{2,1,0:T(8,128)(2,1)S(1)} %get-tuple-element.87), channel_id=1, source_target_pairs={{0,8},{8,0},{16,24},{24,16},{1,9},{9,1},{17,25},{25,17},{2,10},{10... | collective-permute-start | bytes 1572872 | tf_op jit(solution)/shard_map/ppermute | solution.py:14
  89.2 2.8 %collective-permute-start.22 = (bf16[4,128,128]{2,1,0:T(8,128)(2,1)S(1)}, bf16[4,128,128]{2,1,0:T(8,128)(2,1)S(1)}, u32[]{:S(2)}, u32[]{:S(2)}) collective-permute-start(bf16[4,128,128]{2,1,0:T(8,128)(2,1)S(1)} %get-tuple-element.91), channel_id=1, source_target_pairs={{0,8},{8,0},{16,24},{24,16},{1,9},{9,1},{17,25},{25,17},{2,10},{10... | collective-permute-start | bytes 393224 | tf_op jit(solution)/shard_map/ppermute | solution.py:14
  90.4 9.2 %collective-permute-start.21 = (bf16[128,1024]{1,0:T(8,128)(2,1)S(1)}, bf16[128,1024]{1,0:T(8,128)(2,1)S(1)}, u32[]{:S(2)}, u32[]{:S(2)}) collective-permute-start(bf16[128,1024]{1,0:T(8,128)(2,1)S(1)} %get-tuple-element.88), channel_id=1, source_target_pairs={{0,16},{8,24},{16,0},{24,8},{1,17},{9,25},{17,1},{25,9},{2,18},{10... | collective-permute-start | bytes 786440 | tf_op jit(solution)/shard_map/ppermute | solution.py:14
  92.1 14.4 %collective-permute-start.26 = (bf16[4,128,128]{2,1,0:T(8,128)(2,1)S(1)}, bf16[4,128,128]{2,1,0:T(8,128)(2,1)S(1)}, u32[]{:S(2)}, u32[]{:S(2)}) collective-permute-start(bf16[4,128,128]{2,1,0:T(8,128)(2,1)S(1)} %add_convert_fusion), channel_id=1, source_target_pairs={{0,16},{8,24},{16,0},{24,8},{1,17},{9,25},{17,1},{25,9},{2,18},{10... | collective-permute-start | bytes 393224 | tf_op jit(solution)/shard_map/ppermute | solution.py:14
  100.3 10.2 %collective-permute-start.23 = (bf16[128,256]{1,0:T(8,128)(2,1)S(1)}, bf16[128,256]{1,0:T(8,128)(2,1)S(1)}, u32[]{:S(2)}, u32[]{:S(2)}) collective-permute-start(bf16[128,256]{1,0:T(8,128)(2,1)S(1)} %get-tuple-element.95), channel_id=1, source_target_pairs={{0,1},{1,0},{2,3},{3,2},{4,5},{5,4},{6,7},{7,6},{8,9},{9,8},{10,11... | collective-permute-start | bytes 196616 | tf_op jit(solution)/shard_map/ppermute | solution.py:14
  104.0 6.4 %collective-permute-start.24 = (bf16[128,256]{1,0:T(8,128)(2,1)S(1)}, bf16[128,256]{1,0:T(8,128)(2,1)S(1)}, u32[]{:S(2)}, u32[]{:S(2)}) collective-permute-start(bf16[128,256]{1,0:T(8,128)(2,1)S(1)} %get-tuple-element.96), channel_id=1, source_target_pairs={{0,2},{1,3},{2,0},{3,1},{4,6},{5,7},{6,4},{7,5},{8,10},{9,11},{10,... | collective-permute-start | bytes 196616 | tf_op jit(solution)/shard_map/ppermute | solution.py:14
  105.7 6.1 %collective-permute-start.25 = (bf16[128,256]{1,0:T(8,128)(2,1)S(1)}, bf16[128,256]{1,0:T(8,128)(2,1)S(1)}, u32[]{:S(2)}, u32[]{:S(2)}) collective-permute-start(bf16[128,256]{1,0:T(8,128)(2,1)S(1)} %get-tuple-element.97), channel_id=1, source_target_pairs={{0,3},{1,2},{2,1},{3,0},{4,7},{5,6},{6,5},{7,4},{8,11},{9,10},{10,... | collective-permute-start | bytes 196616 | tf_op jit(solution)/shard_map/ppermute | solution.py:14
  112.3 4.3 %collective-permute-start.27 = (bf16[128,256]{1,0:T(8,128)(2,1)S(1)}, bf16[128,256]{1,0:T(8,128)(2,1)S(1)}, u32[]{:S(2)}, u32[]{:S(2)}) collective-permute-start(bf16[128,256]{1,0:T(8,128)(2,1)S(1)} %shard_map.131.refs_0_), channel_id=1, source_target_pairs={{0,16},{8,24},{16,0},{24,8},{1,17},{9,25},{17,1},{25,9},{2,18},{10... | collective-permute-start | bytes 196616 | tf_op jit(solution)/shard_map/ppermute | solution.py:14
  113.9 2.7 %collective-permute-start.28 = (bf16[128,256]{1,0:T(8,128)(2,1)S(1)}, bf16[128,256]{1,0:T(8,128)(2,1)S(1)}, u32[]{:S(2)}, u32[]{:S(2)}) collective-permute-start(bf16[128,256]{1,0:T(8,128)(2,1)S(1)} %shard_map.131.refs_0_), channel_id=1, source_target_pairs={{0,8},{8,0},{16,24},{24,16},{1,9},{9,1},{17,25},{25,17},{2,10},{10... | collective-permute-start | bytes 196616 | tf_op jit(solution)/shard_map/ppermute | solution.py:14
  116.6 1.3 %collective-permute-start.29 = (bf16[128,256]{1,0:T(8,128)(2,1)S(1)}, bf16[128,256]{1,0:T(8,128)(2,1)S(1)}, u32[]{:S(2)}, u32[]{:S(2)}) collective-permute-start(bf16[128,256]{1,0:T(8,128)(2,1)S(1)} %collective-permute-done.27.refs_1_), channel_id=1, source_target_pairs={{0,8},{8,0},{16,24},{24,16},{1,9},{9,1},{17,25},{25,17},{2,10},{10... | collective-permute-start | bytes 196616 | tf_op jit(solution)/shard_map/ppermute | solution.py:14

commit v4 on v3

--- a/solution.py
+++ b/solution.py
@@ -316,7 +316,7 @@
     return copies(views, shaped((t_rows + rows, cols)), [code_table, out_proj, after])
 
 
-def first_parts(where, pieces, t_rows):
+def first_parts(where, pieces, t_rows, early):
     n, d_half, t_cols = pieces.shape
     d_half, d_cols = d_half - t_rows, t_cols // 2
     top, fold = n * t_rows, 2 * d_half
@@ -331,45 +331,34 @@
                 row = pl.multiple_of((place // 2) * fold + half * d_half, d_half)
                 both[pl.ds(pl.multiple_of(top + row, d_half), d_half), cols] = part
                 depth[pl.ds(row, d_half), cols] = part
-        top_fold[...] = depth[:fold]
+        top_fold[...] = depth[:early]
 
     rows = fold * n // 2
-    return run(body, [shaped((top + rows, t_cols)), shaped((rows, t_cols)), shaped((fold, t_cols))], where, pieces)
-
-
-def table_part(where, pieces, t_rows):
-    n, cols = len(pieces), pieces[0].shape[1]
-
-    def body(where_ref, *refs):
-        for k in range(n):
-            refs[n][k * t_rows:(k + 1) * t_rows, :] = refs[k][:t_rows]
-
-    return run(body, [shaped((n * t_rows, cols))], where, *pieces)[0]
-
-
-def out_part(where, pieces, t_rows):
+    return run(body, [shaped((top + rows, t_cols)), shaped((rows, t_cols)), shaped((early, t_cols))], where, pieces)
+
+
+def second_parts(where, pieces, distances, t_rows):
     rows, cols = pieces[0].shape[0] - t_rows, pieces[0].shape[1]
     n = len(pieces)
-    first = 160
+    first = rows * 5 // 8
 
     def body(where_ref, *refs):
-        out, head, tail = refs[n:]
-        for k in range(n):
+        table, head, tail = refs[n:]
+        for k, ref in zip(distances, refs):
             cut = at(where_ref[DP] ^ k, cols)
-            out[:, cut] = refs[k][t_rows:]
-            head[:, cut] = refs[k][t_rows:t_rows + first]
-            tail[:, cut] = refs[k][t_rows + first:]
-
-    outs = [shaped((rows, n * cols)), shaped((first, n * cols)), shaped((rows - first, n * cols))]
+            table[k * t_rows:(k + 1) * t_rows, :] = ref[:t_rows]
+            head[:, cut] = ref[t_rows:t_rows + first]
+            tail[:, cut] = ref[t_rows + first:]
+
+    outs = [shaped((n * t_rows, cols)), shaped((first, n * cols)), shaped((rows - first, n * cols))]
     return run(body, outs, where, *pieces)
 
 
-def embed(where, packed, top, level, n_level, tokens, own, got, half, n_dp):
+def embed(where, packed, top, level, n_level, tokens, own, got, half, n_dp, late):
     folds = tokens // DH
     n_rows = id_rows(n_level, tokens)
     rows, cols = own.shape
     rows_dev, extra = half // n_dp, rows - half
-    late = extra // 2
 
     def body(where_ref, mine_ref, core_ref, far_ref, own_ref, got_ref, *outs):
         def ids_of(ref, start):
@@ -407,7 +396,7 @@
     return run(body, outs, where, *packed, own, got)
 
 
-def depth_grad(where, folds, first, second, mixed, mixed_got, cot):
+def depth_grad(where, folds, rest, late, first, second, mixed, mixed_got, cot):
     arrays, which = [], []
     for array, _ in folds + first + second:
         found = [i for i, other in enumerate(arrays) if other is array]
@@ -425,7 +414,14 @@
         for n in range(16):
             m, x, j = n // 4, n // 2 % 2, n % 2
             place = (where_ref[HEAD] ^ x) * 2 + j
-            full[at(where_ref[m], cols), at(place, cols)] = parts[which[n]][starts[n]:starts[n] + cols]
+            if rest[n] is None:
+                full[at(where_ref[m], cols), at(place, cols)] = parts[which[n]][starts[n]:starts[n] + cols]
+            else:
+                main = pl.ds(pl.multiple_of(where_ref[m] * cols, cols), cols - late)
+                tail = pl.ds(pl.multiple_of(where_ref[m] * cols + cols - late, 16), late)
+                array = next(i for i, other in enumerate(arrays) if other is rest[n][0])
+                full[main, at(place, cols)] = parts[which[n]][starts[n]:starts[n] + cols - late]
+                full[tail, at(place, cols)] = parts[array][rest[n][1]:rest[n][1] + late]
 
         def rows_of(i):
             return pl.ds(pl.multiple_of(i * chunk, chunk), chunk)
@@ -569,17 +565,18 @@
     )
 
 
-def mix_own(where, attended, own_rows):
+def mix_own(where, attended, head, tail):
     length = attended.shape[0] // 2
-    half, width = own_rows.shape
-
-    def body(where_ref, att, own, out):
+    half, width = head.shape[0] + tail.shape[0], head.shape[1]
+
+    def body(where_ref, att, head_ref, tail_ref, out):
         core = where_ref[0] // 2
+        own = jnp.concatenate([head_ref[...], tail_ref[...]], axis=0)
         for k in range(2):
             rows = at(where_ref[HEAD] ^ (1 - k), length)
-            out[k] = jnp.dot(att[rows, at(core, half)], own[...], preferred_element_type=F32)
-
-    return run(body, [shaped((2, length, width), F32)], where, attended, own_rows)[0]
+            out[k] = jnp.dot(att[rows, at(core, half)], own, preferred_element_type=F32)
+
+    return run(body, [shaped((2, length, width), F32)], where, attended, head, tail)[0]
 
 
 def mix(where, attended, part, got_head, got_tail, other):
@@ -667,14 +664,14 @@
     return run(body, [shaped((rows * 4, cols), F32)], where, *pieces)[0]
 
 
-def grad_attend(where, grad_own, grad_got, own_rows, got_head, got_tail, queries):
+def grad_attend(where, grad_own, grad_got, own_head, own_tail, got_head, got_tail, queries):
     tokens, width = grad_own.shape
     length, width_dev = queries.shape
     half = width_dev // 2
 
-    def body(where_ref, own, got, o_own, head, tail, q_ref, rows, back):
-        for c in range(2):
-            block = o_own[...] if c == 0 else jnp.concatenate([head[...], tail[...]], axis=0)
+    def body(where_ref, own, got, head, tail, got_head, got_tail, q_ref, rows, back):
+        for c, ends in enumerate(((head, tail), (got_head, got_tail))):
+            block = jnp.concatenate([ends[0][...], ends[1][...]], axis=0)
             for k, ref in enumerate((own, got)):
                 part = dot(ref[...], block, ((1,), (1,))).astype(BF16)
                 rows[at(where_ref[HEAD] ^ k, tokens), at((where_ref[0] // 2) ^ c, half)] = part
@@ -683,7 +680,7 @@
             back[i] = dot(q_ref[:, cut], rows[:, cut], ((0,), (0,))).astype(BF16)
 
     outs = [shaped((length, width_dev)), shaped((width_dev // DH, DH, DH))]
-    return run(body, outs, where, grad_own, grad_got, own_rows, got_head, got_tail, queries)
+    return run(body, outs, where, grad_own, grad_got, own_head, own_tail, got_head, got_tail, queries)
 
 
 def query_grads(where, grad_rows, keys, values, state, att_scale):
@@ -702,28 +699,39 @@
     return run(body, [shaped((length, width_dev))], where, grad_rows, keys, values, state)[0]
 
 
-def key_value_grads(where, grad_rows, queries, keys, values, from_core, from_far, att_scale):
+def key_value_parts(where, grad_rows, queries, keys, values):
     length, width_dev = keys.shape
 
-    def body(where_ref, g_ref, q_ref, k_ref, v_ref, core_ref, far_ref, dk, dv):
-        near = 1.0 - (where_ref[0] // 2).astype(F32)
-        far = 1.0 - (where_ref[0] % 2).astype(F32)
+    def body(where_ref, g_ref, q_ref, k_ref, v_ref, dk, dv):
         keep = upper(length)
         for i in range(width_dev // DH):
             cut = slice(i * DH, (i + 1) * DH)
             g, q, k, v = g_ref[:, cut], q_ref[:, cut], k_ref[:, cut], v_ref[:, cut]
+            grad_scores = jnp.where(keep, dot(v, g, ((1,), (1,))), 0.0).astype(BF16)
+            dk[:, cut] = jnp.dot(grad_scores, q, preferred_element_type=F32)
+            scores = jnp.where(keep, dot(k, q, ((1,), (1,))), 0.0).astype(BF16)
+            dv[:, cut] = jnp.dot(scores, g, preferred_element_type=F32)
+
+    outs = [shaped((length, width_dev), F32)] * 2
+    return run(body, outs, where, grad_rows, queries, keys, values)
+
+
+def key_value_grads(where, key_part, value_part, keys, values, from_core, from_far, att_scale):
+    length, width_dev = keys.shape
+
+    def body(where_ref, kp_ref, vp_ref, k_ref, v_ref, core_ref, far_ref, dk, dv):
+        near = 1.0 - (where_ref[0] // 2).astype(F32)
+        far = 1.0 - (where_ref[0] % 2).astype(F32)
+        for i in range(width_dev // DH):
+            cut = slice(i * DH, (i + 1) * DH)
             back = (core_ref[i].astype(F32) * near + far_ref[i].astype(F32) * far).astype(BF16)
-            grad_scores = jnp.where(keep, dot(v, g, ((1,), (1,))), 0.0).astype(BF16)
-            both = jnp.dot(grad_scores, q, preferred_element_type=F32)
-            both += dot(v, back, ((1,), (1,)))
+            both = kp_ref[:, cut] + dot(v_ref[:, cut], back, ((1,), (1,)))
             dk[:, cut] = (att_scale * both).astype(BF16)
-            scores = jnp.where(keep, dot(k, q, ((1,), (1,))), 0.0).astype(BF16)
-            both = jnp.dot(scores, g, preferred_element_type=F32)
-            both += jnp.dot(k, back, preferred_element_type=F32)
+            both = vp_ref[:, cut] + jnp.dot(k_ref[:, cut], back, preferred_element_type=F32)
             dv[:, cut] = (att_scale * both).astype(BF16)
 
     outs = [shaped((length, width_dev))] * 2
-    return run(body, outs, where, grad_rows, queries, keys, values, from_core, from_far)
+    return run(body, outs, where, key_part, value_part, keys, values, from_core, from_far)
 
 
 def fits(queries, out_proj, depth_proj, code_table, code_ids):
@@ -771,7 +779,8 @@
     lanes_0 = first_lanes(code_table, depth_proj, n_dp)
     pieces_0 = lax.all_to_all(lanes_0, "dp", 0, 0)
     lanes_1 = second_lanes(code_table, out_proj, lanes_0)
-    pieces_1 = exchange(lanes_1, "dp")
+    distances = [n_dp // 2] + [k for k in range(1, n_dp) if k != n_dp // 2]
+    pieces_1 = [lanes_1] + [swap(lanes_1, "dp", k) for k in distances]
 
     top = keys.shape[1]
     keys, values, _ = lax.optimization_barrier((keys, values, lanes_1))
@@ -784,19 +793,21 @@
     attended, state_in = attend(where, queries, keys, values, from_core, from_far, att_scale)
 
     pieces_0, _ = lax.optimization_barrier((pieces_0, attended))
-    part_0, depth_part, depth_top = first_parts(where, pieces_0, t_rows)
+    fold = depth_proj.shape[0] // 4
+    early = fold + fold * 7 // 16
+    late = 2 * fold - early
+    part_0, depth_part, depth_top = first_parts(where, pieces_0, t_rows, early)
     got_0 = swap(part_0, "head", 1)
     depth_far = far_swap(depth_top)
 
     pieces_1, depth_far = lax.optimization_barrier((pieces_1, depth_far))
-    out_rows, out_head, out_tail = out_part(where, pieces_1, t_rows)
+    part_1, out_head, out_tail = second_parts(where, pieces_1, [0, *distances], t_rows)
     got_head, got_tail = core_swap(out_head), core_swap(out_tail)
-    part_1 = table_part(where, pieces_1, t_rows)
     got_1 = swap(part_1, "head", 1)
 
-    mixed_part = mix_own(where, attended, out_rows)
-    got_0, got_head, _, _ = lax.optimization_barrier((got_0, got_head, part_1, mixed_part))
-    own_0, to_core, to_far = embed(where, packed, top, 0, 2, tokens, part_0, got_0, half, n_dp)
+    mixed_part = mix_own(where, attended, out_head, out_tail)
+    got_0, got_head, _ = lax.optimization_barrier((got_0, got_head, part_1))
+    own_0, to_core, to_far = embed(where, packed, top, 0, 2, tokens, part_0, got_0, half, n_dp, late)
     far_0 = far_swap(to_far)
 
     got_tail, _ = lax.optimization_barrier((got_tail, to_far))
@@ -806,7 +817,7 @@
     core_0 = core_swap(to_core)
 
     got_1, _, _ = lax.optimization_barrier((got_1, mixed, mixed_send))
-    own_1, to_core, to_far = embed(where, packed, top, 1, 2, tokens, part_1, got_1, half, n_dp)
+    own_1, to_core, to_far = embed(where, packed, top, 1, 2, tokens, part_1, got_1, half, n_dp, 0)
     far_1 = far_swap(to_far)
     depth_core, depth_core_far = core_swap(depth_part), core_swap(depth_far)
     far_0, far_1, mixed_got, depth_core, depth_core_far, core_0 = lax.optimization_barrier(
@@ -814,34 +825,42 @@
     )
     core_far_0, core_1, core_far_1 = core_swap(far_0), core_swap(to_core), core_swap(far_1)
 
-    fold, end = depth_top.shape[0], 2 * tokens
+    end = 2 * tokens
     folds = [(depth_part, 0), (depth_part, fold), (got_0, half), (got_0, half + fold)]
-    folds += [(depth_far, 0), (far_0, end + 2 * fold), (far_0, end), (far_0, end + fold)]
+    folds += [(depth_far, 0), (depth_far, fold), (far_0, end), (far_0, end + fold)]
     folds += [(depth_core, 0), (depth_core, fold), (core_0, tokens), (core_0, tokens + fold)]
-    folds += [(depth_core_far, 0), (core_far_0, end + 2 * fold), (core_far_0, end), (core_far_0, end + fold)]
+    folds += [(depth_core_far, 0), (depth_core_far, fold), (core_far_0, end), (core_far_0, end + fold)]
+    rest = [None] * 16
+    rest[5], rest[13] = (far_0, end + 2 * fold), (core_far_0, end + 2 * fold)
     first = [(own_0, 0), (far_0, 0), (core_0, 0), (core_far_0, tokens)]
     second = [(own_1, 0), (far_1, 0), (core_1, 0), (core_far_1, tokens)]
     cot = depth_cotangent[0].reshape(tokens, -1)
-    grad_mixed = depth_grad(where, folds, first, second, mixed, mixed_got, cot)
+    grad_mixed = depth_grad(where, folds, rest, late, first, second, mixed, mixed_got, cot)
 
     grad_got = swap(grad_mixed, "head", 1)
     send, keep = weight_terms(where, attended, grad_mixed, grad_got)
     send, keep = add_core(where, keep, core_swap(send))
     from_far = far_swap(send)
-    grad_rows, back = grad_attend(where, grad_mixed, grad_got, out_rows, got_head, got_tail, queries)
+    grad_rows, back = grad_attend(where, grad_mixed, grad_got, out_head, out_tail, got_head, got_tail, queries)
     back_core = core_swap(back)
+    back_chip = (back.astype(F32) + back_core.astype(F32)).astype(BF16)
+    key_part, value_part = key_value_parts(where, grad_rows, queries, keys, values)
     grad_query = query_grads(where, grad_rows, keys, values, state_in, att_scale)
-    back_chip = (back.astype(F32) + back_core.astype(F32)).astype(BF16)
+    from_far, key_part, value_part, grad_query, back_chip = lax.optimization_barrier(
+        (from_far, key_part, value_part, grad_query, back_chip)
+    )
+    keep, *send = add_far(where, keep, from_far, n_dp)
+    got = [swap(send[k - 1], "dp", k) for k in reversed(range(1, n_dp))]
+    back_chip, keep = lax.optimization_barrier((back_chip, keep))
     back_far = far_swap(back_chip)
-    from_far, grad_query, _ = lax.optimization_barrier((from_far, grad_query, back_chip))
-    keep, *send = add_far(where, keep, from_far, n_dp)
-    got = [swap(s, "dp", k + 1) for k, s in enumerate(send)]
+    block = add_all(where, keep, got)
+    blocks = [block, far_swap(block), core_swap(block), swap(block, "seq", 3)]
+    key_part, block = lax.optimization_barrier((key_part, block))
     grad_key, grad_value = key_value_grads(
-        where, grad_rows, queries, keys, values, back_core, back_far, att_scale
-    )
-    got, grad_key, grad_value = lax.optimization_barrier((got, grad_key, grad_value))
-    block = add_all(where, keep, got)
-    grad_out_proj = rows_together(where, all_lanes(block))
+        where, key_part, value_part, keys, values, back_core, back_far, att_scale
+    )
+    blocks, grad_key, grad_value = lax.optimization_barrier((blocks, grad_key, grad_value))
+    grad_out_proj = rows_together(where, blocks)
     return grad_query[None], grad_key[None], grad_value[None], grad_out_proj
 
 

time: 120 us -> 116 us (0.967)
  waiting for transfers between devices: 49.5 us -> 44.2 us
  starting transfers between devices: 33.9 us -> 35.4 us
    ppermute x30, waiting for transfers between devices: 47.3 us -> 37.8 us  [swap(): lax.ppermute(block, axis, [(i, i ^ mask) for i in range(lax.axis_size(axi...]
    all_to_all x1, waiting for transfers between devices: 2.23 us -> 6.39 us  [on_device(): pieces_0 = lax.all_to_all(lanes_0, 'dp', 0, 0)]
    ppermute x30, starting transfers between devices: 27.4 us -> 29 us  [swap(): lax.ppermute(block, axis, [(i, i ^ mask) for i in range(lax.axis_size(axi...]
  transfers between devices with their start and end apart: 31 -> 31, of which waited for: 11 -> 16; matrix products, arithmetic and copies ran while one was open for 1% -> 1% of each run, Pallas kernels for 19% -> 20%
where the time goes in v4:
time: 116 us; the launch traced here: 115 us
  waiting for transfers between devices  44.2 us (38%)
  starting transfers between devices  35.4 us (31%)
  Pallas kernels  32.8 us (28%)
  local copies, waits for them, and re-layouts  2.05 us (2%)
    ppermute x30, waiting for transfers between devices, swap(): lax.ppermute(block, axis, [(i, i ^ mask) for i in range(lax.axis_size(axi...  37.8 us
    ppermute x30, starting transfers between devices, swap(): lax.ppermute(block, axis, [(i, i ^ mask) for i in range(lax.axis_size(axi...  29 us
    pallas_call x19, Pallas kernels, run(): pl.pallas_call(body, out_shape=outs, in_specs=[pl.BlockSpec(memory_space=...  24.7 us
    all_to_all x1, starting transfers between devices, on_device(): pieces_0 = lax.all_to_all(lanes_0, 'dp', 0, 0)  6.46 us
    all_to_all x1, waiting for transfers between devices, on_device(): pieces_0 = lax.all_to_all(lanes_0, 'dp', 0, 0)  6.39 us
    pallas_call x1, Pallas kernels, depth_grad(): pl.pallas_call(body, out_shape=shaped((tokens, width)), in_specs=[pl.Bloc...  4.27 us
    pallas_call x2, Pallas kernels, copies(): pl.pallas_call(body, out_shape=outs, in_specs=[anywhere] * len(args), out...  3.88 us
  transfers between devices with their start and end apart: 31, of which 16 were waited for; matrix products, arithmetic and copies ran while one was open for 1% of the time, Pallas kernels for 20%

profile of v4, /device:TPU:0, one launch (start us, length us, event | category | flops | bytes accessed | tf_op | source)
XLA Modules:
  0.0 115.5 jit_solution(6704442984073832787)
XLA Ops:
  0.7 2.2 %shard_map.111.refs_2_ = bf16[4,256,256]{2,1,0:T(8,128)(2,1)} custom-call(bf16[2,128,1024]{2,1,0:T(8,128)(2,1)} %refs_0_.3, bf16[1024,128]{1,0:T(8,128)(2,1)} %refs_1_.2), custom_call_target="tpu_custom_call" | custom-call | tf_op jit(solution)/shard_map/pallas_call | solution.py:271
  2.9 6.5 %all-to-all-start = ((bf16[4,256,256]{2,1,0:T(8,128)(2,1)}), bf16[4,256,256]{2,1,0:T(8,128)(2,1)S(1)}, u32[]{:S(2)}, u32[]{:S(2)}) async-start(bf16[4,256,256]{2,1,0:T(8,128)(2,1)} %shard_map.111.refs_2_), calls=%async_computation | async-start | bytes 1048576 | tf_op jit(solution)/shard_map/all_to_all | solution.py:780
  9.4 1.6 %shard_map.112.refs_0_ = bf16[384,256]{1,0:T(8,128)(2,1)} custom-call(bf16[2,128,1024]{2,1,0:T(8,128)(2,1)} %refs_0_.3, bf16[512,256]{1,0:T(8,128)(2,1)} %refs_1_.3, bf16[4,256,256]{2,1,0:T(8,128)(2,1)} %shard_map.111.refs_2_), custom_call_target="tpu_custom_call" | custom-call | tf_op jit(solution)/shard_map/pallas_call | solution.py:271
  11.0 0.1 stack.31.where_ref
  11.1 0.9 shard_map.113.own_ref.mine_ref
  12.0 0.1 collective-permute-start
  12.1 1.3 %collective-permute-done.core_ref = bf16[528,128]{1,0:T(8,128)(2,1)S(1)} collective-permute-done((bf16[528,128]{1,0:T(8,128)(2,1)S(1)}, bf16[528,128]{1,0:T(8,128)(2,1)S(1)}, u32[]{:S(2)}, u32[]{:S(2)}) %collective-permute-start) | collective-permute-done | bytes 135200 | tf_op jit(solution)/shard_map/ppermute | solution.py:14
  13.5 0.6 shard_map.114
  14.0 1.6 %collective-permute-start.1 = (bf16[544,128]{1,0:T(8,128)(2,1)S(1)}, bf16[544,128]{1,0:T(8,128)(2,1)S(1)}, u32[]{:S(2)}, u32[]{:S(2)}) collective-permute-start(bf16[544,128]{1,0:T(8,128)(2,1)S(1)} %shard_map.114), channel_id=1, source_target_pairs={{0,16},{8,24},{16,0},{24,8},{1,17},{9,25},{17,1},{25,9},{2,18},{10... | collective-permute-start | bytes 417800 | tf_op jit(solution)/shard_map/ppermute | solution.py:14
  15.6 2.9 %collective-permute-start.3 = (bf16[384,256]{1,0:T(8,128)(2,1)}, bf16[384,256]{1,0:T(8,128)(2,1)S(1)}, u32[]{:S(2)}, u32[]{:S(2)}) collective-permute-start(bf16[384,256]{1,0:T(8,128)(2,1)} %shard_map.112.refs_0_), channel_id=1, source_target_pairs={{0,2},{1,3},{2,0},{3,1},{4,6},{5,7},{6,4},{7,5},{8,10},{9,11},{10,... | collective-permute-start | bytes 589832 | tf_op jit(solution)/shard_map/ppermute | solution.py:14
  18.5 1.5 %collective-permute-start.4 = (bf16[384,256]{1,0:T(8,128)(2,1)}, bf16[384,256]{1,0:T(8,128)(2,1)}, u32[]{:S(2)}, u32[]{:S(2)}) collective-permute-start(bf16[384,256]{1,0:T(8,128)(2,1)} %shard_map.112.refs_0_), channel_id=1, source_target_pairs={{0,1},{1,0},{2,3},{3,2},{4,5},{5,4},{6,7},{7,6},{8,9},{9,8},{10,11... | collective-permute-start | bytes 589832 | tf_op jit(solution)/shard_map/ppermute | solution.py:14
  20.0 2.0 %shard_map.115 = (bf16[512,512]{1,0:T(8,128)(2,1)S(1)}, bf16[4,128,128]{2,1,0:T(8,128)(2,1)S(1)}) custom-call(s32[7]{0:T(128)S(1)} %stack.31.where_ref, bf16[512,512]{1,0:T(8,128)(2,1)S(1)} %bitcast.29, bf16[512,512]{1,0:T(8,128)(2,1)S(1)} %bitcast.20, bf16[512,512]{1,0:T(8,128)(2,1)S(1)} %bitcast.25, bf16[528,128]{1,0:T(8,128)(2,1)S(1)} %collective-permute-done.core_ref, ...), custom_call_target="tpu_custom_call" | custom-call | tf_op jit(solution)/shard_map/pallas_call | solution.py:234
  22.0 0.6 copy-done.4
  22.7 6.4 %all-to-all-done.ref = bf16[4,256,256]{2,1,0:T(8,128)(2,1)S(1)} async-done(((bf16[4,256,256]{2,1,0:T(8,128)(2,1)}), bf16[4,256,256]{2,1,0:T(8,128)(2,1)S(1)}, u32[]{:S(2)}, u32[]{:S(2)}) %all-to-all-start) | async-done | bytes 524320 | tf_op jit(solution)/shard_map/all_to_all | solution.py:780
  29.0 0.7 shard_map.116
  29.7 1.6 %collective-permute-start.2 = (bf16[1024,256]{1,0:T(8,128)(2,1)S(1)}, bf16[1024,256]{1,0:T(8,128)(2,1)S(1)}, u32[]{:S(2)}, u32[]{:S(2)}) collective-permute-start(bf16[1024,256]{1,0:T(8,128)(2,1)S(1)} %get-tuple-element.69.own_ref), channel_id=1, source_target_pairs={{0,4},{4,0},{1,5},{5,1},{2,6},{6,2},{3,7},{7,3},{8,12},{12,8},{9,1... | collective-permute-start | bytes 1572872 | tf_op jit(solution)/shard_map/ppermute | solution.py:14
  31.3 1.8 %collective-permute-start.6 = (bf16[368,256]{1,0:T(8,128)(2,1)S(1)}, bf16[368,256]{1,0:T(8,128)(2,1)S(1)}, u32[]{:S(2)}, u32[]{:S(2)}) collective-permute-start(bf16[368,256]{1,0:T(8,128)(2,1)S(1)} %get-tuple-element.70), channel_id=1, source_target_pairs={{0,16},{8,24},{16,0},{24,8},{1,17},{9,25},{17,1},{25,9},{2,18},{10... | collective-permute-start | bytes 565256 | tf_op jit(solution)/shard_map/ppermute | solution.py:14
  33.0 4.4 %collective-permute-done.3.refs_1_ = bf16[384,256]{1,0:T(8,128)(2,1)S(1)} collective-permute-done((bf16[384,256]{1,0:T(8,128)(2,1)}, bf16[384,256]{1,0:T(8,128)(2,1)S(1)}, u32[]{:S(2)}, u32[]{:S(2)}) %collective-permute-start.3) | collective-permute-done | bytes 196640 | tf_op jit(solution)/shard_map/ppermute | solution.py:14
  37.5 1.1 shard_map.117
  38.7 0.5 collective-permute-start.10
  39.2 1.1 collective-permute-done.7.head.got_head
  40.3 0.9 collective-permute-done.2.got_ref.refs_1_
  41.2 1.4 %shard_map.118 = (bf16[256,256]{1,0:T(8,128)(2,1)S(1)}, bf16[768,256]{1,0:T(8,128)(2,1)S(1)}, bf16[1168,256]{1,0:T(8,128)(2,1)S(1)}) custom-call(s32[7]{0:T(128)S(1)} %stack.31.where_ref, bf16[528,128]{1,0:T(8,128)(2,1)S(1)} %shard_map.113.own_ref.mine_ref, bf16[528,128]{1,0:T(8,128)(2,1)S(1)} %collective-permute-done.core_ref, ...), custom_call_target="tpu_custom_call" | custom-call | tf_op jit(solution)/shard_map/pallas_call | solution.py:234
  42.6 1.2 %collective-permute-start.8 = (bf16[1168,256]{1,0:T(8,128)(2,1)S(1)}, bf16[1168,256]{1,0:T(8,128)(2,1)S(1)}, u32[]{:S(2)}, u32[]{:S(2)}) collective-permute-start(bf16[1168,256]{1,0:T(8,128)(2,1)S(1)} %get-tuple-element.79), channel_id=1, source_target_pairs={{0,16},{8,24},{16,0},{24,8},{1,17},{9,25},{17,1},{25,9},{2,18},{10... | collective-permute-start | bytes 1794056 | tf_op jit(solution)/shard_map/ppermute | solution.py:14
  43.8 1.5 %collective-permute-start.9 = (bf16[512,256]{1,0:T(8,128)(2,1)S(1)}, bf16[512,256]{1,0:T(8,128)(2,1)S(1)}, u32[]{:S(2)}, u32[]{:S(2)}) collective-permute-start(bf16[512,256]{1,0:T(8,128)(2,1)S(1)} %get-tuple-element.76.own_ref), channel_id=1, source_target_pairs={{0,4},{4,0},{1,5},{5,1},{2,6},{6,2},{3,7},{7,3},{8,12},{12,8},{9,1... | collective-permute-start | bytes 786440 | tf_op jit(solution)/shard_map/ppermute | solution.py:14
  45.3 1.0 shard_map.119.part_ref
  46.3 0.8 shard_map.121
  47.2 0.6 collective-permute-start.12
  47.8 0.5 collective-permute-start.15
  48.3 0.8 shard_map.120.refs_13_
  49.1 3.9 %collective-permute-done.9.got_ref = bf16[512,256]{1,0:T(8,128)(2,1)S(1)} collective-permute-done((bf16[512,256]{1,0:T(8,128)(2,1)S(1)}, bf16[512,256]{1,0:T(8,128)(2,1)S(1)}, u32[]{:S(2)}, u32[]{:S(2)}) %collective-permute-start.9) | collective-permute-done | bytes 262176 | tf_op jit(solution)/shard_map/ppermute | solution.py:14
  53.1 1.4 %shard_map.122 = (bf16[256,256]{1,0:T(8,128)(2,1)S(1)}, bf16[256,256]{1,0:T(8,128)(2,1)S(1)}, bf16[512,256]{1,0:T(8,128)(2,1)S(1)}) custom-call(s32[7]{0:T(128)S(1)} %stack.31.where_ref, bf16[528,128]{1,0:T(8,128)(2,1)S(1)} %shard_map.113.own_ref.mine_ref, bf16[528,128]{1,0:T(8,128)(2,1)S(1)} %collective-permute-done.core_ref, ...), custom_call_target="tpu_custom_call" | custom-call | tf_op jit(solution)/shard_map/pallas_call | solution.py:234
  54.5 0.9 collective-permute-start.11
  55.4 1.4 %collective-permute-done.14.refs_6_ = bf16[368,256]{1,0:T(8,128)(2,1)S(1)} collective-permute-done((bf16[368,256]{1,0:T(8,128)(2,1)S(1)}, bf16[368,256]{1,0:T(8,128)(2,1)S(1)}, u32[]{:S(2)}, u32[]{:S(2)}) %collective-permute-start.14) | collective-permute-done | bytes 188448 | tf_op jit(solution)/shard_map/ppermute | solution.py:14
  56.8 6.1 %collective-permute-done.11.refs_10_ = bf16[512,256]{1,0:T(8,128)(2,1)S(1)} collective-permute-done((bf16[512,256]{1,0:T(8,128)(2,1)S(1)}, bf16[512,256]{1,0:T(8,128)(2,1)S(1)}, u32[]{:S(2)}, u32[]{:S(2)}) %collective-permute-start.11) | collective-permute-done | bytes 262176 | tf_op jit(solution)/shard_map/ppermute | solution.py:14
  63.0 0.5 collective-permute-start.18
  63.5 0.1 collective-permute-start.17
  63.6 1.3 %copy.12 = bf16[32,8,2,1024]{3,1,2,0:T(8,128)(2,1)} copy(bf16[32,8,2,1024]{3,2,1,0:T(2,128)(2,1)S(1)} %bitcast.34) | data formatting | bytes 2097152
  64.9 0.7 collective-permute-done.17.refs_11_
  65.6 4.3 %shard_map.123.own = bf16[256,1024]{1,0:T(8,128)(2,1)S(1)} custom-call(s32[7]{0:T(128)S(1)} %stack.31.where_ref, bf16[512,256]{1,0:T(8,128)(2,1)S(1)} %get-tuple-element.68.refs_0_, bf16[1024,256]{1,0:T(8,128)(2,1)S(1)} %collective-permute-done.2.got_ref.refs_1_, bf16[368,256]{1,0:T(8,128)(2,1)S(1)} %collective-permute-done.6.refs_2_, ...), custom_call_target="tpu_custom_call" | custom-call | tf_op jit(solution)/shard_map/pallas_call | solution.py:482
  69.9 1.6 %collective-permute-start.19 = (bf16[256,1024]{1,0:T(8,128)(2,1)S(1)}, bf16[256,1024]{1,0:T(8,128)(2,1)S(1)}, u32[]{:S(2)}, u32[]{:S(2)}) collective-permute-start(bf16[256,1024]{1,0:T(8,128)(2,1)S(1)} %shard_map.123.own), channel_id=1, source_target_pairs={{0,4},{4,0},{1,5},{5,1},{2,6},{6,2},{3,7},{7,3},{8,12},{12,8},{9,1... | collective-permute-start | bytes 1572872 | tf_op jit(solution)/shard_map/ppermute | solution.py:14
  71.4 12.5 %collective-permute-done.19.got = bf16[256,1024]{1,0:T(8,128)(2,1)S(1)} collective-permute-done((bf16[256,1024]{1,0:T(8,128)(2,1)S(1)}, bf16[256,1024]{1,0:T(8,128)(2,1)S(1)}, u32[]{:S(2)}, u32[]{:S(2)}) %collective-permute-start.19) | collective-permute-done | bytes 524320 | tf_op jit(solution)/shard_map/ppermute | solution.py:14
  83.9 1.3 %shard_map.124 = (bf16[2,128,1024]{2,1,0:T(8,128)(2,1)S(1)}, f32[2,128,1024]{2,1,0:T(8,128)S(1)}) custom-call(s32[7]{0:T(128)S(1)} %stack.31.where_ref, bf16[512,512]{1,0:T(8,128)(2,1)S(1)} %get-tuple-element.66.att, bf16[256,1024]{1,0:T(8,128)(2,1)S(1)} %shard_map.123.own, bf16[256,1024]{1,0:T(8,128)(2,1)S(1)} %collective-permute-done.19.got), custom_call_target="tpu_custom_call" | custom-call | tf_op jit(solution)/shard_map/pallas_call | solution.py:234
  85.3 1.6 %shard_map.126 = (bf16[512,512]{1,0:T(8,128)(2,1)S(1)}, bf16[4,128,128]{2,1,0:T(8,128)(2,1)S(1)}) custom-call(s32[7]{0:T(128)S(1)} %stack.31.where_ref, bf16[256,1024]{1,0:T(8,128)(2,1)S(1)} %shard_map.123.own, bf16[256,1024]{1,0:T(8,128)(2,1)S(1)} %collective-permute-done.19.got, bf16[160,1024]{1,0:T(8,128)(2,1)S(1)} %get-tuple-element.75.head_ref.head, ...), custom_call_target="tpu_custom_call" | custom-call | tf_op jit(solution)/shard_map/pallas_call | solution.py:234
  86.9 0.6 collective-permute-start.22
  87.5 0.6 shard_map.125
  88.1 1.6 %collective-permute-start.21 = (bf16[128,1024]{1,0:T(8,128)(2,1)S(1)}, bf16[128,1024]{1,0:T(8,128)(2,1)S(1)}, u32[]{:S(2)}, u32[]{:S(2)}) collective-permute-start(bf16[128,1024]{1,0:T(8,128)(2,1)S(1)} %get-tuple-element.97), channel_id=1, source_target_pairs={{0,16},{8,24},{16,0},{24,8},{1,17},{9,25},{17,1},{25,9},{2,18},{10... | collective-permute-start | bytes 786440 | tf_op jit(solution)/shard_map/ppermute | solution.py:14
  89.7 3.2 %shard_map.127 = (f32[512,512]{1,0:T(8,128)S(1)}, f32[512,512]{1,0:T(8,128)S(1)}) custom-call(s32[7]{0:T(128)S(1)} %stack.31.where_ref, bf16[512,512]{1,0:T(8,128)(2,1)S(1)} %get-tuple-element.98.g_ref, bf16[512,512]{1,0:T(8,128)(2,1)S(1)} %bitcast.31, bf16[512,512]{1,0:T(8,128)(2,1)S(1)} %bitcast.21, bf16[512,512]{1,0:T(8,128)(2,1)S(1)} %bitcast.26), custom_call_target="tpu_custom_call" | custom-call | tf_op jit(solution)/shard_map/pallas_call | solution.py:234
  92.9 2.7 %shard_map.128 = bf16[512,512]{1,0:T(8,128)(2,1)} custom-call(s32[7]{0:T(128)S(1)} %stack.31.where_ref, bf16[512,512]{1,0:T(8,128)(2,1)S(1)} %get-tuple-element.98.g_ref, bf16[512,512]{1,0:T(8,128)(2,1)S(1)} %bitcast.22, bf16[512,512]{1,0:T(8,128)(2,1)S(1)} %bitcast.27, bf16[4,128,128]{2,1,0:T(8,128)(2,1)S(1)} %copy-done.5), custom_call_target="tpu_custom_call" | custom-call | tf_op jit(solution)/shard_map/pallas_call | solution.py:234
  95.7 0.7 collective-permute-done.21.got_ref
  96.4 0.6 shard_map.129
  97.0 5.3 %collective-permute-start.23 = (bf16[128,256]{1,0:T(8,128)(2,1)S(1)}, bf16[128,256]{1,0:T(8,128)(2,1)S(1)}, u32[]{:S(2)}, u32[]{:S(2)}) collective-permute-start(bf16[128,256]{1,0:T(8,128)(2,1)S(1)} %get-tuple-element.109), channel_id=1, source_target_pairs={{0,3},{1,2},{2,1},{3,0},{4,7},{5,6},{6,5},{7,4},{8,11},{9,10},{10,... | collective-permute-start | bytes 196616 | tf_op jit(solution)/shard_map/ppermute | solution.py:14
  102.3 0.1 collective-permute-start.24
  102.4 1.7 %collective-permute-start.29 = (bf16[4,128,128]{2,1,0:T(8,128)(2,1)S(1)}, bf16[4,128,128]{2,1,0:T(8,128)(2,1)S(1)}, u32[]{:S(2)}, u32[]{:S(2)}) collective-permute-start(bf16[4,128,128]{2,1,0:T(8,128)(2,1)S(1)} %add_convert_fusion), channel_id=1, source_target_pairs={{0,16},{8,24},{16,0},{24,8},{1,17},{9,25},{17,1},{25,9},{2,18},{10... | collective-permute-start | bytes 393224 | tf_op jit(solution)/shard_map/ppermute | solution.py:14
  104.1 0.6 collective-permute-start.25
  104.8 3.0 %collective-permute-done.24.refs_1_ = bf16[128,256]{1,0:T(8,128)(2,1)S(1)} collective-permute-done((bf16[128,256]{1,0:T(8,128)(2,1)S(1)}, bf16[128,256]{1,0:T(8,128)(2,1)S(1)}, u32[]{:S(2)}, u32[]{:S(2)}) %collective-permute-start.24) | collective-permute-done | bytes 65568 | tf_op jit(solution)/shard_map/ppermute | solution.py:14
  107.8 0.7 collective-permute-done.25.refs_2_
  108.4 0.6 shard_map.130.refs_0_
  109.0 1.3 %collective-permute-start.26 = (bf16[128,256]{1,0:T(8,128)(2,1)S(1)}, bf16[128,256]{1,0:T(8,128)(2,1)S(1)}, u32[]{:S(2)}, u32[]{:S(2)}) collective-permute-start(bf16[128,256]{1,0:T(8,128)(2,1)S(1)} %shard_map.130.refs_0_), channel_id=1, source_target_pairs={{0,16},{8,24},{16,0},{24,8},{1,17},{9,25},{17,1},{25,9},{2,18},{10... | collective-permute-start | bytes 196616 | tf_op jit(solution)/shard_map/ppermute | solution.py:14
  110.4 0.9 collective-permute-start.28
  111.2 2.0 %shard_map.131 = (bf16[512,512]{1,0:T(8,128)(2,1)}, bf16[512,512]{1,0:T(8,128)(2,1)}) custom-call(s32[7]{0:T(128)S(1)} %stack.31.where_ref, f32[512,512]{1,0:T(8,128)S(1)} %get-tuple-element.113.kp_ref, f32[512,512]{1,0:T(8,128)S(1)} %get-tuple-element.114.vp_ref, bf16[512,512]{1,0:T(8,128)(2,1)S(1)} %bitcast.23, bf16[512,512]{1,0:T(8,128)(2,1)S(1)} %bitcast.28, ...), custom_call_target="tpu_custom_call" | custom-call | tf_op jit(solution)/shard_map/pallas_call | solution.py:234
  113.2 0.1 collective-permute-done.26.refs_1_
  113.4 0.8 collective-permute-done.28.refs_3_
  114.1 1.4 %shard_map.132 = f32[512,256]{1,0:T(8,128)} custom-call(s32[7]{0:T(128)S(1)} %stack.31.where_ref, bf16[128,256]{1,0:T(8,128)(2,1)S(1)} %shard_map.130.refs_0_, bf16[128,256]{1,0:T(8,128)(2,1)S(1)} %collective-permute-done.26.refs_1_, bf16[128,256]{1,0:T(8,128)(2,1)S(1)} %collective-permute-done.27.refs_2_, bf16[128,256]{1,0:T(8,128)(2,1)S(1)} %collective-permute-done.28.refs_3_), custom_call_target="tpu_custom_call" | custom-call | tf_op jit(solution)/shard_map/pallas_call | solution.py:234
  (39 shorter events, 0.4 us)
Async XLA Ops:
  0.6 10.5 %copy-start = (bf16[1,512,512]{2,1,0:T(8,128)(2,1)S(1)}, bf16[1,512,512]{2,1,0:T(8,128)(2,1)}, u32[]{:S(2)}) copy-start(bf16[1,512,512]{2,1,0:T(8,128)(2,1)} %param.9) | copy-start | bytes 1572868
  0.6 10.5 %copy-start.1 = (bf16[1,512,512]{2,1,0:T(8,128)(2,1)S(1)}, bf16[1,512,512]{2,1,0:T(8,128)(2,1)}, u32[]{:S(2)}) copy-start(bf16[1,512,512]{2,1,0:T(8,128)(2,1)} %param.10) | copy-start | bytes 1572868
  0.7 10.5 %copy-start.6 = (s32[1,256,2]{1,2,0:T(2,128)S(1)}, s32[1,256,2]{1,2,0:T(2,128)}, u32[]{:S(2)}) copy-start(s32[1,256,2]{1,2,0:T(2,128)} %param.14) | copy-start | bytes 6148
  2.9 17.1 %copy-start.2 = (bf16[1,512,512]{2,1,0:T(8,128)(2,1)S(1)}, bf16[1,512,512]{2,1,0:T(8,128)(2,1)}, u32[]{:S(2)}) copy-start(bf16[1,512,512]{2,1,0:T(8,128)(2,1)} %param.8) | copy-start | bytes 1572868
  2.9 26.1 %all-to-all-start = ((bf16[4,256,256]{2,1,0:T(8,128)(2,1)}), bf16[4,256,256]{2,1,0:T(8,128)(2,1)S(1)}, u32[]{:S(2)}, u32[]{:S(2)}) async-start(bf16[4,256,256]{2,1,0:T(8,128)(2,1)} %shard_map.111.refs_2_), calls=%async_computation | async-start | bytes 1048576 | tf_op jit(solution)/shard_map/all_to_all | solution.py:780
  11.0 26.5 %copy-start.3 = (bf16[384,256]{1,0:T(8,128)(2,1)S(1)}, bf16[384,256]{1,0:T(8,128)(2,1)}, u32[]{:S(2)}) copy-start(bf16[384,256]{1,0:T(8,128)(2,1)} %shard_map.112.refs_0_) | copy-start | bytes 589828
  12.0 1.4 %collective-permute-start = (bf16[528,128]{1,0:T(8,128)(2,1)S(1)}, bf16[528,128]{1,0:T(8,128)(2,1)S(1)}, u32[]{:S(2)}, u32[]{:S(2)}) collective-permute-start(bf16[528,128]{1,0:T(8,128)(2,1)S(1)} %shard_map.113.own_ref.mine_ref), channel_id=1, source_target_pairs={{0,8},{8,0},{16,24},{24,16},{1,9},{9,1},{17,25},{25,17},{2,10},{10... | collective-permute-start | bytes 405512 | tf_op jit(solution)/shard_map/ppermute | solution.py:14
  14.0 6.0 %collective-permute-start.1 = (bf16[544,128]{1,0:T(8,128)(2,1)S(1)}, bf16[544,128]{1,0:T(8,128)(2,1)S(1)}, u32[]{:S(2)}, u32[]{:S(2)}) collective-permute-start(bf16[544,128]{1,0:T(8,128)(2,1)S(1)} %shard_map.114), channel_id=1, source_target_pairs={{0,16},{8,24},{16,0},{24,8},{1,17},{9,25},{17,1},{25,9},{2,18},{10... | collective-permute-start | bytes 417800 | tf_op jit(solution)/shard_map/ppermute | solution.py:14
  15.6 21.8 %collective-permute-start.3 = (bf16[384,256]{1,0:T(8,128)(2,1)}, bf16[384,256]{1,0:T(8,128)(2,1)S(1)}, u32[]{:S(2)}, u32[]{:S(2)}) collective-permute-start(bf16[384,256]{1,0:T(8,128)(2,1)} %shard_map.112.refs_0_), channel_id=1, source_target_pairs={{0,2},{1,3},{2,0},{3,1},{4,6},{5,7},{6,4},{7,5},{8,10},{9,11},{10,... | collective-permute-start | bytes 589832 | tf_op jit(solution)/shard_map/ppermute | solution.py:14
  18.5 18.9 %collective-permute-start.4 = (bf16[384,256]{1,0:T(8,128)(2,1)}, bf16[384,256]{1,0:T(8,128)(2,1)}, u32[]{:S(2)}, u32[]{:S(2)}) collective-permute-start(bf16[384,256]{1,0:T(8,128)(2,1)} %shard_map.112.refs_0_), channel_id=1, source_target_pairs={{0,1},{1,0},{2,3},{3,2},{4,5},{5,4},{6,7},{7,6},{8,9},{9,8},{10,11... | collective-permute-start | bytes 589832 | tf_op jit(solution)/shard_map/ppermute | solution.py:14
  20.0 17.5 %collective-permute-start.5 = (bf16[384,256]{1,0:T(8,128)(2,1)}, bf16[384,256]{1,0:T(8,128)(2,1)}, u32[]{:S(2)}, u32[]{:S(2)}) collective-permute-start(bf16[384,256]{1,0:T(8,128)(2,1)} %shard_map.112.refs_0_), channel_id=1, source_target_pairs={{0,3},{1,2},{2,1},{3,0},{4,7},{5,6},{6,5},{7,4},{8,11},{9,10},{10,... | collective-permute-start | bytes 589832 | tf_op jit(solution)/shard_map/ppermute | solution.py:14
  22.0 0.7 copy-start.4
  29.7 11.5 %collective-permute-start.2 = (bf16[1024,256]{1,0:T(8,128)(2,1)S(1)}, bf16[1024,256]{1,0:T(8,128)(2,1)S(1)}, u32[]{:S(2)}, u32[]{:S(2)}) collective-permute-start(bf16[1024,256]{1,0:T(8,128)(2,1)S(1)} %get-tuple-element.69.own_ref), channel_id=1, source_target_pairs={{0,4},{4,0},{1,5},{5,1},{2,6},{6,2},{3,7},{7,3},{8,12},{12,8},{9,1... | collective-permute-start | bytes 1572872 | tf_op jit(solution)/shard_map/ppermute | solution.py:14
  31.3 6.2 %collective-permute-start.6 = (bf16[368,256]{1,0:T(8,128)(2,1)S(1)}, bf16[368,256]{1,0:T(8,128)(2,1)S(1)}, u32[]{:S(2)}, u32[]{:S(2)}) collective-permute-start(bf16[368,256]{1,0:T(8,128)(2,1)S(1)} %get-tuple-element.70), channel_id=1, source_target_pairs={{0,16},{8,24},{16,0},{24,8},{1,17},{9,25},{17,1},{25,9},{2,18},{10... | collective-permute-start | bytes 565256 | tf_op jit(solution)/shard_map/ppermute | solution.py:14
  38.6 1.7 %collective-permute-start.7 = (bf16[160,1024]{1,0:T(8,128)(2,1)S(1)}, bf16[160,1024]{1,0:T(8,128)(2,1)S(1)}, u32[]{:S(2)}, u32[]{:S(2)}) collective-permute-start(bf16[160,1024]{1,0:T(8,128)(2,1)S(1)} %get-tuple-element.75.head_ref.head), channel_id=1, source_target_pairs={{0,8},{8,0},{16,24},{24,16},{1,9},{9,1},{17,25},{25,17},{2,10},{10... | collective-permute-start | bytes 983048 | tf_op jit(solution)/shard_map/ppermute | solution.py:14
  38.7 7.6 %collective-permute-start.10 = (bf16[96,1024]{1,0:T(8,128)(2,1)S(1)}, bf16[96,1024]{1,0:T(8,128)(2,1)S(1)}, u32[]{:S(2)}, u32[]{:S(2)}) collective-permute-start(bf16[96,1024]{1,0:T(8,128)(2,1)S(1)} %get-tuple-element.80.tail_ref.tail), channel_id=1, source_target_pairs={{0,8},{8,0},{16,24},{24,16},{1,9},{9,1},{17,25},{25,17},{2,10},{10... | collective-permute-start | bytes 589832 | tf_op jit(solution)/shard_map/ppermute | solution.py:14
  42.6 20.3 %collective-permute-start.8 = (bf16[1168,256]{1,0:T(8,128)(2,1)S(1)}, bf16[1168,256]{1,0:T(8,128)(2,1)S(1)}, u32[]{:S(2)}, u32[]{:S(2)}) collective-permute-start(bf16[1168,256]{1,0:T(8,128)(2,1)S(1)} %get-tuple-element.79), channel_id=1, source_target_pairs={{0,16},{8,24},{16,0},{24,8},{1,17},{9,25},{17,1},{25,9},{2,18},{10... | collective-permute-start | bytes 1794056 | tf_op jit(solution)/shard_map/ppermute | solution.py:14
  43.8 9.2 %collective-permute-start.9 = (bf16[512,256]{1,0:T(8,128)(2,1)S(1)}, bf16[512,256]{1,0:T(8,128)(2,1)S(1)}, u32[]{:S(2)}, u32[]{:S(2)}) collective-permute-start(bf16[512,256]{1,0:T(8,128)(2,1)S(1)} %get-tuple-element.76.own_ref), channel_id=1, source_target_pairs={{0,4},{4,0},{1,5},{5,1},{2,6},{6,2},{3,7},{7,3},{8,12},{12,8},{9,1... | collective-permute-start | bytes 786440 | tf_op jit(solution)/shard_map/ppermute | solution.py:14
  47.2 15.8 %collective-permute-start.12 = (bf16[256,1024]{1,0:T(8,128)(2,1)S(1)}, bf16[256,1024]{1,0:T(8,128)(2,1)S(1)}, u32[]{:S(2)}, u32[]{:S(2)}) collective-permute-start(bf16[256,1024]{1,0:T(8,128)(2,1)S(1)} %shard_map.121), channel_id=1, source_target_pairs={{0,4},{4,0},{1,5},{5,1},{2,6},{6,2},{3,7},{7,3},{8,12},{12,8},{9,1... | collective-permute-start | bytes 1572872 | tf_op jit(solution)/shard_map/ppermute | solution.py:14
  47.8 7.6 %collective-permute-start.13 = (bf16[512,256]{1,0:T(8,128)(2,1)S(1)}, bf16[512,256]{1,0:T(8,128)(2,1)S(1)}, u32[]{:S(2)}, u32[]{:S(2)}) collective-permute-start(bf16[512,256]{1,0:T(8,128)(2,1)S(1)} %get-tuple-element.68.refs_0_), channel_id=1, source_target_pairs={{0,8},{8,0},{16,24},{24,16},{1,9},{9,1},{17,25},{25,17},{2,10},{10... | collective-permute-start | bytes 786440 | tf_op jit(solution)/shard_map/ppermute | solution.py:14
  47.8 15.8 %copy-start.7 = (bf16[1,256,2,1024]{3,2,1,0:T(2,128)(2,1)S(1)}, bf16[1,256,2,1024]{3,2,1,0:T(2,128)(2,1)}, u32[]{:S(2)}) copy-start(bf16[1,256,2,1024]{3,2,1,0:T(2,128)(2,1)} %param.15) | copy-start | bytes 3145732
  47.8 15.2 %collective-permute-start.15 = (bf16[768,256]{1,0:T(8,128)(2,1)S(1)}, bf16[768,256]{1,0:T(8,128)(2,1)S(1)}, u32[]{:S(2)}, u32[]{:S(2)}) collective-permute-start(bf16[768,256]{1,0:T(8,128)(2,1)S(1)} %get-tuple-element.85), channel_id=1, source_target_pairs={{0,8},{8,0},{16,24},{24,16},{1,9},{9,1},{17,25},{25,17},{2,10},{10... | collective-permute-start | bytes 1179656 | tf_op jit(solution)/shard_map/ppermute | solution.py:14
  54.5 8.5 %collective-permute-start.11 = (bf16[512,256]{1,0:T(8,128)(2,1)S(1)}, bf16[512,256]{1,0:T(8,128)(2,1)S(1)}, u32[]{:S(2)}, u32[]{:S(2)}) collective-permute-start(bf16[512,256]{1,0:T(8,128)(2,1)S(1)} %get-tuple-element.84), channel_id=1, source_target_pairs={{0,16},{8,24},{16,0},{24,8},{1,17},{9,25},{17,1},{25,9},{2,18},{10... | collective-permute-start | bytes 786440 | tf_op jit(solution)/shard_map/ppermute | solution.py:14
  55.4 1.4 %collective-permute-start.14 = (bf16[368,256]{1,0:T(8,128)(2,1)S(1)}, bf16[368,256]{1,0:T(8,128)(2,1)S(1)}, u32[]{:S(2)}, u32[]{:S(2)}) collective-permute-start(bf16[368,256]{1,0:T(8,128)(2,1)S(1)} %collective-permute-done.6.refs_2_), channel_id=1, source_target_pairs={{0,8},{8,0},{16,24},{24,16},{1,9},{9,1},{17,25},{25,17},{2,10},{10... | collective-permute-start | bytes 565256 | tf_op jit(solution)/shard_map/ppermute | solution.py:14
  63.0 2.6 %collective-permute-start.16 = (bf16[1168,256]{1,0:T(8,128)(2,1)S(1)}, bf16[1168,256]{1,0:T(8,128)(2,1)S(1)}, u32[]{:S(2)}, u32[]{:S(2)}) collective-permute-start(bf16[1168,256]{1,0:T(8,128)(2,1)S(1)} %collective-permute-done.8.refs_3_), channel_id=1, source_target_pairs={{0,8},{8,0},{16,24},{24,16},{1,9},{9,1},{17,25},{25,17},{2,10},{10... | collective-permute-start | bytes 1794056 | tf_op jit(solution)/shard_map/ppermute | solution.py:14
  63.0 2.6 %collective-permute-start.18 = (bf16[512,256]{1,0:T(8,128)(2,1)S(1)}, bf16[512,256]{1,0:T(8,128)(2,1)S(1)}, u32[]{:S(2)}, u32[]{:S(2)}) collective-permute-start(bf16[512,256]{1,0:T(8,128)(2,1)S(1)} %collective-permute-done.11.refs_10_), channel_id=1, source_target_pairs={{0,8},{8,0},{16,24},{24,16},{1,9},{9,1},{17,25},{25,17},{2,10},{10... | collective-permute-start | bytes 786440 | tf_op jit(solution)/shard_map/ppermute | solution.py:14
  63.5 2.1 %collective-permute-start.17 = (bf16[256,256]{1,0:T(8,128)(2,1)S(1)}, bf16[256,256]{1,0:T(8,128)(2,1)S(1)}, u32[]{:S(2)}, u32[]{:S(2)}) collective-permute-start(bf16[256,256]{1,0:T(8,128)(2,1)S(1)} %get-tuple-element.93), channel_id=1, source_target_pairs={{0,8},{8,0},{16,24},{24,16},{1,9},{9,1},{17,25},{25,17},{2,10},{10... | collective-permute-start | bytes 393224 | tf_op jit(solution)/shard_map/ppermute | solution.py:14
  69.9 14.0 %collective-permute-start.19 = (bf16[256,1024]{1,0:T(8,128)(2,1)S(1)}, bf16[256,1024]{1,0:T(8,128)(2,1)S(1)}, u32[]{:S(2)}, u32[]{:S(2)}) collective-permute-start(bf16[256,1024]{1,0:T(8,128)(2,1)S(1)} %shard_map.123.own), channel_id=1, source_target_pairs={{0,4},{4,0},{1,5},{5,1},{2,6},{6,2},{3,7},{7,3},{8,12},{12,8},{9,1... | collective-permute-start | bytes 1572872 | tf_op jit(solution)/shard_map/ppermute | solution.py:14
  85.2 2.3 %collective-permute-start.20 = (bf16[2,128,1024]{2,1,0:T(8,128)(2,1)S(1)}, bf16[2,128,1024]{2,1,0:T(8,128)(2,1)S(1)}, u32[]{:S(2)}, u32[]{:S(2)}) collective-permute-start(bf16[2,128,1024]{2,1,0:T(8,128)(2,1)S(1)} %get-tuple-element.96), channel_id=1, source_target_pairs={{0,8},{8,0},{16,24},{24,16},{1,9},{9,1},{17,25},{25,17},{2,10},{10... | collective-permute-start | bytes 1572872 | tf_op jit(solution)/shard_map/ppermute | solution.py:14
  86.9 6.0 %copy-start.5 = (bf16[4,128,128]{2,1,0:T(8,128)(2,1)S(1)}, bf16[4,128,128]{2,1,0:T(8,128)(2,1)}, u32[]{:S(2)}) copy-start(bf16[4,128,128]{2,1,0:T(8,128)(2,1)} %copy-done.4) | copy-start | bytes 393220
  86.9 8.7 %collective-permute-start.22 = (bf16[4,128,128]{2,1,0:T(8,128)(2,1)S(1)}, bf16[4,128,128]{2,1,0:T(8,128)(2,1)S(1)}, u32[]{:S(2)}, u32[]{:S(2)}) collective-permute-start(bf16[4,128,128]{2,1,0:T(8,128)(2,1)S(1)} %get-tuple-element.102), channel_id=1, source_target_pairs={{0,8},{8,0},{16,24},{24,16},{1,9},{9,1},{17,25},{25,17},{2,10},{10... | collective-permute-start | bytes 393224 | tf_op jit(solution)/shard_map/ppermute | solution.py:14
  88.1 8.3 %collective-permute-start.21 = (bf16[128,1024]{1,0:T(8,128)(2,1)S(1)}, bf16[128,1024]{1,0:T(8,128)(2,1)S(1)}, u32[]{:S(2)}, u32[]{:S(2)}) collective-permute-start(bf16[128,1024]{1,0:T(8,128)(2,1)S(1)} %get-tuple-element.97), channel_id=1, source_target_pairs={{0,16},{8,24},{16,0},{24,8},{1,17},{9,25},{17,1},{25,9},{2,18},{10... | collective-permute-start | bytes 786440 | tf_op jit(solution)/shard_map/ppermute | solution.py:14
  97.0 7.7 %collective-permute-start.23 = (bf16[128,256]{1,0:T(8,128)(2,1)S(1)}, bf16[128,256]{1,0:T(8,128)(2,1)S(1)}, u32[]{:S(2)}, u32[]{:S(2)}) collective-permute-start(bf16[128,256]{1,0:T(8,128)(2,1)S(1)} %get-tuple-element.109), channel_id=1, source_target_pairs={{0,3},{1,2},{2,1},{3,0},{4,7},{5,6},{6,5},{7,4},{8,11},{9,10},{10,... | collective-permute-start | bytes 196616 | tf_op jit(solution)/shard_map/ppermute | solution.py:14
  102.3 5.4 %collective-permute-start.24 = (bf16[128,256]{1,0:T(8,128)(2,1)S(1)}, bf16[128,256]{1,0:T(8,128)(2,1)S(1)}, u32[]{:S(2)}, u32[]{:S(2)}) collective-permute-start(bf16[128,256]{1,0:T(8,128)(2,1)S(1)} %get-tuple-element.110), channel_id=1, source_target_pairs={{0,2},{1,3},{2,0},{3,1},{4,6},{5,7},{6,4},{7,5},{8,10},{9,11},{10,... | collective-permute-start | bytes 196616 | tf_op jit(solution)/shard_map/ppermute | solution.py:14
  102.4 8.9 %collective-permute-start.29 = (bf16[4,128,128]{2,1,0:T(8,128)(2,1)S(1)}, bf16[4,128,128]{2,1,0:T(8,128)(2,1)S(1)}, u32[]{:S(2)}, u32[]{:S(2)}) collective-permute-start(bf16[4,128,128]{2,1,0:T(8,128)(2,1)S(1)} %add_convert_fusion), channel_id=1, source_target_pairs={{0,16},{8,24},{16,0},{24,8},{1,17},{9,25},{17,1},{25,9},{2,18},{10... | collective-permute-start | bytes 393224 | tf_op jit(solution)/shard_map/ppermute | solution.py:14
  104.1 4.4 %collective-permute-start.25 = (bf16[128,256]{1,0:T(8,128)(2,1)S(1)}, bf16[128,256]{1,0:T(8,128)(2,1)S(1)}, u32[]{:S(2)}, u32[]{:S(2)}) collective-permute-start(bf16[128,256]{1,0:T(8,128)(2,1)S(1)} %get-tuple-element.111), channel_id=1, source_target_pairs={{0,1},{1,0},{2,3},{3,2},{4,5},{5,4},{6,7},{7,6},{8,9},{9,8},{10,11... | collective-permute-start | bytes 196616 | tf_op jit(solution)/shard_map/ppermute | solution.py:14
  109.0 4.3 %collective-permute-start.26 = (bf16[128,256]{1,0:T(8,128)(2,1)S(1)}, bf16[128,256]{1,0:T(8,128)(2,1)S(1)}, u32[]{:S(2)}, u32[]{:S(2)}) collective-permute-start(bf16[128,256]{1,0:T(8,128)(2,1)S(1)} %shard_map.130.refs_0_), channel_id=1, source_target_pairs={{0,16},{8,24},{16,0},{24,8},{1,17},{9,25},{17,1},{25,9},{2,18},{10... | collective-permute-start | bytes 196616 | tf_op jit(solution)/shard_map/ppermute | solution.py:14
  110.4 3.0 %collective-permute-start.27 = (bf16[128,256]{1,0:T(8,128)(2,1)S(1)}, bf16[128,256]{1,0:T(8,128)(2,1)S(1)}, u32[]{:S(2)}, u32[]{:S(2)}) collective-permute-start(bf16[128,256]{1,0:T(8,128)(2,1)S(1)} %shard_map.130.refs_0_), channel_id=1, source_target_pairs={{0,8},{8,0},{16,24},{24,16},{1,9},{9,1},{17,25},{25,17},{2,10},{10... | collective-permute-start | bytes 196616 | tf_op jit(solution)/shard_map/ppermute | solution.py:14
  110.4 3.7 %collective-permute-start.28 = (bf16[128,256]{1,0:T(8,128)(2,1)S(1)}, bf16[128,256]{1,0:T(8,128)(2,1)S(1)}, u32[]{:S(2)}, u32[]{:S(2)}) collective-permute-start(bf16[128,256]{1,0:T(8,128)(2,1)S(1)} %shard_map.130.refs_0_), channel_id=1, source_target_pairs={{0,24},{8,16},{16,8},{24,0},{1,25},{9,17},{17,9},{25,1},{2,26},{10... | collective-permute-start | bytes 196616 | tf_op jit(solution)/shard_map/ppermute | solution.py:14

commit v5 on v4

--- a/solution.py
+++ b/solution.py
@@ -281,23 +281,26 @@
     t_rows, t_cols = code_table.shape[1], code_table.shape[2] // 4
     d_half, d_cols = depth_proj.shape[0] // 8, depth_proj.shape[1]
 
-    def views(refs):
-        if refs is None:
-            return [0] * (3 * n_dp)
-        table, depth, lanes = refs
-        found = []
-        for k in range(n_dp):
-            found.append((table.at[0, :, at(own_lane(), t_cols)], lanes.at[k, 0:t_rows]))
-            for half in range(2):
-                found.append(
-                    (
-                        depth.at[at(2 * own_lane() + half, d_half)],
-                        lanes.at[k, t_rows:t_rows + d_half, half * d_cols:(half + 1) * d_cols],
-                    )
-                )
-        return found
-
-    return copies(views, shaped((n_dp, t_rows + d_half, t_cols)), [code_table, depth_proj])
+    def body(table, depth, lanes, sems):
+        moves = [(table.at[0, :, at(own_lane(), t_cols)], lanes.at[0, 0:t_rows])]
+        for half in range(2):
+            cols = slice(half * d_cols, (half + 1) * d_cols)
+            moves.append((depth.at[at(2 * own_lane() + half, d_half)], lanes.at[0, t_rows:t_rows + d_half, cols]))
+        going = [pltpu.make_async_copy(src, dst, sems.at[i]) for i, (src, dst) in enumerate(moves)]
+        for copy in going:
+            copy.start()
+        for copy in going:
+            copy.wait()
+        for k in range(1, n_dp):
+            lanes[k] = lanes[0]
+
+    return pl.pallas_call(
+        body,
+        out_shape=shaped((n_dp, t_rows + d_half, t_cols)),
+        in_specs=[pl.BlockSpec(memory_space=pl.ANY)] * 2,
+        out_specs=pl.BlockSpec(memory_space=pltpu.VMEM),
+        scratch_shapes=[pltpu.SemaphoreType.DMA((3,))],
+    )(code_table, depth_proj)
 
 
 def second_lanes(code_table, out_proj, after):
@@ -806,13 +809,14 @@
     got_1 = swap(part_1, "head", 1)
 
     mixed_part = mix_own(where, attended, out_head, out_tail)
-    got_0, got_head, _ = lax.optimization_barrier((got_0, got_head, part_1))
+    got_0, got_head, _, _ = lax.optimization_barrier((got_0, got_head, part_1, mixed_part))
     own_0, to_core, to_far = embed(where, packed, top, 0, 2, tokens, part_0, got_0, half, n_dp, late)
     far_0 = far_swap(to_far)
 
     got_tail, _ = lax.optimization_barrier((got_tail, to_far))
     mixed_send = mix(where, attended, mixed_part, got_head, got_tail, True)
     mixed_got = swap(mixed_send, "head", 1)
+    mixed_part, got_1 = lax.optimization_barrier((mixed_part, got_1))
     mixed = mix(where, attended, mixed_part, got_head, got_tail, False)
     core_0 = core_swap(to_core)
 
@@ -842,6 +846,7 @@
     send, keep = add_core(where, keep, core_swap(send))
     from_far = far_swap(send)
     grad_rows, back = grad_attend(where, grad_mixed, grad_got, out_head, out_tail, got_head, got_tail, queries)
+    back, send = lax.optimization_barrier((back, send))
     back_core = core_swap(back)
     back_chip = (back.astype(F32) + back_core.astype(F32)).astype(BF16)
     key_part, value_part = key_value_parts(where, grad_rows, queries, keys, values)

time: 116 us -> 116 us (level)
  waiting for transfers between devices: 44.2 us -> 45.4 us
    pallas_call x2 -> x1, Pallas kernels: 3.88 us -> 1.64 us  [copies(): pl.pallas_call(body, out_shape=outs, in_specs=[anywhere] * len(args), out...]
    pallas_call x0 -> x1, Pallas kernels: none -> 1.79 us  [first_lanes(): pl.pallas_call(body, out_shape=shaped((n_dp, t_rows + d_half, t_cols)), i...]
  transfers between devices with their start and end apart: 31 -> 31, of which waited for: 16 -> 17; matrix products, arithmetic and copies ran while one was open for 1% -> 1% of each run, Pallas kernels for 20% -> 19%
where the time goes in v5:
time: 116 us
  waiting for transfers between devices  45.4 us (39%)
  starting transfers between devices  35 us (30%)
  Pallas kernels  32.4 us (28%)
  local copies, waits for them, and re-layouts  2.05 us (2%)
    ppermute x30, waiting for transfers between devices, swap(): lax.ppermute(block, axis, [(i, i ^ mask) for i in range(lax.axis_size(axi...  38.9 us
    ppermute x30, starting transfers between devices, swap(): lax.ppermute(block, axis, [(i, i ^ mask) for i in range(lax.axis_size(axi...  28.5 us
    pallas_call x19, Pallas kernels, run(): pl.pallas_call(body, out_shape=outs, in_specs=[pl.BlockSpec(memory_space=...  24.7 us
    all_to_all x1, waiting for transfers between devices, on_device(): pieces_0 = lax.all_to_all(lanes_0, 'dp', 0, 0)  6.48 us
    all_to_all x1, starting transfers between devices, on_device(): pieces_0 = lax.all_to_all(lanes_0, 'dp', 0, 0)  6.46 us
    pallas_call x1, Pallas kernels, depth_grad(): pl.pallas_call(body, out_shape=shaped((tokens, width)), in_specs=[pl.Bloc...  4.27 us
  transfers between devices with their start and end apart: 31, of which 17 were waited for; matrix products, arithmetic and copies ran while one was open for 1% of the time, Pallas kernels for 19%

profile of v5, /device:TPU:0, one launch (start us, length us, event | category | flops | bytes accessed | tf_op | source)
XLA Modules:
  0.0 115.7 jit_solution(5696421499544641903)
XLA Ops:
  0.7 1.8 %shard_map.111.refs_2_ = bf16[4,256,256]{2,1,0:T(8,128)(2,1)} custom-call(bf16[2,128,1024]{2,1,0:T(8,128)(2,1)} %refs_0_.1, bf16[1024,128]{1,0:T(8,128)(2,1)} %depth.1), custom_call_target="tpu_custom_call" | custom-call | tf_op jit(solution)/shard_map/pallas_call | solution.py:297
  2.5 6.5 %all-to-all-start = ((bf16[4,256,256]{2,1,0:T(8,128)(2,1)}), bf16[4,256,256]{2,1,0:T(8,128)(2,1)S(1)}, u32[]{:S(2)}, u32[]{:S(2)}) async-start(bf16[4,256,256]{2,1,0:T(8,128)(2,1)} %shard_map.111.refs_2_), calls=%async_computation | async-start | bytes 1048576 | tf_op jit(solution)/shard_map/all_to_all | solution.py:783
  8.9 1.6 %shard_map.112.refs_0_ = bf16[384,256]{1,0:T(8,128)(2,1)} custom-call(bf16[2,128,1024]{2,1,0:T(8,128)(2,1)} %refs_0_.1, bf16[512,256]{1,0:T(8,128)(2,1)} %refs_1_.1, bf16[4,256,256]{2,1,0:T(8,128)(2,1)} %shard_map.111.refs_2_), custom_call_target="tpu_custom_call" | custom-call | tf_op jit(solution)/shard_map/pallas_call | solution.py:271
  10.6 0.1 stack.31.where_ref
  10.7 0.9 shard_map.113.own_ref.mine_ref
  11.7 1.3 %collective-permute-done.core_ref = bf16[528,128]{1,0:T(8,128)(2,1)S(1)} collective-permute-done((bf16[528,128]{1,0:T(8,128)(2,1)S(1)}, bf16[528,128]{1,0:T(8,128)(2,1)S(1)}, u32[]{:S(2)}, u32[]{:S(2)}) %collective-permute-start) | collective-permute-done | bytes 135200 | tf_op jit(solution)/shard_map/ppermute | solution.py:14
  13.0 0.6 shard_map.114
  13.6 1.6 %collective-permute-start.1 = (bf16[544,128]{1,0:T(8,128)(2,1)S(1)}, bf16[544,128]{1,0:T(8,128)(2,1)S(1)}, u32[]{:S(2)}, u32[]{:S(2)}) collective-permute-start(bf16[544,128]{1,0:T(8,128)(2,1)S(1)} %shard_map.114), channel_id=1, source_target_pairs={{0,16},{8,24},{16,0},{24,8},{1,17},{9,25},{17,1},{25,9},{2,18},{10... | collective-permute-start | bytes 417800 | tf_op jit(solution)/shard_map/ppermute | solution.py:14
  15.2 2.9 %collective-permute-start.3 = (bf16[384,256]{1,0:T(8,128)(2,1)}, bf16[384,256]{1,0:T(8,128)(2,1)S(1)}, u32[]{:S(2)}, u32[]{:S(2)}) collective-permute-start(bf16[384,256]{1,0:T(8,128)(2,1)} %shard_map.112.refs_0_), channel_id=1, source_target_pairs={{0,2},{1,3},{2,0},{3,1},{4,6},{5,7},{6,4},{7,5},{8,10},{9,11},{10,... | collective-permute-start | bytes 589832 | tf_op jit(solution)/shard_map/ppermute | solution.py:14
  18.1 1.5 %collective-permute-start.4 = (bf16[384,256]{1,0:T(8,128)(2,1)}, bf16[384,256]{1,0:T(8,128)(2,1)}, u32[]{:S(2)}, u32[]{:S(2)}) collective-permute-start(bf16[384,256]{1,0:T(8,128)(2,1)} %shard_map.112.refs_0_), channel_id=1, source_target_pairs={{0,1},{1,0},{2,3},{3,2},{4,5},{5,4},{6,7},{7,6},{8,9},{9,8},{10,11... | collective-permute-start | bytes 589832 | tf_op jit(solution)/shard_map/ppermute | solution.py:14
  19.6 2.0 %shard_map.115 = (bf16[512,512]{1,0:T(8,128)(2,1)S(1)}, bf16[4,128,128]{2,1,0:T(8,128)(2,1)S(1)}) custom-call(s32[7]{0:T(128)S(1)} %stack.31.where_ref, bf16[512,512]{1,0:T(8,128)(2,1)S(1)} %bitcast.29, bf16[512,512]{1,0:T(8,128)(2,1)S(1)} %bitcast.20, bf16[512,512]{1,0:T(8,128)(2,1)S(1)} %bitcast.25, bf16[528,128]{1,0:T(8,128)(2,1)S(1)} %collective-permute-done.core_ref, ...), custom_call_target="tpu_custom_call" | custom-call | tf_op jit(solution)/shard_map/pallas_call | solution.py:234
  21.6 0.6 copy-done.4
  22.2 6.5 %all-to-all-done.ref = bf16[4,256,256]{2,1,0:T(8,128)(2,1)S(1)} async-done(((bf16[4,256,256]{2,1,0:T(8,128)(2,1)}), bf16[4,256,256]{2,1,0:T(8,128)(2,1)S(1)}, u32[]{:S(2)}, u32[]{:S(2)}) %all-to-all-start) | async-done | bytes 524320 | tf_op jit(solution)/shard_map/all_to_all | solution.py:783
  28.7 0.7 shard_map.116
  29.3 1.6 %collective-permute-start.2 = (bf16[1024,256]{1,0:T(8,128)(2,1)S(1)}, bf16[1024,256]{1,0:T(8,128)(2,1)S(1)}, u32[]{:S(2)}, u32[]{:S(2)}) collective-permute-start(bf16[1024,256]{1,0:T(8,128)(2,1)S(1)} %get-tuple-element.72.own_ref), channel_id=1, source_target_pairs={{0,4},{4,0},{1,5},{5,1},{2,6},{6,2},{3,7},{7,3},{8,12},{12,8},{9,1... | collective-permute-start | bytes 1572872 | tf_op jit(solution)/shard_map/ppermute | solution.py:14
  30.9 1.6 %collective-permute-start.6 = (bf16[368,256]{1,0:T(8,128)(2,1)S(1)}, bf16[368,256]{1,0:T(8,128)(2,1)S(1)}, u32[]{:S(2)}, u32[]{:S(2)}) collective-permute-start(bf16[368,256]{1,0:T(8,128)(2,1)S(1)} %get-tuple-element.73), channel_id=1, source_target_pairs={{0,16},{8,24},{16,0},{24,8},{1,17},{9,25},{17,1},{25,9},{2,18},{10... | collective-permute-start | bytes 565256 | tf_op jit(solution)/shard_map/ppermute | solution.py:14
  32.5 4.6 %collective-permute-done.3.refs_1_ = bf16[384,256]{1,0:T(8,128)(2,1)S(1)} collective-permute-done((bf16[384,256]{1,0:T(8,128)(2,1)}, bf16[384,256]{1,0:T(8,128)(2,1)S(1)}, u32[]{:S(2)}, u32[]{:S(2)}) %collective-permute-start.3) | collective-permute-done | bytes 196640 | tf_op jit(solution)/shard_map/ppermute | solution.py:14
  37.1 1.1 shard_map.117
  38.3 0.5 collective-permute-start.10
  38.8 1.0 shard_map.118.part_ref
  39.8 0.1 collective-permute-done.7.head.got_head
  39.9 0.8 collective-permute-done.2.got_ref.refs_1_
  40.8 1.4 %shard_map.119 = (bf16[256,256]{1,0:T(8,128)(2,1)S(1)}, bf16[768,256]{1,0:T(8,128)(2,1)S(1)}, bf16[1168,256]{1,0:T(8,128)(2,1)S(1)}) custom-call(s32[7]{0:T(128)S(1)} %stack.31.where_ref, bf16[528,128]{1,0:T(8,128)(2,1)S(1)} %shard_map.113.own_ref.mine_ref, bf16[528,128]{1,0:T(8,128)(2,1)S(1)} %collective-permute-done.core_ref, ...), custom_call_target="tpu_custom_call" | custom-call | tf_op jit(solution)/shard_map/pallas_call | solution.py:234
  42.2 1.5 %collective-permute-start.8 = (bf16[1168,256]{1,0:T(8,128)(2,1)S(1)}, bf16[1168,256]{1,0:T(8,128)(2,1)S(1)}, u32[]{:S(2)}, u32[]{:S(2)}) collective-permute-start(bf16[1168,256]{1,0:T(8,128)(2,1)S(1)} %get-tuple-element.83), channel_id=1, source_target_pairs={{0,16},{8,24},{16,0},{24,8},{1,17},{9,25},{17,1},{25,9},{2,18},{10... | collective-permute-start | bytes 1794056 | tf_op jit(solution)/shard_map/ppermute | solution.py:14
  43.6 1.5 %collective-permute-start.9 = (bf16[512,256]{1,0:T(8,128)(2,1)S(1)}, bf16[512,256]{1,0:T(8,128)(2,1)S(1)}, u32[]{:S(2)}, u32[]{:S(2)}) collective-permute-start(bf16[512,256]{1,0:T(8,128)(2,1)S(1)} %get-tuple-element.79.own_ref), channel_id=1, source_target_pairs={{0,4},{4,0},{1,5},{5,1},{2,6},{6,2},{3,7},{7,3},{8,12},{12,8},{9,1... | collective-permute-start | bytes 786440 | tf_op jit(solution)/shard_map/ppermute | solution.py:14
  45.1 0.8 shard_map.121
  46.0 0.6 collective-permute-start.12
  46.6 0.5 collective-permute-start.15
  47.1 5.8 %collective-permute-done.9.got_ref = bf16[512,256]{1,0:T(8,128)(2,1)S(1)} collective-permute-done((bf16[512,256]{1,0:T(8,128)(2,1)S(1)}, bf16[512,256]{1,0:T(8,128)(2,1)S(1)}, u32[]{:S(2)}, u32[]{:S(2)}) %collective-permute-start.9) | collective-permute-done | bytes 262176 | tf_op jit(solution)/shard_map/ppermute | solution.py:14
  52.9 0.8 shard_map.120.refs_13_
  53.7 1.4 %shard_map.122 = (bf16[256,256]{1,0:T(8,128)(2,1)S(1)}, bf16[256,256]{1,0:T(8,128)(2,1)S(1)}, bf16[512,256]{1,0:T(8,128)(2,1)S(1)}) custom-call(s32[7]{0:T(128)S(1)} %stack.31.where_ref, bf16[528,128]{1,0:T(8,128)(2,1)S(1)} %shard_map.113.own_ref.mine_ref, bf16[528,128]{1,0:T(8,128)(2,1)S(1)} %collective-permute-done.core_ref, ...), custom_call_target="tpu_custom_call" | custom-call | tf_op jit(solution)/shard_map/pallas_call | solution.py:234
  55.1 0.7 collective-permute-start.11
  55.8 1.4 %collective-permute-done.14.refs_6_ = bf16[368,256]{1,0:T(8,128)(2,1)S(1)} collective-permute-done((bf16[368,256]{1,0:T(8,128)(2,1)S(1)}, bf16[368,256]{1,0:T(8,128)(2,1)S(1)}, u32[]{:S(2)}, u32[]{:S(2)}) %collective-permute-start.14) | collective-permute-done | bytes 188448 | tf_op jit(solution)/shard_map/ppermute | solution.py:14
  57.3 5.3 %collective-permute-done.11.refs_10_ = bf16[512,256]{1,0:T(8,128)(2,1)S(1)} collective-permute-done((bf16[512,256]{1,0:T(8,128)(2,1)S(1)}, bf16[512,256]{1,0:T(8,128)(2,1)S(1)}, u32[]{:S(2)}, u32[]{:S(2)}) %collective-permute-start.11) | collective-permute-done | bytes 262176 | tf_op jit(solution)/shard_map/ppermute | solution.py:14
  62.7 0.5 collective-permute-start.18
  63.2 0.1 collective-permute-start.17
  63.2 1.3 %copy.12 = bf16[32,8,2,1024]{3,1,2,0:T(8,128)(2,1)} copy(bf16[32,8,2,1024]{3,2,1,0:T(2,128)(2,1)S(1)} %bitcast.34) | data formatting | bytes 2097152
  64.5 0.7 collective-permute-done.17.refs_11_
  65.2 4.3 %shard_map.123.own = bf16[256,1024]{1,0:T(8,128)(2,1)S(1)} custom-call(s32[7]{0:T(128)S(1)} %stack.31.where_ref, bf16[512,256]{1,0:T(8,128)(2,1)S(1)} %get-tuple-element.71.refs_0_, bf16[1024,256]{1,0:T(8,128)(2,1)S(1)} %collective-permute-done.2.got_ref.refs_1_, bf16[368,256]{1,0:T(8,128)(2,1)S(1)} %collective-permute-done.6.refs_2_, ...), custom_call_target="tpu_custom_call" | custom-call | tf_op jit(solution)/shard_map/pallas_call | solution.py:485
  69.5 1.5 %collective-permute-start.19 = (bf16[256,1024]{1,0:T(8,128)(2,1)S(1)}, bf16[256,1024]{1,0:T(8,128)(2,1)S(1)}, u32[]{:S(2)}, u32[]{:S(2)}) collective-permute-start(bf16[256,1024]{1,0:T(8,128)(2,1)S(1)} %shard_map.123.own), channel_id=1, source_target_pairs={{0,4},{4,0},{1,5},{5,1},{2,6},{6,2},{3,7},{7,3},{8,12},{12,8},{9,1... | collective-permute-start | bytes 1572872 | tf_op jit(solution)/shard_map/ppermute | solution.py:14
  71.1 12.5 %collective-permute-done.19.got = bf16[256,1024]{1,0:T(8,128)(2,1)S(1)} collective-permute-done((bf16[256,1024]{1,0:T(8,128)(2,1)S(1)}, bf16[256,1024]{1,0:T(8,128)(2,1)S(1)}, u32[]{:S(2)}, u32[]{:S(2)}) %collective-permute-start.19) | collective-permute-done | bytes 524320 | tf_op jit(solution)/shard_map/ppermute | solution.py:14
  83.5 1.3 %shard_map.124 = (bf16[2,128,1024]{2,1,0:T(8,128)(2,1)S(1)}, f32[2,128,1024]{2,1,0:T(8,128)S(1)}) custom-call(s32[7]{0:T(128)S(1)} %stack.31.where_ref, bf16[512,512]{1,0:T(8,128)(2,1)S(1)} %get-tuple-element.69.att, bf16[256,1024]{1,0:T(8,128)(2,1)S(1)} %shard_map.123.own, bf16[256,1024]{1,0:T(8,128)(2,1)S(1)} %collective-permute-done.19.got), custom_call_target="tpu_custom_call" | custom-call | tf_op jit(solution)/shard_map/pallas_call | solution.py:234
  84.9 1.6 %shard_map.126 = (bf16[512,512]{1,0:T(8,128)(2,1)S(1)}, bf16[4,128,128]{2,1,0:T(8,128)(2,1)S(1)}) custom-call(s32[7]{0:T(128)S(1)} %stack.31.where_ref, bf16[256,1024]{1,0:T(8,128)(2,1)S(1)} %shard_map.123.own, bf16[256,1024]{1,0:T(8,128)(2,1)S(1)} %collective-permute-done.19.got, bf16[160,1024]{1,0:T(8,128)(2,1)S(1)} %get-tuple-element.78.head_ref.head, ...), custom_call_target="tpu_custom_call" | custom-call | tf_op jit(solution)/shard_map/pallas_call | solution.py:234
  86.6 0.3 collective-permute-done.20.got_ref
  86.8 0.6 shard_map.125
  87.5 0.3 collective-permute-start.22
  87.8 1.5 %collective-permute-start.21 = (bf16[128,1024]{1,0:T(8,128)(2,1)S(1)}, bf16[128,1024]{1,0:T(8,128)(2,1)S(1)}, u32[]{:S(2)}, u32[]{:S(2)}) collective-permute-start(bf16[128,1024]{1,0:T(8,128)(2,1)S(1)} %get-tuple-element.102), channel_id=1, source_target_pairs={{0,16},{8,24},{16,0},{24,8},{1,17},{9,25},{17,1},{25,9},{2,18},{10... | collective-permute-start | bytes 786440 | tf_op jit(solution)/shard_map/ppermute | solution.py:14
  89.3 3.2 %shard_map.127 = (f32[512,512]{1,0:T(8,128)S(1)}, f32[512,512]{1,0:T(8,128)S(1)}) custom-call(s32[7]{0:T(128)S(1)} %stack.31.where_ref, bf16[512,512]{1,0:T(8,128)(2,1)S(1)} %get-tuple-element.103.g_ref, bf16[512,512]{1,0:T(8,128)(2,1)S(1)} %bitcast.31, bf16[512,512]{1,0:T(8,128)(2,1)S(1)} %bitcast.21, bf16[512,512]{1,0:T(8,128)(2,1)S(1)} %bitcast.26), custom_call_target="tpu_custom_call" | custom-call | tf_op jit(solution)/shard_map/pallas_call | solution.py:234
  92.5 2.7 %shard_map.128 = bf16[512,512]{1,0:T(8,128)(2,1)} custom-call(s32[7]{0:T(128)S(1)} %stack.31.where_ref, bf16[512,512]{1,0:T(8,128)(2,1)S(1)} %get-tuple-element.103.g_ref, bf16[512,512]{1,0:T(8,128)(2,1)S(1)} %bitcast.22, bf16[512,512]{1,0:T(8,128)(2,1)S(1)} %bitcast.27, bf16[4,128,128]{2,1,0:T(8,128)(2,1)S(1)} %copy-done.5), custom_call_target="tpu_custom_call" | custom-call | tf_op jit(solution)/shard_map/pallas_call | solution.py:234
  95.3 1.0 collective-permute-done.21.got_ref
  96.2 0.6 shard_map.129
  96.9 5.3 %collective-permute-start.23 = (bf16[128,256]{1,0:T(8,128)(2,1)S(1)}, bf16[128,256]{1,0:T(8,128)(2,1)S(1)}, u32[]{:S(2)}, u32[]{:S(2)}) collective-permute-start(bf16[128,256]{1,0:T(8,128)(2,1)S(1)} %get-tuple-element.115), channel_id=1, source_target_pairs={{0,3},{1,2},{2,1},{3,0},{4,7},{5,6},{6,5},{7,4},{8,11},{9,10},{10,... | collective-permute-start | bytes 196616 | tf_op jit(solution)/shard_map/ppermute | solution.py:14
  102.2 1.7 %collective-permute-start.29 = (bf16[4,128,128]{2,1,0:T(8,128)(2,1)S(1)}, bf16[4,128,128]{2,1,0:T(8,128)(2,1)S(1)}, u32[]{:S(2)}, u32[]{:S(2)}) collective-permute-start(bf16[4,128,128]{2,1,0:T(8,128)(2,1)S(1)} %add_convert_fusion), channel_id=1, source_target_pairs={{0,16},{8,24},{16,0},{24,8},{1,17},{9,25},{17,1},{25,9},{2,18},{10... | collective-permute-start | bytes 393224 | tf_op jit(solution)/shard_map/ppermute | solution.py:14
  103.9 0.6 collective-permute-start.25
  104.5 0.3 collective-permute-done.23.refs_0_
  104.9 3.0 %collective-permute-done.24.refs_1_ = bf16[128,256]{1,0:T(8,128)(2,1)S(1)} collective-permute-done((bf16[128,256]{1,0:T(8,128)(2,1)S(1)}, bf16[128,256]{1,0:T(8,128)(2,1)S(1)}, u32[]{:S(2)}, u32[]{:S(2)}) %collective-permute-start.24) | collective-permute-done | bytes 65568 | tf_op jit(solution)/shard_map/ppermute | solution.py:14
  107.9 0.7 collective-permute-done.25.refs_2_
  108.5 0.6 shard_map.130.refs_0_
  109.1 1.2 %collective-permute-start.26 = (bf16[128,256]{1,0:T(8,128)(2,1)S(1)}, bf16[128,256]{1,0:T(8,128)(2,1)S(1)}, u32[]{:S(2)}, u32[]{:S(2)}) collective-permute-start(bf16[128,256]{1,0:T(8,128)(2,1)S(1)} %shard_map.130.refs_0_), channel_id=1, source_target_pairs={{0,16},{8,24},{16,0},{24,8},{1,17},{9,25},{17,1},{25,9},{2,18},{10... | collective-permute-start | bytes 196616 | tf_op jit(solution)/shard_map/ppermute | solution.py:14
  110.3 1.0 collective-permute-start.28
  111.3 2.0 %shard_map.131 = (bf16[512,512]{1,0:T(8,128)(2,1)}, bf16[512,512]{1,0:T(8,128)(2,1)}) custom-call(s32[7]{0:T(128)S(1)} %stack.31.where_ref, f32[512,512]{1,0:T(8,128)S(1)} %get-tuple-element.119.kp_ref, f32[512,512]{1,0:T(8,128)S(1)} %get-tuple-element.120.vp_ref, bf16[512,512]{1,0:T(8,128)(2,1)S(1)} %bitcast.23, bf16[512,512]{1,0:T(8,128)(2,1)S(1)} %bitcast.28, ...), custom_call_target="tpu_custom_call" | custom-call | tf_op jit(solution)/shard_map/pallas_call | solution.py:234
  113.3 0.3 collective-permute-done.26.refs_1_
  113.6 0.7 collective-permute-done.28.refs_3_
  114.3 1.4 %shard_map.132 = f32[512,256]{1,0:T(8,128)} custom-call(s32[7]{0:T(128)S(1)} %stack.31.where_ref, bf16[128,256]{1,0:T(8,128)(2,1)S(1)} %shard_map.130.refs_0_, bf16[128,256]{1,0:T(8,128)(2,1)S(1)} %collective-permute-done.26.refs_1_, bf16[128,256]{1,0:T(8,128)(2,1)S(1)} %collective-permute-done.27.refs_2_, bf16[128,256]{1,0:T(8,128)(2,1)S(1)} %collective-permute-done.28.refs_3_), custom_call_target="tpu_custom_call" | custom-call | tf_op jit(solution)/shard_map/pallas_call | solution.py:234
  (39 shorter events, 0.5 us)
Async XLA Ops:
  0.6 10.0 %copy-start = (bf16[1,512,512]{2,1,0:T(8,128)(2,1)S(1)}, bf16[1,512,512]{2,1,0:T(8,128)(2,1)}, u32[]{:S(2)}) copy-start(bf16[1,512,512]{2,1,0:T(8,128)(2,1)} %param.9) | copy-start | bytes 1572868
  0.6 10.0 %copy-start.1 = (bf16[1,512,512]{2,1,0:T(8,128)(2,1)S(1)}, bf16[1,512,512]{2,1,0:T(8,128)(2,1)}, u32[]{:S(2)}) copy-start(bf16[1,512,512]{2,1,0:T(8,128)(2,1)} %param.10) | copy-start | bytes 1572868
  0.7 10.0 %copy-start.6 = (s32[1,256,2]{1,2,0:T(2,128)S(1)}, s32[1,256,2]{1,2,0:T(2,128)}, u32[]{:S(2)}) copy-start(s32[1,256,2]{1,2,0:T(2,128)} %param.14) | copy-start | bytes 6148
  2.5 17.1 %copy-start.2 = (bf16[1,512,512]{2,1,0:T(8,128)(2,1)S(1)}, bf16[1,512,512]{2,1,0:T(8,128)(2,1)}, u32[]{:S(2)}) copy-start(bf16[1,512,512]{2,1,0:T(8,128)(2,1)} %param.8) | copy-start | bytes 1572868
  2.5 26.2 %all-to-all-start = ((bf16[4,256,256]{2,1,0:T(8,128)(2,1)}), bf16[4,256,256]{2,1,0:T(8,128)(2,1)S(1)}, u32[]{:S(2)}, u32[]{:S(2)}) async-start(bf16[4,256,256]{2,1,0:T(8,128)(2,1)} %shard_map.111.refs_2_), calls=%async_computation | async-start | bytes 1048576 | tf_op jit(solution)/shard_map/all_to_all | solution.py:783
  10.6 26.5 %copy-start.3 = (bf16[384,256]{1,0:T(8,128)(2,1)S(1)}, bf16[384,256]{1,0:T(8,128)(2,1)}, u32[]{:S(2)}) copy-start(bf16[384,256]{1,0:T(8,128)(2,1)} %shard_map.112.refs_0_) | copy-start | bytes 589828
  11.6 1.4 %collective-permute-start = (bf16[528,128]{1,0:T(8,128)(2,1)S(1)}, bf16[528,128]{1,0:T(8,128)(2,1)S(1)}, u32[]{:S(2)}, u32[]{:S(2)}) collective-permute-start(bf16[528,128]{1,0:T(8,128)(2,1)S(1)} %shard_map.113.own_ref.mine_ref), channel_id=1, source_target_pairs={{0,8},{8,0},{16,24},{24,16},{1,9},{9,1},{17,25},{25,17},{2,10},{10... | collective-permute-start | bytes 405512 | tf_op jit(solution)/shard_map/ppermute | solution.py:14
  13.6 6.0 %collective-permute-start.1 = (bf16[544,128]{1,0:T(8,128)(2,1)S(1)}, bf16[544,128]{1,0:T(8,128)(2,1)S(1)}, u32[]{:S(2)}, u32[]{:S(2)}) collective-permute-start(bf16[544,128]{1,0:T(8,128)(2,1)S(1)} %shard_map.114), channel_id=1, source_target_pairs={{0,16},{8,24},{16,0},{24,8},{1,17},{9,25},{17,1},{25,9},{2,18},{10... | collective-permute-start | bytes 417800 | tf_op jit(solution)/shard_map/ppermute | solution.py:14
  15.2 21.9 %collective-permute-start.3 = (bf16[384,256]{1,0:T(8,128)(2,1)}, bf16[384,256]{1,0:T(8,128)(2,1)S(1)}, u32[]{:S(2)}, u32[]{:S(2)}) collective-permute-start(bf16[384,256]{1,0:T(8,128)(2,1)} %shard_map.112.refs_0_), channel_id=1, source_target_pairs={{0,2},{1,3},{2,0},{3,1},{4,6},{5,7},{6,4},{7,5},{8,10},{9,11},{10,... | collective-permute-start | bytes 589832 | tf_op jit(solution)/shard_map/ppermute | solution.py:14
  18.1 19.0 %collective-permute-start.4 = (bf16[384,256]{1,0:T(8,128)(2,1)}, bf16[384,256]{1,0:T(8,128)(2,1)}, u32[]{:S(2)}, u32[]{:S(2)}) collective-permute-start(bf16[384,256]{1,0:T(8,128)(2,1)} %shard_map.112.refs_0_), channel_id=1, source_target_pairs={{0,1},{1,0},{2,3},{3,2},{4,5},{5,4},{6,7},{7,6},{8,9},{9,8},{10,11... | collective-permute-start | bytes 589832 | tf_op jit(solution)/shard_map/ppermute | solution.py:14
  19.6 17.6 %collective-permute-start.5 = (bf16[384,256]{1,0:T(8,128)(2,1)}, bf16[384,256]{1,0:T(8,128)(2,1)}, u32[]{:S(2)}, u32[]{:S(2)}) collective-permute-start(bf16[384,256]{1,0:T(8,128)(2,1)} %shard_map.112.refs_0_), channel_id=1, source_target_pairs={{0,3},{1,2},{2,1},{3,0},{4,7},{5,6},{6,5},{7,4},{8,11},{9,10},{10,... | collective-permute-start | bytes 589832 | tf_op jit(solution)/shard_map/ppermute | solution.py:14
  21.5 0.7 copy-start.4
  29.3 11.4 %collective-permute-start.2 = (bf16[1024,256]{1,0:T(8,128)(2,1)S(1)}, bf16[1024,256]{1,0:T(8,128)(2,1)S(1)}, u32[]{:S(2)}, u32[]{:S(2)}) collective-permute-start(bf16[1024,256]{1,0:T(8,128)(2,1)S(1)} %get-tuple-element.72.own_ref), channel_id=1, source_target_pairs={{0,4},{4,0},{1,5},{5,1},{2,6},{6,2},{3,7},{7,3},{8,12},{12,8},{9,1... | collective-permute-start | bytes 1572872 | tf_op jit(solution)/shard_map/ppermute | solution.py:14
  30.9 6.2 %collective-permute-start.6 = (bf16[368,256]{1,0:T(8,128)(2,1)S(1)}, bf16[368,256]{1,0:T(8,128)(2,1)S(1)}, u32[]{:S(2)}, u32[]{:S(2)}) collective-permute-start(bf16[368,256]{1,0:T(8,128)(2,1)S(1)} %get-tuple-element.73), channel_id=1, source_target_pairs={{0,16},{8,24},{16,0},{24,8},{1,17},{9,25},{17,1},{25,9},{2,18},{10... | collective-permute-start | bytes 565256 | tf_op jit(solution)/shard_map/ppermute | solution.py:14
  38.2 1.7 %collective-permute-start.7 = (bf16[160,1024]{1,0:T(8,128)(2,1)S(1)}, bf16[160,1024]{1,0:T(8,128)(2,1)S(1)}, u32[]{:S(2)}, u32[]{:S(2)}) collective-permute-start(bf16[160,1024]{1,0:T(8,128)(2,1)S(1)} %get-tuple-element.78.head_ref.head), channel_id=1, source_target_pairs={{0,8},{8,0},{16,24},{24,16},{1,9},{9,1},{17,25},{25,17},{2,10},{10... | collective-permute-start | bytes 983048 | tf_op jit(solution)/shard_map/ppermute | solution.py:14
  38.3 6.8 %collective-permute-start.10 = (bf16[96,1024]{1,0:T(8,128)(2,1)S(1)}, bf16[96,1024]{1,0:T(8,128)(2,1)S(1)}, u32[]{:S(2)}, u32[]{:S(2)}) collective-permute-start(bf16[96,1024]{1,0:T(8,128)(2,1)S(1)} %get-tuple-element.80.tail_ref.tail), channel_id=1, source_target_pairs={{0,8},{8,0},{16,24},{24,16},{1,9},{9,1},{17,25},{25,17},{2,10},{10... | collective-permute-start | bytes 589832 | tf_op jit(solution)/shard_map/ppermute | solution.py:14
  42.2 20.4 %collective-permute-start.8 = (bf16[1168,256]{1,0:T(8,128)(2,1)S(1)}, bf16[1168,256]{1,0:T(8,128)(2,1)S(1)}, u32[]{:S(2)}, u32[]{:S(2)}) collective-permute-start(bf16[1168,256]{1,0:T(8,128)(2,1)S(1)} %get-tuple-element.83), channel_id=1, source_target_pairs={{0,16},{8,24},{16,0},{24,8},{1,17},{9,25},{17,1},{25,9},{2,18},{10... | collective-permute-start | bytes 1794056 | tf_op jit(solution)/shard_map/ppermute | solution.py:14
  43.6 9.2 %collective-permute-start.9 = (bf16[512,256]{1,0:T(8,128)(2,1)S(1)}, bf16[512,256]{1,0:T(8,128)(2,1)S(1)}, u32[]{:S(2)}, u32[]{:S(2)}) collective-permute-start(bf16[512,256]{1,0:T(8,128)(2,1)S(1)} %get-tuple-element.79.own_ref), channel_id=1, source_target_pairs={{0,4},{4,0},{1,5},{5,1},{2,6},{6,2},{3,7},{7,3},{8,12},{12,8},{9,1... | collective-permute-start | bytes 786440 | tf_op jit(solution)/shard_map/ppermute | solution.py:14
  46.0 16.6 %collective-permute-start.12 = (bf16[256,1024]{1,0:T(8,128)(2,1)S(1)}, bf16[256,1024]{1,0:T(8,128)(2,1)S(1)}, u32[]{:S(2)}, u32[]{:S(2)}) collective-permute-start(bf16[256,1024]{1,0:T(8,128)(2,1)S(1)} %shard_map.121), channel_id=1, source_target_pairs={{0,4},{4,0},{1,5},{5,1},{2,6},{6,2},{3,7},{7,3},{8,12},{12,8},{9,1... | collective-permute-start | bytes 1572872 | tf_op jit(solution)/shard_map/ppermute | solution.py:14
  46.6 9.3 %collective-permute-start.13 = (bf16[512,256]{1,0:T(8,128)(2,1)S(1)}, bf16[512,256]{1,0:T(8,128)(2,1)S(1)}, u32[]{:S(2)}, u32[]{:S(2)}) collective-permute-start(bf16[512,256]{1,0:T(8,128)(2,1)S(1)} %get-tuple-element.71.refs_0_), channel_id=1, source_target_pairs={{0,8},{8,0},{16,24},{24,16},{1,9},{9,1},{17,25},{25,17},{2,10},{10... | collective-permute-start | bytes 786440 | tf_op jit(solution)/shard_map/ppermute | solution.py:14
  46.6 16.7 %copy-start.7 = (bf16[1,256,2,1024]{3,2,1,0:T(2,128)(2,1)S(1)}, bf16[1,256,2,1024]{3,2,1,0:T(2,128)(2,1)}, u32[]{:S(2)}) copy-start(bf16[1,256,2,1024]{3,2,1,0:T(2,128)(2,1)} %param.15) | copy-start | bytes 3145732
  46.6 16.0 %collective-permute-start.15 = (bf16[768,256]{1,0:T(8,128)(2,1)S(1)}, bf16[768,256]{1,0:T(8,128)(2,1)S(1)}, u32[]{:S(2)}, u32[]{:S(2)}) collective-permute-start(bf16[768,256]{1,0:T(8,128)(2,1)S(1)} %get-tuple-element.90), channel_id=1, source_target_pairs={{0,8},{8,0},{16,24},{24,16},{1,9},{9,1},{17,25},{25,17},{2,10},{10... | collective-permute-start | bytes 1179656 | tf_op jit(solution)/shard_map/ppermute | solution.py:14
  55.1 7.5 %collective-permute-start.11 = (bf16[512,256]{1,0:T(8,128)(2,1)S(1)}, bf16[512,256]{1,0:T(8,128)(2,1)S(1)}, u32[]{:S(2)}, u32[]{:S(2)}) collective-permute-start(bf16[512,256]{1,0:T(8,128)(2,1)S(1)} %get-tuple-element.89), channel_id=1, source_target_pairs={{0,16},{8,24},{16,0},{24,8},{1,17},{9,25},{17,1},{25,9},{2,18},{10... | collective-permute-start | bytes 786440 | tf_op jit(solution)/shard_map/ppermute | solution.py:14
  55.8 1.4 %collective-permute-start.14 = (bf16[368,256]{1,0:T(8,128)(2,1)S(1)}, bf16[368,256]{1,0:T(8,128)(2,1)S(1)}, u32[]{:S(2)}, u32[]{:S(2)}) collective-permute-start(bf16[368,256]{1,0:T(8,128)(2,1)S(1)} %collective-permute-done.6.refs_2_), channel_id=1, source_target_pairs={{0,8},{8,0},{16,24},{24,16},{1,9},{9,1},{17,25},{25,17},{2,10},{10... | collective-permute-start | bytes 565256 | tf_op jit(solution)/shard_map/ppermute | solution.py:14
  62.6 2.6 %collective-permute-start.16 = (bf16[1168,256]{1,0:T(8,128)(2,1)S(1)}, bf16[1168,256]{1,0:T(8,128)(2,1)S(1)}, u32[]{:S(2)}, u32[]{:S(2)}) collective-permute-start(bf16[1168,256]{1,0:T(8,128)(2,1)S(1)} %collective-permute-done.8.refs_3_), channel_id=1, source_target_pairs={{0,8},{8,0},{16,24},{24,16},{1,9},{9,1},{17,25},{25,17},{2,10},{10... | collective-permute-start | bytes 1794056 | tf_op jit(solution)/shard_map/ppermute | solution.py:14
  62.7 2.6 %collective-permute-start.18 = (bf16[512,256]{1,0:T(8,128)(2,1)S(1)}, bf16[512,256]{1,0:T(8,128)(2,1)S(1)}, u32[]{:S(2)}, u32[]{:S(2)}) collective-permute-start(bf16[512,256]{1,0:T(8,128)(2,1)S(1)} %collective-permute-done.11.refs_10_), channel_id=1, source_target_pairs={{0,8},{8,0},{16,24},{24,16},{1,9},{9,1},{17,25},{25,17},{2,10},{10... | collective-permute-start | bytes 786440 | tf_op jit(solution)/shard_map/ppermute | solution.py:14
  63.2 2.1 %collective-permute-start.17 = (bf16[256,256]{1,0:T(8,128)(2,1)S(1)}, bf16[256,256]{1,0:T(8,128)(2,1)S(1)}, u32[]{:S(2)}, u32[]{:S(2)}) collective-permute-start(bf16[256,256]{1,0:T(8,128)(2,1)S(1)} %get-tuple-element.98), channel_id=1, source_target_pairs={{0,8},{8,0},{16,24},{24,16},{1,9},{9,1},{17,25},{25,17},{2,10},{10... | collective-permute-start | bytes 393224 | tf_op jit(solution)/shard_map/ppermute | solution.py:14
  69.5 14.0 %collective-permute-start.19 = (bf16[256,1024]{1,0:T(8,128)(2,1)S(1)}, bf16[256,1024]{1,0:T(8,128)(2,1)S(1)}, u32[]{:S(2)}, u32[]{:S(2)}) collective-permute-start(bf16[256,1024]{1,0:T(8,128)(2,1)S(1)} %shard_map.123.own), channel_id=1, source_target_pairs={{0,4},{4,0},{1,5},{5,1},{2,6},{6,2},{3,7},{7,3},{8,12},{12,8},{9,1... | collective-permute-start | bytes 1572872 | tf_op jit(solution)/shard_map/ppermute | solution.py:14
  84.8 2.0 %collective-permute-start.20 = (bf16[2,128,1024]{2,1,0:T(8,128)(2,1)S(1)}, bf16[2,128,1024]{2,1,0:T(8,128)(2,1)S(1)}, u32[]{:S(2)}, u32[]{:S(2)}) collective-permute-start(bf16[2,128,1024]{2,1,0:T(8,128)(2,1)S(1)} %get-tuple-element.101), channel_id=1, source_target_pairs={{0,8},{8,0},{16,24},{24,16},{1,9},{9,1},{17,25},{25,17},{2,10},{10... | collective-permute-start | bytes 1572872 | tf_op jit(solution)/shard_map/ppermute | solution.py:14
  86.5 5.9 %copy-start.5 = (bf16[4,128,128]{2,1,0:T(8,128)(2,1)S(1)}, bf16[4,128,128]{2,1,0:T(8,128)(2,1)}, u32[]{:S(2)}) copy-start(bf16[4,128,128]{2,1,0:T(8,128)(2,1)} %copy-done.4) | copy-start | bytes 393220
  87.5 7.8 %collective-permute-start.22 = (bf16[4,128,128]{2,1,0:T(8,128)(2,1)S(1)}, bf16[4,128,128]{2,1,0:T(8,128)(2,1)S(1)}, u32[]{:S(2)}, u32[]{:S(2)}) collective-permute-start(bf16[4,128,128]{2,1,0:T(8,128)(2,1)S(1)} %get-tuple-element.108), channel_id=1, source_target_pairs={{0,8},{8,0},{16,24},{24,16},{1,9},{9,1},{17,25},{25,17},{2,10},{10... | collective-permute-start | bytes 393224 | tf_op jit(solution)/shard_map/ppermute | solution.py:14
  87.8 8.5 %collective-permute-start.21 = (bf16[128,1024]{1,0:T(8,128)(2,1)S(1)}, bf16[128,1024]{1,0:T(8,128)(2,1)S(1)}, u32[]{:S(2)}, u32[]{:S(2)}) collective-permute-start(bf16[128,1024]{1,0:T(8,128)(2,1)S(1)} %get-tuple-element.102), channel_id=1, source_target_pairs={{0,16},{8,24},{16,0},{24,8},{1,17},{9,25},{17,1},{25,9},{2,18},{10... | collective-permute-start | bytes 786440 | tf_op jit(solution)/shard_map/ppermute | solution.py:14
  96.9 8.0 %collective-permute-start.23 = (bf16[128,256]{1,0:T(8,128)(2,1)S(1)}, bf16[128,256]{1,0:T(8,128)(2,1)S(1)}, u32[]{:S(2)}, u32[]{:S(2)}) collective-permute-start(bf16[128,256]{1,0:T(8,128)(2,1)S(1)} %get-tuple-element.115), channel_id=1, source_target_pairs={{0,3},{1,2},{2,1},{3,0},{4,7},{5,6},{6,5},{7,4},{8,11},{9,10},{10,... | collective-permute-start | bytes 196616 | tf_op jit(solution)/shard_map/ppermute | solution.py:14
  102.1 5.7 %collective-permute-start.24 = (bf16[128,256]{1,0:T(8,128)(2,1)S(1)}, bf16[128,256]{1,0:T(8,128)(2,1)S(1)}, u32[]{:S(2)}, u32[]{:S(2)}) collective-permute-start(bf16[128,256]{1,0:T(8,128)(2,1)S(1)} %get-tuple-element.116), channel_id=1, source_target_pairs={{0,2},{1,3},{2,0},{3,1},{4,6},{5,7},{6,4},{7,5},{8,10},{9,11},{10,... | collective-permute-start | bytes 196616 | tf_op jit(solution)/shard_map/ppermute | solution.py:14
  102.2 9.1 %collective-permute-start.29 = (bf16[4,128,128]{2,1,0:T(8,128)(2,1)S(1)}, bf16[4,128,128]{2,1,0:T(8,128)(2,1)S(1)}, u32[]{:S(2)}, u32[]{:S(2)}) collective-permute-start(bf16[4,128,128]{2,1,0:T(8,128)(2,1)S(1)} %add_convert_fusion), channel_id=1, source_target_pairs={{0,16},{8,24},{16,0},{24,8},{1,17},{9,25},{17,1},{25,9},{2,18},{10... | collective-permute-start | bytes 393224 | tf_op jit(solution)/shard_map/ppermute | solution.py:14
  103.9 4.6 %collective-permute-start.25 = (bf16[128,256]{1,0:T(8,128)(2,1)S(1)}, bf16[128,256]{1,0:T(8,128)(2,1)S(1)}, u32[]{:S(2)}, u32[]{:S(2)}) collective-permute-start(bf16[128,256]{1,0:T(8,128)(2,1)S(1)} %get-tuple-element.117), channel_id=1, source_target_pairs={{0,1},{1,0},{2,3},{3,2},{4,5},{5,4},{6,7},{7,6},{8,9},{9,8},{10,11... | collective-permute-start | bytes 196616 | tf_op jit(solution)/shard_map/ppermute | solution.py:14
  109.1 4.5 %collective-permute-start.26 = (bf16[128,256]{1,0:T(8,128)(2,1)S(1)}, bf16[128,256]{1,0:T(8,128)(2,1)S(1)}, u32[]{:S(2)}, u32[]{:S(2)}) collective-permute-start(bf16[128,256]{1,0:T(8,128)(2,1)S(1)} %shard_map.130.refs_0_), channel_id=1, source_target_pairs={{0,16},{8,24},{16,0},{24,8},{1,17},{9,25},{17,1},{25,9},{2,18},{10... | collective-permute-start | bytes 196616 | tf_op jit(solution)/shard_map/ppermute | solution.py:14
  110.3 3.3 %collective-permute-start.27 = (bf16[128,256]{1,0:T(8,128)(2,1)S(1)}, bf16[128,256]{1,0:T(8,128)(2,1)S(1)}, u32[]{:S(2)}, u32[]{:S(2)}) collective-permute-start(bf16[128,256]{1,0:T(8,128)(2,1)S(1)} %shard_map.130.refs_0_), channel_id=1, source_target_pairs={{0,8},{8,0},{16,24},{24,16},{1,9},{9,1},{17,25},{25,17},{2,10},{10... | collective-permute-start | bytes 196616 | tf_op jit(solution)/shard_map/ppermute | solution.py:14
  110.3 4.0 %collective-permute-start.28 = (bf16[128,256]{1,0:T(8,128)(2,1)S(1)}, bf16[128,256]{1,0:T(8,128)(2,1)S(1)}, u32[]{:S(2)}, u32[]{:S(2)}) collective-permute-start(bf16[128,256]{1,0:T(8,128)(2,1)S(1)} %shard_map.130.refs_0_), channel_id=1, source_target_pairs={{0,24},{8,16},{16,8},{24,0},{1,25},{9,17},{17,9},{25,1},{2,26},{10... | collective-permute-start | bytes 196616 | tf_op jit(solution)/shard_map/ppermute | solution.py:14

commit v6 on v5

--- a/solution.py
+++ b/solution.py
@@ -599,17 +599,23 @@
     return run(body, [shaped((length, width), dtype)], where, attended, part, got_head, got_tail)[0]
 
 
-def weight_terms(where, attended, grad_own, grad_got):
+def weight_own(where, attended, grad_own):
     tokens, width = grad_own.shape
 
-    def body(where_ref, att, own, got, send, keep):
+    def body(where_ref, att, own, out):
+        for m in range(4):
+            out[m] = dot(att[at(where_ref[HEAD], tokens), at(where_ref[m], DH)], own[...], ((0,), (0,)))
+
+    return run(body, [shaped((4, DH, width), F32)], where, attended, grad_own)[0]
+
+
+def weight_terms(where, attended, part, grad_got):
+    tokens, width = grad_got.shape
+
+    def body(where_ref, att, part_ref, got, send, keep):
         def term(m):
-            total = None
-            for k, ref in enumerate((own, got)):
-                a = att[at(where_ref[HEAD] ^ k, tokens), at(where_ref[m], DH)]
-                part = dot(a, ref[...], ((0,), (0,)))
-                total = part if total is None else total + part
-            return total
+            a = att[at(1 - where_ref[HEAD], tokens), at(where_ref[m], DH)]
+            return part_ref[m] + dot(a, got[...], ((0,), (0,)))
 
         send[0] = term(2).astype(BF16)
         send[1] = term(3).astype(BF16)
@@ -617,7 +623,7 @@
         keep[1] = term(1)
 
     return run(
-        body, [shaped((2, DH, width)), shaped((2, DH, width), F32)], where, attended, grad_own, grad_got
+        body, [shaped((2, DH, width)), shaped((2, DH, width), F32)], where, attended, part, grad_got
     )
 
 
@@ -842,7 +848,8 @@
     grad_mixed = depth_grad(where, folds, rest, late, first, second, mixed, mixed_got, cot)
 
     grad_got = swap(grad_mixed, "head", 1)
-    send, keep = weight_terms(where, attended, grad_mixed, grad_got)
+    part = weight_own(where, attended, grad_mixed)
+    send, keep = weight_terms(where, attended, part, grad_got)
     send, keep = add_core(where, keep, core_swap(send))
     from_far = far_swap(send)
     grad_rows, back = grad_attend(where, grad_mixed, grad_got, out_head, out_tail, got_head, got_tail, queries)

time: 116 us -> 116 us (level)
    pallas_call x19 -> x20, Pallas kernels: 24.7 us -> 25.5 us  [run(): pl.pallas_call(body, out_shape=outs, in_specs=[pl.BlockSpec(memory_space=...]
  transfers between devices with their start and end apart: 31 -> 31, of which waited for: 17 -> 17; matrix products, arithmetic and copies ran while one was open for 1% -> 1% of each run, Pallas kernels for 19% -> 20%
where the time goes in v6:
time: 116 us; the launch traced here: 115 us
  waiting for transfers between devices  44.3 us (38%)
  starting transfers between devices  35 us (30%)
  Pallas kernels  33.1 us (29%)
  local copies, waits for them, and re-layouts  2.05 us (2%)
    ppermute x30, waiting for transfers between devices, swap(): lax.ppermute(block, axis, [(i, i ^ mask) for i in range(lax.axis_size(axi...  37.8 us
    ppermute x30, starting transfers between devices, swap(): lax.ppermute(block, axis, [(i, i ^ mask) for i in range(lax.axis_size(axi...  28.5 us
    pallas_call x20, Pallas kernels, run(): pl.pallas_call(body, out_shape=outs, in_specs=[pl.BlockSpec(memory_space=...  25.5 us
    all_to_all x1, waiting for transfers between devices, on_device(): pieces_0 = lax.all_to_all(lanes_0, 'dp', 0, 0)  6.48 us
    all_to_all x1, starting transfers between devices, on_device(): pieces_0 = lax.all_to_all(lanes_0, 'dp', 0, 0)  6.46 us
    pallas_call x1, Pallas kernels, depth_grad(): pl.pallas_call(body, out_shape=shaped((tokens, width)), in_specs=[pl.Bloc...  4.27 us
  transfers between devices with their start and end apart: 31, of which 17 were waited for; matrix products, arithmetic and copies ran while one was open for 1% of the time, Pallas kernels for 20%

profile of v6, /device:TPU:0, one launch (start us, length us, event | category | flops | bytes accessed | tf_op | source)
XLA Modules:
  0.0 115.4 jit_solution(13606465960072622393)
XLA Ops:
  0.7 1.8 %shard_map.111.refs_2_ = bf16[4,256,256]{2,1,0:T(8,128)(2,1)} custom-call(bf16[2,128,1024]{2,1,0:T(8,128)(2,1)} %refs_0_.1, bf16[1024,128]{1,0:T(8,128)(2,1)} %depth.1), custom_call_target="tpu_custom_call" | custom-call | tf_op jit(solution)/shard_map/pallas_call | solution.py:297
  2.5 6.5 %all-to-all-start = ((bf16[4,256,256]{2,1,0:T(8,128)(2,1)}), bf16[4,256,256]{2,1,0:T(8,128)(2,1)S(1)}, u32[]{:S(2)}, u32[]{:S(2)}) async-start(bf16[4,256,256]{2,1,0:T(8,128)(2,1)} %shard_map.111.refs_2_), calls=%async_computation | async-start | bytes 1048576 | tf_op jit(solution)/shard_map/all_to_all | solution.py:789
  8.9 1.6 %shard_map.112.refs_0_ = bf16[384,256]{1,0:T(8,128)(2,1)} custom-call(bf16[2,128,1024]{2,1,0:T(8,128)(2,1)} %refs_0_.1, bf16[512,256]{1,0:T(8,128)(2,1)} %refs_1_.1, bf16[4,256,256]{2,1,0:T(8,128)(2,1)} %shard_map.111.refs_2_), custom_call_target="tpu_custom_call" | custom-call | tf_op jit(solution)/shard_map/pallas_call | solution.py:271
  10.6 0.1 stack.31.where_ref
  10.7 0.9 shard_map.113.own_ref.mine_ref
  11.7 1.3 %collective-permute-done.core_ref = bf16[528,128]{1,0:T(8,128)(2,1)S(1)} collective-permute-done((bf16[528,128]{1,0:T(8,128)(2,1)S(1)}, bf16[528,128]{1,0:T(8,128)(2,1)S(1)}, u32[]{:S(2)}, u32[]{:S(2)}) %collective-permute-start) | collective-permute-done | bytes 135200 | tf_op jit(solution)/shard_map/ppermute | solution.py:14
  13.0 0.6 shard_map.114
  13.6 1.6 %collective-permute-start.1 = (bf16[544,128]{1,0:T(8,128)(2,1)S(1)}, bf16[544,128]{1,0:T(8,128)(2,1)S(1)}, u32[]{:S(2)}, u32[]{:S(2)}) collective-permute-start(bf16[544,128]{1,0:T(8,128)(2,1)S(1)} %shard_map.114), channel_id=1, source_target_pairs={{0,16},{8,24},{16,0},{24,8},{1,17},{9,25},{17,1},{25,9},{2,18},{10... | collective-permute-start | bytes 417800 | tf_op jit(solution)/shard_map/ppermute | solution.py:14
  15.2 2.9 %collective-permute-start.3 = (bf16[384,256]{1,0:T(8,128)(2,1)}, bf16[384,256]{1,0:T(8,128)(2,1)S(1)}, u32[]{:S(2)}, u32[]{:S(2)}) collective-permute-start(bf16[384,256]{1,0:T(8,128)(2,1)} %shard_map.112.refs_0_), channel_id=1, source_target_pairs={{0,2},{1,3},{2,0},{3,1},{4,6},{5,7},{6,4},{7,5},{8,10},{9,11},{10,... | collective-permute-start | bytes 589832 | tf_op jit(solution)/shard_map/ppermute | solution.py:14
  18.1 1.5 %collective-permute-start.4 = (bf16[384,256]{1,0:T(8,128)(2,1)}, bf16[384,256]{1,0:T(8,128)(2,1)}, u32[]{:S(2)}, u32[]{:S(2)}) collective-permute-start(bf16[384,256]{1,0:T(8,128)(2,1)} %shard_map.112.refs_0_), channel_id=1, source_target_pairs={{0,1},{1,0},{2,3},{3,2},{4,5},{5,4},{6,7},{7,6},{8,9},{9,8},{10,11... | collective-permute-start | bytes 589832 | tf_op jit(solution)/shard_map/ppermute | solution.py:14
  19.6 2.0 %shard_map.115 = (bf16[512,512]{1,0:T(8,128)(2,1)S(1)}, bf16[4,128,128]{2,1,0:T(8,128)(2,1)S(1)}) custom-call(s32[7]{0:T(128)S(1)} %stack.31.where_ref, bf16[512,512]{1,0:T(8,128)(2,1)S(1)} %bitcast.29, bf16[512,512]{1,0:T(8,128)(2,1)S(1)} %bitcast.20, bf16[512,512]{1,0:T(8,128)(2,1)S(1)} %bitcast.25, bf16[528,128]{1,0:T(8,128)(2,1)S(1)} %collective-permute-done.core_ref, ...), custom_call_target="tpu_custom_call" | custom-call | tf_op jit(solution)/shard_map/pallas_call | solution.py:234
  21.6 0.6 copy-done.4
  22.2 6.5 %all-to-all-done.ref = bf16[4,256,256]{2,1,0:T(8,128)(2,1)S(1)} async-done(((bf16[4,256,256]{2,1,0:T(8,128)(2,1)}), bf16[4,256,256]{2,1,0:T(8,128)(2,1)S(1)}, u32[]{:S(2)}, u32[]{:S(2)}) %all-to-all-start) | async-done | bytes 524320 | tf_op jit(solution)/shard_map/all_to_all | solution.py:789
  28.7 0.7 shard_map.116
  29.3 1.6 %collective-permute-start.2 = (bf16[1024,256]{1,0:T(8,128)(2,1)S(1)}, bf16[1024,256]{1,0:T(8,128)(2,1)S(1)}, u32[]{:S(2)}, u32[]{:S(2)}) collective-permute-start(bf16[1024,256]{1,0:T(8,128)(2,1)S(1)} %get-tuple-element.72.own_ref), channel_id=1, source_target_pairs={{0,4},{4,0},{1,5},{5,1},{2,6},{6,2},{3,7},{7,3},{8,12},{12,8},{9,1... | collective-permute-start | bytes 1572872 | tf_op jit(solution)/shard_map/ppermute | solution.py:14
  30.9 1.6 %collective-permute-start.6 = (bf16[368,256]{1,0:T(8,128)(2,1)S(1)}, bf16[368,256]{1,0:T(8,128)(2,1)S(1)}, u32[]{:S(2)}, u32[]{:S(2)}) collective-permute-start(bf16[368,256]{1,0:T(8,128)(2,1)S(1)} %get-tuple-element.73), channel_id=1, source_target_pairs={{0,16},{8,24},{16,0},{24,8},{1,17},{9,25},{17,1},{25,9},{2,18},{10... | collective-permute-start | bytes 565256 | tf_op jit(solution)/shard_map/ppermute | solution.py:14
  32.5 4.6 %collective-permute-done.3.refs_1_ = bf16[384,256]{1,0:T(8,128)(2,1)S(1)} collective-permute-done((bf16[384,256]{1,0:T(8,128)(2,1)}, bf16[384,256]{1,0:T(8,128)(2,1)S(1)}, u32[]{:S(2)}, u32[]{:S(2)}) %collective-permute-start.3) | collective-permute-done | bytes 196640 | tf_op jit(solution)/shard_map/ppermute | solution.py:14
  37.1 1.1 shard_map.117
  38.3 0.5 collective-permute-start.10
  38.8 1.0 shard_map.118.part_ref
  39.8 0.1 collective-permute-done.7.head.got_head
  39.9 0.8 collective-permute-done.2.got_ref.refs_1_
  40.8 1.4 %shard_map.119 = (bf16[256,256]{1,0:T(8,128)(2,1)S(1)}, bf16[768,256]{1,0:T(8,128)(2,1)S(1)}, bf16[1168,256]{1,0:T(8,128)(2,1)S(1)}) custom-call(s32[7]{0:T(128)S(1)} %stack.31.where_ref, bf16[528,128]{1,0:T(8,128)(2,1)S(1)} %shard_map.113.own_ref.mine_ref, bf16[528,128]{1,0:T(8,128)(2,1)S(1)} %collective-permute-done.core_ref, ...), custom_call_target="tpu_custom_call" | custom-call | tf_op jit(solution)/shard_map/pallas_call | solution.py:234
  42.2 1.5 %collective-permute-start.8 = (bf16[1168,256]{1,0:T(8,128)(2,1)S(1)}, bf16[1168,256]{1,0:T(8,128)(2,1)S(1)}, u32[]{:S(2)}, u32[]{:S(2)}) collective-permute-start(bf16[1168,256]{1,0:T(8,128)(2,1)S(1)} %get-tuple-element.83), channel_id=1, source_target_pairs={{0,16},{8,24},{16,0},{24,8},{1,17},{9,25},{17,1},{25,9},{2,18},{10... | collective-permute-start | bytes 1794056 | tf_op jit(solution)/shard_map/ppermute | solution.py:14
  43.6 1.5 %collective-permute-start.9 = (bf16[512,256]{1,0:T(8,128)(2,1)S(1)}, bf16[512,256]{1,0:T(8,128)(2,1)S(1)}, u32[]{:S(2)}, u32[]{:S(2)}) collective-permute-start(bf16[512,256]{1,0:T(8,128)(2,1)S(1)} %get-tuple-element.79.own_ref), channel_id=1, source_target_pairs={{0,4},{4,0},{1,5},{5,1},{2,6},{6,2},{3,7},{7,3},{8,12},{12,8},{9,1... | collective-permute-start | bytes 786440 | tf_op jit(solution)/shard_map/ppermute | solution.py:14
  45.1 0.9 shard_map.121
  46.0 0.6 collective-permute-start.12
  46.6 0.5 collective-permute-start.15
  47.1 5.8 %collective-permute-done.9.got_ref = bf16[512,256]{1,0:T(8,128)(2,1)S(1)} collective-permute-done((bf16[512,256]{1,0:T(8,128)(2,1)S(1)}, bf16[512,256]{1,0:T(8,128)(2,1)S(1)}, u32[]{:S(2)}, u32[]{:S(2)}) %collective-permute-start.9) | collective-permute-done | bytes 262176 | tf_op jit(solution)/shard_map/ppermute | solution.py:14
  52.9 0.8 shard_map.120.refs_13_
  53.7 1.4 %shard_map.122 = (bf16[256,256]{1,0:T(8,128)(2,1)S(1)}, bf16[256,256]{1,0:T(8,128)(2,1)S(1)}, bf16[512,256]{1,0:T(8,128)(2,1)S(1)}) custom-call(s32[7]{0:T(128)S(1)} %stack.31.where_ref, bf16[528,128]{1,0:T(8,128)(2,1)S(1)} %shard_map.113.own_ref.mine_ref, bf16[528,128]{1,0:T(8,128)(2,1)S(1)} %collective-permute-done.core_ref, ...), custom_call_target="tpu_custom_call" | custom-call | tf_op jit(solution)/shard_map/pallas_call | solution.py:234
  55.1 0.7 collective-permute-start.11
  55.8 1.4 %collective-permute-done.14.refs_6_ = bf16[368,256]{1,0:T(8,128)(2,1)S(1)} collective-permute-done((bf16[368,256]{1,0:T(8,128)(2,1)S(1)}, bf16[368,256]{1,0:T(8,128)(2,1)S(1)}, u32[]{:S(2)}, u32[]{:S(2)}) %collective-permute-start.14) | collective-permute-done | bytes 188448 | tf_op jit(solution)/shard_map/ppermute | solution.py:14
  57.3 5.3 %collective-permute-done.11.refs_10_ = bf16[512,256]{1,0:T(8,128)(2,1)S(1)} collective-permute-done((bf16[512,256]{1,0:T(8,128)(2,1)S(1)}, bf16[512,256]{1,0:T(8,128)(2,1)S(1)}, u32[]{:S(2)}, u32[]{:S(2)}) %collective-permute-start.11) | collective-permute-done | bytes 262176 | tf_op jit(solution)/shard_map/ppermute | solution.py:14
  62.7 0.5 collective-permute-start.18
  63.2 1.3 %copy.12 = bf16[32,8,2,1024]{3,1,2,0:T(8,128)(2,1)} copy(bf16[32,8,2,1024]{3,2,1,0:T(2,128)(2,1)S(1)} %bitcast.34) | data formatting | bytes 2097152
  64.5 0.7 collective-permute-done.17.refs_11_
  65.2 4.3 %shard_map.123.own = bf16[256,1024]{1,0:T(8,128)(2,1)S(1)} custom-call(s32[7]{0:T(128)S(1)} %stack.31.where_ref, bf16[512,256]{1,0:T(8,128)(2,1)S(1)} %get-tuple-element.71.refs_0_, bf16[1024,256]{1,0:T(8,128)(2,1)S(1)} %collective-permute-done.2.got_ref.refs_1_, bf16[368,256]{1,0:T(8,128)(2,1)S(1)} %collective-permute-done.6.refs_2_, ...), custom_call_target="tpu_custom_call" | custom-call | tf_op jit(solution)/shard_map/pallas_call | solution.py:485
  69.5 1.5 %collective-permute-start.19 = (bf16[256,1024]{1,0:T(8,128)(2,1)S(1)}, bf16[256,1024]{1,0:T(8,128)(2,1)S(1)}, u32[]{:S(2)}, u32[]{:S(2)}) collective-permute-start(bf16[256,1024]{1,0:T(8,128)(2,1)S(1)} %shard_map.123.own), channel_id=1, source_target_pairs={{0,4},{4,0},{1,5},{5,1},{2,6},{6,2},{3,7},{7,3},{8,12},{12,8},{9,1... | collective-permute-start | bytes 1572872 | tf_op jit(solution)/shard_map/ppermute | solution.py:14
  71.1 1.0 shard_map.124.part_ref
  72.1 11.5 %collective-permute-done.19.got = bf16[256,1024]{1,0:T(8,128)(2,1)S(1)} collective-permute-done((bf16[256,1024]{1,0:T(8,128)(2,1)S(1)}, bf16[256,1024]{1,0:T(8,128)(2,1)S(1)}, u32[]{:S(2)}, u32[]{:S(2)}) %collective-permute-start.19) | collective-permute-done | bytes 524320 | tf_op jit(solution)/shard_map/ppermute | solution.py:14
  83.5 1.0 shard_map.125
  84.7 1.6 %shard_map.127 = (bf16[512,512]{1,0:T(8,128)(2,1)S(1)}, bf16[4,128,128]{2,1,0:T(8,128)(2,1)S(1)}) custom-call(s32[7]{0:T(128)S(1)} %stack.31.where_ref, bf16[256,1024]{1,0:T(8,128)(2,1)S(1)} %shard_map.123.own, bf16[256,1024]{1,0:T(8,128)(2,1)S(1)} %collective-permute-done.19.got, bf16[160,1024]{1,0:T(8,128)(2,1)S(1)} %get-tuple-element.78.head_ref.head, ...), custom_call_target="tpu_custom_call" | custom-call | tf_op jit(solution)/shard_map/pallas_call | solution.py:234
  86.3 0.3 collective-permute-done.20.got_ref
  86.6 0.6 shard_map.126
  87.2 0.3 collective-permute-start.22
  87.5 1.5 %collective-permute-start.21 = (bf16[128,1024]{1,0:T(8,128)(2,1)S(1)}, bf16[128,1024]{1,0:T(8,128)(2,1)S(1)}, u32[]{:S(2)}, u32[]{:S(2)}) collective-permute-start(bf16[128,1024]{1,0:T(8,128)(2,1)S(1)} %get-tuple-element.102), channel_id=1, source_target_pairs={{0,16},{8,24},{16,0},{24,8},{1,17},{9,25},{17,1},{25,9},{2,18},{10... | collective-permute-start | bytes 786440 | tf_op jit(solution)/shard_map/ppermute | solution.py:14
  89.0 3.2 %shard_map.128 = (f32[512,512]{1,0:T(8,128)S(1)}, f32[512,512]{1,0:T(8,128)S(1)}) custom-call(s32[7]{0:T(128)S(1)} %stack.31.where_ref, bf16[512,512]{1,0:T(8,128)(2,1)S(1)} %get-tuple-element.103.g_ref, bf16[512,512]{1,0:T(8,128)(2,1)S(1)} %bitcast.31, bf16[512,512]{1,0:T(8,128)(2,1)S(1)} %bitcast.21, bf16[512,512]{1,0:T(8,128)(2,1)S(1)} %bitcast.26), custom_call_target="tpu_custom_call" | custom-call | tf_op jit(solution)/shard_map/pallas_call | solution.py:234
  92.2 2.7 %shard_map.129 = bf16[512,512]{1,0:T(8,128)(2,1)} custom-call(s32[7]{0:T(128)S(1)} %stack.31.where_ref, bf16[512,512]{1,0:T(8,128)(2,1)S(1)} %get-tuple-element.103.g_ref, bf16[512,512]{1,0:T(8,128)(2,1)S(1)} %bitcast.22, bf16[512,512]{1,0:T(8,128)(2,1)S(1)} %bitcast.27, bf16[4,128,128]{2,1,0:T(8,128)(2,1)S(1)} %copy-done.5), custom_call_target="tpu_custom_call" | custom-call | tf_op jit(solution)/shard_map/pallas_call | solution.py:234
  95.0 1.0 collective-permute-done.21.got_ref
  96.0 0.6 shard_map.130
  96.6 5.3 %collective-permute-start.23 = (bf16[128,256]{1,0:T(8,128)(2,1)S(1)}, bf16[128,256]{1,0:T(8,128)(2,1)S(1)}, u32[]{:S(2)}, u32[]{:S(2)}) collective-permute-start(bf16[128,256]{1,0:T(8,128)(2,1)S(1)} %get-tuple-element.115), channel_id=1, source_target_pairs={{0,3},{1,2},{2,1},{3,0},{4,7},{5,6},{6,5},{7,4},{8,11},{9,10},{10,... | collective-permute-start | bytes 196616 | tf_op jit(solution)/shard_map/ppermute | solution.py:14
  101.9 1.7 %collective-permute-start.29 = (bf16[4,128,128]{2,1,0:T(8,128)(2,1)S(1)}, bf16[4,128,128]{2,1,0:T(8,128)(2,1)S(1)}, u32[]{:S(2)}, u32[]{:S(2)}) collective-permute-start(bf16[4,128,128]{2,1,0:T(8,128)(2,1)S(1)} %add_convert_fusion), channel_id=1, source_target_pairs={{0,16},{8,24},{16,0},{24,8},{1,17},{9,25},{17,1},{25,9},{2,18},{10... | collective-permute-start | bytes 393224 | tf_op jit(solution)/shard_map/ppermute | solution.py:14
  103.6 0.6 collective-permute-start.25
  104.3 0.4 collective-permute-done.23.refs_0_
  104.6 3.0 %collective-permute-done.24.refs_1_ = bf16[128,256]{1,0:T(8,128)(2,1)S(1)} collective-permute-done((bf16[128,256]{1,0:T(8,128)(2,1)S(1)}, bf16[128,256]{1,0:T(8,128)(2,1)S(1)}, u32[]{:S(2)}, u32[]{:S(2)}) %collective-permute-start.24) | collective-permute-done | bytes 65568 | tf_op jit(solution)/shard_map/ppermute | solution.py:14
  107.6 0.7 collective-permute-done.25.refs_2_
  108.3 0.6 shard_map.131.refs_0_
  108.8 1.2 %collective-permute-start.26 = (bf16[128,256]{1,0:T(8,128)(2,1)S(1)}, bf16[128,256]{1,0:T(8,128)(2,1)S(1)}, u32[]{:S(2)}, u32[]{:S(2)}) collective-permute-start(bf16[128,256]{1,0:T(8,128)(2,1)S(1)} %shard_map.131.refs_0_), channel_id=1, source_target_pairs={{0,16},{8,24},{16,0},{24,8},{1,17},{9,25},{17,1},{25,9},{2,18},{10... | collective-permute-start | bytes 196616 | tf_op jit(solution)/shard_map/ppermute | solution.py:14
  110.1 1.0 collective-permute-start.28
  111.1 2.0 %shard_map.132 = (bf16[512,512]{1,0:T(8,128)(2,1)}, bf16[512,512]{1,0:T(8,128)(2,1)}) custom-call(s32[7]{0:T(128)S(1)} %stack.31.where_ref, f32[512,512]{1,0:T(8,128)S(1)} %get-tuple-element.119.kp_ref, f32[512,512]{1,0:T(8,128)S(1)} %get-tuple-element.120.vp_ref, bf16[512,512]{1,0:T(8,128)(2,1)S(1)} %bitcast.23, bf16[512,512]{1,0:T(8,128)(2,1)S(1)} %bitcast.28, ...), custom_call_target="tpu_custom_call" | custom-call | tf_op jit(solution)/shard_map/pallas_call | solution.py:234
  113.1 0.3 collective-permute-done.26.refs_1_
  113.4 0.7 collective-permute-done.28.refs_3_
  114.1 1.4 %shard_map.133 = f32[512,256]{1,0:T(8,128)} custom-call(s32[7]{0:T(128)S(1)} %stack.31.where_ref, bf16[128,256]{1,0:T(8,128)(2,1)S(1)} %shard_map.131.refs_0_, bf16[128,256]{1,0:T(8,128)(2,1)S(1)} %collective-permute-done.26.refs_1_, bf16[128,256]{1,0:T(8,128)(2,1)S(1)} %collective-permute-done.27.refs_2_, bf16[128,256]{1,0:T(8,128)(2,1)S(1)} %collective-permute-done.28.refs_3_), custom_call_target="tpu_custom_call" | custom-call | tf_op jit(solution)/shard_map/pallas_call | solution.py:234
  (40 shorter events, 0.5 us)
Async XLA Ops:
  0.6 10.0 %copy-start = (bf16[1,512,512]{2,1,0:T(8,128)(2,1)S(1)}, bf16[1,512,512]{2,1,0:T(8,128)(2,1)}, u32[]{:S(2)}) copy-start(bf16[1,512,512]{2,1,0:T(8,128)(2,1)} %param.9) | copy-start | bytes 1572868
  0.6 10.0 %copy-start.1 = (bf16[1,512,512]{2,1,0:T(8,128)(2,1)S(1)}, bf16[1,512,512]{2,1,0:T(8,128)(2,1)}, u32[]{:S(2)}) copy-start(bf16[1,512,512]{2,1,0:T(8,128)(2,1)} %param.10) | copy-start | bytes 1572868
  0.7 10.0 %copy-start.6 = (s32[1,256,2]{1,2,0:T(2,128)S(1)}, s32[1,256,2]{1,2,0:T(2,128)}, u32[]{:S(2)}) copy-start(s32[1,256,2]{1,2,0:T(2,128)} %param.14) | copy-start | bytes 6148
  2.5 17.1 %copy-start.2 = (bf16[1,512,512]{2,1,0:T(8,128)(2,1)S(1)}, bf16[1,512,512]{2,1,0:T(8,128)(2,1)}, u32[]{:S(2)}) copy-start(bf16[1,512,512]{2,1,0:T(8,128)(2,1)} %param.8) | copy-start | bytes 1572868
  2.5 26.2 %all-to-all-start = ((bf16[4,256,256]{2,1,0:T(8,128)(2,1)}), bf16[4,256,256]{2,1,0:T(8,128)(2,1)S(1)}, u32[]{:S(2)}, u32[]{:S(2)}) async-start(bf16[4,256,256]{2,1,0:T(8,128)(2,1)} %shard_map.111.refs_2_), calls=%async_computation | async-start | bytes 1048576 | tf_op jit(solution)/shard_map/all_to_all | solution.py:789
  10.6 26.5 %copy-start.3 = (bf16[384,256]{1,0:T(8,128)(2,1)S(1)}, bf16[384,256]{1,0:T(8,128)(2,1)}, u32[]{:S(2)}) copy-start(bf16[384,256]{1,0:T(8,128)(2,1)} %shard_map.112.refs_0_) | copy-start | bytes 589828
  11.6 1.4 %collective-permute-start = (bf16[528,128]{1,0:T(8,128)(2,1)S(1)}, bf16[528,128]{1,0:T(8,128)(2,1)S(1)}, u32[]{:S(2)}, u32[]{:S(2)}) collective-permute-start(bf16[528,128]{1,0:T(8,128)(2,1)S(1)} %shard_map.113.own_ref.mine_ref), channel_id=1, source_target_pairs={{0,8},{8,0},{16,24},{24,16},{1,9},{9,1},{17,25},{25,17},{2,10},{10... | collective-permute-start | bytes 405512 | tf_op jit(solution)/shard_map/ppermute | solution.py:14
  13.6 6.0 %collective-permute-start.1 = (bf16[544,128]{1,0:T(8,128)(2,1)S(1)}, bf16[544,128]{1,0:T(8,128)(2,1)S(1)}, u32[]{:S(2)}, u32[]{:S(2)}) collective-permute-start(bf16[544,128]{1,0:T(8,128)(2,1)S(1)} %shard_map.114), channel_id=1, source_target_pairs={{0,16},{8,24},{16,0},{24,8},{1,17},{9,25},{17,1},{25,9},{2,18},{10... | collective-permute-start | bytes 417800 | tf_op jit(solution)/shard_map/ppermute | solution.py:14
  15.2 21.9 %collective-permute-start.3 = (bf16[384,256]{1,0:T(8,128)(2,1)}, bf16[384,256]{1,0:T(8,128)(2,1)S(1)}, u32[]{:S(2)}, u32[]{:S(2)}) collective-permute-start(bf16[384,256]{1,0:T(8,128)(2,1)} %shard_map.112.refs_0_), channel_id=1, source_target_pairs={{0,2},{1,3},{2,0},{3,1},{4,6},{5,7},{6,4},{7,5},{8,10},{9,11},{10,... | collective-permute-start | bytes 589832 | tf_op jit(solution)/shard_map/ppermute | solution.py:14
  18.1 19.0 %collective-permute-start.4 = (bf16[384,256]{1,0:T(8,128)(2,1)}, bf16[384,256]{1,0:T(8,128)(2,1)}, u32[]{:S(2)}, u32[]{:S(2)}) collective-permute-start(bf16[384,256]{1,0:T(8,128)(2,1)} %shard_map.112.refs_0_), channel_id=1, source_target_pairs={{0,1},{1,0},{2,3},{3,2},{4,5},{5,4},{6,7},{7,6},{8,9},{9,8},{10,11... | collective-permute-start | bytes 589832 | tf_op jit(solution)/shard_map/ppermute | solution.py:14
  19.6 17.6 %collective-permute-start.5 = (bf16[384,256]{1,0:T(8,128)(2,1)}, bf16[384,256]{1,0:T(8,128)(2,1)}, u32[]{:S(2)}, u32[]{:S(2)}) collective-permute-start(bf16[384,256]{1,0:T(8,128)(2,1)} %shard_map.112.refs_0_), channel_id=1, source_target_pairs={{0,3},{1,2},{2,1},{3,0},{4,7},{5,6},{6,5},{7,4},{8,11},{9,10},{10,... | collective-permute-start | bytes 589832 | tf_op jit(solution)/shard_map/ppermute | solution.py:14
  21.5 0.7 copy-start.4
  29.3 11.4 %collective-permute-start.2 = (bf16[1024,256]{1,0:T(8,128)(2,1)S(1)}, bf16[1024,256]{1,0:T(8,128)(2,1)S(1)}, u32[]{:S(2)}, u32[]{:S(2)}) collective-permute-start(bf16[1024,256]{1,0:T(8,128)(2,1)S(1)} %get-tuple-element.72.own_ref), channel_id=1, source_target_pairs={{0,4},{4,0},{1,5},{5,1},{2,6},{6,2},{3,7},{7,3},{8,12},{12,8},{9,1... | collective-permute-start | bytes 1572872 | tf_op jit(solution)/shard_map/ppermute | solution.py:14
  30.9 6.2 %collective-permute-start.6 = (bf16[368,256]{1,0:T(8,128)(2,1)S(1)}, bf16[368,256]{1,0:T(8,128)(2,1)S(1)}, u32[]{:S(2)}, u32[]{:S(2)}) collective-permute-start(bf16[368,256]{1,0:T(8,128)(2,1)S(1)} %get-tuple-element.73), channel_id=1, source_target_pairs={{0,16},{8,24},{16,0},{24,8},{1,17},{9,25},{17,1},{25,9},{2,18},{10... | collective-permute-start | bytes 565256 | tf_op jit(solution)/shard_map/ppermute | solution.py:14
  38.2 1.7 %collective-permute-start.7 = (bf16[160,1024]{1,0:T(8,128)(2,1)S(1)}, bf16[160,1024]{1,0:T(8,128)(2,1)S(1)}, u32[]{:S(2)}, u32[]{:S(2)}) collective-permute-start(bf16[160,1024]{1,0:T(8,128)(2,1)S(1)} %get-tuple-element.78.head_ref.head), channel_id=1, source_target_pairs={{0,8},{8,0},{16,24},{24,16},{1,9},{9,1},{17,25},{25,17},{2,10},{10... | collective-permute-start | bytes 983048 | tf_op jit(solution)/shard_map/ppermute | solution.py:14
  38.3 6.8 %collective-permute-start.10 = (bf16[96,1024]{1,0:T(8,128)(2,1)S(1)}, bf16[96,1024]{1,0:T(8,128)(2,1)S(1)}, u32[]{:S(2)}, u32[]{:S(2)}) collective-permute-start(bf16[96,1024]{1,0:T(8,128)(2,1)S(1)} %get-tuple-element.80.tail_ref.tail), channel_id=1, source_target_pairs={{0,8},{8,0},{16,24},{24,16},{1,9},{9,1},{17,25},{25,17},{2,10},{10... | collective-permute-start | bytes 589832 | tf_op jit(solution)/shard_map/ppermute | solution.py:14
  42.2 20.4 %collective-permute-start.8 = (bf16[1168,256]{1,0:T(8,128)(2,1)S(1)}, bf16[1168,256]{1,0:T(8,128)(2,1)S(1)}, u32[]{:S(2)}, u32[]{:S(2)}) collective-permute-start(bf16[1168,256]{1,0:T(8,128)(2,1)S(1)} %get-tuple-element.83), channel_id=1, source_target_pairs={{0,16},{8,24},{16,0},{24,8},{1,17},{9,25},{17,1},{25,9},{2,18},{10... | collective-permute-start | bytes 1794056 | tf_op jit(solution)/shard_map/ppermute | solution.py:14
  43.6 9.2 %collective-permute-start.9 = (bf16[512,256]{1,0:T(8,128)(2,1)S(1)}, bf16[512,256]{1,0:T(8,128)(2,1)S(1)}, u32[]{:S(2)}, u32[]{:S(2)}) collective-permute-start(bf16[512,256]{1,0:T(8,128)(2,1)S(1)} %get-tuple-element.79.own_ref), channel_id=1, source_target_pairs={{0,4},{4,0},{1,5},{5,1},{2,6},{6,2},{3,7},{7,3},{8,12},{12,8},{9,1... | collective-permute-start | bytes 786440 | tf_op jit(solution)/shard_map/ppermute | solution.py:14
  46.0 16.6 %collective-permute-start.12 = (bf16[256,1024]{1,0:T(8,128)(2,1)S(1)}, bf16[256,1024]{1,0:T(8,128)(2,1)S(1)}, u32[]{:S(2)}, u32[]{:S(2)}) collective-permute-start(bf16[256,1024]{1,0:T(8,128)(2,1)S(1)} %shard_map.121), channel_id=1, source_target_pairs={{0,4},{4,0},{1,5},{5,1},{2,6},{6,2},{3,7},{7,3},{8,12},{12,8},{9,1... | collective-permute-start | bytes 1572872 | tf_op jit(solution)/shard_map/ppermute | solution.py:14
  46.6 9.3 %collective-permute-start.13 = (bf16[512,256]{1,0:T(8,128)(2,1)S(1)}, bf16[512,256]{1,0:T(8,128)(2,1)S(1)}, u32[]{:S(2)}, u32[]{:S(2)}) collective-permute-start(bf16[512,256]{1,0:T(8,128)(2,1)S(1)} %get-tuple-element.71.refs_0_), channel_id=1, source_target_pairs={{0,8},{8,0},{16,24},{24,16},{1,9},{9,1},{17,25},{25,17},{2,10},{10... | collective-permute-start | bytes 786440 | tf_op jit(solution)/shard_map/ppermute | solution.py:14
  46.6 16.7 %copy-start.7 = (bf16[1,256,2,1024]{3,2,1,0:T(2,128)(2,1)S(1)}, bf16[1,256,2,1024]{3,2,1,0:T(2,128)(2,1)}, u32[]{:S(2)}) copy-start(bf16[1,256,2,1024]{3,2,1,0:T(2,128)(2,1)} %param.15) | copy-start | bytes 3145732
  46.6 16.0 %collective-permute-start.15 = (bf16[768,256]{1,0:T(8,128)(2,1)S(1)}, bf16[768,256]{1,0:T(8,128)(2,1)S(1)}, u32[]{:S(2)}, u32[]{:S(2)}) collective-permute-start(bf16[768,256]{1,0:T(8,128)(2,1)S(1)} %get-tuple-element.90), channel_id=1, source_target_pairs={{0,8},{8,0},{16,24},{24,16},{1,9},{9,1},{17,25},{25,17},{2,10},{10... | collective-permute-start | bytes 1179656 | tf_op jit(solution)/shard_map/ppermute | solution.py:14
  55.1 7.5 %collective-permute-start.11 = (bf16[512,256]{1,0:T(8,128)(2,1)S(1)}, bf16[512,256]{1,0:T(8,128)(2,1)S(1)}, u32[]{:S(2)}, u32[]{:S(2)}) collective-permute-start(bf16[512,256]{1,0:T(8,128)(2,1)S(1)} %get-tuple-element.89), channel_id=1, source_target_pairs={{0,16},{8,24},{16,0},{24,8},{1,17},{9,25},{17,1},{25,9},{2,18},{10... | collective-permute-start | bytes 786440 | tf_op jit(solution)/shard_map/ppermute | solution.py:14
  55.8 1.4 %collective-permute-start.14 = (bf16[368,256]{1,0:T(8,128)(2,1)S(1)}, bf16[368,256]{1,0:T(8,128)(2,1)S(1)}, u32[]{:S(2)}, u32[]{:S(2)}) collective-permute-start(bf16[368,256]{1,0:T(8,128)(2,1)S(1)} %collective-permute-done.6.refs_2_), channel_id=1, source_target_pairs={{0,8},{8,0},{16,24},{24,16},{1,9},{9,1},{17,25},{25,17},{2,10},{10... | collective-permute-start | bytes 565256 | tf_op jit(solution)/shard_map/ppermute | solution.py:14
  62.6 2.6 %collective-permute-start.16 = (bf16[1168,256]{1,0:T(8,128)(2,1)S(1)}, bf16[1168,256]{1,0:T(8,128)(2,1)S(1)}, u32[]{:S(2)}, u32[]{:S(2)}) collective-permute-start(bf16[1168,256]{1,0:T(8,128)(2,1)S(1)} %collective-permute-done.8.refs_3_), channel_id=1, source_target_pairs={{0,8},{8,0},{16,24},{24,16},{1,9},{9,1},{17,25},{25,17},{2,10},{10... | collective-permute-start | bytes 1794056 | tf_op jit(solution)/shard_map/ppermute | solution.py:14
  62.7 2.6 %collective-permute-start.18 = (bf16[512,256]{1,0:T(8,128)(2,1)S(1)}, bf16[512,256]{1,0:T(8,128)(2,1)S(1)}, u32[]{:S(2)}, u32[]{:S(2)}) collective-permute-start(bf16[512,256]{1,0:T(8,128)(2,1)S(1)} %collective-permute-done.11.refs_10_), channel_id=1, source_target_pairs={{0,8},{8,0},{16,24},{24,16},{1,9},{9,1},{17,25},{25,17},{2,10},{10... | collective-permute-start | bytes 786440 | tf_op jit(solution)/shard_map/ppermute | solution.py:14
  63.2 2.1 %collective-permute-start.17 = (bf16[256,256]{1,0:T(8,128)(2,1)S(1)}, bf16[256,256]{1,0:T(8,128)(2,1)S(1)}, u32[]{:S(2)}, u32[]{:S(2)}) collective-permute-start(bf16[256,256]{1,0:T(8,128)(2,1)S(1)} %get-tuple-element.98), channel_id=1, source_target_pairs={{0,8},{8,0},{16,24},{24,16},{1,9},{9,1},{17,25},{25,17},{2,10},{10... | collective-permute-start | bytes 393224 | tf_op jit(solution)/shard_map/ppermute | solution.py:14
  69.5 14.0 %collective-permute-start.19 = (bf16[256,1024]{1,0:T(8,128)(2,1)S(1)}, bf16[256,1024]{1,0:T(8,128)(2,1)S(1)}, u32[]{:S(2)}, u32[]{:S(2)}) collective-permute-start(bf16[256,1024]{1,0:T(8,128)(2,1)S(1)} %shard_map.123.own), channel_id=1, source_target_pairs={{0,4},{4,0},{1,5},{5,1},{2,6},{6,2},{3,7},{7,3},{8,12},{12,8},{9,1... | collective-permute-start | bytes 1572872 | tf_op jit(solution)/shard_map/ppermute | solution.py:14
  84.6 2.0 %collective-permute-start.20 = (bf16[2,128,1024]{2,1,0:T(8,128)(2,1)S(1)}, bf16[2,128,1024]{2,1,0:T(8,128)(2,1)S(1)}, u32[]{:S(2)}, u32[]{:S(2)}) collective-permute-start(bf16[2,128,1024]{2,1,0:T(8,128)(2,1)S(1)} %get-tuple-element.101), channel_id=1, source_target_pairs={{0,8},{8,0},{16,24},{24,16},{1,9},{9,1},{17,25},{25,17},{2,10},{10... | collective-permute-start | bytes 1572872 | tf_op jit(solution)/shard_map/ppermute | solution.py:14
  86.3 5.9 %copy-start.5 = (bf16[4,128,128]{2,1,0:T(8,128)(2,1)S(1)}, bf16[4,128,128]{2,1,0:T(8,128)(2,1)}, u32[]{:S(2)}) copy-start(bf16[4,128,128]{2,1,0:T(8,128)(2,1)} %copy-done.4) | copy-start | bytes 393220
  87.2 7.8 %collective-permute-start.22 = (bf16[4,128,128]{2,1,0:T(8,128)(2,1)S(1)}, bf16[4,128,128]{2,1,0:T(8,128)(2,1)S(1)}, u32[]{:S(2)}, u32[]{:S(2)}) collective-permute-start(bf16[4,128,128]{2,1,0:T(8,128)(2,1)S(1)} %get-tuple-element.108), channel_id=1, source_target_pairs={{0,8},{8,0},{16,24},{24,16},{1,9},{9,1},{17,25},{25,17},{2,10},{10... | collective-permute-start | bytes 393224 | tf_op jit(solution)/shard_map/ppermute | solution.py:14
  87.5 8.5 %collective-permute-start.21 = (bf16[128,1024]{1,0:T(8,128)(2,1)S(1)}, bf16[128,1024]{1,0:T(8,128)(2,1)S(1)}, u32[]{:S(2)}, u32[]{:S(2)}) collective-permute-start(bf16[128,1024]{1,0:T(8,128)(2,1)S(1)} %get-tuple-element.102), channel_id=1, source_target_pairs={{0,16},{8,24},{16,0},{24,8},{1,17},{9,25},{17,1},{25,9},{2,18},{10... | collective-permute-start | bytes 786440 | tf_op jit(solution)/shard_map/ppermute | solution.py:14
  96.6 8.0 %collective-permute-start.23 = (bf16[128,256]{1,0:T(8,128)(2,1)S(1)}, bf16[128,256]{1,0:T(8,128)(2,1)S(1)}, u32[]{:S(2)}, u32[]{:S(2)}) collective-permute-start(bf16[128,256]{1,0:T(8,128)(2,1)S(1)} %get-tuple-element.115), channel_id=1, source_target_pairs={{0,3},{1,2},{2,1},{3,0},{4,7},{5,6},{6,5},{7,4},{8,11},{9,10},{10,... | collective-permute-start | bytes 196616 | tf_op jit(solution)/shard_map/ppermute | solution.py:14
  101.9 5.7 %collective-permute-start.24 = (bf16[128,256]{1,0:T(8,128)(2,1)S(1)}, bf16[128,256]{1,0:T(8,128)(2,1)S(1)}, u32[]{:S(2)}, u32[]{:S(2)}) collective-permute-start(bf16[128,256]{1,0:T(8,128)(2,1)S(1)} %get-tuple-element.116), channel_id=1, source_target_pairs={{0,2},{1,3},{2,0},{3,1},{4,6},{5,7},{6,4},{7,5},{8,10},{9,11},{10,... | collective-permute-start | bytes 196616 | tf_op jit(solution)/shard_map/ppermute | solution.py:14
  101.9 9.1 %collective-permute-start.29 = (bf16[4,128,128]{2,1,0:T(8,128)(2,1)S(1)}, bf16[4,128,128]{2,1,0:T(8,128)(2,1)S(1)}, u32[]{:S(2)}, u32[]{:S(2)}) collective-permute-start(bf16[4,128,128]{2,1,0:T(8,128)(2,1)S(1)} %add_convert_fusion), channel_id=1, source_target_pairs={{0,16},{8,24},{16,0},{24,8},{1,17},{9,25},{17,1},{25,9},{2,18},{10... | collective-permute-start | bytes 393224 | tf_op jit(solution)/shard_map/ppermute | solution.py:14
  103.6 4.6 %collective-permute-start.25 = (bf16[128,256]{1,0:T(8,128)(2,1)S(1)}, bf16[128,256]{1,0:T(8,128)(2,1)S(1)}, u32[]{:S(2)}, u32[]{:S(2)}) collective-permute-start(bf16[128,256]{1,0:T(8,128)(2,1)S(1)} %get-tuple-element.117), channel_id=1, source_target_pairs={{0,1},{1,0},{2,3},{3,2},{4,5},{5,4},{6,7},{7,6},{8,9},{9,8},{10,11... | collective-permute-start | bytes 196616 | tf_op jit(solution)/shard_map/ppermute | solution.py:14
  108.8 4.5 %collective-permute-start.26 = (bf16[128,256]{1,0:T(8,128)(2,1)S(1)}, bf16[128,256]{1,0:T(8,128)(2,1)S(1)}, u32[]{:S(2)}, u32[]{:S(2)}) collective-permute-start(bf16[128,256]{1,0:T(8,128)(2,1)S(1)} %shard_map.131.refs_0_), channel_id=1, source_target_pairs={{0,16},{8,24},{16,0},{24,8},{1,17},{9,25},{17,1},{25,9},{2,18},{10... | collective-permute-start | bytes 196616 | tf_op jit(solution)/shard_map/ppermute | solution.py:14
  110.1 3.3 %collective-permute-start.27 = (bf16[128,256]{1,0:T(8,128)(2,1)S(1)}, bf16[128,256]{1,0:T(8,128)(2,1)S(1)}, u32[]{:S(2)}, u32[]{:S(2)}) collective-permute-start(bf16[128,256]{1,0:T(8,128)(2,1)S(1)} %shard_map.131.refs_0_), channel_id=1, source_target_pairs={{0,8},{8,0},{16,24},{24,16},{1,9},{9,1},{17,25},{25,17},{2,10},{10... | collective-permute-start | bytes 196616 | tf_op jit(solution)/shard_map/ppermute | solution.py:14
  110.1 4.0 %collective-permute-start.28 = (bf16[128,256]{1,0:T(8,128)(2,1)S(1)}, bf16[128,256]{1,0:T(8,128)(2,1)S(1)}, u32[]{:S(2)}, u32[]{:S(2)}) collective-permute-start(bf16[128,256]{1,0:T(8,128)(2,1)S(1)} %shard_map.131.refs_0_), channel_id=1, source_target_pairs={{0,24},{8,16},{16,8},{24,0},{1,25},{9,17},{17,9},{25,1},{2,26},{10... | collective-permute-start | bytes 196616 | tf_op jit(solution)/shard_map/ppermute | solution.py:14

commit v7 on v6

--- a/solution.py
+++ b/solution.py
@@ -357,7 +357,7 @@
     return run(body, outs, where, *pieces)
 
 
-def embed(where, packed, top, level, n_level, tokens, own, got, half, n_dp, late):
+def embed(where, packed, top, level, n_level, tokens, own, got, half, n_dp, late, away):
     folds = tokens // DH
     n_rows = id_rows(n_level, tokens)
     rows, cols = own.shape
@@ -377,7 +377,7 @@
         base = owner * rows_dev + place % rows_dev
         rows_of = [(mine_ref, top), (core_ref, top), (far_ref, top), (far_ref, top + n_rows)]
         columns = jnp.concatenate([ids_of(*r) for r in rows_of], axis=0).T.astype(jnp.int32)
-        for m in (2, 3, 1, 0):
+        for m in (2, 3) if away else (1, 0):
             col = columns[:, m:m + 1]
             total = None
             for k, ref in enumerate((own_ref, got_ref)):
@@ -386,16 +386,20 @@
                 part = jnp.dot(hot, ref[:half], preferred_element_type=F32)
                 total = part if total is None else total + part
             total = total.astype(BF16)
-            if m < 2:
+            if away:
+                outs[0][(m - 2) * tokens:(m - 1) * tokens, :] = total
+            else:
                 outs[m][:tokens] = total
-            else:
-                outs[2][(m - 2) * tokens:(m - 1) * tokens, :] = total
-        if extra:
+        if extra and away:
+            outs[0][2 * tokens:2 * tokens + extra] = got_ref[half:]
+            outs[0][2 * tokens + extra:] = own_ref[rows - late:]
+        elif extra:
             outs[1][tokens:] = got_ref[half:]
-            outs[2][2 * tokens:2 * tokens + extra] = got_ref[half:]
-            outs[2][2 * tokens + extra:] = own_ref[rows - late:]
-
-    outs = [shaped((tokens, cols)), shaped((tokens + extra, cols)), shaped((2 * tokens + extra + late, cols))]
+
+    if away:
+        outs = [shaped((2 * tokens + extra + late, cols))]
+    else:
+        outs = [shaped((tokens, cols)), shaped((tokens + extra, cols))]
     return run(body, outs, where, *packed, own, got)
 
 
@@ -815,8 +819,8 @@
     got_1 = swap(part_1, "head", 1)
 
     mixed_part = mix_own(where, attended, out_head, out_tail)
-    got_0, got_head, _, _ = lax.optimization_barrier((got_0, got_head, part_1, mixed_part))
-    own_0, to_core, to_far = embed(where, packed, top, 0, 2, tokens, part_0, got_0, half, n_dp, late)
+    got_0, got_head, _ = lax.optimization_barrier((got_0, got_head, part_1))
+    (to_far,) = embed(where, packed, top, 0, 2, tokens, part_0, got_0, half, n_dp, late, True)
     far_0 = far_swap(to_far)
 
     got_tail, _ = lax.optimization_barrier((got_tail, to_far))
@@ -824,14 +828,18 @@
     mixed_got = swap(mixed_send, "head", 1)
     mixed_part, got_1 = lax.optimization_barrier((mixed_part, got_1))
     mixed = mix(where, attended, mixed_part, got_head, got_tail, False)
+    near_0, _, _ = lax.optimization_barrier((got_0, mixed, mixed_send))
+    own_0, to_core = embed(where, packed, top, 0, 2, tokens, part_0, near_0, half, n_dp, late, False)
     core_0 = core_swap(to_core)
 
     got_1, _, _ = lax.optimization_barrier((got_1, mixed, mixed_send))
-    own_1, to_core, to_far = embed(where, packed, top, 1, 2, tokens, part_1, got_1, half, n_dp, 0)
+    (to_far,) = embed(where, packed, top, 1, 2, tokens, part_1, got_1, half, n_dp, 0, True)
+    near_1, _ = lax.optimization_barrier((got_1, to_far))
+    own_1, to_core = embed(where, packed, top, 1, 2, tokens, part_1, near_1, half, n_dp, 0, False)
     far_1 = far_swap(to_far)
     depth_core, depth_core_far = core_swap(depth_part), core_swap(depth_far)
-    far_0, far_1, mixed_got, depth_core, depth_core_far, core_0 = lax.optimization_barrier(
-        (far_0, far_1, mixed_got, depth_core, depth_core_far, core_0)
+    far_0, far_1, mixed_got, depth_core, depth_core_far, core_0, to_core, own_1 = lax.optimization_barrier(
+        (far_0, far_1, mixed_got, depth_core, depth_core_far, core_0, to_core, own_1)
     )
     core_far_0, core_1, core_far_1 = core_swap(far_0), core_swap(to_core), core_swap(far_1)
 

time: 116 us -> 115 us (level)
  waiting for transfers between devices: 44.3 us -> 40 us
  starting transfers between devices: 35 us -> 37.4 us
  Pallas kernels: 33.1 us -> 34.7 us
    ppermute x30, waiting for transfers between devices: 37.8 us -> 33.5 us  [swap(): lax.ppermute(block, axis, [(i, i ^ mask) for i in range(lax.axis_size(axi...]
    ppermute x30, starting transfers between devices: 28.5 us -> 31 us  [swap(): lax.ppermute(block, axis, [(i, i ^ mask) for i in range(lax.axis_size(axi...]
    pallas_call x20 -> x22, Pallas kernels: 25.5 us -> 27.1 us  [run(): pl.pallas_call(body, out_shape=outs, in_specs=[pl.BlockSpec(memory_space=...]
  transfers between devices with their start and end apart: 31 -> 31, of which waited for: 17 -> 16; matrix products, arithmetic and copies ran while one was open for 1% -> 1% of each run, Pallas kernels for 20% -> 22%
where the time goes in v7:
time: 115 us
  waiting for transfers between devices  40 us (35%)
  starting transfers between devices  37.4 us (33%)
  Pallas kernels  34.7 us (30%)
  local copies, waits for them, and re-layouts  2.05 us (2%)
    ppermute x30, waiting for transfers between devices, swap(): lax.ppermute(block, axis, [(i, i ^ mask) for i in range(lax.axis_size(axi...  33.5 us
    ppermute x30, starting transfers between devices, swap(): lax.ppermute(block, axis, [(i, i ^ mask) for i in range(lax.axis_size(axi...  31 us
    pallas_call x22, Pallas kernels, run(): pl.pallas_call(body, out_shape=outs, in_specs=[pl.BlockSpec(memory_space=...  27.1 us
    all_to_all x1, waiting for transfers between devices, on_device(): pieces_0 = lax.all_to_all(lanes_0, 'dp', 0, 0)  6.48 us
    all_to_all x1, starting transfers between devices, on_device(): pieces_0 = lax.all_to_all(lanes_0, 'dp', 0, 0)  6.46 us
    pallas_call x1, Pallas kernels, depth_grad(): pl.pallas_call(body, out_shape=shaped((tokens, width)), in_specs=[pl.Bloc...  4.26 us
  transfers between devices with their start and end apart: 31, of which 16 were waited for; matrix products, arithmetic and copies ran while one was open for 1% of the time, Pallas kernels for 22%

profile of v7, /device:TPU:0, one launch (start us, length us, event | category | flops | bytes accessed | tf_op | source)
XLA Modules:
  0.0 115.2 jit_solution(12761295760029889240)
XLA Ops:
  0.7 1.8 %shard_map.111.refs_2_ = bf16[4,256,256]{2,1,0:T(8,128)(2,1)} custom-call(bf16[2,128,1024]{2,1,0:T(8,128)(2,1)} %refs_0_.1, bf16[1024,128]{1,0:T(8,128)(2,1)} %depth.1), custom_call_target="tpu_custom_call" | custom-call | tf_op jit(solution)/shard_map/pallas_call | solution.py:297
  2.5 6.5 %all-to-all-start = ((bf16[4,256,256]{2,1,0:T(8,128)(2,1)}), bf16[4,256,256]{2,1,0:T(8,128)(2,1)S(1)}, u32[]{:S(2)}, u32[]{:S(2)}) async-start(bf16[4,256,256]{2,1,0:T(8,128)(2,1)} %shard_map.111.refs_2_), calls=%async_computation | async-start | bytes 1048576 | tf_op jit(solution)/shard_map/all_to_all | solution.py:793
  8.9 1.6 %shard_map.112.refs_0_ = bf16[384,256]{1,0:T(8,128)(2,1)} custom-call(bf16[2,128,1024]{2,1,0:T(8,128)(2,1)} %refs_0_.1, bf16[512,256]{1,0:T(8,128)(2,1)} %refs_1_.1, bf16[4,256,256]{2,1,0:T(8,128)(2,1)} %shard_map.111.refs_2_), custom_call_target="tpu_custom_call" | custom-call | tf_op jit(solution)/shard_map/pallas_call | solution.py:271
  10.7 0.9 shard_map.113.own_ref.mine_ref
  11.7 1.3 %collective-permute-done.core_ref = bf16[528,128]{1,0:T(8,128)(2,1)S(1)} collective-permute-done((bf16[528,128]{1,0:T(8,128)(2,1)S(1)}, bf16[528,128]{1,0:T(8,128)(2,1)S(1)}, u32[]{:S(2)}, u32[]{:S(2)}) %collective-permute-start) | collective-permute-done | bytes 135200 | tf_op jit(solution)/shard_map/ppermute | solution.py:14
  13.0 0.6 shard_map.114
  13.6 1.6 %collective-permute-start.1 = (bf16[544,128]{1,0:T(8,128)(2,1)S(1)}, bf16[544,128]{1,0:T(8,128)(2,1)S(1)}, u32[]{:S(2)}, u32[]{:S(2)}) collective-permute-start(bf16[544,128]{1,0:T(8,128)(2,1)S(1)} %shard_map.114), channel_id=1, source_target_pairs={{0,16},{8,24},{16,0},{24,8},{1,17},{9,25},{17,1},{25,9},{2,18},{10... | collective-permute-start | bytes 417800 | tf_op jit(solution)/shard_map/ppermute | solution.py:14
  15.2 2.9 %collective-permute-start.3 = (bf16[384,256]{1,0:T(8,128)(2,1)}, bf16[384,256]{1,0:T(8,128)(2,1)S(1)}, u32[]{:S(2)}, u32[]{:S(2)}) collective-permute-start(bf16[384,256]{1,0:T(8,128)(2,1)} %shard_map.112.refs_0_), channel_id=1, source_target_pairs={{0,2},{1,3},{2,0},{3,1},{4,6},{5,7},{6,4},{7,5},{8,10},{9,11},{10,... | collective-permute-start | bytes 589832 | tf_op jit(solution)/shard_map/ppermute | solution.py:14
  18.1 1.5 %collective-permute-start.4 = (bf16[384,256]{1,0:T(8,128)(2,1)}, bf16[384,256]{1,0:T(8,128)(2,1)}, u32[]{:S(2)}, u32[]{:S(2)}) collective-permute-start(bf16[384,256]{1,0:T(8,128)(2,1)} %shard_map.112.refs_0_), channel_id=1, source_target_pairs={{0,1},{1,0},{2,3},{3,2},{4,5},{5,4},{6,7},{7,6},{8,9},{9,8},{10,11... | collective-permute-start | bytes 589832 | tf_op jit(solution)/shard_map/ppermute | solution.py:14
  19.6 2.0 %shard_map.115 = (bf16[512,512]{1,0:T(8,128)(2,1)S(1)}, bf16[4,128,128]{2,1,0:T(8,128)(2,1)S(1)}) custom-call(s32[7]{0:T(128)S(1)} %stack.31.where_ref, bf16[512,512]{1,0:T(8,128)(2,1)S(1)} %bitcast.29, bf16[512,512]{1,0:T(8,128)(2,1)S(1)} %bitcast.20, bf16[512,512]{1,0:T(8,128)(2,1)S(1)} %bitcast.25, bf16[528,128]{1,0:T(8,128)(2,1)S(1)} %collective-permute-done.core_ref, ...), custom_call_target="tpu_custom_call" | custom-call | tf_op jit(solution)/shard_map/pallas_call | solution.py:234
  21.6 0.6 copy-done.4
  22.2 6.5 %all-to-all-done.ref = bf16[4,256,256]{2,1,0:T(8,128)(2,1)S(1)} async-done(((bf16[4,256,256]{2,1,0:T(8,128)(2,1)}), bf16[4,256,256]{2,1,0:T(8,128)(2,1)S(1)}, u32[]{:S(2)}, u32[]{:S(2)}) %all-to-all-start) | async-done | bytes 524320 | tf_op jit(solution)/shard_map/all_to_all | solution.py:793
  28.7 0.7 shard_map.116
  29.3 1.6 %collective-permute-start.2 = (bf16[1024,256]{1,0:T(8,128)(2,1)S(1)}, bf16[1024,256]{1,0:T(8,128)(2,1)S(1)}, u32[]{:S(2)}, u32[]{:S(2)}) collective-permute-start(bf16[1024,256]{1,0:T(8,128)(2,1)S(1)} %get-tuple-element.74.own_ref), channel_id=1, source_target_pairs={{0,4},{4,0},{1,5},{5,1},{2,6},{6,2},{3,7},{7,3},{8,12},{12,8},{9,1... | collective-permute-start | bytes 1572872 | tf_op jit(solution)/shard_map/ppermute | solution.py:14
  30.9 1.6 %collective-permute-start.6 = (bf16[368,256]{1,0:T(8,128)(2,1)S(1)}, bf16[368,256]{1,0:T(8,128)(2,1)S(1)}, u32[]{:S(2)}, u32[]{:S(2)}) collective-permute-start(bf16[368,256]{1,0:T(8,128)(2,1)S(1)} %get-tuple-element.75), channel_id=1, source_target_pairs={{0,16},{8,24},{16,0},{24,8},{1,17},{9,25},{17,1},{25,9},{2,18},{10... | collective-permute-start | bytes 565256 | tf_op jit(solution)/shard_map/ppermute | solution.py:14
  32.5 4.6 %collective-permute-done.3.refs_1_ = bf16[384,256]{1,0:T(8,128)(2,1)S(1)} collective-permute-done((bf16[384,256]{1,0:T(8,128)(2,1)}, bf16[384,256]{1,0:T(8,128)(2,1)S(1)}, u32[]{:S(2)}, u32[]{:S(2)}) %collective-permute-start.3) | collective-permute-done | bytes 196640 | tf_op jit(solution)/shard_map/ppermute | solution.py:14
  37.1 1.1 shard_map.117
  38.3 0.5 collective-permute-start.10
  38.8 1.5 %collective-permute-start.9 = (bf16[512,256]{1,0:T(8,128)(2,1)S(1)}, bf16[512,256]{1,0:T(8,128)(2,1)S(1)}, u32[]{:S(2)}, u32[]{:S(2)}) collective-permute-start(bf16[512,256]{1,0:T(8,128)(2,1)S(1)} %get-tuple-element.81.own_ref), channel_id=1, source_target_pairs={{0,4},{4,0},{1,5},{5,1},{2,6},{6,2},{3,7},{7,3},{8,12},{12,8},{9,1... | collective-permute-start | bytes 786440 | tf_op jit(solution)/shard_map/ppermute | solution.py:14
  40.3 0.4 collective-permute-done.2.got_ref.refs_1_
  40.8 1.1 shard_map.118
  41.9 1.5 %collective-permute-start.8 = (bf16[1168,256]{1,0:T(8,128)(2,1)S(1)}, bf16[1168,256]{1,0:T(8,128)(2,1)S(1)}, u32[]{:S(2)}, u32[]{:S(2)}) collective-permute-start(bf16[1168,256]{1,0:T(8,128)(2,1)S(1)} %shard_map.118), channel_id=1, source_target_pairs={{0,16},{8,24},{16,0},{24,8},{1,17},{9,25},{17,1},{25,9},{2,18},{10... | collective-permute-start | bytes 1794056 | tf_op jit(solution)/shard_map/ppermute | solution.py:14
  43.3 1.0 shard_map.119.part_ref
  44.3 0.8 shard_map.121
  45.2 1.6 %collective-permute-start.12 = (bf16[256,1024]{1,0:T(8,128)(2,1)S(1)}, bf16[256,1024]{1,0:T(8,128)(2,1)S(1)}, u32[]{:S(2)}, u32[]{:S(2)}) collective-permute-start(bf16[256,1024]{1,0:T(8,128)(2,1)S(1)} %shard_map.121), channel_id=1, source_target_pairs={{0,4},{4,0},{1,5},{5,1},{2,6},{6,2},{3,7},{7,3},{8,12},{12,8},{9,1... | collective-permute-start | bytes 1572872 | tf_op jit(solution)/shard_map/ppermute | solution.py:14
  46.7 0.4 collective-permute-done.9.got_ref
  47.1 0.8 shard_map.120.refs_13_
  48.0 1.1 shard_map.123
  49.1 0.2 collective-permute-start.15
  49.3 1.1 shard_map.122
  50.4 2.3 %collective-permute-start.11 = (bf16[512,256]{1,0:T(8,128)(2,1)S(1)}, bf16[512,256]{1,0:T(8,128)(2,1)S(1)}, u32[]{:S(2)}, u32[]{:S(2)}) collective-permute-start(bf16[512,256]{1,0:T(8,128)(2,1)S(1)} %shard_map.122), channel_id=1, source_target_pairs={{0,16},{8,24},{16,0},{24,8},{1,17},{9,25},{17,1},{25,9},{2,18},{10... | collective-permute-start | bytes 786440 | tf_op jit(solution)/shard_map/ppermute | solution.py:14
  52.8 0.2 collective-permute-start.14
  53.0 1.1 shard_map.124
  54.2 8.1 %collective-permute-done.11.refs_10_ = bf16[512,256]{1,0:T(8,128)(2,1)S(1)} collective-permute-done((bf16[512,256]{1,0:T(8,128)(2,1)S(1)}, bf16[512,256]{1,0:T(8,128)(2,1)S(1)}, u32[]{:S(2)}, u32[]{:S(2)}) %collective-permute-start.11) | collective-permute-done | bytes 262176 | tf_op jit(solution)/shard_map/ppermute | solution.py:14
  62.4 0.5 collective-permute-start.18
  63.0 1.3 %copy.12 = bf16[32,8,2,1024]{3,1,2,0:T(8,128)(2,1)} copy(bf16[32,8,2,1024]{3,2,1,0:T(2,128)(2,1)S(1)} %bitcast.34) | data formatting | bytes 2097152
  64.3 0.7 collective-permute-done.17.refs_11_
  65.0 4.3 %shard_map.125.own = bf16[256,1024]{1,0:T(8,128)(2,1)S(1)} custom-call(s32[7]{0:T(128)S(1)} %stack.31.where_ref, bf16[512,256]{1,0:T(8,128)(2,1)S(1)} %get-tuple-element.73.refs_0_, bf16[1024,256]{1,0:T(8,128)(2,1)S(1)} %collective-permute-done.2.got_ref.refs_1_, bf16[368,256]{1,0:T(8,128)(2,1)S(1)} %collective-permute-done.6.refs_2_, ...), custom_call_target="tpu_custom_call" | custom-call | tf_op jit(solution)/shard_map/pallas_call | solution.py:489
  69.3 1.5 %collective-permute-start.19 = (bf16[256,1024]{1,0:T(8,128)(2,1)S(1)}, bf16[256,1024]{1,0:T(8,128)(2,1)S(1)}, u32[]{:S(2)}, u32[]{:S(2)}) collective-permute-start(bf16[256,1024]{1,0:T(8,128)(2,1)S(1)} %shard_map.125.own), channel_id=1, source_target_pairs={{0,4},{4,0},{1,5},{5,1},{2,6},{6,2},{3,7},{7,3},{8,12},{12,8},{9,1... | collective-permute-start | bytes 1572872 | tf_op jit(solution)/shard_map/ppermute | solution.py:14
  70.8 1.0 shard_map.126.part_ref
  71.8 11.5 %collective-permute-done.19.got = bf16[256,1024]{1,0:T(8,128)(2,1)S(1)} collective-permute-done((bf16[256,1024]{1,0:T(8,128)(2,1)S(1)}, bf16[256,1024]{1,0:T(8,128)(2,1)S(1)}, u32[]{:S(2)}, u32[]{:S(2)}) %collective-permute-start.19) | collective-permute-done | bytes 524320 | tf_op jit(solution)/shard_map/ppermute | solution.py:14
  83.3 1.0 shard_map.127
  84.4 1.6 %shard_map.129 = (bf16[512,512]{1,0:T(8,128)(2,1)S(1)}, bf16[4,128,128]{2,1,0:T(8,128)(2,1)S(1)}) custom-call(s32[7]{0:T(128)S(1)} %stack.31.where_ref, bf16[256,1024]{1,0:T(8,128)(2,1)S(1)} %shard_map.125.own, bf16[256,1024]{1,0:T(8,128)(2,1)S(1)} %collective-permute-done.19.got, bf16[160,1024]{1,0:T(8,128)(2,1)S(1)} %get-tuple-element.80.head_ref.head, ...), custom_call_target="tpu_custom_call" | custom-call | tf_op jit(solution)/shard_map/pallas_call | solution.py:234
  86.0 0.3 collective-permute-done.20.got_ref
  86.3 0.6 shard_map.128
  86.9 0.3 collective-permute-start.22
  87.3 1.5 %collective-permute-start.21 = (bf16[128,1024]{1,0:T(8,128)(2,1)S(1)}, bf16[128,1024]{1,0:T(8,128)(2,1)S(1)}, u32[]{:S(2)}, u32[]{:S(2)}) collective-permute-start(bf16[128,1024]{1,0:T(8,128)(2,1)S(1)} %get-tuple-element.106), channel_id=1, source_target_pairs={{0,16},{8,24},{16,0},{24,8},{1,17},{9,25},{17,1},{25,9},{2,18},{10... | collective-permute-start | bytes 786440 | tf_op jit(solution)/shard_map/ppermute | solution.py:14
  88.8 3.2 %shard_map.130 = (f32[512,512]{1,0:T(8,128)S(1)}, f32[512,512]{1,0:T(8,128)S(1)}) custom-call(s32[7]{0:T(128)S(1)} %stack.31.where_ref, bf16[512,512]{1,0:T(8,128)(2,1)S(1)} %get-tuple-element.107.g_ref, bf16[512,512]{1,0:T(8,128)(2,1)S(1)} %bitcast.31, bf16[512,512]{1,0:T(8,128)(2,1)S(1)} %bitcast.21, bf16[512,512]{1,0:T(8,128)(2,1)S(1)} %bitcast.26), custom_call_target="tpu_custom_call" | custom-call | tf_op jit(solution)/shard_map/pallas_call | solution.py:234
  92.0 2.7 %shard_map.131 = bf16[512,512]{1,0:T(8,128)(2,1)} custom-call(s32[7]{0:T(128)S(1)} %stack.31.where_ref, bf16[512,512]{1,0:T(8,128)(2,1)S(1)} %get-tuple-element.107.g_ref, bf16[512,512]{1,0:T(8,128)(2,1)S(1)} %bitcast.22, bf16[512,512]{1,0:T(8,128)(2,1)S(1)} %bitcast.27, bf16[4,128,128]{2,1,0:T(8,128)(2,1)S(1)} %copy-done.5), custom_call_target="tpu_custom_call" | custom-call | tf_op jit(solution)/shard_map/pallas_call | solution.py:234
  94.8 1.0 collective-permute-done.21.got_ref
  95.7 0.6 shard_map.132
  96.4 5.3 %collective-permute-start.23 = (bf16[128,256]{1,0:T(8,128)(2,1)S(1)}, bf16[128,256]{1,0:T(8,128)(2,1)S(1)}, u32[]{:S(2)}, u32[]{:S(2)}) collective-permute-start(bf16[128,256]{1,0:T(8,128)(2,1)S(1)} %get-tuple-element.119), channel_id=1, source_target_pairs={{0,3},{1,2},{2,1},{3,0},{4,7},{5,6},{6,5},{7,4},{8,11},{9,10},{10,... | collective-permute-start | bytes 196616 | tf_op jit(solution)/shard_map/ppermute | solution.py:14
  101.7 1.7 %collective-permute-start.29 = (bf16[4,128,128]{2,1,0:T(8,128)(2,1)S(1)}, bf16[4,128,128]{2,1,0:T(8,128)(2,1)S(1)}, u32[]{:S(2)}, u32[]{:S(2)}) collective-permute-start(bf16[4,128,128]{2,1,0:T(8,128)(2,1)S(1)} %add_convert_fusion), channel_id=1, source_target_pairs={{0,16},{8,24},{16,0},{24,8},{1,17},{9,25},{17,1},{25,9},{2,18},{10... | collective-permute-start | bytes 393224 | tf_op jit(solution)/shard_map/ppermute | solution.py:14
  103.4 0.6 collective-permute-start.25
  104.0 0.4 collective-permute-done.23.refs_0_
  104.4 3.0 %collective-permute-done.24.refs_1_ = bf16[128,256]{1,0:T(8,128)(2,1)S(1)} collective-permute-done((bf16[128,256]{1,0:T(8,128)(2,1)S(1)}, bf16[128,256]{1,0:T(8,128)(2,1)S(1)}, u32[]{:S(2)}, u32[]{:S(2)}) %collective-permute-start.24) | collective-permute-done | bytes 65568 | tf_op jit(solution)/shard_map/ppermute | solution.py:14
  107.4 0.7 collective-permute-done.25.refs_2_
  108.0 0.6 shard_map.133.refs_0_
  108.6 1.2 %collective-permute-start.26 = (bf16[128,256]{1,0:T(8,128)(2,1)S(1)}, bf16[128,256]{1,0:T(8,128)(2,1)S(1)}, u32[]{:S(2)}, u32[]{:S(2)}) collective-permute-start(bf16[128,256]{1,0:T(8,128)(2,1)S(1)} %shard_map.133.refs_0_), channel_id=1, source_target_pairs={{0,16},{8,24},{16,0},{24,8},{1,17},{9,25},{17,1},{25,9},{2,18},{10... | collective-permute-start | bytes 196616 | tf_op jit(solution)/shard_map/ppermute | solution.py:14
  109.8 1.0 collective-permute-start.28
  110.8 2.0 %shard_map.134 = (bf16[512,512]{1,0:T(8,128)(2,1)}, bf16[512,512]{1,0:T(8,128)(2,1)}) custom-call(s32[7]{0:T(128)S(1)} %stack.31.where_ref, f32[512,512]{1,0:T(8,128)S(1)} %get-tuple-element.123.kp_ref, f32[512,512]{1,0:T(8,128)S(1)} %get-tuple-element.124.vp_ref, bf16[512,512]{1,0:T(8,128)(2,1)S(1)} %bitcast.23, bf16[512,512]{1,0:T(8,128)(2,1)S(1)} %bitcast.28, ...), custom_call_target="tpu_custom_call" | custom-call | tf_op jit(solution)/shard_map/pallas_call | solution.py:234
  112.8 0.3 collective-permute-done.26.refs_1_
  113.1 0.7 collective-permute-done.28.refs_3_
  113.8 1.4 %shard_map.135 = f32[512,256]{1,0:T(8,128)} custom-call(s32[7]{0:T(128)S(1)} %stack.31.where_ref, bf16[128,256]{1,0:T(8,128)(2,1)S(1)} %shard_map.133.refs_0_, bf16[128,256]{1,0:T(8,128)(2,1)S(1)} %collective-permute-done.26.refs_1_, bf16[128,256]{1,0:T(8,128)(2,1)S(1)} %collective-permute-done.27.refs_2_, bf16[128,256]{1,0:T(8,128)(2,1)S(1)} %collective-permute-done.28.refs_3_), custom_call_target="tpu_custom_call" | custom-call | tf_op jit(solution)/shard_map/pallas_call | solution.py:234
  (42 shorter events, 0.8 us)
Async XLA Ops:
  0.6 10.0 %copy-start = (bf16[1,512,512]{2,1,0:T(8,128)(2,1)S(1)}, bf16[1,512,512]{2,1,0:T(8,128)(2,1)}, u32[]{:S(2)}) copy-start(bf16[1,512,512]{2,1,0:T(8,128)(2,1)} %param.9) | copy-start | bytes 1572868
  0.6 10.0 %copy-start.1 = (bf16[1,512,512]{2,1,0:T(8,128)(2,1)S(1)}, bf16[1,512,512]{2,1,0:T(8,128)(2,1)}, u32[]{:S(2)}) copy-start(bf16[1,512,512]{2,1,0:T(8,128)(2,1)} %param.10) | copy-start | bytes 1572868
  0.7 10.0 %copy-start.6 = (s32[1,256,2]{1,2,0:T(2,128)S(1)}, s32[1,256,2]{1,2,0:T(2,128)}, u32[]{:S(2)}) copy-start(s32[1,256,2]{1,2,0:T(2,128)} %param.14) | copy-start | bytes 6148
  2.5 17.1 %copy-start.2 = (bf16[1,512,512]{2,1,0:T(8,128)(2,1)S(1)}, bf16[1,512,512]{2,1,0:T(8,128)(2,1)}, u32[]{:S(2)}) copy-start(bf16[1,512,512]{2,1,0:T(8,128)(2,1)} %param.8) | copy-start | bytes 1572868
  2.5 26.2 %all-to-all-start = ((bf16[4,256,256]{2,1,0:T(8,128)(2,1)}), bf16[4,256,256]{2,1,0:T(8,128)(2,1)S(1)}, u32[]{:S(2)}, u32[]{:S(2)}) async-start(bf16[4,256,256]{2,1,0:T(8,128)(2,1)} %shard_map.111.refs_2_), calls=%async_computation | async-start | bytes 1048576 | tf_op jit(solution)/shard_map/all_to_all | solution.py:793
  10.6 26.5 %copy-start.3 = (bf16[384,256]{1,0:T(8,128)(2,1)S(1)}, bf16[384,256]{1,0:T(8,128)(2,1)}, u32[]{:S(2)}) copy-start(bf16[384,256]{1,0:T(8,128)(2,1)} %shard_map.112.refs_0_) | copy-start | bytes 589828
  11.6 1.4 %collective-permute-start = (bf16[528,128]{1,0:T(8,128)(2,1)S(1)}, bf16[528,128]{1,0:T(8,128)(2,1)S(1)}, u32[]{:S(2)}, u32[]{:S(2)}) collective-permute-start(bf16[528,128]{1,0:T(8,128)(2,1)S(1)} %shard_map.113.own_ref.mine_ref), channel_id=1, source_target_pairs={{0,8},{8,0},{16,24},{24,16},{1,9},{9,1},{17,25},{25,17},{2,10},{10... | collective-permute-start | bytes 405512 | tf_op jit(solution)/shard_map/ppermute | solution.py:14
  13.6 6.0 %collective-permute-start.1 = (bf16[544,128]{1,0:T(8,128)(2,1)S(1)}, bf16[544,128]{1,0:T(8,128)(2,1)S(1)}, u32[]{:S(2)}, u32[]{:S(2)}) collective-permute-start(bf16[544,128]{1,0:T(8,128)(2,1)S(1)} %shard_map.114), channel_id=1, source_target_pairs={{0,16},{8,24},{16,0},{24,8},{1,17},{9,25},{17,1},{25,9},{2,18},{10... | collective-permute-start | bytes 417800 | tf_op jit(solution)/shard_map/ppermute | solution.py:14
  15.2 21.9 %collective-permute-start.3 = (bf16[384,256]{1,0:T(8,128)(2,1)}, bf16[384,256]{1,0:T(8,128)(2,1)S(1)}, u32[]{:S(2)}, u32[]{:S(2)}) collective-permute-start(bf16[384,256]{1,0:T(8,128)(2,1)} %shard_map.112.refs_0_), channel_id=1, source_target_pairs={{0,2},{1,3},{2,0},{3,1},{4,6},{5,7},{6,4},{7,5},{8,10},{9,11},{10,... | collective-permute-start | bytes 589832 | tf_op jit(solution)/shard_map/ppermute | solution.py:14
  18.1 19.0 %collective-permute-start.4 = (bf16[384,256]{1,0:T(8,128)(2,1)}, bf16[384,256]{1,0:T(8,128)(2,1)}, u32[]{:S(2)}, u32[]{:S(2)}) collective-permute-start(bf16[384,256]{1,0:T(8,128)(2,1)} %shard_map.112.refs_0_), channel_id=1, source_target_pairs={{0,1},{1,0},{2,3},{3,2},{4,5},{5,4},{6,7},{7,6},{8,9},{9,8},{10,11... | collective-permute-start | bytes 589832 | tf_op jit(solution)/shard_map/ppermute | solution.py:14
  19.6 17.6 %collective-permute-start.5 = (bf16[384,256]{1,0:T(8,128)(2,1)}, bf16[384,256]{1,0:T(8,128)(2,1)}, u32[]{:S(2)}, u32[]{:S(2)}) collective-permute-start(bf16[384,256]{1,0:T(8,128)(2,1)} %shard_map.112.refs_0_), channel_id=1, source_target_pairs={{0,3},{1,2},{2,1},{3,0},{4,7},{5,6},{6,5},{7,4},{8,11},{9,10},{10,... | collective-permute-start | bytes 589832 | tf_op jit(solution)/shard_map/ppermute | solution.py:14
  21.5 0.7 copy-start.4
  29.3 11.4 %collective-permute-start.2 = (bf16[1024,256]{1,0:T(8,128)(2,1)S(1)}, bf16[1024,256]{1,0:T(8,128)(2,1)S(1)}, u32[]{:S(2)}, u32[]{:S(2)}) collective-permute-start(bf16[1024,256]{1,0:T(8,128)(2,1)S(1)} %get-tuple-element.74.own_ref), channel_id=1, source_target_pairs={{0,4},{4,0},{1,5},{5,1},{2,6},{6,2},{3,7},{7,3},{8,12},{12,8},{9,1... | collective-permute-start | bytes 1572872 | tf_op jit(solution)/shard_map/ppermute | solution.py:14
  30.9 6.2 %collective-permute-start.6 = (bf16[368,256]{1,0:T(8,128)(2,1)S(1)}, bf16[368,256]{1,0:T(8,128)(2,1)S(1)}, u32[]{:S(2)}, u32[]{:S(2)}) collective-permute-start(bf16[368,256]{1,0:T(8,128)(2,1)S(1)} %get-tuple-element.75), channel_id=1, source_target_pairs={{0,16},{8,24},{16,0},{24,8},{1,17},{9,25},{17,1},{25,9},{2,18},{10... | collective-permute-start | bytes 565256 | tf_op jit(solution)/shard_map/ppermute | solution.py:14
  38.2 2.1 %collective-permute-start.7 = (bf16[160,1024]{1,0:T(8,128)(2,1)S(1)}, bf16[160,1024]{1,0:T(8,128)(2,1)S(1)}, u32[]{:S(2)}, u32[]{:S(2)}) collective-permute-start(bf16[160,1024]{1,0:T(8,128)(2,1)S(1)} %get-tuple-element.80.head_ref.head), channel_id=1, source_target_pairs={{0,8},{8,0},{16,24},{24,16},{1,9},{9,1},{17,25},{25,17},{2,10},{10... | collective-permute-start | bytes 983048 | tf_op jit(solution)/shard_map/ppermute | solution.py:14
  38.3 6.0 %collective-permute-start.10 = (bf16[96,1024]{1,0:T(8,128)(2,1)S(1)}, bf16[96,1024]{1,0:T(8,128)(2,1)S(1)}, u32[]{:S(2)}, u32[]{:S(2)}) collective-permute-start(bf16[96,1024]{1,0:T(8,128)(2,1)S(1)} %get-tuple-element.84.tail_ref.tail), channel_id=1, source_target_pairs={{0,8},{8,0},{16,24},{24,16},{1,9},{9,1},{17,25},{25,17},{2,10},{10... | collective-permute-start | bytes 589832 | tf_op jit(solution)/shard_map/ppermute | solution.py:14
  38.8 8.3 %collective-permute-start.9 = (bf16[512,256]{1,0:T(8,128)(2,1)S(1)}, bf16[512,256]{1,0:T(8,128)(2,1)S(1)}, u32[]{:S(2)}, u32[]{:S(2)}) collective-permute-start(bf16[512,256]{1,0:T(8,128)(2,1)S(1)} %get-tuple-element.81.own_ref), channel_id=1, source_target_pairs={{0,4},{4,0},{1,5},{5,1},{2,6},{6,2},{3,7},{7,3},{8,12},{12,8},{9,1... | collective-permute-start | bytes 786440 | tf_op jit(solution)/shard_map/ppermute | solution.py:14
  41.9 20.5 %collective-permute-start.8 = (bf16[1168,256]{1,0:T(8,128)(2,1)S(1)}, bf16[1168,256]{1,0:T(8,128)(2,1)S(1)}, u32[]{:S(2)}, u32[]{:S(2)}) collective-permute-start(bf16[1168,256]{1,0:T(8,128)(2,1)S(1)} %shard_map.118), channel_id=1, source_target_pairs={{0,16},{8,24},{16,0},{24,8},{1,17},{9,25},{17,1},{25,9},{2,18},{10... | collective-permute-start | bytes 1794056 | tf_op jit(solution)/shard_map/ppermute | solution.py:14
  45.2 17.2 %collective-permute-start.12 = (bf16[256,1024]{1,0:T(8,128)(2,1)S(1)}, bf16[256,1024]{1,0:T(8,128)(2,1)S(1)}, u32[]{:S(2)}, u32[]{:S(2)}) collective-permute-start(bf16[256,1024]{1,0:T(8,128)(2,1)S(1)} %shard_map.121), channel_id=1, source_target_pairs={{0,4},{4,0},{1,5},{5,1},{2,6},{6,2},{3,7},{7,3},{8,12},{12,8},{9,1... | collective-permute-start | bytes 1572872 | tf_op jit(solution)/shard_map/ppermute | solution.py:14
  46.7 6.0 %collective-permute-start.13 = (bf16[512,256]{1,0:T(8,128)(2,1)S(1)}, bf16[512,256]{1,0:T(8,128)(2,1)S(1)}, u32[]{:S(2)}, u32[]{:S(2)}) collective-permute-start(bf16[512,256]{1,0:T(8,128)(2,1)S(1)} %get-tuple-element.73.refs_0_), channel_id=1, source_target_pairs={{0,8},{8,0},{16,24},{24,16},{1,9},{9,1},{17,25},{25,17},{2,10},{10... | collective-permute-start | bytes 786440 | tf_op jit(solution)/shard_map/ppermute | solution.py:14
  48.0 15.0 %copy-start.7 = (bf16[1,256,2,1024]{3,2,1,0:T(2,128)(2,1)S(1)}, bf16[1,256,2,1024]{3,2,1,0:T(2,128)(2,1)}, u32[]{:S(2)}) copy-start(bf16[1,256,2,1024]{3,2,1,0:T(2,128)(2,1)} %param.15) | copy-start | bytes 3145732
  49.1 13.2 %collective-permute-start.15 = (bf16[768,256]{1,0:T(8,128)(2,1)S(1)}, bf16[768,256]{1,0:T(8,128)(2,1)S(1)}, u32[]{:S(2)}, u32[]{:S(2)}) collective-permute-start(bf16[768,256]{1,0:T(8,128)(2,1)S(1)} %get-tuple-element.91), channel_id=1, source_target_pairs={{0,8},{8,0},{16,24},{24,16},{1,9},{9,1},{17,25},{25,17},{2,10},{10... | collective-permute-start | bytes 1179656 | tf_op jit(solution)/shard_map/ppermute | solution.py:14
  50.4 11.9 %collective-permute-start.11 = (bf16[512,256]{1,0:T(8,128)(2,1)S(1)}, bf16[512,256]{1,0:T(8,128)(2,1)S(1)}, u32[]{:S(2)}, u32[]{:S(2)}) collective-permute-start(bf16[512,256]{1,0:T(8,128)(2,1)S(1)} %shard_map.122), channel_id=1, source_target_pairs={{0,16},{8,24},{16,0},{24,8},{1,17},{9,25},{17,1},{25,9},{2,18},{10... | collective-permute-start | bytes 786440 | tf_op jit(solution)/shard_map/ppermute | solution.py:14
  52.8 1.4 %collective-permute-start.14 = (bf16[368,256]{1,0:T(8,128)(2,1)S(1)}, bf16[368,256]{1,0:T(8,128)(2,1)S(1)}, u32[]{:S(2)}, u32[]{:S(2)}) collective-permute-start(bf16[368,256]{1,0:T(8,128)(2,1)S(1)} %collective-permute-done.6.refs_2_), channel_id=1, source_target_pairs={{0,8},{8,0},{16,24},{24,16},{1,9},{9,1},{17,25},{25,17},{2,10},{10... | collective-permute-start | bytes 565256 | tf_op jit(solution)/shard_map/ppermute | solution.py:14
  62.3 2.6 %collective-permute-start.16 = (bf16[1168,256]{1,0:T(8,128)(2,1)S(1)}, bf16[1168,256]{1,0:T(8,128)(2,1)S(1)}, u32[]{:S(2)}, u32[]{:S(2)}) collective-permute-start(bf16[1168,256]{1,0:T(8,128)(2,1)S(1)} %collective-permute-done.8.refs_3_), channel_id=1, source_target_pairs={{0,8},{8,0},{16,24},{24,16},{1,9},{9,1},{17,25},{25,17},{2,10},{10... | collective-permute-start | bytes 1794056 | tf_op jit(solution)/shard_map/ppermute | solution.py:14
  62.4 2.6 %collective-permute-start.18 = (bf16[512,256]{1,0:T(8,128)(2,1)S(1)}, bf16[512,256]{1,0:T(8,128)(2,1)S(1)}, u32[]{:S(2)}, u32[]{:S(2)}) collective-permute-start(bf16[512,256]{1,0:T(8,128)(2,1)S(1)} %collective-permute-done.11.refs_10_), channel_id=1, source_target_pairs={{0,8},{8,0},{16,24},{24,16},{1,9},{9,1},{17,25},{25,17},{2,10},{10... | collective-permute-start | bytes 786440 | tf_op jit(solution)/shard_map/ppermute | solution.py:14
  62.9 2.1 %collective-permute-start.17 = (bf16[256,256]{1,0:T(8,128)(2,1)S(1)}, bf16[256,256]{1,0:T(8,128)(2,1)S(1)}, u32[]{:S(2)}, u32[]{:S(2)}) collective-permute-start(bf16[256,256]{1,0:T(8,128)(2,1)S(1)} %get-tuple-element.102), channel_id=1, source_target_pairs={{0,8},{8,0},{16,24},{24,16},{1,9},{9,1},{17,25},{25,17},{2,10},{10... | collective-permute-start | bytes 393224 | tf_op jit(solution)/shard_map/ppermute | solution.py:14
  69.3 14.0 %collective-permute-start.19 = (bf16[256,1024]{1,0:T(8,128)(2,1)S(1)}, bf16[256,1024]{1,0:T(8,128)(2,1)S(1)}, u32[]{:S(2)}, u32[]{:S(2)}) collective-permute-start(bf16[256,1024]{1,0:T(8,128)(2,1)S(1)} %shard_map.125.own), channel_id=1, source_target_pairs={{0,4},{4,0},{1,5},{5,1},{2,6},{6,2},{3,7},{7,3},{8,12},{12,8},{9,1... | collective-permute-start | bytes 1572872 | tf_op jit(solution)/shard_map/ppermute | solution.py:14
  84.3 2.0 %collective-permute-start.20 = (bf16[2,128,1024]{2,1,0:T(8,128)(2,1)S(1)}, bf16[2,128,1024]{2,1,0:T(8,128)(2,1)S(1)}, u32[]{:S(2)}, u32[]{:S(2)}) collective-permute-start(bf16[2,128,1024]{2,1,0:T(8,128)(2,1)S(1)} %get-tuple-element.105), channel_id=1, source_target_pairs={{0,8},{8,0},{16,24},{24,16},{1,9},{9,1},{17,25},{25,17},{2,10},{10... | collective-permute-start | bytes 1572872 | tf_op jit(solution)/shard_map/ppermute | solution.py:14
  86.0 5.9 %copy-start.5 = (bf16[4,128,128]{2,1,0:T(8,128)(2,1)S(1)}, bf16[4,128,128]{2,1,0:T(8,128)(2,1)}, u32[]{:S(2)}) copy-start(bf16[4,128,128]{2,1,0:T(8,128)(2,1)} %copy-done.4) | copy-start | bytes 393220
  86.9 7.8 %collective-permute-start.22 = (bf16[4,128,128]{2,1,0:T(8,128)(2,1)S(1)}, bf16[4,128,128]{2,1,0:T(8,128)(2,1)S(1)}, u32[]{:S(2)}, u32[]{:S(2)}) collective-permute-start(bf16[4,128,128]{2,1,0:T(8,128)(2,1)S(1)} %get-tuple-element.112), channel_id=1, source_target_pairs={{0,8},{8,0},{16,24},{24,16},{1,9},{9,1},{17,25},{25,17},{2,10},{10... | collective-permute-start | bytes 393224 | tf_op jit(solution)/shard_map/ppermute | solution.py:14
  87.3 8.5 %collective-permute-start.21 = (bf16[128,1024]{1,0:T(8,128)(2,1)S(1)}, bf16[128,1024]{1,0:T(8,128)(2,1)S(1)}, u32[]{:S(2)}, u32[]{:S(2)}) collective-permute-start(bf16[128,1024]{1,0:T(8,128)(2,1)S(1)} %get-tuple-element.106), channel_id=1, source_target_pairs={{0,16},{8,24},{16,0},{24,8},{1,17},{9,25},{17,1},{25,9},{2,18},{10... | collective-permute-start | bytes 786440 | tf_op jit(solution)/shard_map/ppermute | solution.py:14
  96.4 8.0 %collective-permute-start.23 = (bf16[128,256]{1,0:T(8,128)(2,1)S(1)}, bf16[128,256]{1,0:T(8,128)(2,1)S(1)}, u32[]{:S(2)}, u32[]{:S(2)}) collective-permute-start(bf16[128,256]{1,0:T(8,128)(2,1)S(1)} %get-tuple-element.119), channel_id=1, source_target_pairs={{0,3},{1,2},{2,1},{3,0},{4,7},{5,6},{6,5},{7,4},{8,11},{9,10},{10,... | collective-permute-start | bytes 196616 | tf_op jit(solution)/shard_map/ppermute | solution.py:14
  101.6 5.8 %collective-permute-start.24 = (bf16[128,256]{1,0:T(8,128)(2,1)S(1)}, bf16[128,256]{1,0:T(8,128)(2,1)S(1)}, u32[]{:S(2)}, u32[]{:S(2)}) collective-permute-start(bf16[128,256]{1,0:T(8,128)(2,1)S(1)} %get-tuple-element.120), channel_id=1, source_target_pairs={{0,2},{1,3},{2,0},{3,1},{4,6},{5,7},{6,4},{7,5},{8,10},{9,11},{10,... | collective-permute-start | bytes 196616 | tf_op jit(solution)/shard_map/ppermute | solution.py:14
  101.7 9.1 %collective-permute-start.29 = (bf16[4,128,128]{2,1,0:T(8,128)(2,1)S(1)}, bf16[4,128,128]{2,1,0:T(8,128)(2,1)S(1)}, u32[]{:S(2)}, u32[]{:S(2)}) collective-permute-start(bf16[4,128,128]{2,1,0:T(8,128)(2,1)S(1)} %add_convert_fusion), channel_id=1, source_target_pairs={{0,16},{8,24},{16,0},{24,8},{1,17},{9,25},{17,1},{25,9},{2,18},{10... | collective-permute-start | bytes 393224 | tf_op jit(solution)/shard_map/ppermute | solution.py:14
  103.4 4.7 %collective-permute-start.25 = (bf16[128,256]{1,0:T(8,128)(2,1)S(1)}, bf16[128,256]{1,0:T(8,128)(2,1)S(1)}, u32[]{:S(2)}, u32[]{:S(2)}) collective-permute-start(bf16[128,256]{1,0:T(8,128)(2,1)S(1)} %get-tuple-element.121), channel_id=1, source_target_pairs={{0,1},{1,0},{2,3},{3,2},{4,5},{5,4},{6,7},{7,6},{8,9},{9,8},{10,11... | collective-permute-start | bytes 196616 | tf_op jit(solution)/shard_map/ppermute | solution.py:14
  108.6 4.5 %collective-permute-start.26 = (bf16[128,256]{1,0:T(8,128)(2,1)S(1)}, bf16[128,256]{1,0:T(8,128)(2,1)S(1)}, u32[]{:S(2)}, u32[]{:S(2)}) collective-permute-start(bf16[128,256]{1,0:T(8,128)(2,1)S(1)} %shard_map.133.refs_0_), channel_id=1, source_target_pairs={{0,16},{8,24},{16,0},{24,8},{1,17},{9,25},{17,1},{25,9},{2,18},{10... | collective-permute-start | bytes 196616 | tf_op jit(solution)/shard_map/ppermute | solution.py:14
  109.8 3.3 %collective-permute-start.27 = (bf16[128,256]{1,0:T(8,128)(2,1)S(1)}, bf16[128,256]{1,0:T(8,128)(2,1)S(1)}, u32[]{:S(2)}, u32[]{:S(2)}) collective-permute-start(bf16[128,256]{1,0:T(8,128)(2,1)S(1)} %shard_map.133.refs_0_), channel_id=1, source_target_pairs={{0,8},{8,0},{16,24},{24,16},{1,9},{9,1},{17,25},{25,17},{2,10},{10... | collective-permute-start | bytes 196616 | tf_op jit(solution)/shard_map/ppermute | solution.py:14
  109.8 4.0 %collective-permute-start.28 = (bf16[128,256]{1,0:T(8,128)(2,1)S(1)}, bf16[128,256]{1,0:T(8,128)(2,1)S(1)}, u32[]{:S(2)}, u32[]{:S(2)}) collective-permute-start(bf16[128,256]{1,0:T(8,128)(2,1)S(1)} %shard_map.133.refs_0_), channel_id=1, source_target_pairs={{0,24},{8,16},{16,8},{24,0},{1,25},{9,17},{17,9},{25,1},{2,26},{10... | collective-permute-start | bytes 196616 | tf_op jit(solution)/shard_map/ppermute | solution.py:14

commit v8 on v7

--- a/solution.py
+++ b/solution.py
@@ -828,12 +828,12 @@
     mixed_got = swap(mixed_send, "head", 1)
     mixed_part, got_1 = lax.optimization_barrier((mixed_part, got_1))
     mixed = mix(where, attended, mixed_part, got_head, got_tail, False)
-    near_0, _, _ = lax.optimization_barrier((got_0, mixed, mixed_send))
+
+    got_1, _, _ = lax.optimization_barrier((got_1, mixed, mixed_send))
+    (to_far,) = embed(where, packed, top, 1, 2, tokens, part_1, got_1, half, n_dp, 0, True)
+    near_0, _ = lax.optimization_barrier((got_0, to_far))
     own_0, to_core = embed(where, packed, top, 0, 2, tokens, part_0, near_0, half, n_dp, late, False)
     core_0 = core_swap(to_core)
-
-    got_1, _, _ = lax.optimization_barrier((got_1, mixed, mixed_send))
-    (to_far,) = embed(where, packed, top, 1, 2, tokens, part_1, got_1, half, n_dp, 0, True)
     near_1, _ = lax.optimization_barrier((got_1, to_far))
     own_1, to_core = embed(where, packed, top, 1, 2, tokens, part_1, near_1, half, n_dp, 0, False)
     far_1 = far_swap(to_far)

time: 115 us -> 115 us (level)
  no operation moved by 1% of the time
where the time goes in v8:
time: 115 us
  waiting for transfers between devices  40.1 us (35%)
  starting transfers between devices  37.4 us (33%)
  Pallas kernels  34.7 us (30%)
  local copies, waits for them, and re-layouts  2.05 us (2%)
    ppermute x30, waiting for transfers between devices, swap(): lax.ppermute(block, axis, [(i, i ^ mask) for i in range(lax.axis_size(axi...  33.6 us
    ppermute x30, starting transfers between devices, swap(): lax.ppermute(block, axis, [(i, i ^ mask) for i in range(lax.axis_size(axi...  30.9 us
    pallas_call x22, Pallas kernels, run(): pl.pallas_call(body, out_shape=outs, in_specs=[pl.BlockSpec(memory_space=...  27.1 us
    all_to_all x1, waiting for transfers between devices, on_device(): pieces_0 = lax.all_to_all(lanes_0, 'dp', 0, 0)  6.48 us
    all_to_all x1, starting transfers between devices, on_device(): pieces_0 = lax.all_to_all(lanes_0, 'dp', 0, 0)  6.46 us
    pallas_call x1, Pallas kernels, depth_grad(): pl.pallas_call(body, out_shape=shaped((tokens, width)), in_specs=[pl.Bloc...  4.26 us
  transfers between devices with their start and end apart: 31, of which 16 were waited for; matrix products, arithmetic and copies ran while one was open for 1% of the time, Pallas kernels for 22%

profile of v8, /device:TPU:0, one launch (start us, length us, event | category | flops | bytes accessed | tf_op | source)
XLA Modules:
  0.0 115.2 jit_solution(16765752244397640192)
XLA Ops:
  0.7 1.8 %shard_map.111.refs_2_ = bf16[4,256,256]{2,1,0:T(8,128)(2,1)} custom-call(bf16[2,128,1024]{2,1,0:T(8,128)(2,1)} %refs_0_.1, bf16[1024,128]{1,0:T(8,128)(2,1)} %depth.1), custom_call_target="tpu_custom_call" | custom-call | tf_op jit(solution)/shard_map/pallas_call | solution.py:297
  2.5 6.5 %all-to-all-start = ((bf16[4,256,256]{2,1,0:T(8,128)(2,1)}), bf16[4,256,256]{2,1,0:T(8,128)(2,1)S(1)}, u32[]{:S(2)}, u32[]{:S(2)}) async-start(bf16[4,256,256]{2,1,0:T(8,128)(2,1)} %shard_map.111.refs_2_), calls=%async_computation | async-start | bytes 1048576 | tf_op jit(solution)/shard_map/all_to_all | solution.py:793
  8.9 1.6 %shard_map.112.refs_0_ = bf16[384,256]{1,0:T(8,128)(2,1)} custom-call(bf16[2,128,1024]{2,1,0:T(8,128)(2,1)} %refs_0_.1, bf16[512,256]{1,0:T(8,128)(2,1)} %refs_1_.1, bf16[4,256,256]{2,1,0:T(8,128)(2,1)} %shard_map.111.refs_2_), custom_call_target="tpu_custom_call" | custom-call | tf_op jit(solution)/shard_map/pallas_call | solution.py:271
  10.7 0.9 shard_map.113.own_ref.mine_ref
  11.7 1.3 %collective-permute-done.core_ref = bf16[528,128]{1,0:T(8,128)(2,1)S(1)} collective-permute-done((bf16[528,128]{1,0:T(8,128)(2,1)S(1)}, bf16[528,128]{1,0:T(8,128)(2,1)S(1)}, u32[]{:S(2)}, u32[]{:S(2)}) %collective-permute-start) | collective-permute-done | bytes 135200 | tf_op jit(solution)/shard_map/ppermute | solution.py:14
  13.0 0.6 shard_map.114
  13.6 1.6 %collective-permute-start.1 = (bf16[544,128]{1,0:T(8,128)(2,1)S(1)}, bf16[544,128]{1,0:T(8,128)(2,1)S(1)}, u32[]{:S(2)}, u32[]{:S(2)}) collective-permute-start(bf16[544,128]{1,0:T(8,128)(2,1)S(1)} %shard_map.114), channel_id=1, source_target_pairs={{0,16},{8,24},{16,0},{24,8},{1,17},{9,25},{17,1},{25,9},{2,18},{10... | collective-permute-start | bytes 417800 | tf_op jit(solution)/shard_map/ppermute | solution.py:14
  15.2 2.9 %collective-permute-start.3 = (bf16[384,256]{1,0:T(8,128)(2,1)}, bf16[384,256]{1,0:T(8,128)(2,1)S(1)}, u32[]{:S(2)}, u32[]{:S(2)}) collective-permute-start(bf16[384,256]{1,0:T(8,128)(2,1)} %shard_map.112.refs_0_), channel_id=1, source_target_pairs={{0,2},{1,3},{2,0},{3,1},{4,6},{5,7},{6,4},{7,5},{8,10},{9,11},{10,... | collective-permute-start | bytes 589832 | tf_op jit(solution)/shard_map/ppermute | solution.py:14
  18.1 1.5 %collective-permute-start.4 = (bf16[384,256]{1,0:T(8,128)(2,1)}, bf16[384,256]{1,0:T(8,128)(2,1)}, u32[]{:S(2)}, u32[]{:S(2)}) collective-permute-start(bf16[384,256]{1,0:T(8,128)(2,1)} %shard_map.112.refs_0_), channel_id=1, source_target_pairs={{0,1},{1,0},{2,3},{3,2},{4,5},{5,4},{6,7},{7,6},{8,9},{9,8},{10,11... | collective-permute-start | bytes 589832 | tf_op jit(solution)/shard_map/ppermute | solution.py:14
  19.6 2.0 %shard_map.115 = (bf16[512,512]{1,0:T(8,128)(2,1)S(1)}, bf16[4,128,128]{2,1,0:T(8,128)(2,1)S(1)}) custom-call(s32[7]{0:T(128)S(1)} %stack.31.where_ref, bf16[512,512]{1,0:T(8,128)(2,1)S(1)} %bitcast.29, bf16[512,512]{1,0:T(8,128)(2,1)S(1)} %bitcast.20, bf16[512,512]{1,0:T(8,128)(2,1)S(1)} %bitcast.25, bf16[528,128]{1,0:T(8,128)(2,1)S(1)} %collective-permute-done.core_ref, ...), custom_call_target="tpu_custom_call" | custom-call | tf_op jit(solution)/shard_map/pallas_call | solution.py:234
  21.6 0.6 copy-done.4
  22.2 6.5 %all-to-all-done.ref = bf16[4,256,256]{2,1,0:T(8,128)(2,1)S(1)} async-done(((bf16[4,256,256]{2,1,0:T(8,128)(2,1)}), bf16[4,256,256]{2,1,0:T(8,128)(2,1)S(1)}, u32[]{:S(2)}, u32[]{:S(2)}) %all-to-all-start) | async-done | bytes 524320 | tf_op jit(solution)/shard_map/all_to_all | solution.py:793
  28.7 0.7 shard_map.116
  29.3 1.6 %collective-permute-start.2 = (bf16[1024,256]{1,0:T(8,128)(2,1)S(1)}, bf16[1024,256]{1,0:T(8,128)(2,1)S(1)}, u32[]{:S(2)}, u32[]{:S(2)}) collective-permute-start(bf16[1024,256]{1,0:T(8,128)(2,1)S(1)} %get-tuple-element.74.own_ref), channel_id=1, source_target_pairs={{0,4},{4,0},{1,5},{5,1},{2,6},{6,2},{3,7},{7,3},{8,12},{12,8},{9,1... | collective-permute-start | bytes 1572872 | tf_op jit(solution)/shard_map/ppermute | solution.py:14
  30.9 1.6 %collective-permute-start.6 = (bf16[368,256]{1,0:T(8,128)(2,1)S(1)}, bf16[368,256]{1,0:T(8,128)(2,1)S(1)}, u32[]{:S(2)}, u32[]{:S(2)}) collective-permute-start(bf16[368,256]{1,0:T(8,128)(2,1)S(1)} %get-tuple-element.75), channel_id=1, source_target_pairs={{0,16},{8,24},{16,0},{24,8},{1,17},{9,25},{17,1},{25,9},{2,18},{10... | collective-permute-start | bytes 565256 | tf_op jit(solution)/shard_map/ppermute | solution.py:14
  32.5 4.6 %collective-permute-done.3.refs_1_ = bf16[384,256]{1,0:T(8,128)(2,1)S(1)} collective-permute-done((bf16[384,256]{1,0:T(8,128)(2,1)}, bf16[384,256]{1,0:T(8,128)(2,1)S(1)}, u32[]{:S(2)}, u32[]{:S(2)}) %collective-permute-start.3) | collective-permute-done | bytes 196640 | tf_op jit(solution)/shard_map/ppermute | solution.py:14
  37.1 1.1 shard_map.117
  38.3 0.5 collective-permute-start.10
  38.8 1.5 %collective-permute-start.9 = (bf16[512,256]{1,0:T(8,128)(2,1)S(1)}, bf16[512,256]{1,0:T(8,128)(2,1)S(1)}, u32[]{:S(2)}, u32[]{:S(2)}) collective-permute-start(bf16[512,256]{1,0:T(8,128)(2,1)S(1)} %get-tuple-element.81.own_ref), channel_id=1, source_target_pairs={{0,4},{4,0},{1,5},{5,1},{2,6},{6,2},{3,7},{7,3},{8,12},{12,8},{9,1... | collective-permute-start | bytes 786440 | tf_op jit(solution)/shard_map/ppermute | solution.py:14
  40.3 0.4 collective-permute-done.2.got_ref.refs_1_
  40.8 1.1 shard_map.118
  41.9 1.5 %collective-permute-start.8 = (bf16[1168,256]{1,0:T(8,128)(2,1)S(1)}, bf16[1168,256]{1,0:T(8,128)(2,1)S(1)}, u32[]{:S(2)}, u32[]{:S(2)}) collective-permute-start(bf16[1168,256]{1,0:T(8,128)(2,1)S(1)} %shard_map.118), channel_id=1, source_target_pairs={{0,16},{8,24},{16,0},{24,8},{1,17},{9,25},{17,1},{25,9},{2,18},{10... | collective-permute-start | bytes 1794056 | tf_op jit(solution)/shard_map/ppermute | solution.py:14
  43.3 1.0 shard_map.119.part_ref
  44.3 0.8 shard_map.121
  45.2 1.6 %collective-permute-start.12 = (bf16[256,1024]{1,0:T(8,128)(2,1)S(1)}, bf16[256,1024]{1,0:T(8,128)(2,1)S(1)}, u32[]{:S(2)}, u32[]{:S(2)}) collective-permute-start(bf16[256,1024]{1,0:T(8,128)(2,1)S(1)} %shard_map.121), channel_id=1, source_target_pairs={{0,4},{4,0},{1,5},{5,1},{2,6},{6,2},{3,7},{7,3},{8,12},{12,8},{9,1... | collective-permute-start | bytes 1572872 | tf_op jit(solution)/shard_map/ppermute | solution.py:14
  46.7 0.4 collective-permute-done.9.got_ref
  47.1 0.8 shard_map.120.refs_13_
  48.0 1.1 shard_map.122
  49.1 1.1 shard_map.123
  50.2 0.2 collective-permute-start.15
  50.4 2.3 %collective-permute-start.11 = (bf16[512,256]{1,0:T(8,128)(2,1)S(1)}, bf16[512,256]{1,0:T(8,128)(2,1)S(1)}, u32[]{:S(2)}, u32[]{:S(2)}) collective-permute-start(bf16[512,256]{1,0:T(8,128)(2,1)S(1)} %shard_map.122), channel_id=1, source_target_pairs={{0,16},{8,24},{16,0},{24,8},{1,17},{9,25},{17,1},{25,9},{2,18},{10... | collective-permute-start | bytes 786440 | tf_op jit(solution)/shard_map/ppermute | solution.py:14
  52.8 0.2 collective-permute-start.14
  52.9 1.1 shard_map.124
  54.2 8.1 %collective-permute-done.11.refs_10_ = bf16[512,256]{1,0:T(8,128)(2,1)S(1)} collective-permute-done((bf16[512,256]{1,0:T(8,128)(2,1)S(1)}, bf16[512,256]{1,0:T(8,128)(2,1)S(1)}, u32[]{:S(2)}, u32[]{:S(2)}) %collective-permute-start.11) | collective-permute-done | bytes 262176 | tf_op jit(solution)/shard_map/ppermute | solution.py:14
  62.4 0.5 collective-permute-start.18
  63.0 1.3 %copy.12 = bf16[32,8,2,1024]{3,1,2,0:T(8,128)(2,1)} copy(bf16[32,8,2,1024]{3,2,1,0:T(2,128)(2,1)S(1)} %bitcast.34) | data formatting | bytes 2097152
  64.3 0.7 collective-permute-done.17.refs_11_
  65.0 4.3 %shard_map.125.own = bf16[256,1024]{1,0:T(8,128)(2,1)S(1)} custom-call(s32[7]{0:T(128)S(1)} %stack.31.where_ref, bf16[512,256]{1,0:T(8,128)(2,1)S(1)} %get-tuple-element.73.refs_0_, bf16[1024,256]{1,0:T(8,128)(2,1)S(1)} %collective-permute-done.2.got_ref.refs_1_, bf16[368,256]{1,0:T(8,128)(2,1)S(1)} %collective-permute-done.6.refs_2_, ...), custom_call_target="tpu_custom_call" | custom-call | tf_op jit(solution)/shard_map/pallas_call | solution.py:489
  69.3 1.5 %collective-permute-start.19 = (bf16[256,1024]{1,0:T(8,128)(2,1)S(1)}, bf16[256,1024]{1,0:T(8,128)(2,1)S(1)}, u32[]{:S(2)}, u32[]{:S(2)}) collective-permute-start(bf16[256,1024]{1,0:T(8,128)(2,1)S(1)} %shard_map.125.own), channel_id=1, source_target_pairs={{0,4},{4,0},{1,5},{5,1},{2,6},{6,2},{3,7},{7,3},{8,12},{12,8},{9,1... | collective-permute-start | bytes 1572872 | tf_op jit(solution)/shard_map/ppermute | solution.py:14
  70.8 1.0 shard_map.126.part_ref
  71.8 11.5 %collective-permute-done.19.got = bf16[256,1024]{1,0:T(8,128)(2,1)S(1)} collective-permute-done((bf16[256,1024]{1,0:T(8,128)(2,1)S(1)}, bf16[256,1024]{1,0:T(8,128)(2,1)S(1)}, u32[]{:S(2)}, u32[]{:S(2)}) %collective-permute-start.19) | collective-permute-done | bytes 524320 | tf_op jit(solution)/shard_map/ppermute | solution.py:14
  83.3 1.0 shard_map.127
  84.4 1.6 %shard_map.129 = (bf16[512,512]{1,0:T(8,128)(2,1)S(1)}, bf16[4,128,128]{2,1,0:T(8,128)(2,1)S(1)}) custom-call(s32[7]{0:T(128)S(1)} %stack.31.where_ref, bf16[256,1024]{1,0:T(8,128)(2,1)S(1)} %shard_map.125.own, bf16[256,1024]{1,0:T(8,128)(2,1)S(1)} %collective-permute-done.19.got, bf16[160,1024]{1,0:T(8,128)(2,1)S(1)} %get-tuple-element.80.head_ref.head, ...), custom_call_target="tpu_custom_call" | custom-call | tf_op jit(solution)/shard_map/pallas_call | solution.py:234
  86.0 0.3 collective-permute-done.20.got_ref
  86.3 0.6 shard_map.128
  86.9 0.3 collective-permute-start.22
  87.3 1.5 %collective-permute-start.21 = (bf16[128,1024]{1,0:T(8,128)(2,1)S(1)}, bf16[128,1024]{1,0:T(8,128)(2,1)S(1)}, u32[]{:S(2)}, u32[]{:S(2)}) collective-permute-start(bf16[128,1024]{1,0:T(8,128)(2,1)S(1)} %get-tuple-element.106), channel_id=1, source_target_pairs={{0,16},{8,24},{16,0},{24,8},{1,17},{9,25},{17,1},{25,9},{2,18},{10... | collective-permute-start | bytes 786440 | tf_op jit(solution)/shard_map/ppermute | solution.py:14
  88.8 3.2 %shard_map.130 = (f32[512,512]{1,0:T(8,128)S(1)}, f32[512,512]{1,0:T(8,128)S(1)}) custom-call(s32[7]{0:T(128)S(1)} %stack.31.where_ref, bf16[512,512]{1,0:T(8,128)(2,1)S(1)} %get-tuple-element.107.g_ref, bf16[512,512]{1,0:T(8,128)(2,1)S(1)} %bitcast.31, bf16[512,512]{1,0:T(8,128)(2,1)S(1)} %bitcast.21, bf16[512,512]{1,0:T(8,128)(2,1)S(1)} %bitcast.26), custom_call_target="tpu_custom_call" | custom-call | tf_op jit(solution)/shard_map/pallas_call | solution.py:234
  92.0 2.7 %shard_map.131 = bf16[512,512]{1,0:T(8,128)(2,1)} custom-call(s32[7]{0:T(128)S(1)} %stack.31.where_ref, bf16[512,512]{1,0:T(8,128)(2,1)S(1)} %get-tuple-element.107.g_ref, bf16[512,512]{1,0:T(8,128)(2,1)S(1)} %bitcast.22, bf16[512,512]{1,0:T(8,128)(2,1)S(1)} %bitcast.27, bf16[4,128,128]{2,1,0:T(8,128)(2,1)S(1)} %copy-done.5), custom_call_target="tpu_custom_call" | custom-call | tf_op jit(solution)/shard_map/pallas_call | solution.py:234
  94.8 1.0 collective-permute-done.21.got_ref
  95.7 0.6 shard_map.132
  96.4 5.3 %collective-permute-start.23 = (bf16[128,256]{1,0:T(8,128)(2,1)S(1)}, bf16[128,256]{1,0:T(8,128)(2,1)S(1)}, u32[]{:S(2)}, u32[]{:S(2)}) collective-permute-start(bf16[128,256]{1,0:T(8,128)(2,1)S(1)} %get-tuple-element.119), channel_id=1, source_target_pairs={{0,3},{1,2},{2,1},{3,0},{4,7},{5,6},{6,5},{7,4},{8,11},{9,10},{10,... | collective-permute-start | bytes 196616 | tf_op jit(solution)/shard_map/ppermute | solution.py:14
  101.7 1.7 %collective-permute-start.29 = (bf16[4,128,128]{2,1,0:T(8,128)(2,1)S(1)}, bf16[4,128,128]{2,1,0:T(8,128)(2,1)S(1)}, u32[]{:S(2)}, u32[]{:S(2)}) collective-permute-start(bf16[4,128,128]{2,1,0:T(8,128)(2,1)S(1)} %add_convert_fusion), channel_id=1, source_target_pairs={{0,16},{8,24},{16,0},{24,8},{1,17},{9,25},{17,1},{25,9},{2,18},{10... | collective-permute-start | bytes 393224 | tf_op jit(solution)/shard_map/ppermute | solution.py:14
  103.4 0.6 collective-permute-start.25
  104.0 0.4 collective-permute-done.23.refs_0_
  104.4 3.0 %collective-permute-done.24.refs_1_ = bf16[128,256]{1,0:T(8,128)(2,1)S(1)} collective-permute-done((bf16[128,256]{1,0:T(8,128)(2,1)S(1)}, bf16[128,256]{1,0:T(8,128)(2,1)S(1)}, u32[]{:S(2)}, u32[]{:S(2)}) %collective-permute-start.24) | collective-permute-done | bytes 65568 | tf_op jit(solution)/shard_map/ppermute | solution.py:14
  107.4 0.7 collective-permute-done.25.refs_2_
  108.0 0.6 shard_map.133.refs_0_
  108.6 1.2 %collective-permute-start.26 = (bf16[128,256]{1,0:T(8,128)(2,1)S(1)}, bf16[128,256]{1,0:T(8,128)(2,1)S(1)}, u32[]{:S(2)}, u32[]{:S(2)}) collective-permute-start(bf16[128,256]{1,0:T(8,128)(2,1)S(1)} %shard_map.133.refs_0_), channel_id=1, source_target_pairs={{0,16},{8,24},{16,0},{24,8},{1,17},{9,25},{17,1},{25,9},{2,18},{10... | collective-permute-start | bytes 196616 | tf_op jit(solution)/shard_map/ppermute | solution.py:14
  109.8 1.0 collective-permute-start.28
  110.8 2.0 %shard_map.134 = (bf16[512,512]{1,0:T(8,128)(2,1)}, bf16[512,512]{1,0:T(8,128)(2,1)}) custom-call(s32[7]{0:T(128)S(1)} %stack.31.where_ref, f32[512,512]{1,0:T(8,128)S(1)} %get-tuple-element.123.kp_ref, f32[512,512]{1,0:T(8,128)S(1)} %get-tuple-element.124.vp_ref, bf16[512,512]{1,0:T(8,128)(2,1)S(1)} %bitcast.23, bf16[512,512]{1,0:T(8,128)(2,1)S(1)} %bitcast.28, ...), custom_call_target="tpu_custom_call" | custom-call | tf_op jit(solution)/shard_map/pallas_call | solution.py:234
  112.8 0.3 collective-permute-done.26.refs_1_
  113.1 0.7 collective-permute-done.28.refs_3_
  113.8 1.4 %shard_map.135 = f32[512,256]{1,0:T(8,128)} custom-call(s32[7]{0:T(128)S(1)} %stack.31.where_ref, bf16[128,256]{1,0:T(8,128)(2,1)S(1)} %shard_map.133.refs_0_, bf16[128,256]{1,0:T(8,128)(2,1)S(1)} %collective-permute-done.26.refs_1_, bf16[128,256]{1,0:T(8,128)(2,1)S(1)} %collective-permute-done.27.refs_2_, bf16[128,256]{1,0:T(8,128)(2,1)S(1)} %collective-permute-done.28.refs_3_), custom_call_target="tpu_custom_call" | custom-call | tf_op jit(solution)/shard_map/pallas_call | solution.py:234
  (42 shorter events, 0.8 us)
Async XLA Ops:
  0.6 10.0 %copy-start = (bf16[1,512,512]{2,1,0:T(8,128)(2,1)S(1)}, bf16[1,512,512]{2,1,0:T(8,128)(2,1)}, u32[]{:S(2)}) copy-start(bf16[1,512,512]{2,1,0:T(8,128)(2,1)} %param.9) | copy-start | bytes 1572868
  0.6 10.0 %copy-start.1 = (bf16[1,512,512]{2,1,0:T(8,128)(2,1)S(1)}, bf16[1,512,512]{2,1,0:T(8,128)(2,1)}, u32[]{:S(2)}) copy-start(bf16[1,512,512]{2,1,0:T(8,128)(2,1)} %param.10) | copy-start | bytes 1572868
  0.7 10.0 %copy-start.6 = (s32[1,256,2]{1,2,0:T(2,128)S(1)}, s32[1,256,2]{1,2,0:T(2,128)}, u32[]{:S(2)}) copy-start(s32[1,256,2]{1,2,0:T(2,128)} %param.14) | copy-start | bytes 6148
  2.5 17.1 %copy-start.2 = (bf16[1,512,512]{2,1,0:T(8,128)(2,1)S(1)}, bf16[1,512,512]{2,1,0:T(8,128)(2,1)}, u32[]{:S(2)}) copy-start(bf16[1,512,512]{2,1,0:T(8,128)(2,1)} %param.8) | copy-start | bytes 1572868
  2.5 26.2 %all-to-all-start = ((bf16[4,256,256]{2,1,0:T(8,128)(2,1)}), bf16[4,256,256]{2,1,0:T(8,128)(2,1)S(1)}, u32[]{:S(2)}, u32[]{:S(2)}) async-start(bf16[4,256,256]{2,1,0:T(8,128)(2,1)} %shard_map.111.refs_2_), calls=%async_computation | async-start | bytes 1048576 | tf_op jit(solution)/shard_map/all_to_all | solution.py:793
  10.6 26.5 %copy-start.3 = (bf16[384,256]{1,0:T(8,128)(2,1)S(1)}, bf16[384,256]{1,0:T(8,128)(2,1)}, u32[]{:S(2)}) copy-start(bf16[384,256]{1,0:T(8,128)(2,1)} %shard_map.112.refs_0_) | copy-start | bytes 589828
  11.6 1.4 %collective-permute-start = (bf16[528,128]{1,0:T(8,128)(2,1)S(1)}, bf16[528,128]{1,0:T(8,128)(2,1)S(1)}, u32[]{:S(2)}, u32[]{:S(2)}) collective-permute-start(bf16[528,128]{1,0:T(8,128)(2,1)S(1)} %shard_map.113.own_ref.mine_ref), channel_id=1, source_target_pairs={{0,8},{8,0},{16,24},{24,16},{1,9},{9,1},{17,25},{25,17},{2,10},{10... | collective-permute-start | bytes 405512 | tf_op jit(solution)/shard_map/ppermute | solution.py:14
  13.6 6.0 %collective-permute-start.1 = (bf16[544,128]{1,0:T(8,128)(2,1)S(1)}, bf16[544,128]{1,0:T(8,128)(2,1)S(1)}, u32[]{:S(2)}, u32[]{:S(2)}) collective-permute-start(bf16[544,128]{1,0:T(8,128)(2,1)S(1)} %shard_map.114), channel_id=1, source_target_pairs={{0,16},{8,24},{16,0},{24,8},{1,17},{9,25},{17,1},{25,9},{2,18},{10... | collective-permute-start | bytes 417800 | tf_op jit(solution)/shard_map/ppermute | solution.py:14
  15.2 21.9 %collective-permute-start.3 = (bf16[384,256]{1,0:T(8,128)(2,1)}, bf16[384,256]{1,0:T(8,128)(2,1)S(1)}, u32[]{:S(2)}, u32[]{:S(2)}) collective-permute-start(bf16[384,256]{1,0:T(8,128)(2,1)} %shard_map.112.refs_0_), channel_id=1, source_target_pairs={{0,2},{1,3},{2,0},{3,1},{4,6},{5,7},{6,4},{7,5},{8,10},{9,11},{10,... | collective-permute-start | bytes 589832 | tf_op jit(solution)/shard_map/ppermute | solution.py:14
  18.1 19.0 %collective-permute-start.4 = (bf16[384,256]{1,0:T(8,128)(2,1)}, bf16[384,256]{1,0:T(8,128)(2,1)}, u32[]{:S(2)}, u32[]{:S(2)}) collective-permute-start(bf16[384,256]{1,0:T(8,128)(2,1)} %shard_map.112.refs_0_), channel_id=1, source_target_pairs={{0,1},{1,0},{2,3},{3,2},{4,5},{5,4},{6,7},{7,6},{8,9},{9,8},{10,11... | collective-permute-start | bytes 589832 | tf_op jit(solution)/shard_map/ppermute | solution.py:14
  19.6 17.6 %collective-permute-start.5 = (bf16[384,256]{1,0:T(8,128)(2,1)}, bf16[384,256]{1,0:T(8,128)(2,1)}, u32[]{:S(2)}, u32[]{:S(2)}) collective-permute-start(bf16[384,256]{1,0:T(8,128)(2,1)} %shard_map.112.refs_0_), channel_id=1, source_target_pairs={{0,3},{1,2},{2,1},{3,0},{4,7},{5,6},{6,5},{7,4},{8,11},{9,10},{10,... | collective-permute-start | bytes 589832 | tf_op jit(solution)/shard_map/ppermute | solution.py:14
  21.5 0.7 copy-start.4
  29.3 11.4 %collective-permute-start.2 = (bf16[1024,256]{1,0:T(8,128)(2,1)S(1)}, bf16[1024,256]{1,0:T(8,128)(2,1)S(1)}, u32[]{:S(2)}, u32[]{:S(2)}) collective-permute-start(bf16[1024,256]{1,0:T(8,128)(2,1)S(1)} %get-tuple-element.74.own_ref), channel_id=1, source_target_pairs={{0,4},{4,0},{1,5},{5,1},{2,6},{6,2},{3,7},{7,3},{8,12},{12,8},{9,1... | collective-permute-start | bytes 1572872 | tf_op jit(solution)/shard_map/ppermute | solution.py:14
  30.9 6.2 %collective-permute-start.6 = (bf16[368,256]{1,0:T(8,128)(2,1)S(1)}, bf16[368,256]{1,0:T(8,128)(2,1)S(1)}, u32[]{:S(2)}, u32[]{:S(2)}) collective-permute-start(bf16[368,256]{1,0:T(8,128)(2,1)S(1)} %get-tuple-element.75), channel_id=1, source_target_pairs={{0,16},{8,24},{16,0},{24,8},{1,17},{9,25},{17,1},{25,9},{2,18},{10... | collective-permute-start | bytes 565256 | tf_op jit(solution)/shard_map/ppermute | solution.py:14
  38.2 2.1 %collective-permute-start.7 = (bf16[160,1024]{1,0:T(8,128)(2,1)S(1)}, bf16[160,1024]{1,0:T(8,128)(2,1)S(1)}, u32[]{:S(2)}, u32[]{:S(2)}) collective-permute-start(bf16[160,1024]{1,0:T(8,128)(2,1)S(1)} %get-tuple-element.80.head_ref.head), channel_id=1, source_target_pairs={{0,8},{8,0},{16,24},{24,16},{1,9},{9,1},{17,25},{25,17},{2,10},{10... | collective-permute-start | bytes 983048 | tf_op jit(solution)/shard_map/ppermute | solution.py:14
  38.3 6.0 %collective-permute-start.10 = (bf16[96,1024]{1,0:T(8,128)(2,1)S(1)}, bf16[96,1024]{1,0:T(8,128)(2,1)S(1)}, u32[]{:S(2)}, u32[]{:S(2)}) collective-permute-start(bf16[96,1024]{1,0:T(8,128)(2,1)S(1)} %get-tuple-element.84.tail_ref.tail), channel_id=1, source_target_pairs={{0,8},{8,0},{16,24},{24,16},{1,9},{9,1},{17,25},{25,17},{2,10},{10... | collective-permute-start | bytes 589832 | tf_op jit(solution)/shard_map/ppermute | solution.py:14
  38.8 8.3 %collective-permute-start.9 = (bf16[512,256]{1,0:T(8,128)(2,1)S(1)}, bf16[512,256]{1,0:T(8,128)(2,1)S(1)}, u32[]{:S(2)}, u32[]{:S(2)}) collective-permute-start(bf16[512,256]{1,0:T(8,128)(2,1)S(1)} %get-tuple-element.81.own_ref), channel_id=1, source_target_pairs={{0,4},{4,0},{1,5},{5,1},{2,6},{6,2},{3,7},{7,3},{8,12},{12,8},{9,1... | collective-permute-start | bytes 786440 | tf_op jit(solution)/shard_map/ppermute | solution.py:14
  41.9 20.5 %collective-permute-start.8 = (bf16[1168,256]{1,0:T(8,128)(2,1)S(1)}, bf16[1168,256]{1,0:T(8,128)(2,1)S(1)}, u32[]{:S(2)}, u32[]{:S(2)}) collective-permute-start(bf16[1168,256]{1,0:T(8,128)(2,1)S(1)} %shard_map.118), channel_id=1, source_target_pairs={{0,16},{8,24},{16,0},{24,8},{1,17},{9,25},{17,1},{25,9},{2,18},{10... | collective-permute-start | bytes 1794056 | tf_op jit(solution)/shard_map/ppermute | solution.py:14
  45.2 17.2 %collective-permute-start.12 = (bf16[256,1024]{1,0:T(8,128)(2,1)S(1)}, bf16[256,1024]{1,0:T(8,128)(2,1)S(1)}, u32[]{:S(2)}, u32[]{:S(2)}) collective-permute-start(bf16[256,1024]{1,0:T(8,128)(2,1)S(1)} %shard_map.121), channel_id=1, source_target_pairs={{0,4},{4,0},{1,5},{5,1},{2,6},{6,2},{3,7},{7,3},{8,12},{12,8},{9,1... | collective-permute-start | bytes 1572872 | tf_op jit(solution)/shard_map/ppermute | solution.py:14
  46.7 6.0 %collective-permute-start.13 = (bf16[512,256]{1,0:T(8,128)(2,1)S(1)}, bf16[512,256]{1,0:T(8,128)(2,1)S(1)}, u32[]{:S(2)}, u32[]{:S(2)}) collective-permute-start(bf16[512,256]{1,0:T(8,128)(2,1)S(1)} %get-tuple-element.73.refs_0_), channel_id=1, source_target_pairs={{0,8},{8,0},{16,24},{24,16},{1,9},{9,1},{17,25},{25,17},{2,10},{10... | collective-permute-start | bytes 786440 | tf_op jit(solution)/shard_map/ppermute | solution.py:14
  48.0 15.0 %copy-start.7 = (bf16[1,256,2,1024]{3,2,1,0:T(2,128)(2,1)S(1)}, bf16[1,256,2,1024]{3,2,1,0:T(2,128)(2,1)}, u32[]{:S(2)}) copy-start(bf16[1,256,2,1024]{3,2,1,0:T(2,128)(2,1)} %param.15) | copy-start | bytes 3145732
  50.2 12.1 %collective-permute-start.15 = (bf16[768,256]{1,0:T(8,128)(2,1)S(1)}, bf16[768,256]{1,0:T(8,128)(2,1)S(1)}, u32[]{:S(2)}, u32[]{:S(2)}) collective-permute-start(bf16[768,256]{1,0:T(8,128)(2,1)S(1)} %get-tuple-element.91), channel_id=1, source_target_pairs={{0,8},{8,0},{16,24},{24,16},{1,9},{9,1},{17,25},{25,17},{2,10},{10... | collective-permute-start | bytes 1179656 | tf_op jit(solution)/shard_map/ppermute | solution.py:14
  50.4 11.9 %collective-permute-start.11 = (bf16[512,256]{1,0:T(8,128)(2,1)S(1)}, bf16[512,256]{1,0:T(8,128)(2,1)S(1)}, u32[]{:S(2)}, u32[]{:S(2)}) collective-permute-start(bf16[512,256]{1,0:T(8,128)(2,1)S(1)} %shard_map.122), channel_id=1, source_target_pairs={{0,16},{8,24},{16,0},{24,8},{1,17},{9,25},{17,1},{25,9},{2,18},{10... | collective-permute-start | bytes 786440 | tf_op jit(solution)/shard_map/ppermute | solution.py:14
  52.8 1.4 %collective-permute-start.14 = (bf16[368,256]{1,0:T(8,128)(2,1)S(1)}, bf16[368,256]{1,0:T(8,128)(2,1)S(1)}, u32[]{:S(2)}, u32[]{:S(2)}) collective-permute-start(bf16[368,256]{1,0:T(8,128)(2,1)S(1)} %collective-permute-done.6.refs_2_), channel_id=1, source_target_pairs={{0,8},{8,0},{16,24},{24,16},{1,9},{9,1},{17,25},{25,17},{2,10},{10... | collective-permute-start | bytes 565256 | tf_op jit(solution)/shard_map/ppermute | solution.py:14
  62.3 2.6 %collective-permute-start.16 = (bf16[1168,256]{1,0:T(8,128)(2,1)S(1)}, bf16[1168,256]{1,0:T(8,128)(2,1)S(1)}, u32[]{:S(2)}, u32[]{:S(2)}) collective-permute-start(bf16[1168,256]{1,0:T(8,128)(2,1)S(1)} %collective-permute-done.8.refs_3_), channel_id=1, source_target_pairs={{0,8},{8,0},{16,24},{24,16},{1,9},{9,1},{17,25},{25,17},{2,10},{10... | collective-permute-start | bytes 1794056 | tf_op jit(solution)/shard_map/ppermute | solution.py:14
  62.4 2.6 %collective-permute-start.18 = (bf16[512,256]{1,0:T(8,128)(2,1)S(1)}, bf16[512,256]{1,0:T(8,128)(2,1)S(1)}, u32[]{:S(2)}, u32[]{:S(2)}) collective-permute-start(bf16[512,256]{1,0:T(8,128)(2,1)S(1)} %collective-permute-done.11.refs_10_), channel_id=1, source_target_pairs={{0,8},{8,0},{16,24},{24,16},{1,9},{9,1},{17,25},{25,17},{2,10},{10... | collective-permute-start | bytes 786440 | tf_op jit(solution)/shard_map/ppermute | solution.py:14
  62.9 2.1 %collective-permute-start.17 = (bf16[256,256]{1,0:T(8,128)(2,1)S(1)}, bf16[256,256]{1,0:T(8,128)(2,1)S(1)}, u32[]{:S(2)}, u32[]{:S(2)}) collective-permute-start(bf16[256,256]{1,0:T(8,128)(2,1)S(1)} %get-tuple-element.102), channel_id=1, source_target_pairs={{0,8},{8,0},{16,24},{24,16},{1,9},{9,1},{17,25},{25,17},{2,10},{10... | collective-permute-start | bytes 393224 | tf_op jit(solution)/shard_map/ppermute | solution.py:14
  69.3 14.0 %collective-permute-start.19 = (bf16[256,1024]{1,0:T(8,128)(2,1)S(1)}, bf16[256,1024]{1,0:T(8,128)(2,1)S(1)}, u32[]{:S(2)}, u32[]{:S(2)}) collective-permute-start(bf16[256,1024]{1,0:T(8,128)(2,1)S(1)} %shard_map.125.own), channel_id=1, source_target_pairs={{0,4},{4,0},{1,5},{5,1},{2,6},{6,2},{3,7},{7,3},{8,12},{12,8},{9,1... | collective-permute-start | bytes 1572872 | tf_op jit(solution)/shard_map/ppermute | solution.py:14
  84.3 2.0 %collective-permute-start.20 = (bf16[2,128,1024]{2,1,0:T(8,128)(2,1)S(1)}, bf16[2,128,1024]{2,1,0:T(8,128)(2,1)S(1)}, u32[]{:S(2)}, u32[]{:S(2)}) collective-permute-start(bf16[2,128,1024]{2,1,0:T(8,128)(2,1)S(1)} %get-tuple-element.105), channel_id=1, source_target_pairs={{0,8},{8,0},{16,24},{24,16},{1,9},{9,1},{17,25},{25,17},{2,10},{10... | collective-permute-start | bytes 1572872 | tf_op jit(solution)/shard_map/ppermute | solution.py:14
  86.0 5.9 %copy-start.5 = (bf16[4,128,128]{2,1,0:T(8,128)(2,1)S(1)}, bf16[4,128,128]{2,1,0:T(8,128)(2,1)}, u32[]{:S(2)}) copy-start(bf16[4,128,128]{2,1,0:T(8,128)(2,1)} %copy-done.4) | copy-start | bytes 393220
  86.9 7.8 %collective-permute-start.22 = (bf16[4,128,128]{2,1,0:T(8,128)(2,1)S(1)}, bf16[4,128,128]{2,1,0:T(8,128)(2,1)S(1)}, u32[]{:S(2)}, u32[]{:S(2)}) collective-permute-start(bf16[4,128,128]{2,1,0:T(8,128)(2,1)S(1)} %get-tuple-element.112), channel_id=1, source_target_pairs={{0,8},{8,0},{16,24},{24,16},{1,9},{9,1},{17,25},{25,17},{2,10},{10... | collective-permute-start | bytes 393224 | tf_op jit(solution)/shard_map/ppermute | solution.py:14
  87.3 8.5 %collective-permute-start.21 = (bf16[128,1024]{1,0:T(8,128)(2,1)S(1)}, bf16[128,1024]{1,0:T(8,128)(2,1)S(1)}, u32[]{:S(2)}, u32[]{:S(2)}) collective-permute-start(bf16[128,1024]{1,0:T(8,128)(2,1)S(1)} %get-tuple-element.106), channel_id=1, source_target_pairs={{0,16},{8,24},{16,0},{24,8},{1,17},{9,25},{17,1},{25,9},{2,18},{10... | collective-permute-start | bytes 786440 | tf_op jit(solution)/shard_map/ppermute | solution.py:14
  96.4 8.0 %collective-permute-start.23 = (bf16[128,256]{1,0:T(8,128)(2,1)S(1)}, bf16[128,256]{1,0:T(8,128)(2,1)S(1)}, u32[]{:S(2)}, u32[]{:S(2)}) collective-permute-start(bf16[128,256]{1,0:T(8,128)(2,1)S(1)} %get-tuple-element.119), channel_id=1, source_target_pairs={{0,3},{1,2},{2,1},{3,0},{4,7},{5,6},{6,5},{7,4},{8,11},{9,10},{10,... | collective-permute-start | bytes 196616 | tf_op jit(solution)/shard_map/ppermute | solution.py:14
  101.6 5.8 %collective-permute-start.24 = (bf16[128,256]{1,0:T(8,128)(2,1)S(1)}, bf16[128,256]{1,0:T(8,128)(2,1)S(1)}, u32[]{:S(2)}, u32[]{:S(2)}) collective-permute-start(bf16[128,256]{1,0:T(8,128)(2,1)S(1)} %get-tuple-element.120), channel_id=1, source_target_pairs={{0,2},{1,3},{2,0},{3,1},{4,6},{5,7},{6,4},{7,5},{8,10},{9,11},{10,... | collective-permute-start | bytes 196616 | tf_op jit(solution)/shard_map/ppermute | solution.py:14
  101.7 9.1 %collective-permute-start.29 = (bf16[4,128,128]{2,1,0:T(8,128)(2,1)S(1)}, bf16[4,128,128]{2,1,0:T(8,128)(2,1)S(1)}, u32[]{:S(2)}, u32[]{:S(2)}) collective-permute-start(bf16[4,128,128]{2,1,0:T(8,128)(2,1)S(1)} %add_convert_fusion), channel_id=1, source_target_pairs={{0,16},{8,24},{16,0},{24,8},{1,17},{9,25},{17,1},{25,9},{2,18},{10... | collective-permute-start | bytes 393224 | tf_op jit(solution)/shard_map/ppermute | solution.py:14
  103.4 4.7 %collective-permute-start.25 = (bf16[128,256]{1,0:T(8,128)(2,1)S(1)}, bf16[128,256]{1,0:T(8,128)(2,1)S(1)}, u32[]{:S(2)}, u32[]{:S(2)}) collective-permute-start(bf16[128,256]{1,0:T(8,128)(2,1)S(1)} %get-tuple-element.121), channel_id=1, source_target_pairs={{0,1},{1,0},{2,3},{3,2},{4,5},{5,4},{6,7},{7,6},{8,9},{9,8},{10,11... | collective-permute-start | bytes 196616 | tf_op jit(solution)/shard_map/ppermute | solution.py:14
  108.6 4.5 %collective-permute-start.26 = (bf16[128,256]{1,0:T(8,128)(2,1)S(1)}, bf16[128,256]{1,0:T(8,128)(2,1)S(1)}, u32[]{:S(2)}, u32[]{:S(2)}) collective-permute-start(bf16[128,256]{1,0:T(8,128)(2,1)S(1)} %shard_map.133.refs_0_), channel_id=1, source_target_pairs={{0,16},{8,24},{16,0},{24,8},{1,17},{9,25},{17,1},{25,9},{2,18},{10... | collective-permute-start | bytes 196616 | tf_op jit(solution)/shard_map/ppermute | solution.py:14
  109.8 3.3 %collective-permute-start.27 = (bf16[128,256]{1,0:T(8,128)(2,1)S(1)}, bf16[128,256]{1,0:T(8,128)(2,1)S(1)}, u32[]{:S(2)}, u32[]{:S(2)}) collective-permute-start(bf16[128,256]{1,0:T(8,128)(2,1)S(1)} %shard_map.133.refs_0_), channel_id=1, source_target_pairs={{0,8},{8,0},{16,24},{24,16},{1,9},{9,1},{17,25},{25,17},{2,10},{10... | collective-permute-start | bytes 196616 | tf_op jit(solution)/shard_map/ppermute | solution.py:14
  109.8 4.0 %collective-permute-start.28 = (bf16[128,256]{1,0:T(8,128)(2,1)S(1)}, bf16[128,256]{1,0:T(8,128)(2,1)S(1)}, u32[]{:S(2)}, u32[]{:S(2)}) collective-permute-start(bf16[128,256]{1,0:T(8,128)(2,1)S(1)} %shard_map.133.refs_0_), channel_id=1, source_target_pairs={{0,24},{8,16},{16,8},{24,0},{1,25},{9,17},{17,9},{25,1},{2,26},{10... | collective-permute-start | bytes 196616 | tf_op jit(solution)/shard_map/ppermute | solution.py:14
